TPU v7x, 256 devices: a whole 4x4x8 slice. The times are simulated.
256 devices in a mesh: row: 8 (over x, y_lo), col: 32 (over y_hi, z, core).
Axes of the slice: x: 4, y: 4 (y_hi: 2, y_lo: 2; y = y_hi * 2 + y_lo), z: 8, core: 2. Of those that a mesh axis runs over, the one named last changes fastest.
Arguments:
- scores: float32 [65536, 256], P(('row', 'col')), may hold values from 0.2 to 2, as said below
- tile_values: bfloat16 [24576, 128, 128], P(('row', 'col')), as said below
- tile_rows: int32 [24576], P(('row', 'col')), may hold values from 0 to 511, as said below
- tile_cols: int32 [24576], P(('row', 'col')), may hold values from 0 to 511, as said below
- tile_count: int32 [256], P(('row', 'col')), may hold values from 48 to 96, as said below
- seed_ids: int32 [256, 1024], replicated, may hold values from 0 to 65535
Outputs:
- ranks: float32 [65536, 256], P(('row', 'col'))
Inputs may be any that keep to these rules, and one draw needn't show every extreme that they name: Device d = r * 32 + c has its tiles in slots d * 96 to d * 96 + tile_count[d] - 1; some device has all 96 slots in use. Every slot of device (r, c) has (tile_rows // 2) % 32 == c; coordinates may repeat, and tiles at equal coordinates add. Every slot of device (r, c) has tile_cols // 64 == r; on each device the active slots are in nondecreasing order of tile_cols. `tile_values`: entries are positive. `scores`: entries are positive.
All inputs are finite; a program needn't handle non-finite values.
Results may differ from a plain program's by a relative error of at most 0.0004.
Values may be sent and summed in bfloat16 or wider, within the bound.
No kernel may reach another device: no remote copies, remote signals or barrier semaphores. Data moves between devices by JAX's collectives and lax.ppermute only.
A program may use at most 64 MiB of HBM per device.

v0:
```python
import jax
import jax.numpy as jnp
from jax import lax
from jax.sharding import PartitionSpec as P

BT = 2
ITERS = 2


damping = 0.85
teleport = 0.15


def tile_products(
    partial_value, tile_values, targets, sources, panels, first_tile, start_slot, end_slot
):
    slot_total = tile_values.shape[0]
    group_size = min(32, slot_total)
    tile_size = tile_values.shape[1]
    columns = panels.shape[2]
    piece_tiles = panels.shape[0]
    dest_blocks = partial_value.shape[0]
    flat_panels = panels.reshape(piece_tiles, tile_size * columns)
    rounds = (end_slot - start_slot + group_size - 1) // group_size

    def tile_block(number, summed):
        wanted_start = start_slot + number * group_size
        block_start = jnp.minimum(wanted_start, slot_total - group_size)
        slot_ids = block_start + jnp.arange(group_size, dtype=jnp.int32)
        live = (slot_ids >= wanted_start) & (slot_ids < end_slot)
        block_tiles = lax.dynamic_slice_in_dim(tile_values, block_start, group_size, 0)
        block_sources = lax.dynamic_slice_in_dim(sources, block_start, group_size, 0) - first_tile
        block_targets = lax.dynamic_slice_in_dim(targets, block_start, group_size, 0)
        pick = (block_sources[:, None] == jnp.arange(piece_tiles, dtype=jnp.int32)[None, :]).astype(
            jnp.bfloat16
        )
        gathered = jnp.dot(pick, flat_panels, preferred_element_type=jnp.float32)
        gathered = gathered.astype(jnp.bfloat16).reshape(group_size, tile_size, columns)
        products = jnp.einsum(
            "kab,kbs->kas", block_tiles, gathered, preferred_element_type=jnp.float32
        )
        place = (
            (block_targets[:, None] == jnp.arange(dest_blocks, dtype=jnp.int32)[None, :])
            & live[:, None]
        ).astype(jnp.float32)
        added = jnp.einsum(
            "kt,kas->tas",
            place,
            products,
            precision=lax.Precision.HIGHEST,
            preferred_element_type=jnp.float32,
        )
        return summed + added

    return lax.fori_loop(0, rounds, tile_block, partial_value)


def per_device(scores, tile_values, tile_rows, tile_cols, tile_count, seed_ids):
    tile_size = tile_values.shape[1]
    columns = seed_ids.shape[0]
    seed_total = seed_ids.shape[1]
    grid_rows = lax.axis_size("row")
    grid_cols = lax.axis_size("col")
    row_index = lax.axis_index("row")
    col_index = lax.axis_index("col")
    band_tiles = grid_cols * BT
    own_rows = BT * tile_size
    sources = tile_cols - row_index * band_tiles
    targets = tile_rows // band_tiles * BT + tile_rows % BT
    live_count = tile_count[0]
    active = jnp.arange(tile_values.shape[0], dtype=jnp.int32) < live_count
    tile_sums = jnp.sum(tile_values, axis=1, dtype=jnp.float32)
    member = (
        (sources[:, None] == jnp.arange(band_tiles, dtype=jnp.int32)[None, :]) & active[:, None]
    ).astype(jnp.float32)
    column_part = jnp.dot(
        member.T, tile_sums, precision=lax.Precision.HIGHEST, preferred_element_type=jnp.float32
    ).reshape(band_tiles * tile_size)
    totals = lax.psum(column_part, "col")
    own_totals = lax.dynamic_slice_in_dim(totals, col_index * own_rows, own_rows)
    inverse = 1.0 / jnp.maximum(own_totals, 1.0)
    first_vertex = (row_index * grid_cols + col_index) * own_rows
    local_ids = seed_ids - first_vertex
    seed_block = min(128, seed_total)
    page_range = jnp.arange(own_rows, dtype=jnp.int32)

    def count_seeds(number, counted):
        block_ids = lax.dynamic_slice_in_dim(local_ids, number * seed_block, seed_block, 1)
        equal = (block_ids[:, :, None] == page_range[None, None, :]).astype(jnp.float32)
        return counted + jnp.sum(equal, axis=1).T

    restart = lax.fori_loop(
        0, seed_total // seed_block, count_seeds, jnp.zeros((own_rows, columns), jnp.float32)
    )
    current = scores
    for sweep in range(ITERS):
        panel_own = (current * inverse[:, None]).astype(jnp.bfloat16)
        zero_sums = jnp.zeros((grid_rows * BT, tile_size, columns), jnp.float32)
        band_panel = lax.all_gather(panel_own, "col", axis=0, tiled=True)
        summed = tile_products(
            zero_sums,
            tile_values,
            targets,
            sources,
            band_panel.reshape(band_tiles, tile_size, columns),
            0,
            0,
            live_count,
        )
        reduced = lax.psum_scatter(
            summed.reshape(grid_rows * BT * tile_size, columns),
            "row",
            scatter_dimension=0,
            tiled=True,
        )
        current = damping * reduced + teleport * restart
    return current


def solution(mesh):
    placed = (
        P(("row", "col"), None),
        P(("row", "col"), None, None),
        P(("row", "col")),
        P(("row", "col")),
        P(("row", "col")),
        P(),
    )
    return jax.shard_map(
        per_device, mesh=mesh, in_specs=placed, out_specs=P(("row", "col"), None), check_vma=False
    )
```

profile of v0, /device:TPU:1, one launch (start us, length us, event | category | flops | bytes accessed | tf_op | source)
XLA Modules:
  0.0 514.9 jit_solution(8946702192114800121)
XLA Ops:
  7.3 2.8 convert_reduce_fusion.1
  10.4 131.9 %psum.7 = f32[8192]{0:T(1024)S(1)} all-reduce(f32[8192]{0:T(1024)S(1)} %convolution_bitcast_fusion), channel_id=1, replica_groups=mesh['row'=8,'col'=32] {'col'}, use_global_device_ids=true, to_apply=%region_1.2 | all-reduce | flops 8192 | bytes 65536 | tf_op jit(solution)/shard_map/psum | solution.py:79
  142.4 0.8 multiply_convert_fusion.1
  143.5 86.7 %all-gather.3.cloned.1.call-done = bf16[8192,256]{1,0:T(8,128)(2,1)} async-done(((bf16[256,256]{1,0:T(8,128)(2,1)}), bf16[8192,256]{1,0:T(8,128)(2,1)}) %all-gather.3.cloned.1.call-update) | async-done | bytes 4194320 | tf_op jit(solution)/shard_map/all_gather | solution.py:99
  230.2 7.4 %reshape_reshape.6 = bf16[64,32768]{1,0:T(8,128)(2,1)} reshape(bf16[8192,256]{1,0:T(8,128)(2,1)} %all-gather.3.cloned.1.call-done) | data formatting | bytes 8388608 | tf_op jit(solution)/shard_map/reshape;reshape | solution.py:23
  237.8 32.9 %while.34 = (s32[]{:T(128)}, f32[16,128,256]{2,0,1:T(8,128)S(1)}, s32[]{:T(128)}, s32[96]{0:T(128)S(1)}, s32[]{:T(128)}, /*index=5*/bf16[96,128,128]{2,1,0:T(8,1...) while((s32[]{:T(128)}, f32[16,128,256]{2,0,1:T(8,128)S(1)}, ...), condition=%wide.region_3.4_spmd, body=%wide.region_2.3_spmd.sunk | while | flops 605555840 | bytes 26215440 | solution.py:55
  237.9 2.9 convolution_convert_fusion.4
  241.3 1.9 fusion.59
  243.4 0.7 compare_and_fusion.4
  244.0 4.7 fusion.60
  248.9 2.9 convolution_convert_fusion.4
  252.3 1.9 fusion.59
  254.3 0.7 compare_and_fusion.4
  255.0 4.7 fusion.60
  259.8 2.9 convolution_convert_fusion.4
  263.2 1.9 fusion.59
  265.3 0.7 compare_and_fusion.4
  265.9 4.7 fusion.60
  270.7 2.5 copy.9
  273.3 46.7 %while.36 = (s32[]{:T(128)}, f32[256,256]{0,1:T(8,128)S(1)}, s32[256,1024]{1,0:T(8,128)S(1)}, s32[]{:T(128)}, s32[]{:T(128)}, /*index=5*/s32[]{:T(128)}, s32[]{:T(128)}) while((s32[]{:T(128)}, f32[256,256]{0,1:T(8,128)S(1)}, s32[256,1024]{1,0:T(8,128)S(1)}, s32[]{:T(128)}, s32[]{:T(128)}, /*index=5*/s32[]{:T(128)}, s32[]{:T(128)}) %tuple.61), condition=%wide.region_7.8_spmd.clone, body=%wide.region_5.7_spmd.clone.sunk | while | flops 25231364 | bytes 1441929 | solution.py:92
  273.3 5.7 %convert_reduce_fusion.3 = f32[256,256]{1,0:T(8,128)S(1)} fusion(s32[256,128]{1,0:T(8,128)S(1)} %constant_dynamic-slice_fusion.2), kind=kLoop, calls=%fused_computation.32.clone.1 | loop fusion | flops 25100288 | bytes 393216 | tf_op jit(solution)/shard_map/while/body/eval_jaxpr/reduce_sum | solution.py:90
  279.2 5.7 %convert_reduce_fusion.3 = f32[256,256]{1,0:T(8,128)S(1)} fusion(s32[256,128]{1,0:T(8,128)S(1)} %constant_dynamic-slice_fusion.2), kind=kLoop, calls=%fused_computation.32.clone.1 | loop fusion | flops 25100288 | bytes 393216 | tf_op jit(solution)/shard_map/while/body/eval_jaxpr/reduce_sum | solution.py:90
  285.0 5.7 %convert_reduce_fusion.3 = f32[256,256]{1,0:T(8,128)S(1)} fusion(s32[256,128]{1,0:T(8,128)S(1)} %constant_dynamic-slice_fusion.2), kind=kLoop, calls=%fused_computation.32.clone.1 | loop fusion | flops 25100288 | bytes 393216 | tf_op jit(solution)/shard_map/while/body/eval_jaxpr/reduce_sum | solution.py:90
  290.8 5.7 %convert_reduce_fusion.3 = f32[256,256]{1,0:T(8,128)S(1)} fusion(s32[256,128]{1,0:T(8,128)S(1)} %constant_dynamic-slice_fusion.2), kind=kLoop, calls=%fused_computation.32.clone.1 | loop fusion | flops 25100288 | bytes 393216 | tf_op jit(solution)/shard_map/while/body/eval_jaxpr/reduce_sum | solution.py:90
  296.7 5.7 %convert_reduce_fusion.3 = f32[256,256]{1,0:T(8,128)S(1)} fusion(s32[256,128]{1,0:T(8,128)S(1)} %constant_dynamic-slice_fusion.2), kind=kLoop, calls=%fused_computation.32.clone.1 | loop fusion | flops 25100288 | bytes 393216 | tf_op jit(solution)/shard_map/while/body/eval_jaxpr/reduce_sum | solution.py:90
  302.5 5.7 %convert_reduce_fusion.3 = f32[256,256]{1,0:T(8,128)S(1)} fusion(s32[256,128]{1,0:T(8,128)S(1)} %constant_dynamic-slice_fusion.2), kind=kLoop, calls=%fused_computation.32.clone.1 | loop fusion | flops 25100288 | bytes 393216 | tf_op jit(solution)/shard_map/while/body/eval_jaxpr/reduce_sum | solution.py:90
  308.3 5.7 %convert_reduce_fusion.3 = f32[256,256]{1,0:T(8,128)S(1)} fusion(s32[256,128]{1,0:T(8,128)S(1)} %constant_dynamic-slice_fusion.2), kind=kLoop, calls=%fused_computation.32.clone.1 | loop fusion | flops 25100288 | bytes 393216 | tf_op jit(solution)/shard_map/while/body/eval_jaxpr/reduce_sum | solution.py:90
  314.2 5.7 %convert_reduce_fusion.3 = f32[256,256]{1,0:T(8,128)S(1)} fusion(s32[256,128]{1,0:T(8,128)S(1)} %constant_dynamic-slice_fusion.2), kind=kLoop, calls=%fused_computation.32.clone.1 | loop fusion | flops 25100288 | bytes 393216 | tf_op jit(solution)/shard_map/while/body/eval_jaxpr/reduce_sum | solution.py:90
  320.1 2.2 reduce-scatter.3.cloned.1.call-done
  322.3 1.7 multiply_convert_fusion
  324.1 90.1 %all-gather.5.cloned.1.call-done = bf16[8192,256]{1,0:T(8,128)(2,1)} async-done(((bf16[256,256]{1,0:T(8,128)(2,1)}), bf16[8192,256]{1,0:T(8,128)(2,1)}) %all-gather.5.cloned.1.call-update) | async-done | bytes 4194320 | tf_op jit(solution)/shard_map/all_gather | solution.py:99
  414.2 7.4 %reshape_reshape.7 = bf16[64,32768]{1,0:T(8,128)(2,1)} reshape(bf16[8192,256]{1,0:T(8,128)(2,1)} %all-gather.5.cloned.1.call-done) | data formatting | bytes 8388608 | tf_op jit(solution)/shard_map/reshape;reshape | solution.py:23
  421.9 33.0 %while.35 = (s32[]{:T(128)}, f32[16,128,256]{2,0,1:T(8,128)S(1)}, s32[]{:T(128)}, s32[96]{0:T(128)S(1)}, s32[]{:T(128)}, /*index=5*/bf16[96,128,128]{2,1,0:T(8,1...) while((s32[]{:T(128)}, f32[16,128,256]{2,0,1:T(8,128)S(1)}, ...), condition=%wide.region_9.10_spmd, body=%wide.region_8.9_spmd.sunk | while | flops 605555840 | bytes 26215440 | solution.py:55
  422.2 2.9 convolution_convert_fusion.5
  425.6 1.9 fusion.66
  427.6 0.7 compare_and_fusion.5
  428.3 4.7 fusion.67
  433.1 2.9 convolution_convert_fusion.5
  436.6 1.9 fusion.66
  438.6 0.7 compare_and_fusion.5
  439.2 4.7 fusion.67
  444.1 2.9 convolution_convert_fusion.5
  447.5 1.9 fusion.66
  449.5 0.7 compare_and_fusion.5
  450.2 4.7 fusion.67
  454.9 2.5 copy.11
  457.5 49.1 %reduce-scatter.5.cloned.1.call-done = f32[256,256]{1,0:T(8,128)} async-done(((f32[2048,256]{1,0:T(8,128)}), f32[256,256]{1,0:T(8,128)}) %reduce-scatter.5.cloned.1.call-update) | async-done | bytes 262160 | tf_op jit(solution)/shard_map/reduce_scatter | solution.py:110
  506.6 1.7 multiply_add_fusion
  (60 shorter events, 6.0 us)
Async XLA Ops:
  6.5 3.6 copy-start.2
  6.5 135.9 %copy-start.1 = (f32[256,256]{1,0:T(8,128)S(1)}, f32[256,256]{1,0:T(8,128)}, u32[]{:S(2)}) copy-start(f32[256,256]{1,0:T(8,128)} %param.12) | copy-start | bytes 786436
  6.5 136.8 %copy-start.3 = (s32[96]{0:T(128)S(1)}, s32[96]{0:T(128)}, u32[]{:S(2)}) copy-start(s32[96]{0:T(128)} %param.14) | copy-start | bytes 1156
  6.5 136.8 %copy-start = (s32[256,1024]{1,0:T(8,128)S(1)}, s32[256,1024]{1,0:T(8,128)}, u32[]{:S(2)}) copy-start(s32[256,1024]{1,0:T(8,128)} %param.17) | copy-start | bytes 3145732
  6.5 223.6 %all-gather.3.cloned.1.call-start = ((), (), s32[]{:S(2)}) async-start(), calls=%async_computation.2 | async-start | bytes 4325376 | tf_op jit(solution)/shard_map/all_gather | solution.py:99
  143.2 179.1 %reduce-scatter.3.cloned.1.call-start = ((), (), s32[]{:S(2)}) async-start(), calls=%async_computation.3 | async-start | bytes 2359296 | tf_op jit(solution)/shard_map/reduce_scatter | solution.py:110
  273.2 141.0 %all-gather.5.cloned.1.call-start = ((), (), s32[]{:S(2)}) async-start(), calls=%async_computation.4 | async-start | bytes 4325376 | tf_op jit(solution)/shard_map/all_gather | solution.py:99
  324.1 182.6 %reduce-scatter.5.cloned.1.call-start = ((), (), s32[]{:S(2)}) async-start(), calls=%async_computation.5 | async-start | bytes 2359296 | tf_op jit(solution)/shard_map/reduce_scatter | solution.py:110
Sparse Core Ops, SparseCore 0:
  143.3 86.7 all-gather.2
  273.3 48.9 reduce-scatter.2
  325.1 89.0 all-gather.4
  457.6 48.9 reduce-scatter.4
where the time goes:
time: 516 us; the launch traced here: 515 us
  waiting for transfers between devices  228 us (44%)
  blocking collectives  132 us (26%)
  matrix products  57.9 us (11%)
  other arithmetic  57.1 us (11%)
  local copies, waits for them, and re-layouts  24.6 us (5%)
  between operations  14.1 us (3%)
    all_gather x2, waiting for transfers between devices, per_device(): band_panel = lax.all_gather(panel_own, 'col', axis=0, tiled=True)  177 us
    psum x1, blocking collectives, per_device(): totals = lax.psum(column_part, 'col')  132 us
    reduce_scatter x2, waiting for transfers between devices, per_device(): lax.psum_scatter(summed.reshape(grid_rows * BT * tile_size, columns), 'ro...  51.4 us
    reduce_sum x8, other arithmetic, count_seeds(): return counted + jnp.sum(equal, axis=1).T  45.5 us
    dot_general x6, matrix products, tile_block(): jnp.einsum('kt,kas->tas', place, products, precision=lax.Precision.HIGHES...  28.3 us
    dot_general x6, matrix products, tile_block(): gathered = jnp.dot(pick, flat_panels, preferred_element_type=jnp.float32)  17.7 us
    another operation x2, local copies, waits for them, and re-layouts, tile_products(): flat_panels = panels.reshape(piece_tiles, tile_size * columns)  14.8 us
    dot_general x6, matrix products, tile_block(): jnp.einsum('kab,kbs->kas', block_tiles, gathered, preferred_element_type=...  11.6 us
  transfers between devices with their start and end apart: 4, of which 4 were waited for; matrix products, arithmetic and copies ran while one was open for 9% of the time, Pallas kernels for 0%

commit v1 on v0

v1 whole, which is shorter than its diff:
```python
import jax
import jax.numpy as jnp
from jax import lax
from jax.experimental import pallas as pl
from jax.experimental.pallas import tpu as pltpu
from jax.sharding import PartitionSpec as P

BT = 2
TILE = 128
LANES = 128
damping = 0.85
teleport = 0.15
LOW, HIGH = 0.2, 2.0
STEPS = 65535.0
HALF = 32768.0
FAR = 1 << 30
VMEM = pltpu.VMEM
SMEM = pltpu.SMEM


def vmem(*_):
    return pl.BlockSpec(memory_space=VMEM)


def smem(*_):
    return pl.BlockSpec(memory_space=SMEM)


def params():
    return pltpu.CompilerParams(vmem_limit_bytes=40 * 1024 * 1024)


def column_kernel(source_ref, count_ref, tiles_ref, sums_ref):
    sums_ref[...] = jnp.zeros_like(sums_ref)

    def slot(k, carry):
        column = jnp.sum(tiles_ref[k].astype(jnp.float32), axis=0, keepdims=True)
        sums_ref[pl.ds(source_ref[k], 1), :] += column
        return carry

    lax.fori_loop(0, count_ref[0], slot, 0)


def seed_kernel(first_ref, ids_ref, counts_ref):
    total, lanes = ids_ref.shape
    pages = counts_ref.shape[0]
    first = first_ref[0]
    chunk = 64
    counts_ref[...] = jnp.zeros_like(counts_ref)

    def above(low):
        def step(i, best):
            page = ids_ref[pl.ds(pl.multiple_of(i * chunk, chunk), chunk), :] - first
            found = jnp.where(page > low, page, FAR).reshape(chunk // 8, 8, lanes)
            return jnp.minimum(best, jnp.min(found, axis=0))

        best = lax.fori_loop(0, total // chunk, step, jnp.full((8, lanes), FAR, jnp.int32))
        return jnp.min(best, axis=0, keepdims=True)

    def more(carry):
        return carry[1] < pages

    def walk(carry):
        page_now, _ = carry

        def step(i, inner):
            best, seen = inner
            page = ids_ref[pl.ds(pl.multiple_of(i * chunk, chunk), chunk), :] - first
            found = jnp.where(page > page_now, page, FAR).reshape(chunk // 8, 8, lanes)
            same = jnp.where(page == page_now, 1.0, 0.0).reshape(chunk // 8, 8, lanes)
            return jnp.minimum(best, jnp.min(found, axis=0)), seen + jnp.sum(same, axis=0)

        best, seen = lax.fori_loop(
            0,
            total // chunk,
            step,
            (jnp.full((8, lanes), FAR, jnp.int32), jnp.zeros((8, lanes), jnp.float32)),
        )
        seen = jnp.sum(seen, axis=0, keepdims=True)

        def place(i, inner):
            rows = pl.ds(pl.multiple_of(i * chunk, chunk), chunk)
            here = lax.broadcasted_iota(jnp.int32, (chunk, lanes), 0) + i * chunk
            counts_ref[rows, :] += jnp.where(here == page_now, seen, 0.0)
            return inner

        lax.fori_loop(0, pages // chunk, place, 0)
        later = jnp.min(best, axis=0, keepdims=True)
        return later, jnp.min(later)

    start = above(jnp.full((1, lanes), -1, jnp.int32))
    lax.while_loop(more, walk, (start, jnp.min(start)))


def products(source_ref, target_ref, count_ref, tiles_refs, panel, total, out_ref):
    unroll = 8
    slots = tiles_refs[0].shape[0]
    total[...] = jnp.zeros_like(total)
    for which, tiles_ref in enumerate(tiles_refs):

        def group(g, carry, which=which, tiles_ref=tiles_ref):
            for u in range(unroll):
                k = g * unroll + u
                at = which * slots + k
                target = target_ref[at]
                total[target] += jnp.dot(
                    tiles_ref[k], panel[source_ref[at]], preferred_element_type=jnp.float32
                )
            return carry

        lax.fori_loop(0, (count_ref[which] + unroll - 1) // unroll, group, 0)
    receivers = out_ref.shape[0]
    per = (out_ref.shape[1] - 16) // TILE

    def send(r, carry):
        exponents = []
        for t in range(per):
            block = total[r * per + t]
            top = jnp.maximum(jnp.max(block, axis=0, keepdims=True), 1e-30)
            exponent = jnp.floor(jnp.log2(top)) + 1.0
            exponents.append(exponent)
            code = block * jnp.exp2(16.0 - exponent) + 0.5
            code = jnp.clip(code.astype(jnp.int32), 0, 65535) - 32768
            out_ref[r, t * TILE : (t + 1) * TILE, :] = code.astype(jnp.int16)
        rows = exponents + [jnp.zeros((16 - per, LANES), jnp.float32)]
        tail = jnp.concatenate(rows, axis=0).astype(jnp.int32).astype(jnp.int16)
        out_ref[r, per * TILE : per * TILE + 16, :] = tail
        return carry

    lax.fori_loop(0, receivers, send, 0)


def first_kernel(pieces, source_ref, target_ref, count_ref, chip_ref, sums_ref, own_ref, sib_ref, *refs):
    piece_refs = refs[:pieces]
    out_ref, inverse_ref, panel, total, ordered = refs[pieces:]
    per = piece_refs[0].shape[0] // TILE
    ordered[...] = jnp.zeros_like(ordered)
    for p in range(pieces):
        ordered[p * per : (p + 1) * per, :] = sums_ref[chip_ref[p]]
    inverse = (1.0 / jnp.maximum(ordered[...], 1.0)).T
    for p in range(pieces):
        for t in range(per):
            column = inverse[:, p * per + t : p * per + t + 1]
            code = piece_refs[p][t * TILE : (t + 1) * TILE, :].astype(jnp.float32)
            score = (code + HALF) * ((HIGH - LOW) / STEPS) + LOW
            panel[chip_ref[p] * per + t] = (score * column).astype(jnp.bfloat16)
            if p == 0:
                inverse_ref[t * TILE : (t + 1) * TILE, :] = jnp.broadcast_to(column, (TILE, LANES))
    products(source_ref, target_ref, count_ref, (own_ref, sib_ref), panel, total, out_ref)


def later_kernel(pieces, source_ref, target_ref, count_ref, chip_ref, own_ref, sib_ref, *refs):
    piece_refs = refs[:pieces]
    out_ref, panel, total = refs[pieces:]
    per = piece_refs[0].shape[0] // TILE
    for p in range(pieces):
        for t in range(per):
            panel[chip_ref[p] * per + t] = piece_refs[p][t * TILE : (t + 1) * TILE, :]
    products(source_ref, target_ref, count_ref, (own_ref, sib_ref), panel, total, out_ref)


def current_kernel(scaled, parts_ref, restart_ref, inverse_ref, out_ref):
    senders = parts_ref.shape[0]
    per = (parts_ref.shape[1] - 16) // TILE
    for t in range(per):
        rows = slice(t * TILE, (t + 1) * TILE)
        summed = jnp.zeros((TILE, LANES), jnp.float32)
        for r in range(senders):
            tail = parts_ref[r, per * TILE : per * TILE + 16, :].astype(jnp.float32)
            scale = jnp.exp2(tail[t : t + 1, :] - 16.0)
            summed += (parts_ref[r, rows, :].astype(jnp.float32) + HALF) * scale
        current = damping * summed + teleport * restart_ref[rows, :]
        if scaled:
            current = current * inverse_ref[rows, :]
        out_ref[rows, :] = current.astype(out_ref.dtype)


def per_device(scores, tile_values, tile_rows, tile_cols, tile_count, seed_ids):
    grid_rows = lax.axis_size("row")
    grid_cols = lax.axis_size("col")
    row_index = lax.axis_index("row")
    col_index = lax.axis_index("col")
    depth = grid_cols // 4
    high, z, core = col_index // (2 * depth), col_index // 2 % depth, col_index % 2
    own_rows = scores.shape[0]
    columns = scores.shape[1]
    slots = tile_values.shape[0]
    seed_total = seed_ids.shape[1]
    band_tiles = grid_cols * BT
    chips = grid_cols // 2
    per = 2 * BT

    def by_col(value, move):
        pairs = []
        for c in range(grid_cols):
            y, at, k = move(c // (2 * depth), c // 2 % depth, c % 2)
            pairs.append((c, (y * depth + at) * 2 + k))
        return lax.ppermute(value, "col", pairs)

    def sibling(value):
        return by_col(value, lambda y, at, k: (y, at, 1 - k))

    def along(value, step):
        return by_col(value, lambda y, at, k: (y, (at + step) % depth, k))

    def across(value):
        return by_col(value, lambda y, at, k: (1 - y, at, k))

    def gather(block):
        other = across(block)
        pieces = [block, other]
        names = [(0, 0), (1, 0)]
        a, b, c, d = block, block, other, other
        for step in range(1, depth // 2):
            a, b = along(a, 1), along(b, -1)
            c, d = along(c, 1), along(d, -1)
            pieces += [a, b, c, d]
            names += [(0, -step), (0, step), (1, -step), (1, step)]
        pieces += [along(a, 1), along(d, -1)]
        names += [(0, depth // 2), (1, depth // 2)]
        return pieces, names

    half = columns // 2
    code = ((scores - LOW) * (STEPS / (HIGH - LOW)) + 0.5).astype(jnp.int32)
    code = (jnp.clip(code, 0, 65535) - 32768).astype(jnp.int16)
    mine = lax.dynamic_slice_in_dim(code, core * half, half, 1)
    theirs = sibling(lax.dynamic_slice_in_dim(code, (1 - core) * half, half, 1))
    block = jnp.where(
        core == 0, jnp.concatenate([mine, theirs]), jnp.concatenate([theirs, mine])
    )
    sources = tile_cols - row_index * band_tiles
    targets = tile_rows // band_tiles * per + core * BT + tile_rows % BT
    targets = jnp.where(jnp.arange(slots) < tile_count[0], targets, grid_rows * per)
    facts = jnp.stack([sources, targets, jnp.broadcast_to(tile_count, (slots,))])
    sib_facts = sibling(facts)
    sib_tiles = sibling(tile_values)

    sums = pl.pallas_call(
        column_kernel,
        out_shape=jax.ShapeDtypeStruct((band_tiles, TILE), jnp.float32),
        in_specs=[smem(), smem(), vmem()],
        out_specs=vmem(),
        compiler_params=params(),
        name="column_sums",
    )(sources, tile_count, tile_values)
    sums = sums + sibling(sums)
    step = 1
    while step < depth:
        sums = sums + by_col(sums, lambda y, at, k, step=step: (y, at ^ step, k))
        step *= 2
    sums = sums + across(sums)

    first_page = (row_index * grid_cols + col_index - core) * own_rows
    ids = lax.dynamic_slice_in_dim(seed_ids, core * half, half, 0).T
    restart = pl.pallas_call(
        seed_kernel,
        out_shape=jax.ShapeDtypeStruct((2 * own_rows, half), jnp.float32),
        in_specs=[smem(), vmem()],
        out_specs=vmem(),
        compiler_params=params(),
        name="seed_counts",
    )(first_page.reshape(1), ids)

    slot_sources = jnp.concatenate([sources, sib_facts[0]])
    slot_targets = jnp.concatenate([targets, sib_facts[1]])
    counts = jnp.concatenate([tile_count, sib_facts[2, :1]])

    def multiply(pieces, names, sums):
        order = jnp.stack([(high ^ y) * depth + (z + d) % depth for y, d in names])
        n = len(pieces)
        parts = jax.ShapeDtypeStruct((grid_rows, per * TILE + 16, half), jnp.int16)
        scratch = [
            VMEM((band_tiles, TILE, half), jnp.bfloat16),
            VMEM((grid_rows * per + 1, TILE, half), jnp.float32),
        ]
        if sums is not None:
            return pl.pallas_call(
                lambda *refs: first_kernel(n, *refs),
                out_shape=(parts, jax.ShapeDtypeStruct((per * TILE, half), jnp.float32)),
                in_specs=[smem()] * 4 + [vmem()] * (3 + n),
                out_specs=(vmem(), vmem()),
                scratch_shapes=scratch + [VMEM((TILE, TILE), jnp.float32)],
                compiler_params=params(),
                name="first_products",
            )(
                slot_sources, slot_targets, counts, order,
                sums.reshape(chips, per, TILE), tile_values, sib_tiles, *pieces,
            )
        return pl.pallas_call(
            lambda *refs: later_kernel(n, *refs),
            out_shape=parts,
            in_specs=[smem()] * 4 + [vmem()] * (2 + n),
            out_specs=vmem(),
            scratch_shapes=scratch,
            compiler_params=params(),
            name="later_products",
        )(slot_sources, slot_targets, counts, order, tile_values, sib_tiles, *pieces)

    def update(parts, inverse, scaled):
        return pl.pallas_call(
            lambda *refs: current_kernel(scaled, *refs),
            out_shape=jax.ShapeDtypeStruct(
                (per * TILE, half), jnp.bfloat16 if scaled else jnp.float32
            ),
            in_specs=[vmem()] * 3,
            out_specs=vmem(),
            compiler_params=params(),
            name="current",
        )(parts, restart, inverse)

    pieces, names = gather(block)
    parts, inverse = multiply(pieces, names, sums)
    parts = lax.all_to_all(parts, "row", 0, 0, tiled=True)
    panel = update(parts, inverse, True)
    pieces, names = gather(panel)
    parts = multiply(pieces, names, None)
    parts = lax.all_to_all(parts, "row", 0, 0, tiled=True)
    current = update(parts, inverse, False)
    mine = lax.dynamic_slice_in_dim(current, core * own_rows, own_rows, 0)
    theirs = sibling(lax.dynamic_slice_in_dim(current, (1 - core) * own_rows, own_rows, 0))
    return jnp.where(
        core == 0,
        jnp.concatenate([mine, theirs], axis=1),
        jnp.concatenate([theirs, mine], axis=1),
    )


def solution(mesh):
    placed = (
        P(("row", "col"), None),
        P(("row", "col"), None, None),
        P(("row", "col")),
        P(("row", "col")),
        P(("row", "col")),
        P(),
    )
    return jax.shard_map(
        per_device, mesh=mesh, in_specs=placed, out_specs=P(("row", "col"), None), check_vma=False
    )
```

time: 516 us -> 153 us (0.30)
  waiting for transfers between devices: 228 us -> 40.8 us
  blocking collectives: 132 us -> 0 us
  starting transfers between devices: 0.16 us -> 70.3 us
  matrix products: 57.9 us -> 0 us
  other arithmetic: 57.1 us -> 2.54 us
  Pallas kernels: 0 us -> 31.1 us
  local copies, waits for them, and re-layouts: 24.6 us -> 6.72 us
  between operations: 14.1 us -> 0.89 us
    all_gather x2 -> x0, waiting for transfers between devices: 177 us -> none  [per_device(): band_panel = lax.all_gather(panel_own, 'col', axis=0, tiled=True)]
    psum x1 -> x0, blocking collectives: 132 us -> none  [per_device(): totals = lax.psum(column_part, 'col')]
    ppermute x0 -> x39, starting transfers between devices: none -> 61.7 us  [by_col(): return lax.ppermute(value, 'col', pairs)]
    dot_general x19 -> x0, matrix products: 57.9 us -> none  [the longest x6 28.3 us: tile_block(): jnp.einsum('kt,kas->tas', place, products, precision=lax.Precision.HIGHES...]
    reduce_scatter x2 -> x0, waiting for transfers between devices: 51.4 us -> none  [per_device(): lax.psum_scatter(summed.reshape(grid_rows * BT * tile_size, columns), 'ro...]
    reduce_sum x9 -> x0, other arithmetic: 48.3 us -> none  [the longest x8 45.5 us: count_seeds(): return counted + jnp.sum(equal, axis=1).T]
    pallas_call x0 -> x6, Pallas kernels: none -> 31.1 us  [the longest x1 10.1 us: multiply(): pl.pallas_call(lambda *refs: first_kernel(n, *refs), out_shape=(parts, ja...]
    ppermute x0 -> x39, waiting for transfers between devices: none -> 26 us  [by_col(): return lax.ppermute(value, 'col', pairs)]
  transfers between devices with their start and end apart: 4 -> 41, of which waited for: 4 -> 18; matrix products, arithmetic and copies ran while one was open for 9% -> 2% of each run, Pallas kernels for 0% -> 8%
where the time goes in v1:
time: 153 us; the launch traced here: 152 us
  starting transfers between devices  70.3 us (46%)
  waiting for transfers between devices  40.8 us (27%)
  Pallas kernels  31.1 us (20%)
  local copies, waits for them, and re-layouts  6.72 us (4%)
  other arithmetic  2.54 us (2%)
    ppermute x39, starting transfers between devices, by_col(): return lax.ppermute(value, 'col', pairs)  61.7 us
    ppermute x39, waiting for transfers between devices, by_col(): return lax.ppermute(value, 'col', pairs)  26 us
    all_to_all x2, waiting for transfers between devices, per_device(): parts = lax.all_to_all(parts, 'row', 0, 0, tiled=True)  14.8 us
    pallas_call x1, Pallas kernels, multiply(): pl.pallas_call(lambda *refs: first_kernel(n, *refs), out_shape=(parts, ja...  10.1 us
    pallas_call x1, Pallas kernels, multiply(): pl.pallas_call(lambda *refs: later_kernel(n, *refs), out_shape=parts, in_...  8.8 us
    all_to_all x2, starting transfers between devices, per_device(): parts = lax.all_to_all(parts, 'row', 0, 0, tiled=True)  8.53 us
    pallas_call x1, Pallas kernels, per_device(): pl.pallas_call(seed_kernel, out_shape=jax.ShapeDtypeStruct((2 * own_rows,...  8.51 us
    unnamed x15, local copies, waits for them, and re-layouts  5.87 us
  transfers between devices with their start and end apart: 41, of which 18 were waited for; matrix products, arithmetic and copies ran while one was open for 2% of the time, Pallas kernels for 8%

profile of v1, /device:TPU:1, one launch (start us, length us, event | category | flops | bytes accessed | tf_op | source)
XLA Modules:
  0.0 152.4 jit_solution(4124043926332815601)
XLA Ops:
  0.0 3.2 %collective-permute-start.1 = (bf16[96,128,128]{2,1,0:T(8,128)(2,1)}, bf16[96,128,128]{2,1,0:T(8,128)(2,1)}, u32[]{:S(2)}, u32[]{:S(2)}) collective-permute-start(bf16[96,128,128]{2,1,0:T(8,128)(2,1)} %refs_4_.1), channel_id=1, source_target_pairs={{0,1},{1,0},{2,3},{3,2},{4,5},{5,4},{6,7},{7,6},{8,9},{9,8},{10,11... | collective-permute-start | bytes 9437192 | tf_op jit(solution)/shard_map/ppermute | solution.py:198
  4.6 1.9 %copy-done.1 = bf16[96,128,128]{2,1,0:T(8,128)(2,1)S(1)} copy-done((bf16[96,128,128]{2,1,0:T(8,128)(2,1)S(1)}, bf16[96,128,128]{2,1,0:T(8,128)(2,1)}, u32[]{:S(2)}) %copy-start.1) | copy-done | bytes 3145752
  6.5 3.0 %column_sums.1 = f32[64,128]{1,0:T(8,128)S(1)} custom-call(s32[96]{0:T(128)S(1)} %broadcast_subtract_fusion.source_ref, s32[1]{0:T(128)} %copy.9.count_ref, bf16[96,128,128]{2,1,0:T(8,128)(2,1)S(1)} %copy-done.1), custom_call_target="tpu_custom_call" | custom-call | tf_op jit(solution)/shard_map/column_sums/pallas_call | solution.py:238
  10.8 2.7 %collective-permute-done.3 = f32[64,128]{1,0:T(8,128)S(1)} collective-permute-done((f32[64,128]{1,0:T(8,128)S(1)}, f32[64,128]{1,0:T(8,128)S(1)}, u32[]{:S(2)}, u32[]{:S(2)}) %collective-permute-start.3) | collective-permute-done | bytes 32800 | tf_op jit(solution)/shard_map/ppermute | solution.py:198
  13.5 1.1 collective-permute-start.4
  14.6 3.5 %collective-permute-start.8 = (s16[512,128]{1,0:T(8,128)(2,1)S(1)}, s16[512,128]{1,0:T(8,128)(2,1)S(1)}, u32[]{:S(2)}, u32[]{:S(2)}) collective-permute-start(s16[512,128]{1,0:T(8,128)(2,1)S(1)} %add_select_fusion.refs_7_), channel_id=1, source_target_pairs={{0,16},{1,17},{2,18},{3,19},{4,20},{5,21},{6,22},{7,23},{8,24},{9,... | collective-permute-start | bytes 393224 | tf_op jit(solution)/shard_map/ppermute | solution.py:198
  18.1 4.8 %collective-permute-start.5 = (f32[64,128]{1,0:T(8,128)S(1)}, f32[64,128]{1,0:T(8,128)S(1)}, u32[]{:S(2)}, u32[]{:S(2)}) collective-permute-start(f32[64,128]{1,0:T(8,128)S(1)} %add.257), channel_id=1, source_target_pairs={{0,8},{1,9},{2,10},{3,11},{4,12},{5,13},{6,14},{7,15},{8,0},{9,1},... | collective-permute-start | bytes 98312 | tf_op jit(solution)/shard_map/ppermute | solution.py:198
  22.9 0.9 collective-permute-start.9
  23.8 1.1 collective-permute-done.5
  24.9 1.4 collective-permute-start.6
  26.3 4.3 %collective-permute-start.12 = (s16[512,128]{1,0:T(8,128)(2,1)S(1)}, s16[512,128]{1,0:T(8,128)(2,1)S(1)}, u32[]{:S(2)}, u32[]{:S(2)}) collective-permute-start(s16[512,128]{1,0:T(8,128)(2,1)S(1)} %collective-permute-done.8.refs_8_), channel_id=1, source_target_pairs={{0,14},{1,15},{2,0},{3,1},{4,2},{5,3},{6,4},{7,5},{8,6},{9,7},{10,... | collective-permute-start | bytes 393224 | tf_op jit(solution)/shard_map/ppermute | solution.py:198
  30.7 4.5 %collective-permute-start = (s32[3,96]{1,0:T(4,128)S(1)}, s32[3,96]{1,0:T(4,128)S(1)}, u32[]{:S(2)}, u32[]{:S(2)}) collective-permute-start(s32[3,96]{1,0:T(4,128)S(1)} %add_add_fusion), channel_id=1, source_target_pairs={{0,1},{1,0},{2,3},{3,2},{4,5},{5,4},{6,7},{7,6},{8,9},{9,8},{10,11... | collective-permute-start | bytes 3464 | tf_op jit(solution)/shard_map/ppermute | solution.py:198
  35.3 0.7 collective-permute-done
  36.0 1.1 collective-permute-start.10
  37.6 2.6 %collective-permute-start.16 = (s16[512,128]{1,0:T(8,128)(2,1)S(1)}, s16[512,128]{1,0:T(8,128)(2,1)S(1)}, u32[]{:S(2)}, u32[]{:S(2)}) collective-permute-start(s16[512,128]{1,0:T(8,128)(2,1)S(1)} %collective-permute-done.12.refs_12_), channel_id=1, source_target_pairs={{0,14},{1,15},{2,0},{3,1},{4,2},{5,3},{6,4},{7,5},{8,6},{9,7},{10,... | collective-permute-start | bytes 393224 | tf_op jit(solution)/shard_map/ppermute | solution.py:198
  40.7 2.3 %collective-permute-start.14 = (s16[512,128]{1,0:T(8,128)(2,1)S(1)}, s16[512,128]{1,0:T(8,128)(2,1)S(1)}, u32[]{:S(2)}, u32[]{:S(2)}) collective-permute-start(s16[512,128]{1,0:T(8,128)(2,1)S(1)} %collective-permute-done.10.refs_10_), channel_id=1, source_target_pairs={{0,14},{1,15},{2,0},{3,1},{4,2},{5,3},{6,4},{7,5},{8,6},{9,7},{10,... | collective-permute-start | bytes 393224 | tf_op jit(solution)/shard_map/ppermute | solution.py:198
  43.0 2.5 %collective-permute-done.13.refs_13_ = s16[512,128]{1,0:T(8,128)(2,1)S(1)} collective-permute-done((s16[512,128]{1,0:T(8,128)(2,1)S(1)}, s16[512,128]{1,0:T(8,128)(2,1)S(1)}, u32[]{:S(2)}, u32[]{:S(2)}) %collective-permute-start.13) | collective-permute-done | bytes 131104 | tf_op jit(solution)/shard_map/ppermute | solution.py:198
  45.5 2.7 %collective-permute-start.20 = (s16[512,128]{1,0:T(8,128)(2,1)S(1)}, s16[512,128]{1,0:T(8,128)(2,1)S(1)}, u32[]{:S(2)}, u32[]{:S(2)}) collective-permute-start(s16[512,128]{1,0:T(8,128)(2,1)S(1)} %collective-permute-done.16.refs_16_), channel_id=1, source_target_pairs={{0,14},{1,15},{2,0},{3,1},{4,2},{5,3},{6,4},{7,5},{8,6},{9,7},{10,... | collective-permute-start | bytes 393224 | tf_op jit(solution)/shard_map/ppermute | solution.py:198
  48.9 1.4 collective-permute-start.19
  50.3 1.7 %collective-permute-done.17.refs_17_ = s16[512,128]{1,0:T(8,128)(2,1)S(1)} collective-permute-done((s16[512,128]{1,0:T(8,128)(2,1)S(1)}, s16[512,128]{1,0:T(8,128)(2,1)S(1)}, u32[]{:S(2)}, u32[]{:S(2)}) %collective-permute-start.17) | collective-permute-done | bytes 131104 | tf_op jit(solution)/shard_map/ppermute | solution.py:198
  52.0 2.7 %collective-permute-start.22 = (s16[512,128]{1,0:T(8,128)(2,1)S(1)}, s16[512,128]{1,0:T(8,128)(2,1)S(1)}, u32[]{:S(2)}, u32[]{:S(2)}) collective-permute-start(s16[512,128]{1,0:T(8,128)(2,1)S(1)} %collective-permute-done.20.refs_20_), channel_id=1, source_target_pairs={{0,14},{1,15},{2,0},{3,1},{4,2},{5,3},{6,4},{7,5},{8,6},{9,7},{10,... | collective-permute-start | bytes 393224 | tf_op jit(solution)/shard_map/ppermute | solution.py:198
  54.7 0.8 pad_add_fusion.2.refs_2_
  55.6 2.1 %collective-permute-done.21.refs_21_ = s16[512,128]{1,0:T(8,128)(2,1)S(1)} collective-permute-done((s16[512,128]{1,0:T(8,128)(2,1)S(1)}, s16[512,128]{1,0:T(8,128)(2,1)S(1)}, u32[]{:S(2)}, u32[]{:S(2)}) %collective-permute-start.21) | collective-permute-done | bytes 131104 | tf_op jit(solution)/shard_map/ppermute | solution.py:198
  57.7 1.9 %copy-done.2 = bf16[96,128,128]{2,1,0:T(8,128)(2,1)S(1)} copy-done((bf16[96,128,128]{2,1,0:T(8,128)(2,1)S(1)}, bf16[96,128,128]{2,1,0:T(8,128)(2,1)}, u32[]{:S(2)}) %copy-start.2) | copy-done | bytes 3145752
  59.6 10.1 %first_products.1 = (s16[8,528,128]{2,1,0:T(8,128)(2,1)}, f32[512,128]{1,0:T(8,128)S(1)}) custom-call(s32[192]{0:T(256)S(1)} %pad_add_fusion.refs_0_, s32[192]{0:T(256)S(1)} %pad_add_fusion.1.refs_1_, s32[2]{0:T(128)S(1)} %pad_add_fusion.2.refs_2_, s32[16]{0:T(128)S(1)} %stack.96.refs_3_, f32[16,4,128]{2,1,0:T(4,128)S(1)} %bitcast.32, ...), custom_call_target="tpu_custom_call" | custom-call | tf_op jit(solution)/shard_map/first_products/pallas_call | solution.py:277
  69.7 4.3 %all-to-all-start = ((s16[8,528,128]{2,1,0:T(8,128)(2,1)}), s16[8,528,128]{2,1,0:T(8,128)(2,1)S(1)}, u32[]{:S(2)}, u32[]{:S(2)}) async-start(s16[8,528,128]{2,1,0:T(8,128)(2,1)} %get-tuple-element.7), calls=%async_computation | async-start | bytes 2162688 | tf_op jit(solution)/shard_map/all_to_all | solution.py:313
  74.2 8.5 %seed_counts.1.refs_1_ = f32[512,128]{1,0:T(8,128)S(1)} custom-call(s32[1]{0:T(128)} %bitcast.23.first_ref, s32[1024,128]{1,0:T(8,128)S(1)} %bitcast.31), custom_call_target="tpu_custom_call" | custom-call | tf_op jit(solution)/shard_map/seed_counts/pallas_call | solution.py:255
  82.7 4.3 %all-to-all-done.refs_0_ = s16[8,528,128]{2,1,0:T(8,128)(2,1)S(1)} async-done(((s16[8,528,128]{2,1,0:T(8,128)(2,1)}), s16[8,528,128]{2,1,0:T(8,128)(2,1)S(1)}, u32[]{:S(2)}, u32[]{:S(2)}) %all-to-all-start) | async-done | bytes 1081376 | tf_op jit(solution)/shard_map/all_to_all | solution.py:313
  87.4 0.9 collective-permute-start.23
  88.3 4.5 %collective-permute-done.23.refs_7_ = bf16[512,128]{1,0:T(8,128)(2,1)S(1)} collective-permute-done((bf16[512,128]{1,0:T(8,128)(2,1)S(1)}, bf16[512,128]{1,0:T(8,128)(2,1)S(1)}, u32[]{:S(2)}, u32[]{:S(2)}) %collective-permute-start.23) | collective-permute-done | bytes 131104 | tf_op jit(solution)/shard_map/ppermute | solution.py:198
  93.1 1.4 collective-permute-start.26
  94.6 1.2 collective-permute-start.28
  95.8 1.2 collective-permute-done.27.refs_11_
  97.0 1.5 collective-permute-start.31
  98.4 1.1 collective-permute-start.29
  99.9 1.1 collective-permute-done.28.refs_12_
  101.0 3.1 %collective-permute-start.35 = (bf16[512,128]{1,0:T(8,128)(2,1)S(1)}, bf16[512,128]{1,0:T(8,128)(2,1)S(1)}, u32[]{:S(2)}, u32[]{:S(2)}) collective-permute-start(bf16[512,128]{1,0:T(8,128)(2,1)S(1)} %collective-permute-done.31.refs_15_), channel_id=1, source_target_pairs={{0,14},{1,15},{2,0},{3,1},{4,2},{5,3},{6,4},{7,5},{8,6},{9,7},{10,... | collective-permute-start | bytes 393224 | tf_op jit(solution)/shard_map/ppermute | solution.py:198
  104.1 2.8 %collective-permute-start.33 = (bf16[512,128]{1,0:T(8,128)(2,1)S(1)}, bf16[512,128]{1,0:T(8,128)(2,1)S(1)}, u32[]{:S(2)}, u32[]{:S(2)}) collective-permute-start(bf16[512,128]{1,0:T(8,128)(2,1)S(1)} %collective-permute-done.29.refs_13_), channel_id=1, source_target_pairs={{0,14},{1,15},{2,0},{3,1},{4,2},{5,3},{6,4},{7,5},{8,6},{9,7},{10,... | collective-permute-start | bytes 393224 | tf_op jit(solution)/shard_map/ppermute | solution.py:198
  106.9 2.2 %collective-permute-done.32.refs_16_ = bf16[512,128]{1,0:T(8,128)(2,1)S(1)} collective-permute-done((bf16[512,128]{1,0:T(8,128)(2,1)S(1)}, bf16[512,128]{1,0:T(8,128)(2,1)S(1)}, u32[]{:S(2)}, u32[]{:S(2)}) %collective-permute-start.32) | collective-permute-done | bytes 131104 | tf_op jit(solution)/shard_map/ppermute | solution.py:198
  109.1 2.7 %collective-permute-start.37 = (bf16[512,128]{1,0:T(8,128)(2,1)S(1)}, bf16[512,128]{1,0:T(8,128)(2,1)S(1)}, u32[]{:S(2)}, u32[]{:S(2)}) collective-permute-start(bf16[512,128]{1,0:T(8,128)(2,1)S(1)} %collective-permute-done.35.refs_19_), channel_id=1, source_target_pairs={{0,14},{1,15},{2,0},{3,1},{4,2},{5,3},{6,4},{7,5},{8,6},{9,7},{10,... | collective-permute-start | bytes 393224 | tf_op jit(solution)/shard_map/ppermute | solution.py:198
  112.0 3.9 %collective-permute-done.36.refs_20_ = bf16[512,128]{1,0:T(8,128)(2,1)S(1)} collective-permute-done((bf16[512,128]{1,0:T(8,128)(2,1)S(1)}, bf16[512,128]{1,0:T(8,128)(2,1)S(1)}, u32[]{:S(2)}, u32[]{:S(2)}) %collective-permute-start.36) | collective-permute-done | bytes 131104 | tf_op jit(solution)/shard_map/ppermute | solution.py:198
  115.8 1.9 %copy-done.3 = bf16[96,128,128]{2,1,0:T(8,128)(2,1)S(1)} copy-done((bf16[96,128,128]{2,1,0:T(8,128)(2,1)S(1)}, bf16[96,128,128]{2,1,0:T(8,128)(2,1)}, u32[]{:S(2)}) %copy-start.3) | copy-done | bytes 3145752
  117.7 8.8 %later_products.1 = s16[8,528,128]{2,1,0:T(8,128)(2,1)} custom-call(s32[192]{0:T(256)S(1)} %pad_add_fusion.refs_0_, s32[192]{0:T(256)S(1)} %pad_add_fusion.1.refs_1_, s32[2]{0:T(128)S(1)} %pad_add_fusion.2.refs_2_, s32[16]{0:T(128)S(1)} %stack.96.refs_3_, bf16[96,128,128]{2,1,0:T(8,128)(2,1)S(1)} %copy-done.3, ...), custom_call_target="tpu_custom_call" | custom-call | tf_op jit(solution)/shard_map/later_products/pallas_call | solution.py:289
  126.5 4.3 %all-to-all-start.1 = ((s16[8,528,128]{2,1,0:T(8,128)(2,1)}), s16[8,528,128]{2,1,0:T(8,128)(2,1)S(1)}, u32[]{:S(2)}, u32[]{:S(2)}) async-start(s16[8,528,128]{2,1,0:T(8,128)(2,1)} %later_products.1), calls=%async_computation.1 | async-start | bytes 2162688 | tf_op jit(solution)/shard_map/all_to_all | solution.py:317
  130.8 10.4 %all-to-all-done.1.refs_0_ = s16[8,528,128]{2,1,0:T(8,128)(2,1)S(1)} async-done(((s16[8,528,128]{2,1,0:T(8,128)(2,1)}), s16[8,528,128]{2,1,0:T(8,128)(2,1)S(1)}, u32[]{:S(2)}, u32[]{:S(2)}) %all-to-all-start.1) | async-done | bytes 1081376 | tf_op jit(solution)/shard_map/all_to_all | solution.py:317
  141.7 9.0 %collective-permute-start.38 = (f32[256,128]{1,0:T(8,128)S(1)}, f32[256,128]{1,0:T(8,128)S(1)}, u32[]{:S(2)}, u32[]{:S(2)}) collective-permute-start(f32[256,128]{1,0:T(8,128)S(1)} %get-tuple-element.10), channel_id=1, source_target_pairs={{0,1},{1,0},{2,3},{3,2},{4,5},{5,4},{6,7},{7,6},{8,9},{9,8},{10,11... | collective-permute-start | bytes 393224 | tf_op jit(solution)/shard_map/ppermute | solution.py:198
  150.7 1.0 collective-permute-done.38
  151.7 0.7 maximum_select_fusion
  (78 shorter events, 6.0 us)
Async XLA Ops:
  0.0 73.9 %copy-start = (s32[256,1024]{1,0:T(8,128)S(1)}, s32[256,1024]{1,0:T(8,128)}, u32[]{:S(2)}) copy-start(s32[256,1024]{1,0:T(8,128)} %param.11) | copy-start | bytes 3145732
  0.0 57.7 %collective-permute-start.1 = (bf16[96,128,128]{2,1,0:T(8,128)(2,1)}, bf16[96,128,128]{2,1,0:T(8,128)(2,1)}, u32[]{:S(2)}, u32[]{:S(2)}) collective-permute-start(bf16[96,128,128]{2,1,0:T(8,128)(2,1)} %refs_4_.1), channel_id=1, source_target_pairs={{0,1},{1,0},{2,3},{3,2},{4,5},{5,4},{6,7},{7,6},{8,9},{9,8},{10,11... | collective-permute-start | bytes 9437192 | tf_op jit(solution)/shard_map/ppermute | solution.py:198
  4.6 1.9 %copy-start.1 = (bf16[96,128,128]{2,1,0:T(8,128)(2,1)S(1)}, bf16[96,128,128]{2,1,0:T(8,128)(2,1)}, u32[]{:S(2)}) copy-start(bf16[96,128,128]{2,1,0:T(8,128)(2,1)} %refs_4_.1) | copy-start | bytes 9437188
  6.4 3.1 %copy-start.4 = (f32[256,256]{1,0:T(8,128)S(1)}, f32[256,256]{1,0:T(8,128)}, u32[]{:S(2)}) copy-start(f32[256,256]{1,0:T(8,128)} %param.6) | copy-start | bytes 786436
  6.5 4.3 %copy-start.6 = (s32[96]{0:T(128)S(1)}, s32[96]{0:T(128)}, u32[]{:S(2)}) copy-start(s32[96]{0:T(128)} %param.9) | copy-start | bytes 1156
  9.4 13.4 %copy-start.5 = (s32[96]{0:T(128)S(1)}, s32[96]{0:T(128)}, u32[]{:S(2)}) copy-start(s32[96]{0:T(128)} %param.8) | copy-start | bytes 1156
  9.4 1.3 collective-permute-start.2
  9.7 4.9 %collective-permute-start.7 = (s16[256,128]{1,0:T(8,128)(2,1)S(1)}, s16[256,128]{1,0:T(8,128)(2,1)S(1)}, u32[]{:S(2)}, u32[]{:S(2)}) collective-permute-start(s16[256,128]{1,0:T(8,128)(2,1)S(1)} %get-tuple-element.12), channel_id=1, source_target_pairs={{0,1},{1,0},{2,3},{3,2},{4,5},{5,4},{6,7},{7,6},{8,9},{9,8},{10,11... | collective-permute-start | bytes 196616 | tf_op jit(solution)/shard_map/ppermute | solution.py:198
  10.7 2.8 %collective-permute-start.3 = (f32[64,128]{1,0:T(8,128)S(1)}, f32[64,128]{1,0:T(8,128)S(1)}, u32[]{:S(2)}, u32[]{:S(2)}) collective-permute-start(f32[64,128]{1,0:T(8,128)S(1)} %add.255), channel_id=1, source_target_pairs={{0,2},{1,3},{2,0},{3,1},{4,6},{5,7},{6,4},{7,5},{8,10},{9,11},{10,... | collective-permute-start | bytes 98312 | tf_op jit(solution)/shard_map/ppermute | solution.py:198
  13.5 4.6 %collective-permute-start.4 = (f32[64,128]{1,0:T(8,128)S(1)}, f32[64,128]{1,0:T(8,128)S(1)}, u32[]{:S(2)}, u32[]{:S(2)}) collective-permute-start(f32[64,128]{1,0:T(8,128)S(1)} %add.256), channel_id=1, source_target_pairs={{0,4},{1,5},{2,6},{3,7},{4,0},{5,1},{6,2},{7,3},{8,12},{9,13},{10,... | collective-permute-start | bytes 98312 | tf_op jit(solution)/shard_map/ppermute | solution.py:198
  14.6 11.7 %collective-permute-start.8 = (s16[512,128]{1,0:T(8,128)(2,1)S(1)}, s16[512,128]{1,0:T(8,128)(2,1)S(1)}, u32[]{:S(2)}, u32[]{:S(2)}) collective-permute-start(s16[512,128]{1,0:T(8,128)(2,1)S(1)} %add_select_fusion.refs_7_), channel_id=1, source_target_pairs={{0,16},{1,17},{2,18},{3,19},{4,20},{5,21},{6,22},{7,23},{8,24},{9,... | collective-permute-start | bytes 393224 | tf_op jit(solution)/shard_map/ppermute | solution.py:198
  18.1 6.9 %collective-permute-start.5 = (f32[64,128]{1,0:T(8,128)S(1)}, f32[64,128]{1,0:T(8,128)S(1)}, u32[]{:S(2)}, u32[]{:S(2)}) collective-permute-start(f32[64,128]{1,0:T(8,128)S(1)} %add.257), channel_id=1, source_target_pairs={{0,8},{1,9},{2,10},{3,11},{4,12},{5,13},{6,14},{7,15},{8,0},{9,1},... | collective-permute-start | bytes 98312 | tf_op jit(solution)/shard_map/ppermute | solution.py:198
  22.9 14.5 %collective-permute-start.9 = (s16[512,128]{1,0:T(8,128)(2,1)S(1)}, s16[512,128]{1,0:T(8,128)(2,1)S(1)}, u32[]{:S(2)}, u32[]{:S(2)}) collective-permute-start(s16[512,128]{1,0:T(8,128)(2,1)S(1)} %add_select_fusion.refs_7_), channel_id=1, source_target_pairs={{0,2},{1,3},{2,4},{3,5},{4,6},{5,7},{6,8},{7,9},{8,10},{9,11},{10,... | collective-permute-start | bytes 393224 | tf_op jit(solution)/shard_map/ppermute | solution.py:198
  24.9 12.1 %collective-permute-start.6 = (f32[64,128]{1,0:T(8,128)S(1)}, f32[64,128]{1,0:T(8,128)S(1)}, u32[]{:S(2)}, u32[]{:S(2)}) collective-permute-start(f32[64,128]{1,0:T(8,128)S(1)} %add.258), channel_id=1, source_target_pairs={{0,16},{1,17},{2,18},{3,19},{4,20},{5,21},{6,22},{7,23},{8,24},{9,... | collective-permute-start | bytes 98312 | tf_op jit(solution)/shard_map/ppermute | solution.py:198
  26.3 11.2 %collective-permute-start.12 = (s16[512,128]{1,0:T(8,128)(2,1)S(1)}, s16[512,128]{1,0:T(8,128)(2,1)S(1)}, u32[]{:S(2)}, u32[]{:S(2)}) collective-permute-start(s16[512,128]{1,0:T(8,128)(2,1)S(1)} %collective-permute-done.8.refs_8_), channel_id=1, source_target_pairs={{0,14},{1,15},{2,0},{3,1},{4,2},{5,3},{6,4},{7,5},{8,6},{9,7},{10,... | collective-permute-start | bytes 393224 | tf_op jit(solution)/shard_map/ppermute | solution.py:198
  30.7 5.3 %collective-permute-start = (s32[3,96]{1,0:T(4,128)S(1)}, s32[3,96]{1,0:T(4,128)S(1)}, u32[]{:S(2)}, u32[]{:S(2)}) collective-permute-start(s32[3,96]{1,0:T(4,128)S(1)} %add_add_fusion), channel_id=1, source_target_pairs={{0,1},{1,0},{2,3},{3,2},{4,5},{5,4},{6,7},{7,6},{8,9},{9,8},{10,11... | collective-permute-start | bytes 3464 | tf_op jit(solution)/shard_map/ppermute | solution.py:198
  36.0 4.7 %collective-permute-start.10 = (s16[512,128]{1,0:T(8,128)(2,1)S(1)}, s16[512,128]{1,0:T(8,128)(2,1)S(1)}, u32[]{:S(2)}, u32[]{:S(2)}) collective-permute-start(s16[512,128]{1,0:T(8,128)(2,1)S(1)} %add_select_fusion.refs_7_), channel_id=1, source_target_pairs={{0,14},{1,15},{2,0},{3,1},{4,2},{5,3},{6,4},{7,5},{8,6},{9,7},{10,... | collective-permute-start | bytes 393224 | tf_op jit(solution)/shard_map/ppermute | solution.py:198
  37.1 6.0 %collective-permute-start.11 = (s16[512,128]{1,0:T(8,128)(2,1)S(1)}, s16[512,128]{1,0:T(8,128)(2,1)S(1)}, u32[]{:S(2)}, u32[]{:S(2)}) collective-permute-start(s16[512,128]{1,0:T(8,128)(2,1)S(1)} %collective-permute-done.8.refs_8_), channel_id=1, source_target_pairs={{0,2},{1,3},{2,4},{3,5},{4,6},{5,7},{6,8},{7,9},{8,10},{9,11},{10,... | collective-permute-start | bytes 393224 | tf_op jit(solution)/shard_map/ppermute | solution.py:198
  37.5 8.1 %collective-permute-start.13 = (s16[512,128]{1,0:T(8,128)(2,1)S(1)}, s16[512,128]{1,0:T(8,128)(2,1)S(1)}, u32[]{:S(2)}, u32[]{:S(2)}) collective-permute-start(s16[512,128]{1,0:T(8,128)(2,1)S(1)} %collective-permute-done.9.refs_9_), channel_id=1, source_target_pairs={{0,2},{1,3},{2,4},{3,5},{4,6},{5,7},{6,8},{7,9},{8,10},{9,11},{10,... | collective-permute-start | bytes 393224 | tf_op jit(solution)/shard_map/ppermute | solution.py:198
  37.6 8.0 %collective-permute-start.16 = (s16[512,128]{1,0:T(8,128)(2,1)S(1)}, s16[512,128]{1,0:T(8,128)(2,1)S(1)}, u32[]{:S(2)}, u32[]{:S(2)}) collective-permute-start(s16[512,128]{1,0:T(8,128)(2,1)S(1)} %collective-permute-done.12.refs_12_), channel_id=1, source_target_pairs={{0,14},{1,15},{2,0},{3,1},{4,2},{5,3},{6,4},{7,5},{8,6},{9,7},{10,... | collective-permute-start | bytes 393224 | tf_op jit(solution)/shard_map/ppermute | solution.py:198
  40.7 8.1 %collective-permute-start.14 = (s16[512,128]{1,0:T(8,128)(2,1)S(1)}, s16[512,128]{1,0:T(8,128)(2,1)S(1)}, u32[]{:S(2)}, u32[]{:S(2)}) collective-permute-start(s16[512,128]{1,0:T(8,128)(2,1)S(1)} %collective-permute-done.10.refs_10_), channel_id=1, source_target_pairs={{0,14},{1,15},{2,0},{3,1},{4,2},{5,3},{6,4},{7,5},{8,6},{9,7},{10,... | collective-permute-start | bytes 393224 | tf_op jit(solution)/shard_map/ppermute | solution.py:198
  43.0 5.9 %collective-permute-start.15 = (s16[512,128]{1,0:T(8,128)(2,1)S(1)}, s16[512,128]{1,0:T(8,128)(2,1)S(1)}, u32[]{:S(2)}, u32[]{:S(2)}) collective-permute-start(s16[512,128]{1,0:T(8,128)(2,1)S(1)} %collective-permute-done.11.refs_11_), channel_id=1, source_target_pairs={{0,2},{1,3},{2,4},{3,5},{4,6},{5,7},{6,8},{7,9},{8,10},{9,11},{10,... | collective-permute-start | bytes 393224 | tf_op jit(solution)/shard_map/ppermute | solution.py:198
  45.5 6.5 %collective-permute-start.17 = (s16[512,128]{1,0:T(8,128)(2,1)S(1)}, s16[512,128]{1,0:T(8,128)(2,1)S(1)}, u32[]{:S(2)}, u32[]{:S(2)}) collective-permute-start(s16[512,128]{1,0:T(8,128)(2,1)S(1)} %collective-permute-done.13.refs_13_), channel_id=1, source_target_pairs={{0,2},{1,3},{2,4},{3,5},{4,6},{5,7},{6,8},{7,9},{8,10},{9,11},{10,... | collective-permute-start | bytes 393224 | tf_op jit(solution)/shard_map/ppermute | solution.py:198
  45.5 6.5 %collective-permute-start.20 = (s16[512,128]{1,0:T(8,128)(2,1)S(1)}, s16[512,128]{1,0:T(8,128)(2,1)S(1)}, u32[]{:S(2)}, u32[]{:S(2)}) collective-permute-start(s16[512,128]{1,0:T(8,128)(2,1)S(1)} %collective-permute-done.16.refs_16_), channel_id=1, source_target_pairs={{0,14},{1,15},{2,0},{3,1},{4,2},{5,3},{6,4},{7,5},{8,6},{9,7},{10,... | collective-permute-start | bytes 393224 | tf_op jit(solution)/shard_map/ppermute | solution.py:198
  48.9 6.7 %collective-permute-start.18 = (s16[512,128]{1,0:T(8,128)(2,1)S(1)}, s16[512,128]{1,0:T(8,128)(2,1)S(1)}, u32[]{:S(2)}, u32[]{:S(2)}) collective-permute-start(s16[512,128]{1,0:T(8,128)(2,1)S(1)} %collective-permute-done.14.refs_14_), channel_id=1, source_target_pairs={{0,14},{1,15},{2,0},{3,1},{4,2},{5,3},{6,4},{7,5},{8,6},{9,7},{10,... | collective-permute-start | bytes 393224 | tf_op jit(solution)/shard_map/ppermute | solution.py:198
  48.9 6.6 %collective-permute-start.19 = (s16[512,128]{1,0:T(8,128)(2,1)S(1)}, s16[512,128]{1,0:T(8,128)(2,1)S(1)}, u32[]{:S(2)}, u32[]{:S(2)}) collective-permute-start(s16[512,128]{1,0:T(8,128)(2,1)S(1)} %collective-permute-done.15.refs_15_), channel_id=1, source_target_pairs={{0,2},{1,3},{2,4},{3,5},{4,6},{5,7},{6,8},{7,9},{8,10},{9,11},{10,... | collective-permute-start | bytes 393224 | tf_op jit(solution)/shard_map/ppermute | solution.py:198
  52.0 5.6 %collective-permute-start.21 = (s16[512,128]{1,0:T(8,128)(2,1)S(1)}, s16[512,128]{1,0:T(8,128)(2,1)S(1)}, u32[]{:S(2)}, u32[]{:S(2)}) collective-permute-start(s16[512,128]{1,0:T(8,128)(2,1)S(1)} %collective-permute-done.17.refs_17_), channel_id=1, source_target_pairs={{0,2},{1,3},{2,4},{3,5},{4,6},{5,7},{6,8},{7,9},{8,10},{9,11},{10,... | collective-permute-start | bytes 393224 | tf_op jit(solution)/shard_map/ppermute | solution.py:198
  52.0 5.6 %collective-permute-start.22 = (s16[512,128]{1,0:T(8,128)(2,1)S(1)}, s16[512,128]{1,0:T(8,128)(2,1)S(1)}, u32[]{:S(2)}, u32[]{:S(2)}) collective-permute-start(s16[512,128]{1,0:T(8,128)(2,1)S(1)} %collective-permute-done.20.refs_20_), channel_id=1, source_target_pairs={{0,14},{1,15},{2,0},{3,1},{4,2},{5,3},{6,4},{7,5},{8,6},{9,7},{10,... | collective-permute-start | bytes 393224 | tf_op jit(solution)/shard_map/ppermute | solution.py:198
  57.7 1.9 %copy-start.2 = (bf16[96,128,128]{2,1,0:T(8,128)(2,1)S(1)}, bf16[96,128,128]{2,1,0:T(8,128)(2,1)}, u32[]{:S(2)}) copy-start(bf16[96,128,128]{2,1,0:T(8,128)(2,1)} %refs_4_.1) | copy-start | bytes 9437188
  69.7 17.4 %all-to-all-start = ((s16[8,528,128]{2,1,0:T(8,128)(2,1)}), s16[8,528,128]{2,1,0:T(8,128)(2,1)S(1)}, u32[]{:S(2)}, u32[]{:S(2)}) async-start(s16[8,528,128]{2,1,0:T(8,128)(2,1)} %get-tuple-element.7), calls=%async_computation | async-start | bytes 2162688 | tf_op jit(solution)/shard_map/all_to_all | solution.py:313
  87.4 5.4 %collective-permute-start.23 = (bf16[512,128]{1,0:T(8,128)(2,1)S(1)}, bf16[512,128]{1,0:T(8,128)(2,1)S(1)}, u32[]{:S(2)}, u32[]{:S(2)}) collective-permute-start(bf16[512,128]{1,0:T(8,128)(2,1)S(1)} %current.2.refs_6_), channel_id=1, source_target_pairs={{0,16},{1,17},{2,18},{3,19},{4,20},{5,21},{6,22},{7,23},{8,24},{9,... | collective-permute-start | bytes 393224 | tf_op jit(solution)/shard_map/ppermute | solution.py:198
  88.3 6.3 %collective-permute-start.24 = (bf16[512,128]{1,0:T(8,128)(2,1)S(1)}, bf16[512,128]{1,0:T(8,128)(2,1)S(1)}, u32[]{:S(2)}, u32[]{:S(2)}) collective-permute-start(bf16[512,128]{1,0:T(8,128)(2,1)S(1)} %current.2.refs_6_), channel_id=1, source_target_pairs={{0,2},{1,3},{2,4},{3,5},{4,6},{5,7},{6,8},{7,9},{8,10},{9,11},{10,... | collective-permute-start | bytes 393224 | tf_op jit(solution)/shard_map/ppermute | solution.py:198
  92.9 4.1 %collective-permute-start.27 = (bf16[512,128]{1,0:T(8,128)(2,1)S(1)}, bf16[512,128]{1,0:T(8,128)(2,1)S(1)}, u32[]{:S(2)}, u32[]{:S(2)}) collective-permute-start(bf16[512,128]{1,0:T(8,128)(2,1)S(1)} %collective-permute-done.23.refs_7_), channel_id=1, source_target_pairs={{0,14},{1,15},{2,0},{3,1},{4,2},{5,3},{6,4},{7,5},{8,6},{9,7},{10,... | collective-permute-start | bytes 393224 | tf_op jit(solution)/shard_map/ppermute | solution.py:198
  93.1 5.3 %collective-permute-start.25 = (bf16[512,128]{1,0:T(8,128)(2,1)S(1)}, bf16[512,128]{1,0:T(8,128)(2,1)S(1)}, u32[]{:S(2)}, u32[]{:S(2)}) collective-permute-start(bf16[512,128]{1,0:T(8,128)(2,1)S(1)} %current.2.refs_6_), channel_id=1, source_target_pairs={{0,14},{1,15},{2,0},{3,1},{4,2},{5,3},{6,4},{7,5},{8,6},{9,7},{10,... | collective-permute-start | bytes 393224 | tf_op jit(solution)/shard_map/ppermute | solution.py:198
  93.1 6.5 %collective-permute-start.26 = (bf16[512,128]{1,0:T(8,128)(2,1)S(1)}, bf16[512,128]{1,0:T(8,128)(2,1)S(1)}, u32[]{:S(2)}, u32[]{:S(2)}) collective-permute-start(bf16[512,128]{1,0:T(8,128)(2,1)S(1)} %collective-permute-done.23.refs_7_), channel_id=1, source_target_pairs={{0,2},{1,3},{2,4},{3,5},{4,6},{5,7},{6,8},{7,9},{8,10},{9,11},{10,... | collective-permute-start | bytes 393224 | tf_op jit(solution)/shard_map/ppermute | solution.py:198
  94.6 6.4 %collective-permute-start.28 = (bf16[512,128]{1,0:T(8,128)(2,1)S(1)}, bf16[512,128]{1,0:T(8,128)(2,1)S(1)}, u32[]{:S(2)}, u32[]{:S(2)}) collective-permute-start(bf16[512,128]{1,0:T(8,128)(2,1)S(1)} %collective-permute-done.24.refs_8_), channel_id=1, source_target_pairs={{0,2},{1,3},{2,4},{3,5},{4,6},{5,7},{6,8},{7,9},{8,10},{9,11},{10,... | collective-permute-start | bytes 393224 | tf_op jit(solution)/shard_map/ppermute | solution.py:198
  97.0 4.0 %collective-permute-start.31 = (bf16[512,128]{1,0:T(8,128)(2,1)S(1)}, bf16[512,128]{1,0:T(8,128)(2,1)S(1)}, u32[]{:S(2)}, u32[]{:S(2)}) collective-permute-start(bf16[512,128]{1,0:T(8,128)(2,1)S(1)} %collective-permute-done.27.refs_11_), channel_id=1, source_target_pairs={{0,14},{1,15},{2,0},{3,1},{4,2},{5,3},{6,4},{7,5},{8,6},{9,7},{10,... | collective-permute-start | bytes 393224 | tf_op jit(solution)/shard_map/ppermute | solution.py:198
  98.4 5.7 %collective-permute-start.29 = (bf16[512,128]{1,0:T(8,128)(2,1)S(1)}, bf16[512,128]{1,0:T(8,128)(2,1)S(1)}, u32[]{:S(2)}, u32[]{:S(2)}) collective-permute-start(bf16[512,128]{1,0:T(8,128)(2,1)S(1)} %collective-permute-done.25.refs_9_), channel_id=1, source_target_pairs={{0,14},{1,15},{2,0},{3,1},{4,2},{5,3},{6,4},{7,5},{8,6},{9,7},{10,... | collective-permute-start | bytes 393224 | tf_op jit(solution)/shard_map/ppermute | solution.py:198
  99.7 7.3 %collective-permute-start.30 = (bf16[512,128]{1,0:T(8,128)(2,1)S(1)}, bf16[512,128]{1,0:T(8,128)(2,1)S(1)}, u32[]{:S(2)}, u32[]{:S(2)}) collective-permute-start(bf16[512,128]{1,0:T(8,128)(2,1)S(1)} %collective-permute-done.26.refs_10_), channel_id=1, source_target_pairs={{0,2},{1,3},{2,4},{3,5},{4,6},{5,7},{6,8},{7,9},{8,10},{9,11},{10,... | collective-permute-start | bytes 393224 | tf_op jit(solution)/shard_map/ppermute | solution.py:198
  101.0 8.1 %collective-permute-start.32 = (bf16[512,128]{1,0:T(8,128)(2,1)S(1)}, bf16[512,128]{1,0:T(8,128)(2,1)S(1)}, u32[]{:S(2)}, u32[]{:S(2)}) collective-permute-start(bf16[512,128]{1,0:T(8,128)(2,1)S(1)} %collective-permute-done.28.refs_12_), channel_id=1, source_target_pairs={{0,2},{1,3},{2,4},{3,5},{4,6},{5,7},{6,8},{7,9},{8,10},{9,11},{10,... | collective-permute-start | bytes 393224 | tf_op jit(solution)/shard_map/ppermute | solution.py:198
  101.0 8.1 %collective-permute-start.35 = (bf16[512,128]{1,0:T(8,128)(2,1)S(1)}, bf16[512,128]{1,0:T(8,128)(2,1)S(1)}, u32[]{:S(2)}, u32[]{:S(2)}) collective-permute-start(bf16[512,128]{1,0:T(8,128)(2,1)S(1)} %collective-permute-done.31.refs_15_), channel_id=1, source_target_pairs={{0,14},{1,15},{2,0},{3,1},{4,2},{5,3},{6,4},{7,5},{8,6},{9,7},{10,... | collective-permute-start | bytes 393224 | tf_op jit(solution)/shard_map/ppermute | solution.py:198
  104.1 7.7 %collective-permute-start.33 = (bf16[512,128]{1,0:T(8,128)(2,1)S(1)}, bf16[512,128]{1,0:T(8,128)(2,1)S(1)}, u32[]{:S(2)}, u32[]{:S(2)}) collective-permute-start(bf16[512,128]{1,0:T(8,128)(2,1)S(1)} %collective-permute-done.29.refs_13_), channel_id=1, source_target_pairs={{0,14},{1,15},{2,0},{3,1},{4,2},{5,3},{6,4},{7,5},{8,6},{9,7},{10,... | collective-permute-start | bytes 393224 | tf_op jit(solution)/shard_map/ppermute | solution.py:198
  106.9 5.0 %collective-permute-start.34 = (bf16[512,128]{1,0:T(8,128)(2,1)S(1)}, bf16[512,128]{1,0:T(8,128)(2,1)S(1)}, u32[]{:S(2)}, u32[]{:S(2)}) collective-permute-start(bf16[512,128]{1,0:T(8,128)(2,1)S(1)} %collective-permute-done.30.refs_14_), channel_id=1, source_target_pairs={{0,2},{1,3},{2,4},{3,5},{4,6},{5,7},{6,8},{7,9},{8,10},{9,11},{10,... | collective-permute-start | bytes 393224 | tf_op jit(solution)/shard_map/ppermute | solution.py:198
  109.1 6.7 %collective-permute-start.36 = (bf16[512,128]{1,0:T(8,128)(2,1)S(1)}, bf16[512,128]{1,0:T(8,128)(2,1)S(1)}, u32[]{:S(2)}, u32[]{:S(2)}) collective-permute-start(bf16[512,128]{1,0:T(8,128)(2,1)S(1)} %collective-permute-done.32.refs_16_), channel_id=1, source_target_pairs={{0,2},{1,3},{2,4},{3,5},{4,6},{5,7},{6,8},{7,9},{8,10},{9,11},{10,... | collective-permute-start | bytes 393224 | tf_op jit(solution)/shard_map/ppermute | solution.py:198
  109.1 6.7 %collective-permute-start.37 = (bf16[512,128]{1,0:T(8,128)(2,1)S(1)}, bf16[512,128]{1,0:T(8,128)(2,1)S(1)}, u32[]{:S(2)}, u32[]{:S(2)}) collective-permute-start(bf16[512,128]{1,0:T(8,128)(2,1)S(1)} %collective-permute-done.35.refs_19_), channel_id=1, source_target_pairs={{0,14},{1,15},{2,0},{3,1},{4,2},{5,3},{6,4},{7,5},{8,6},{9,7},{10,... | collective-permute-start | bytes 393224 | tf_op jit(solution)/shard_map/ppermute | solution.py:198
  115.8 1.9 %copy-start.3 = (bf16[96,128,128]{2,1,0:T(8,128)(2,1)S(1)}, bf16[96,128,128]{2,1,0:T(8,128)(2,1)}, u32[]{:S(2)}) copy-start(bf16[96,128,128]{2,1,0:T(8,128)(2,1)} %refs_4_.1) | copy-start | bytes 9437188
  126.5 14.7 %all-to-all-start.1 = ((s16[8,528,128]{2,1,0:T(8,128)(2,1)}), s16[8,528,128]{2,1,0:T(8,128)(2,1)S(1)}, u32[]{:S(2)}, u32[]{:S(2)}) async-start(s16[8,528,128]{2,1,0:T(8,128)(2,1)} %later_products.1), calls=%async_computation.1 | async-start | bytes 2162688 | tf_op jit(solution)/shard_map/all_to_all | solution.py:317
  141.7 10.0 %collective-permute-start.38 = (f32[256,128]{1,0:T(8,128)S(1)}, f32[256,128]{1,0:T(8,128)S(1)}, u32[]{:S(2)}, u32[]{:S(2)}) collective-permute-start(f32[256,128]{1,0:T(8,128)S(1)} %get-tuple-element.10), channel_id=1, source_target_pairs={{0,1},{1,0},{2,3},{3,2},{4,5},{5,4},{6,7},{7,6},{8,9},{9,8},{10,11... | collective-permute-start | bytes 393224 | tf_op jit(solution)/shard_map/ppermute | solution.py:198

commit v2 on v1

--- a/solution.py
+++ b/solution.py
@@ -26,11 +26,24 @@
     return pl.BlockSpec(memory_space=SMEM)
 
 
+def in_hbm(value):
+    return pltpu.with_memory_space_constraint(value, pltpu.HBM)
+
+
 def params():
-    return pltpu.CompilerParams(vmem_limit_bytes=40 * 1024 * 1024)
-
-
-def column_kernel(source_ref, count_ref, tiles_ref, sums_ref):
+    return pltpu.CompilerParams(vmem_limit_bytes=16 * 1024 * 1024)
+
+
+def column_kernel(source_ref, count_ref, given_ref, sums_ref, tiles_ref, arrived):
+    slots = given_ref.shape[0]
+    chunk = slots // arrived.shape[0]
+    copies = []
+    for c in range(arrived.shape[0]):
+        span = pl.ds(c * chunk, chunk)
+        copies.append(
+            pltpu.make_async_copy(given_ref.at[span], tiles_ref.at[span], arrived.at[c])
+        )
+        copies[c].start()
     sums_ref[...] = jnp.zeros_like(sums_ref)
 
     def slot(k, carry):
@@ -38,7 +51,9 @@
         sums_ref[pl.ds(source_ref[k], 1), :] += column
         return carry
 
-    lax.fori_loop(0, count_ref[0], slot, 0)
+    for c in range(arrived.shape[0]):
+        copies[c].wait()
+        lax.fori_loop(c * chunk, jnp.minimum((c + 1) * chunk, count_ref[0]), slot, 0)
 
 
 def seed_kernel(first_ref, ids_ref, counts_ref):
@@ -92,24 +107,54 @@
     lax.while_loop(more, walk, (start, jnp.min(start)))
 
 
-def products(source_ref, target_ref, count_ref, tiles_refs, panel, total, out_ref):
-    unroll = 8
-    slots = tiles_refs[0].shape[0]
-    total[...] = jnp.zeros_like(total)
-    for which, tiles_ref in enumerate(tiles_refs):
-
-        def group(g, carry, which=which, tiles_ref=tiles_ref):
-            for u in range(unroll):
-                k = g * unroll + u
-                at = which * slots + k
-                target = target_ref[at]
-                total[target] += jnp.dot(
-                    tiles_ref[k], panel[source_ref[at]], preferred_element_type=jnp.float32
-                )
-            return carry
-
-        lax.fori_loop(0, (count_ref[which] + unroll - 1) // unroll, group, 0)
-    receivers = out_ref.shape[0]
+UNROLL = 8
+
+
+def fetch(group, first, facts_ref, own_ref, sib_ref, tiles, arrived):
+    slots = own_ref.shape[0]
+    side = group % 2
+    for u in range(UNROLL):
+        tile = facts_ref[0, jnp.minimum(first + group * UNROLL + u, 2 * slots - 1)]
+
+        @pl.when(tile < slots)
+        def _(tile=tile, u=u):
+            pltpu.make_async_copy(own_ref.at[tile], tiles.at[side, u], arrived.at[side]).start()
+
+        @pl.when(tile >= slots)
+        def _(tile=tile, u=u):
+            pltpu.make_async_copy(
+                sib_ref.at[tile - slots], tiles.at[side, u], arrived.at[side]
+            ).start()
+
+
+def products(first, last, facts_ref, own_ref, sib_ref, panel, total, tiles, arrived):
+    slots = own_ref.shape[0]
+    dummy = total.shape[0] - 1
+    groups = (last - first + UNROLL - 1) // UNROLL
+
+    def step(g, carry):
+        @pl.when(g + 1 < groups)
+        def _():
+            fetch(g + 1, first, facts_ref, own_ref, sib_ref, tiles, arrived)
+
+        side = g % 2
+        pltpu.make_async_copy(own_ref.at[pl.ds(0, UNROLL)], tiles.at[side], arrived.at[side]).wait()
+        for u in range(UNROLL):
+            wanted = first + g * UNROLL + u
+            k = jnp.minimum(wanted, 2 * slots - 1)
+            live = wanted < last
+            target = jnp.where(live, facts_ref[2, k], dummy)
+            source = jnp.where(live, facts_ref[1, k], 0)
+            rows = pl.ds(pl.multiple_of(source * TILE, TILE), TILE)
+            total[target] += jnp.dot(
+                tiles[side, u], panel[rows, :], preferred_element_type=jnp.float32
+            )
+        return carry
+
+    lax.fori_loop(0, groups, step, 0)
+
+
+def encode(total, out_ref):
     per = (out_ref.shape[1] - 16) // TILE
 
     def send(r, carry):
@@ -127,36 +172,57 @@
         out_ref[r, per * TILE : per * TILE + 16, :] = tail
         return carry
 
-    lax.fori_loop(0, receivers, send, 0)
-
-
-def first_kernel(pieces, source_ref, target_ref, count_ref, chip_ref, sums_ref, own_ref, sib_ref, *refs):
-    piece_refs = refs[:pieces]
-    out_ref, inverse_ref, panel, total, ordered = refs[pieces:]
-    per = piece_refs[0].shape[0] // TILE
-    ordered[...] = jnp.zeros_like(ordered)
-    for p in range(pieces):
-        ordered[p * per : (p + 1) * per, :] = sums_ref[chip_ref[p]]
-    inverse = (1.0 / jnp.maximum(ordered[...], 1.0)).T
-    for p in range(pieces):
-        for t in range(per):
-            column = inverse[:, p * per + t : p * per + t + 1]
-            code = piece_refs[p][t * TILE : (t + 1) * TILE, :].astype(jnp.float32)
-            score = (code + HALF) * ((HIGH - LOW) / STEPS) + LOW
-            panel[chip_ref[p] * per + t] = (score * column).astype(jnp.bfloat16)
-            if p == 0:
-                inverse_ref[t * TILE : (t + 1) * TILE, :] = jnp.broadcast_to(column, (TILE, LANES))
-    products(source_ref, target_ref, count_ref, (own_ref, sib_ref), panel, total, out_ref)
-
-
-def later_kernel(pieces, source_ref, target_ref, count_ref, chip_ref, own_ref, sib_ref, *refs):
-    piece_refs = refs[:pieces]
-    out_ref, panel, total = refs[pieces:]
-    per = piece_refs[0].shape[0] // TILE
-    for p in range(pieces):
-        for t in range(per):
-            panel[chip_ref[p] * per + t] = piece_refs[p][t * TILE : (t + 1) * TILE, :]
-    products(source_ref, target_ref, count_ref, (own_ref, sib_ref), panel, total, out_ref)
+    lax.fori_loop(0, out_ref.shape[0], send, 0)
+
+
+def stage_kernel(stage, first, last, coded, counts, *refs):
+    refs = list(refs)
+    facts_ref, bound_ref, chip_ref = refs[:3]
+    del refs[:3]
+    sums_ref = refs.pop(0) if coded else None
+    own_ref, sib_ref = refs[:2]
+    del refs[:2]
+    piece_refs = refs[: len(counts)]
+    del refs[: len(counts)]
+    if not first:
+        before = refs.pop(0)
+    out_ref = refs.pop(0)
+    inverse_ref = refs.pop(0) if coded and first else None
+    panel = refs.pop(0)
+    ordered = refs.pop(0) if coded else None
+    tiles, arrived = refs
+    start, end = bound_ref[stage], bound_ref[stage + 1]
+
+    @pl.when(end > start)
+    def _():
+        fetch(0, start, facts_ref, own_ref, sib_ref, tiles, arrived)
+
+    total = before if last else out_ref
+    if first:
+        total[...] = jnp.zeros_like(total)
+    per = piece_refs[0].shape[0] // TILE // counts[0]
+    if coded:
+        ordered[...] = jnp.zeros_like(ordered)
+        for p in range(sum(counts)):
+            ordered[p * per : (p + 1) * per, :] = sums_ref[chip_ref[p]]
+        inverse = (1.0 / jnp.maximum(ordered[...], 1.0)).T
+    at = 0
+    for piece_ref in piece_refs:
+        for t in range(piece_ref.shape[0] // TILE):
+            rows = piece_ref[t * TILE : (t + 1) * TILE, :]
+            if coded:
+                column = inverse[:, at : at + 1]
+                score = (rows.astype(jnp.float32) + HALF) * ((HIGH - LOW) / STEPS) + LOW
+                rows = (score * column).astype(jnp.bfloat16)
+                if first and at < per:
+                    inverse_ref[at * TILE : (at + 1) * TILE, :] = jnp.broadcast_to(
+                        column, (TILE, LANES)
+                    )
+            panel[at * TILE : (at + 1) * TILE, :] = rows
+            at += 1
+    products(start, end, facts_ref, own_ref, sib_ref, panel, total, tiles, arrived)
+    if last:
+        encode(total, out_ref)
 
 
 def current_kernel(scaled, parts_ref, restart_ref, inverse_ref, out_ref):
@@ -206,20 +272,6 @@
     def across(value):
         return by_col(value, lambda y, at, k: (1 - y, at, k))
 
-    def gather(block):
-        other = across(block)
-        pieces = [block, other]
-        names = [(0, 0), (1, 0)]
-        a, b, c, d = block, block, other, other
-        for step in range(1, depth // 2):
-            a, b = along(a, 1), along(b, -1)
-            c, d = along(c, 1), along(d, -1)
-            pieces += [a, b, c, d]
-            names += [(0, -step), (0, step), (1, -step), (1, step)]
-        pieces += [along(a, 1), along(d, -1)]
-        names += [(0, depth // 2), (1, depth // 2)]
-        return pieces, names
-
     half = columns // 2
     code = ((scores - LOW) * (STEPS / (HIGH - LOW)) + 0.5).astype(jnp.int32)
     code = (jnp.clip(code, 0, 65535) - 32768).astype(jnp.int16)
@@ -238,17 +290,13 @@
     sums = pl.pallas_call(
         column_kernel,
         out_shape=jax.ShapeDtypeStruct((band_tiles, TILE), jnp.float32),
-        in_specs=[smem(), smem(), vmem()],
+        in_specs=[smem(), smem(), pl.BlockSpec(memory_space=pl.ANY)],
         out_specs=vmem(),
+        scratch_shapes=[VMEM(tile_values.shape, tile_values.dtype), pltpu.SemaphoreType.DMA((4,))],
         compiler_params=params(),
         name="column_sums",
-    )(sources, tile_count, tile_values)
+    )(sources, tile_count, in_hbm(tile_values))
     sums = sums + sibling(sums)
-    step = 1
-    while step < depth:
-        sums = sums + by_col(sums, lambda y, at, k, step=step: (y, at ^ step, k))
-        step *= 2
-    sums = sums + across(sums)
 
     first_page = (row_index * grid_cols + col_index - core) * own_rows
     ids = lax.dynamic_slice_in_dim(seed_ids, core * half, half, 0).T
@@ -261,40 +309,121 @@
         name="seed_counts",
     )(first_page.reshape(1), ids)
 
-    slot_sources = jnp.concatenate([sources, sib_facts[0]])
-    slot_targets = jnp.concatenate([targets, sib_facts[1]])
-    counts = jnp.concatenate([tile_count, sib_facts[2, :1]])
-
-    def multiply(pieces, names, sums):
-        order = jnp.stack([(high ^ y) * depth + (z + d) % depth for y, d in names])
-        n = len(pieces)
-        parts = jax.ShapeDtypeStruct((grid_rows, per * TILE + 16, half), jnp.int16)
-        scratch = [
-            VMEM((band_tiles, TILE, half), jnp.bfloat16),
-            VMEM((grid_rows * per + 1, TILE, half), jnp.float32),
-        ]
-        if sums is not None:
-            return pl.pallas_call(
-                lambda *refs: first_kernel(n, *refs),
-                out_shape=(parts, jax.ShapeDtypeStruct((per * TILE, half), jnp.float32)),
-                in_specs=[smem()] * 4 + [vmem()] * (3 + n),
-                out_specs=(vmem(), vmem()),
-                scratch_shapes=scratch + [VMEM((TILE, TILE), jnp.float32)],
-                compiler_params=params(),
-                name="first_products",
-            )(
-                slot_sources, slot_targets, counts, order,
-                sums.reshape(chips, per, TILE), tile_values, sib_tiles, *pieces,
-            )
-        return pl.pallas_call(
-            lambda *refs: later_kernel(n, *refs),
-            out_shape=parts,
-            in_specs=[smem()] * 4 + [vmem()] * (2 + n),
-            out_specs=vmem(),
+    def stage_names():
+        yield [(0, 0), (1, 0)]
+        for step in range(1, depth // 2):
+            yield [(0, -step), (1, -step), (0, step), (1, step)]
+        yield [(0, depth // 2), (1, depth // 2)]
+
+    chip_lists = [
+        jnp.stack([(high ^ y) * depth + (z + d) % depth for y, d in names])
+        for names in stage_names()
+    ]
+    stage_of = jnp.concatenate(
+        [jnp.full((c.shape[0],), i, jnp.int32) for i, c in enumerate(chip_lists)]
+    )
+    place_of = jnp.concatenate([jnp.arange(c.shape[0], dtype=jnp.int32) for c in chip_lists])
+    all_chips = jnp.concatenate(chip_lists)
+    stage_total = len(chip_lists)
+    slot_ids = jnp.arange(2 * slots, dtype=jnp.int32)
+    source = jnp.concatenate([sources, sib_facts[0]])
+    target = jnp.concatenate([targets, sib_facts[1]])
+    hit = (source // per)[:, None] == all_chips[None, :]
+    stage = jnp.sum(jnp.where(hit, stage_of[None, :], 0), axis=1)
+    place = jnp.sum(jnp.where(hit, place_of[None, :], 0), axis=1) * per + source % per
+    stage = jnp.where(target < grid_rows * per, stage, stage_total)
+    key = stage * 2 * slots + slot_ids
+    position = jnp.sum((key[None, :] < key[:, None]).astype(jnp.int32), axis=1)
+    moved = position[:, None] == slot_ids[None, :]
+    slot_facts = jnp.stack(
+        [jnp.sum(jnp.where(moved, v[:, None], 0), axis=0) for v in (slot_ids, place, target)]
+    )
+    edges = jnp.arange(stage_total + 1, dtype=jnp.int32)
+    bounds = jnp.sum((stage[:, None] < edges[None, :]).astype(jnp.int32), axis=0)
+
+    parts_type = jax.ShapeDtypeStruct((grid_rows, per * TILE + 16, half), jnp.int16)
+    total_type = jax.ShapeDtypeStruct((grid_rows * per + 1, TILE, half), jnp.float32)
+
+    def multiply(i, pieces, total, sums):
+        coded, first, last = sums is not None, i == 0, i + 1 == stage_total
+        chip_list = chip_lists[i]
+        each = chip_list.shape[0]
+        counts = [each // len(pieces)] * len(pieces)
+        args = [slot_facts, bounds, chip_list]
+        specs = [smem()] * 3
+        if coded:
+            args.append(sums.reshape(chips, per, TILE))
+        specs += [vmem()] * (len(args) - len(specs)) + [pl.BlockSpec(memory_space=pl.ANY)] * 2
+        args += [in_hbm(tile_values), in_hbm(sib_tiles), *pieces]
+        aliases = {}
+        if not first:
+            if not last:
+                aliases = {len(args): 0}
+            args.append(total)
+        specs += [vmem()] * (len(args) - len(specs))
+        outs = [parts_type if last else total_type]
+        if coded and first:
+            outs.append(jax.ShapeDtypeStruct((per * TILE, half), jnp.float32))
+        scratch = [VMEM((each * per * TILE, half), jnp.bfloat16)]
+        if coded:
+            scratch.append(VMEM((TILE, TILE), jnp.float32))
+        scratch.append(VMEM((2, UNROLL, TILE, TILE), tile_values.dtype))
+        scratch.append(pltpu.SemaphoreType.DMA((2,)))
+        results = pl.pallas_call(
+            lambda *refs: stage_kernel(i, first, last, coded, counts, *refs),
+            out_shape=tuple(outs),
+            in_specs=specs,
+            out_specs=tuple([vmem()] * len(outs)),
             scratch_shapes=scratch,
+            input_output_aliases=aliases,
             compiler_params=params(),
-            name="later_products",
-        )(slot_sources, slot_targets, counts, order, tile_values, sib_tiles, *pieces)
+            cost_estimate=pl.CostEstimate(
+                flops=each * 9 * 2 * TILE * TILE * half,
+                bytes_accessed=each * 9 * TILE * TILE * 2,
+                transcendentals=0,
+            ),
+            name="products",
+        )(*args)
+        return results[0], results[1] if coded and first else None
+
+    tie = lax.optimization_barrier
+
+    def hop(sums, step):
+        return sums + by_col(sums, lambda y, at, k: (y, at ^ step, k))
+
+    def gather_and_multiply(block, sums):
+        coded = sums is not None
+        rows = block.shape[0]
+        both = jnp.concatenate([block, across(block)])
+        if coded:
+            both, sums = tie((both, sums))
+        arrived = [[both]]
+        a, b = both, both
+        total, inverse, done = None, None, 0
+        hops = 1
+        for step in range(1, depth // 2 + 1):
+            if step < depth // 2:
+                a, b = along(a, 1), along(b, -1)
+            else:
+                a, b = along(a[:rows], 1), along(b[rows:], -1)
+            if coded and step <= 2:
+                for _ in range(2):
+                    sums = hop(sums, hops) if hops < depth else sums + across(sums)
+                    hops *= 2
+                a, b, sums = tie((a, b, sums))
+            else:
+                most = done + 2 if coded else step
+                while done < min(most, step):
+                    total, found = multiply(done, arrived[done], total, sums)
+                    inverse = found if done == 0 else inverse
+                    done += 1
+                if step < depth // 2:
+                    a, b, total = tie((a, b, total))
+            arrived.append([a, b])
+        while done < len(arrived):
+            total, _ = multiply(done, arrived[done], total, sums)
+            done += 1
+        return total, inverse
 
     def update(parts, inverse, scaled):
         return pl.pallas_call(
@@ -308,12 +437,10 @@
             name="current",
         )(parts, restart, inverse)
 
-    pieces, names = gather(block)
-    parts, inverse = multiply(pieces, names, sums)
+    parts, inverse = gather_and_multiply(block, sums)
     parts = lax.all_to_all(parts, "row", 0, 0, tiled=True)
     panel = update(parts, inverse, True)
-    pieces, names = gather(panel)
-    parts = multiply(pieces, names, None)
+    parts, _ = gather_and_multiply(panel, None)
     parts = lax.all_to_all(parts, "row", 0, 0, tiled=True)
     current = update(parts, inverse, False)
     mine = lax.dynamic_slice_in_dim(current, core * own_rows, own_rows, 0)

time: 153 us -> 162 us (1.059); the launches traced: 152 us -> 160 us
  Pallas kernels: 31.1 us -> 51 us
  waiting for transfers between devices: 40.8 us -> 35.4 us
  local copies, waits for them, and re-layouts: 6.72 us -> 2.44 us
  starting transfers between devices: 70.3 us -> 66.1 us
    pallas_call x2 -> x10, Pallas kernels: 18.9 us -> 36.8 us  [multiply(): pl.pallas_call(lambda *refs: stage_kernel(i, first, last, coded, counts,...]
    ppermute x39 -> x27, starting transfers between devices: 61.7 us -> 51.5 us  [by_col(): return lax.ppermute(value, 'col', pairs)]
    all_to_all x2, starting transfers between devices: 8.53 us -> 14.7 us  [per_device(): parts = lax.all_to_all(parts, 'row', 0, 0, tiled=True)]
    unnamed x15 -> x9, local copies, waits for them, and re-layouts: 5.87 us -> 1.24 us
    all_to_all x2, waiting for transfers between devices: 14.8 us -> 10.5 us  [per_device(): parts = lax.all_to_all(parts, 'row', 0, 0, tiled=True)]
    ppermute x39 -> x27, waiting for transfers between devices: 26 us -> 25 us  [by_col(): return lax.ppermute(value, 'col', pairs)]
  transfers between devices with their start and end apart: 41 -> 29, of which waited for: 18 -> 12; matrix products, arithmetic and copies ran while one was open for 2% -> 3% of each run, Pallas kernels for 8% -> 25%
where the time goes in v2:
time: 162 us; the launch traced here: 160 us
  starting transfers between devices  66.1 us (41%)
  Pallas kernels  51 us (31%)
  waiting for transfers between devices  35.4 us (22%)
  other arithmetic  3.73 us (2%)
  local copies, waits for them, and re-layouts  2.44 us (2%)
    ppermute x27, starting transfers between devices, by_col(): return lax.ppermute(value, 'col', pairs)  51.5 us
    pallas_call x10, Pallas kernels, multiply(): pl.pallas_call(lambda *refs: stage_kernel(i, first, last, coded, counts,...  36.8 us
    ppermute x27, waiting for transfers between devices, by_col(): return lax.ppermute(value, 'col', pairs)  25 us
    all_to_all x2, starting transfers between devices, per_device(): parts = lax.all_to_all(parts, 'row', 0, 0, tiled=True)  14.7 us
    all_to_all x2, waiting for transfers between devices, per_device(): parts = lax.all_to_all(parts, 'row', 0, 0, tiled=True)  10.5 us
    pallas_call x1, Pallas kernels, per_device(): pl.pallas_call(seed_kernel, out_shape=jax.ShapeDtypeStruct((2 * own_rows,...  9.59 us
    pallas_call x1, Pallas kernels, per_device(): pl.pallas_call(column_kernel, out_shape=jax.ShapeDtypeStruct((band_tiles,...  3.78 us
  transfers between devices with their start and end apart: 29, of which 12 were waited for; matrix products, arithmetic and copies ran while one was open for 3% of the time, Pallas kernels for 25%

profile of v2, /device:TPU:1, one launch (start us, length us, event | category | flops | bytes accessed | tf_op | source)
XLA Modules:
  0.0 159.7 jit_solution(5588145133259189244)
XLA Ops:
  0.0 3.2 %collective-permute-start.1 = (bf16[96,128,128]{2,1,0:T(8,128)(2,1)}, bf16[96,128,128]{2,1,0:T(8,128)(2,1)}, u32[]{:S(2)}, u32[]{:S(2)}) collective-permute-start(bf16[96,128,128]{2,1,0:T(8,128)(2,1)} %refs_3_.9), channel_id=1, source_target_pairs={{0,1},{1,0},{2,3},{3,2},{4,5},{5,4},{6,7},{7,6},{8,9},{9,8},{10,11... | collective-permute-start | bytes 9437192 | tf_op jit(solution)/shard_map/ppermute | solution.py:264
  3.2 1.0 add_convert_fusion
  5.2 0.7 broadcast_subtract_fusion.source_ref
  5.8 3.8 %column_sums.1 = f32[64,128]{1,0:T(8,128)S(1)} custom-call(s32[96]{0:T(128)S(1)} %broadcast_subtract_fusion.source_ref, s32[1]{0:T(128)} %copy.22.count_ref, bf16[96,128,128]{2,1,0:T(8,128)(2,1)} %refs_3_.9), custom_call_target="tpu_custom_call" | custom-call | tf_op jit(solution)/shard_map/column_sums/pallas_call | solution.py:290
  10.9 1.4 collective-permute-start.3
  12.4 5.0 %collective-permute-done.3 = s16[512,128]{1,0:T(8,128)(2,1)S(1)} collective-permute-done((s16[512,128]{1,0:T(8,128)(2,1)S(1)}, s16[512,128]{1,0:T(8,128)(2,1)S(1)}, u32[]{:S(2)}, u32[]{:S(2)}) %collective-permute-start.3) | collective-permute-done | bytes 131104 | tf_op jit(solution)/shard_map/ppermute | solution.py:264
  17.8 3.9 %collective-permute-start.6 = (s16[1024,128]{1,0:T(8,128)(2,1)S(1)}, s16[1024,128]{1,0:T(8,128)(2,1)S(1)}, u32[]{:S(2)}, u32[]{:S(2)}) collective-permute-start(s16[1024,128]{1,0:T(8,128)(2,1)S(1)} %pad_add_fusion.refs_6_), channel_id=1, source_target_pairs={{0,14},{1,15},{2,0},{3,1},{4,2},{5,3},{6,4},{7,5},{8,6},{9,7},{10,... | collective-permute-start | bytes 786440 | tf_op jit(solution)/shard_map/ppermute | solution.py:264
  21.8 3.6 %collective-permute-done.7 = f32[64,128]{1,0:T(8,128)S(1)} collective-permute-done((f32[64,128]{1,0:T(8,128)S(1)}, f32[64,128]{1,0:T(8,128)S(1)}, u32[]{:S(2)}, u32[]{:S(2)}) %collective-permute-start.7) | collective-permute-done | bytes 32800 | tf_op jit(solution)/shard_map/ppermute | solution.py:264
  25.5 4.6 %collective-permute-start.8 = (f32[64,128]{1,0:T(8,128)S(1)}, f32[64,128]{1,0:T(8,128)S(1)}, u32[]{:S(2)}, u32[]{:S(2)}) collective-permute-start(f32[64,128]{1,0:T(8,128)S(1)} %add.250), channel_id=1, source_target_pairs={{0,4},{1,5},{2,6},{3,7},{4,0},{5,1},{6,2},{7,3},{8,12},{9,13},{10,... | collective-permute-start | bytes 98312 | tf_op jit(solution)/shard_map/ppermute | solution.py:264
  30.1 1.2 collective-permute-done.8
  31.4 3.8 %collective-permute-start.11 = (f32[64,128]{1,0:T(8,128)S(1)}, f32[64,128]{1,0:T(8,128)S(1)}, u32[]{:S(2)}, u32[]{:S(2)}) collective-permute-start(f32[64,128]{1,0:T(8,128)S(1)} %add.251), channel_id=1, source_target_pairs={{0,8},{1,9},{2,10},{3,11},{4,12},{5,13},{6,14},{7,15},{8,0},{9,1},... | collective-permute-start | bytes 98312 | tf_op jit(solution)/shard_map/ppermute | solution.py:264
  35.5 1.2 collective-permute-start.9
  36.7 1.4 collective-permute-done.11
  38.1 2.3 %collective-permute-start.12 = (f32[64,128]{1,0:T(8,128)S(1)}, f32[64,128]{1,0:T(8,128)S(1)}, u32[]{:S(2)}, u32[]{:S(2)}) collective-permute-start(f32[64,128]{1,0:T(8,128)S(1)} %add.252), channel_id=1, source_target_pairs={{0,16},{1,17},{2,18},{3,19},{4,20},{5,21},{6,22},{7,23},{8,24},{9,... | collective-permute-start | bytes 98312 | tf_op jit(solution)/shard_map/ppermute | solution.py:264
  40.6 1.8 %collective-permute-done.12 = f32[64,128]{1,0:T(8,128)S(1)} collective-permute-done((f32[64,128]{1,0:T(8,128)S(1)}, f32[64,128]{1,0:T(8,128)S(1)}, u32[]{:S(2)}, u32[]{:S(2)}) %collective-permute-start.12) | collective-permute-done | bytes 32800 | tf_op jit(solution)/shard_map/ppermute | solution.py:264
  42.9 2.4 %collective-permute-start.14 = (s16[1024,128]{1,0:T(8,128)(2,1)S(1)}, s16[1024,128]{1,0:T(8,128)(2,1)S(1)}, u32[]{:S(2)}, u32[]{:S(2)}) collective-permute-start(s16[1024,128]{1,0:T(8,128)(2,1)S(1)} %collective-permute-done.10.refs_7_), channel_id=1, source_target_pairs={{0,14},{1,15},{2,0},{3,1},{4,2},{5,3},{6,4},{7,5},{8,6},{9,7},{10,... | collective-permute-start | bytes 786440 | tf_op jit(solution)/shard_map/ppermute | solution.py:264
  45.6 2.9 %products.10 = (f32[33,128,128]{2,1,0:T(8,128)S(1)}, f32[512,128]{1,0:T(8,128)S(1)}) custom-call(s32[3,192]{1,0:T(4,128)S(1)} %pad_add_fusion.1.refs_0_, s32[6]{0:T(128)S(1)} %convert_reduce_fusion.1.refs_1_, s32[2]{0:T(128)S(1)} %pad_add_fusion.6.refs_2_, f32[16,4,128]{2,1,0:T(4,128)S(1)} %bitcast.34, bf16[96,128,128]{2,1,0:T(8,128)(2,1)} %refs_3_.9, ...), custom_call_target="tpu_custom_call" | custom-call | flops 75497472 | bytes 589824 | tf_op jit(solution)/shard_map/products/pallas_call | solution.py:372
  48.5 3.5 %products.11.refs_8_ = f32[33,128,128]{2,1,0:T(8,128)S(1)} custom-call(s32[3,192]{1,0:T(4,128)S(1)} %pad_add_fusion.1.refs_0_, s32[6]{0:T(128)S(1)} %convert_reduce_fusion.1.refs_1_, s32[4]{0:T(128)S(1)} %get-tuple-element.63.refs_2_, f32[16,4,128]{2,1,0:T(4,128)S(1)} %bitcast.35, bf16[96,128,128]{2,1,0:T(8,128)(2,1)} %refs_3_.9, ...), custom_call_target="tpu_custom_call", output_to_operand_aliasing={{}: (8, {})} | custom-call | flops 150994944 | bytes 1179648 | tf_op jit(solution)/shard_map/products/pallas_call | solution.py:372
  52.0 2.0 %collective-permute-start.15 = (s16[512,128]{1,0:T(8,128)(2,1)S(1)}, s16[512,128]{1,0:T(8,128)(2,1)S(1)}, u32[]{:S(2)}, u32[]{:S(2)}) collective-permute-start(s16[512,128]{1,0:T(8,128)(2,1)S(1)} %slice.20), channel_id=1, source_target_pairs={{0,2},{1,3},{2,4},{3,5},{4,6},{5,7},{6,8},{7,9},{8,10},{9,11},{10,... | collective-permute-start | bytes 393224 | tf_op jit(solution)/shard_map/ppermute | solution.py:264
  54.1 1.0 collective-permute-start.16
  55.1 4.0 %products.12.refs_8_ = f32[33,128,128]{2,1,0:T(8,128)S(1)} custom-call(s32[3,192]{1,0:T(4,128)S(1)} %pad_add_fusion.1.refs_0_, s32[6]{0:T(128)S(1)} %convert_reduce_fusion.1.refs_1_, s32[4]{0:T(128)S(1)} %get-tuple-element.64.refs_2_, f32[16,4,128]{2,1,0:T(4,128)S(1)} %bitcast.36, bf16[96,128,128]{2,1,0:T(8,128)(2,1)} %refs_3_.9, ...), custom_call_target="tpu_custom_call", output_to_operand_aliasing={{}: (8, {})} | custom-call | flops 150994944 | bytes 1179648 | tf_op jit(solution)/shard_map/products/pallas_call | solution.py:372
  59.2 3.5 %products.13.refs_8_ = f32[33,128,128]{2,1,0:T(8,128)S(1)} custom-call(s32[3,192]{1,0:T(4,128)S(1)} %pad_add_fusion.1.refs_0_, s32[6]{0:T(128)S(1)} %convert_reduce_fusion.1.refs_1_, s32[4]{0:T(128)S(1)} %pad_add_fusion.7.refs_2_, f32[16,4,128]{2,1,0:T(4,128)S(1)} %bitcast.37, bf16[96,128,128]{2,1,0:T(8,128)(2,1)} %refs_3_.9, ...), custom_call_target="tpu_custom_call", output_to_operand_aliasing={{}: (8, {})} | custom-call | flops 150994944 | bytes 1179648 | tf_op jit(solution)/shard_map/products/pallas_call | solution.py:372
  62.7 4.9 %products.14 = s16[8,528,128]{2,1,0:T(8,128)(2,1)} custom-call(s32[3,192]{1,0:T(4,128)S(1)} %pad_add_fusion.1.refs_0_, s32[6]{0:T(128)S(1)} %convert_reduce_fusion.1.refs_1_, s32[2]{0:T(128)S(1)} %pad_add_fusion.4.refs_2_, f32[16,4,128]{2,1,0:T(4,128)S(1)} %bitcast.38, bf16[96,128,128]{2,1,0:T(8,128)(2,1)} %refs_3_.9, ...), custom_call_target="tpu_custom_call" | custom-call | flops 75497472 | bytes 589824 | tf_op jit(solution)/shard_map/products/pallas_call | solution.py:372
  67.5 7.0 %all-to-all-start = ((s16[8,528,128]{2,1,0:T(8,128)(2,1)}), s16[8,528,128]{2,1,0:T(8,128)(2,1)S(1)}, u32[]{:S(2)}, u32[]{:S(2)}) async-start(s16[8,528,128]{2,1,0:T(8,128)(2,1)} %products.14), calls=%async_computation | async-start | bytes 2162688 | tf_op jit(solution)/shard_map/all_to_all | solution.py:441
  74.6 0.9 constant_dynamic-slice_fusion.2
  75.4 1.2 copy.15
  76.7 9.6 %seed_counts.1.refs_1_ = f32[512,128]{1,0:T(8,128)S(1)} custom-call(s32[1]{0:T(128)} %bitcast.25.first_ref, s32[1024,128]{1,0:T(8,128)S(1)} %bitcast.33), custom_call_target="tpu_custom_call" | custom-call | tf_op jit(solution)/shard_map/seed_counts/pallas_call | solution.py:303
  86.7 1.4 collective-permute-start.17
  88.1 5.4 %collective-permute-done.17 = bf16[512,128]{1,0:T(8,128)(2,1)S(1)} collective-permute-done((bf16[512,128]{1,0:T(8,128)(2,1)S(1)}, bf16[512,128]{1,0:T(8,128)(2,1)S(1)}, u32[]{:S(2)}, u32[]{:S(2)}) %collective-permute-start.17) | collective-permute-done | bytes 131104 | tf_op jit(solution)/shard_map/ppermute | solution.py:264
  93.7 2.7 %collective-permute-start.19 = (bf16[1024,128]{1,0:T(8,128)(2,1)S(1)}, bf16[1024,128]{1,0:T(8,128)(2,1)S(1)}, u32[]{:S(2)}, u32[]{:S(2)}) collective-permute-start(bf16[1024,128]{1,0:T(8,128)(2,1)S(1)} %pad_maximum_fusion.refs_5_), channel_id=1, source_target_pairs={{0,14},{1,15},{2,0},{3,1},{4,2},{5,3},{6,4},{7,5},{8,6},{9,7},{10,... | collective-permute-start | bytes 786440 | tf_op jit(solution)/shard_map/ppermute | solution.py:264
  96.3 2.9 %products.15.refs_7_ = f32[33,128,128]{2,1,0:T(8,128)S(1)} custom-call(s32[3,192]{1,0:T(4,128)S(1)} %pad_add_fusion.1.refs_0_, s32[6]{0:T(128)S(1)} %convert_reduce_fusion.1.refs_1_, s32[2]{0:T(128)S(1)} %pad_add_fusion.6.refs_2_, bf16[96,128,128]{2,1,0:T(8,128)(2,1)} %refs_3_.9, bf16[96,128,128]{2,1,0:T(8,128)(2,1)} %collective-permute-done.1.refs_5_.refs_4_, ...), custom_call_target="tpu_custom_call" | custom-call | flops 75497472 | bytes 589824 | tf_op jit(solution)/shard_map/products/pallas_call | solution.py:372
  99.2 0.9 collective-permute-done.18.refs_5_
  100.1 2.7 %collective-permute-start.21 = (bf16[1024,128]{1,0:T(8,128)(2,1)S(1)}, bf16[1024,128]{1,0:T(8,128)(2,1)S(1)}, u32[]{:S(2)}, u32[]{:S(2)}) collective-permute-start(bf16[1024,128]{1,0:T(8,128)(2,1)S(1)} %collective-permute-done.19.refs_6_), channel_id=1, source_target_pairs={{0,14},{1,15},{2,0},{3,1},{4,2},{5,3},{6,4},{7,5},{8,6},{9,7},{10,... | collective-permute-start | bytes 786440 | tf_op jit(solution)/shard_map/ppermute | solution.py:264
  102.8 3.2 %products.16.refs_7_ = f32[33,128,128]{2,1,0:T(8,128)S(1)} custom-call(s32[3,192]{1,0:T(4,128)S(1)} %pad_add_fusion.1.refs_0_, s32[6]{0:T(128)S(1)} %convert_reduce_fusion.1.refs_1_, s32[4]{0:T(128)S(1)} %get-tuple-element.63.refs_2_, bf16[96,128,128]{2,1,0:T(8,128)(2,1)} %refs_3_.9, ...), custom_call_target="tpu_custom_call", output_to_operand_aliasing={{}: (7, {})} | custom-call | flops 150994944 | bytes 1179648 | tf_op jit(solution)/shard_map/products/pallas_call | solution.py:372
  106.0 3.1 %collective-permute-done.20.refs_5_ = bf16[1024,128]{1,0:T(8,128)(2,1)S(1)} collective-permute-done((bf16[1024,128]{1,0:T(8,128)(2,1)S(1)}, bf16[1024,128]{1,0:T(8,128)(2,1)S(1)}, u32[]{:S(2)}, u32[]{:S(2)}) %collective-permute-start.20) | collective-permute-done | bytes 262176 | tf_op jit(solution)/shard_map/ppermute | solution.py:264
  109.1 1.0 collective-permute-start.22
  110.0 1.7 %collective-permute-start.23 = (bf16[1024,128]{1,0:T(8,128)(2,1)S(1)}, bf16[1024,128]{1,0:T(8,128)(2,1)S(1)}, u32[]{:S(2)}, u32[]{:S(2)}) collective-permute-start(bf16[1024,128]{1,0:T(8,128)(2,1)S(1)} %collective-permute-done.21.refs_6_), channel_id=1, source_target_pairs={{0,14},{1,15},{2,0},{3,1},{4,2},{5,3},{6,4},{7,5},{8,6},{9,7},{10,... | collective-permute-start | bytes 786440 | tf_op jit(solution)/shard_map/ppermute | solution.py:264
  111.8 4.0 %products.17.refs_7_ = f32[33,128,128]{2,1,0:T(8,128)S(1)} custom-call(s32[3,192]{1,0:T(4,128)S(1)} %pad_add_fusion.1.refs_0_, s32[6]{0:T(128)S(1)} %convert_reduce_fusion.1.refs_1_, s32[4]{0:T(128)S(1)} %get-tuple-element.64.refs_2_, bf16[96,128,128]{2,1,0:T(8,128)(2,1)} %refs_3_.9, ...), custom_call_target="tpu_custom_call", output_to_operand_aliasing={{}: (7, {})} | custom-call | flops 150994944 | bytes 1179648 | tf_op jit(solution)/shard_map/products/pallas_call | solution.py:372
  115.8 1.4 collective-permute-done.22.refs_5_
  117.1 1.2 collective-permute-start.24
  118.4 1.6 %collective-permute-start.25 = (bf16[512,128]{1,0:T(8,128)(2,1)S(1)}, bf16[512,128]{1,0:T(8,128)(2,1)S(1)}, u32[]{:S(2)}, u32[]{:S(2)}) collective-permute-start(bf16[512,128]{1,0:T(8,128)(2,1)S(1)} %slice.23), channel_id=1, source_target_pairs={{0,14},{1,15},{2,0},{3,1},{4,2},{5,3},{6,4},{7,5},{8,6},{9,7},{10,... | collective-permute-start | bytes 393224 | tf_op jit(solution)/shard_map/ppermute | solution.py:264
  120.0 3.2 %products.18.refs_7_ = f32[33,128,128]{2,1,0:T(8,128)S(1)} custom-call(s32[3,192]{1,0:T(4,128)S(1)} %pad_add_fusion.1.refs_0_, s32[6]{0:T(128)S(1)} %convert_reduce_fusion.1.refs_1_, s32[4]{0:T(128)S(1)} %pad_add_fusion.7.refs_2_, bf16[96,128,128]{2,1,0:T(8,128)(2,1)} %refs_3_.9, ...), custom_call_target="tpu_custom_call", output_to_operand_aliasing={{}: (7, {})} | custom-call | flops 150994944 | bytes 1179648 | tf_op jit(solution)/shard_map/products/pallas_call | solution.py:372
  123.2 4.8 %products.19 = s16[8,528,128]{2,1,0:T(8,128)(2,1)} custom-call(s32[3,192]{1,0:T(4,128)S(1)} %pad_add_fusion.1.refs_0_, s32[6]{0:T(128)S(1)} %convert_reduce_fusion.1.refs_1_, s32[2]{0:T(128)S(1)} %pad_add_fusion.4.refs_2_, bf16[96,128,128]{2,1,0:T(8,128)(2,1)} %refs_3_.9, bf16[96,128,128]{2,1,0:T(8,128)(2,1)} %collective-permute-done.1.refs_5_.refs_4_, ...), custom_call_target="tpu_custom_call" | custom-call | flops 75497472 | bytes 589824 | tf_op jit(solution)/shard_map/products/pallas_call | solution.py:372
  128.1 7.6 %all-to-all-start.1 = ((s16[8,528,128]{2,1,0:T(8,128)(2,1)}), s16[8,528,128]{2,1,0:T(8,128)(2,1)S(1)}, u32[]{:S(2)}, u32[]{:S(2)}) async-start(s16[8,528,128]{2,1,0:T(8,128)(2,1)} %products.19), calls=%async_computation.1 | async-start | bytes 2162688 | tf_op jit(solution)/shard_map/all_to_all | solution.py:444
  135.7 10.4 %all-to-all-done.1.refs_0_ = s16[8,528,128]{2,1,0:T(8,128)(2,1)S(1)} async-done(((s16[8,528,128]{2,1,0:T(8,128)(2,1)}), s16[8,528,128]{2,1,0:T(8,128)(2,1)S(1)}, u32[]{:S(2)}, u32[]{:S(2)}) %all-to-all-start.1) | async-done | bytes 1081376 | tf_op jit(solution)/shard_map/all_to_all | solution.py:444
  146.5 11.5 %collective-permute-start.26 = (f32[256,128]{1,0:T(8,128)S(1)}, f32[256,128]{1,0:T(8,128)S(1)}, u32[]{:S(2)}, u32[]{:S(2)}) collective-permute-start(f32[256,128]{1,0:T(8,128)S(1)} %get-tuple-element.57), channel_id=1, source_target_pairs={{0,1},{1,0},{2,3},{3,2},{4,5},{5,4},{6,7},{7,6},{8,9},{9,8},{10,11... | collective-permute-start | bytes 393224 | tf_op jit(solution)/shard_map/ppermute | solution.py:264
  158.0 1.0 collective-permute-done.26
  159.0 0.7 maximum_select_fusion
  (73 shorter events, 4.6 us)
Async XLA Ops:
  0.0 74.6 %copy-start = (s32[256,1024]{1,0:T(8,128)S(1)}, s32[256,1024]{1,0:T(8,128)}, u32[]{:S(2)}) copy-start(s32[256,1024]{1,0:T(8,128)} %param.11) | copy-start | bytes 3145732
  0.0 9.8 %copy-start.3 = (s32[96]{0:T(128)S(1)}, s32[96]{0:T(128)}, u32[]{:S(2)}) copy-start(s32[96]{0:T(128)} %param.9) | copy-start | bytes 1156
  0.0 9.8 %copy-start.1 = (s32[96]{0:T(128)S(1)}, s32[96]{0:T(128)}, u32[]{:S(2)}) copy-start(s32[96]{0:T(128)} %param.8) | copy-start | bytes 1156
  0.0 45.6 %collective-permute-start.1 = (bf16[96,128,128]{2,1,0:T(8,128)(2,1)}, bf16[96,128,128]{2,1,0:T(8,128)(2,1)}, u32[]{:S(2)}, u32[]{:S(2)}) collective-permute-start(bf16[96,128,128]{2,1,0:T(8,128)(2,1)} %refs_3_.9), channel_id=1, source_target_pairs={{0,1},{1,0},{2,3},{3,2},{4,5},{5,4},{6,7},{7,6},{8,9},{9,8},{10,11... | collective-permute-start | bytes 9437192 | tf_op jit(solution)/shard_map/ppermute | solution.py:264
  4.3 6.5 %collective-permute-start.2 = (s16[256,128]{1,0:T(8,128)(2,1)S(1)}, s16[256,128]{1,0:T(8,128)(2,1)S(1)}, u32[]{:S(2)}, u32[]{:S(2)}) collective-permute-start(s16[256,128]{1,0:T(8,128)(2,1)S(1)} %get-tuple-element.59), channel_id=1, source_target_pairs={{0,1},{1,0},{2,3},{3,2},{4,5},{5,4},{6,7},{7,6},{8,9},{9,8},{10,11... | collective-permute-start | bytes 196616 | tf_op jit(solution)/shard_map/ppermute | solution.py:264
  5.8 15.9 %copy-start.2 = (s32[16]{0:T(128)S(1)}, s32[16]{0:T(128)}, u32[]{:S(2)}) copy-start(s32[16]{0:T(128)} %constant.176.clone.1) | copy-start | bytes 196
  9.6 2.8 %collective-permute-start.4 = (f32[64,128]{1,0:T(8,128)S(1)}, f32[64,128]{1,0:T(8,128)S(1)}, u32[]{:S(2)}, u32[]{:S(2)}) collective-permute-start(f32[64,128]{1,0:T(8,128)S(1)} %column_sums.1), channel_id=1, source_target_pairs={{0,1},{1,0},{2,3},{3,2},{4,5},{5,4},{6,7},{7,6},{8,9},{9,8},{10,11... | collective-permute-start | bytes 98312 | tf_op jit(solution)/shard_map/ppermute | solution.py:264
  9.9 2.4 %collective-permute-start = (s32[3,96]{1,0:T(4,128)S(1)}, s32[3,96]{1,0:T(4,128)S(1)}, u32[]{:S(2)}, u32[]{:S(2)}) collective-permute-start(s32[3,96]{1,0:T(4,128)S(1)} %add_add_fusion), channel_id=1, source_target_pairs={{0,1},{1,0},{2,3},{3,2},{4,5},{5,4},{6,7},{7,6},{8,9},{9,8},{10,11... | collective-permute-start | bytes 3464 | tf_op jit(solution)/shard_map/ppermute | solution.py:264
  10.9 6.5 %collective-permute-start.3 = (s16[512,128]{1,0:T(8,128)(2,1)S(1)}, s16[512,128]{1,0:T(8,128)(2,1)S(1)}, u32[]{:S(2)}, u32[]{:S(2)}) collective-permute-start(s16[512,128]{1,0:T(8,128)(2,1)S(1)} %add_select_fusion), channel_id=1, source_target_pairs={{0,16},{1,17},{2,18},{3,19},{4,20},{5,21},{6,22},{7,23},{8,24},{9,... | collective-permute-start | bytes 393224 | tf_op jit(solution)/shard_map/ppermute | solution.py:264
  17.4 13.9 %collective-permute-start.5 = (s16[1024,128]{1,0:T(8,128)(2,1)S(1)}, s16[1024,128]{1,0:T(8,128)(2,1)S(1)}, u32[]{:S(2)}, u32[]{:S(2)}) collective-permute-start(s16[1024,128]{1,0:T(8,128)(2,1)S(1)} %pad_add_fusion.refs_6_), channel_id=1, source_target_pairs={{0,2},{1,3},{2,4},{3,5},{4,6},{5,7},{6,8},{7,9},{8,10},{9,11},{10,... | collective-permute-start | bytes 786440 | tf_op jit(solution)/shard_map/ppermute | solution.py:264
  17.8 13.5 %collective-permute-start.6 = (s16[1024,128]{1,0:T(8,128)(2,1)S(1)}, s16[1024,128]{1,0:T(8,128)(2,1)S(1)}, u32[]{:S(2)}, u32[]{:S(2)}) collective-permute-start(s16[1024,128]{1,0:T(8,128)(2,1)S(1)} %pad_add_fusion.refs_6_), channel_id=1, source_target_pairs={{0,14},{1,15},{2,0},{3,1},{4,2},{5,3},{6,4},{7,5},{8,6},{9,7},{10,... | collective-permute-start | bytes 786440 | tf_op jit(solution)/shard_map/ppermute | solution.py:264
  21.7 3.7 %collective-permute-start.7 = (f32[64,128]{1,0:T(8,128)S(1)}, f32[64,128]{1,0:T(8,128)S(1)}, u32[]{:S(2)}, u32[]{:S(2)}) collective-permute-start(f32[64,128]{1,0:T(8,128)S(1)} %add.249), channel_id=1, source_target_pairs={{0,2},{1,3},{2,0},{3,1},{4,6},{5,7},{6,4},{7,5},{8,10},{9,11},{10,... | collective-permute-start | bytes 98312 | tf_op jit(solution)/shard_map/ppermute | solution.py:264
  25.5 5.9 %collective-permute-start.8 = (f32[64,128]{1,0:T(8,128)S(1)}, f32[64,128]{1,0:T(8,128)S(1)}, u32[]{:S(2)}, u32[]{:S(2)}) collective-permute-start(f32[64,128]{1,0:T(8,128)S(1)} %add.250), channel_id=1, source_target_pairs={{0,4},{1,5},{2,6},{3,7},{4,0},{5,1},{6,2},{7,3},{8,12},{9,13},{10,... | collective-permute-start | bytes 98312 | tf_op jit(solution)/shard_map/ppermute | solution.py:264
  31.4 6.8 %collective-permute-start.11 = (f32[64,128]{1,0:T(8,128)S(1)}, f32[64,128]{1,0:T(8,128)S(1)}, u32[]{:S(2)}, u32[]{:S(2)}) collective-permute-start(f32[64,128]{1,0:T(8,128)S(1)} %add.251), channel_id=1, source_target_pairs={{0,8},{1,9},{2,10},{3,11},{4,12},{5,13},{6,14},{7,15},{8,0},{9,1},... | collective-permute-start | bytes 98312 | tf_op jit(solution)/shard_map/ppermute | solution.py:264
  35.2 7.2 %collective-permute-start.10 = (s16[1024,128]{1,0:T(8,128)(2,1)S(1)}, s16[1024,128]{1,0:T(8,128)(2,1)S(1)}, u32[]{:S(2)}, u32[]{:S(2)}) collective-permute-start(s16[1024,128]{1,0:T(8,128)(2,1)S(1)} %collective-permute-done.6.refs_7_), channel_id=1, source_target_pairs={{0,14},{1,15},{2,0},{3,1},{4,2},{5,3},{6,4},{7,5},{8,6},{9,7},{10,... | collective-permute-start | bytes 786440 | tf_op jit(solution)/shard_map/ppermute | solution.py:264
  35.5 7.1 %collective-permute-start.9 = (s16[1024,128]{1,0:T(8,128)(2,1)S(1)}, s16[1024,128]{1,0:T(8,128)(2,1)S(1)}, u32[]{:S(2)}, u32[]{:S(2)}) collective-permute-start(s16[1024,128]{1,0:T(8,128)(2,1)S(1)} %collective-permute-done.5.refs_6_), channel_id=1, source_target_pairs={{0,2},{1,3},{2,4},{3,5},{4,6},{5,7},{6,8},{7,9},{8,10},{9,11},{10,... | collective-permute-start | bytes 786440 | tf_op jit(solution)/shard_map/ppermute | solution.py:264
  38.1 4.3 %collective-permute-start.12 = (f32[64,128]{1,0:T(8,128)S(1)}, f32[64,128]{1,0:T(8,128)S(1)}, u32[]{:S(2)}, u32[]{:S(2)}) collective-permute-start(f32[64,128]{1,0:T(8,128)S(1)} %add.252), channel_id=1, source_target_pairs={{0,16},{1,17},{2,18},{3,19},{4,20},{5,21},{6,22},{7,23},{8,24},{9,... | collective-permute-start | bytes 98312 | tf_op jit(solution)/shard_map/ppermute | solution.py:264
  42.6 9.4 %collective-permute-start.13 = (s16[1024,128]{1,0:T(8,128)(2,1)S(1)}, s16[1024,128]{1,0:T(8,128)(2,1)S(1)}, u32[]{:S(2)}, u32[]{:S(2)}) collective-permute-start(s16[1024,128]{1,0:T(8,128)(2,1)S(1)} %collective-permute-done.9.refs_6_), channel_id=1, source_target_pairs={{0,2},{1,3},{2,4},{3,5},{4,6},{5,7},{6,8},{7,9},{8,10},{9,11},{10,... | collective-permute-start | bytes 786440 | tf_op jit(solution)/shard_map/ppermute | solution.py:264
  42.9 9.1 %collective-permute-start.14 = (s16[1024,128]{1,0:T(8,128)(2,1)S(1)}, s16[1024,128]{1,0:T(8,128)(2,1)S(1)}, u32[]{:S(2)}, u32[]{:S(2)}) collective-permute-start(s16[1024,128]{1,0:T(8,128)(2,1)S(1)} %collective-permute-done.10.refs_7_), channel_id=1, source_target_pairs={{0,14},{1,15},{2,0},{3,1},{4,2},{5,3},{6,4},{7,5},{8,6},{9,7},{10,... | collective-permute-start | bytes 786440 | tf_op jit(solution)/shard_map/ppermute | solution.py:264
  52.0 10.6 %collective-permute-start.15 = (s16[512,128]{1,0:T(8,128)(2,1)S(1)}, s16[512,128]{1,0:T(8,128)(2,1)S(1)}, u32[]{:S(2)}, u32[]{:S(2)}) collective-permute-start(s16[512,128]{1,0:T(8,128)(2,1)S(1)} %slice.20), channel_id=1, source_target_pairs={{0,2},{1,3},{2,4},{3,5},{4,6},{5,7},{6,8},{7,9},{8,10},{9,11},{10,... | collective-permute-start | bytes 393224 | tf_op jit(solution)/shard_map/ppermute | solution.py:264
  54.1 8.6 %collective-permute-start.16 = (s16[512,128]{1,0:T(8,128)(2,1)S(1)}, s16[512,128]{1,0:T(8,128)(2,1)S(1)}, u32[]{:S(2)}, u32[]{:S(2)}) collective-permute-start(s16[512,128]{1,0:T(8,128)(2,1)S(1)} %slice.21), channel_id=1, source_target_pairs={{0,14},{1,15},{2,0},{3,1},{4,2},{5,3},{6,4},{7,5},{8,6},{9,7},{10,... | collective-permute-start | bytes 393224 | tf_op jit(solution)/shard_map/ppermute | solution.py:264
  67.5 18.8 %all-to-all-start = ((s16[8,528,128]{2,1,0:T(8,128)(2,1)}), s16[8,528,128]{2,1,0:T(8,128)(2,1)S(1)}, u32[]{:S(2)}, u32[]{:S(2)}) async-start(s16[8,528,128]{2,1,0:T(8,128)(2,1)} %products.14), calls=%async_computation | async-start | bytes 2162688 | tf_op jit(solution)/shard_map/all_to_all | solution.py:441
  86.7 6.9 %collective-permute-start.17 = (bf16[512,128]{1,0:T(8,128)(2,1)S(1)}, bf16[512,128]{1,0:T(8,128)(2,1)S(1)}, u32[]{:S(2)}, u32[]{:S(2)}) collective-permute-start(bf16[512,128]{1,0:T(8,128)(2,1)S(1)} %current.2), channel_id=1, source_target_pairs={{0,16},{1,17},{2,18},{3,19},{4,20},{5,21},{6,22},{7,23},{8,24},{9,... | collective-permute-start | bytes 393224 | tf_op jit(solution)/shard_map/ppermute | solution.py:264
  93.6 6.5 %collective-permute-start.18 = (bf16[1024,128]{1,0:T(8,128)(2,1)S(1)}, bf16[1024,128]{1,0:T(8,128)(2,1)S(1)}, u32[]{:S(2)}, u32[]{:S(2)}) collective-permute-start(bf16[1024,128]{1,0:T(8,128)(2,1)S(1)} %pad_maximum_fusion.refs_5_), channel_id=1, source_target_pairs={{0,2},{1,3},{2,4},{3,5},{4,6},{5,7},{6,8},{7,9},{8,10},{9,11},{10,... | collective-permute-start | bytes 786440 | tf_op jit(solution)/shard_map/ppermute | solution.py:264
  93.7 6.4 %collective-permute-start.19 = (bf16[1024,128]{1,0:T(8,128)(2,1)S(1)}, bf16[1024,128]{1,0:T(8,128)(2,1)S(1)}, u32[]{:S(2)}, u32[]{:S(2)}) collective-permute-start(bf16[1024,128]{1,0:T(8,128)(2,1)S(1)} %pad_maximum_fusion.refs_5_), channel_id=1, source_target_pairs={{0,14},{1,15},{2,0},{3,1},{4,2},{5,3},{6,4},{7,5},{8,6},{9,7},{10,... | collective-permute-start | bytes 786440 | tf_op jit(solution)/shard_map/ppermute | solution.py:264
  100.1 9.0 %collective-permute-start.20 = (bf16[1024,128]{1,0:T(8,128)(2,1)S(1)}, bf16[1024,128]{1,0:T(8,128)(2,1)S(1)}, u32[]{:S(2)}, u32[]{:S(2)}) collective-permute-start(bf16[1024,128]{1,0:T(8,128)(2,1)S(1)} %collective-permute-done.18.refs_5_), channel_id=1, source_target_pairs={{0,2},{1,3},{2,4},{3,5},{4,6},{5,7},{6,8},{7,9},{8,10},{9,11},{10,... | collective-permute-start | bytes 786440 | tf_op jit(solution)/shard_map/ppermute | solution.py:264
  100.1 9.0 %collective-permute-start.21 = (bf16[1024,128]{1,0:T(8,128)(2,1)S(1)}, bf16[1024,128]{1,0:T(8,128)(2,1)S(1)}, u32[]{:S(2)}, u32[]{:S(2)}) collective-permute-start(bf16[1024,128]{1,0:T(8,128)(2,1)S(1)} %collective-permute-done.19.refs_6_), channel_id=1, source_target_pairs={{0,14},{1,15},{2,0},{3,1},{4,2},{5,3},{6,4},{7,5},{8,6},{9,7},{10,... | collective-permute-start | bytes 786440 | tf_op jit(solution)/shard_map/ppermute | solution.py:264
  109.1 8.1 %collective-permute-start.22 = (bf16[1024,128]{1,0:T(8,128)(2,1)S(1)}, bf16[1024,128]{1,0:T(8,128)(2,1)S(1)}, u32[]{:S(2)}, u32[]{:S(2)}) collective-permute-start(bf16[1024,128]{1,0:T(8,128)(2,1)S(1)} %collective-permute-done.20.refs_5_), channel_id=1, source_target_pairs={{0,2},{1,3},{2,4},{3,5},{4,6},{5,7},{6,8},{7,9},{8,10},{9,11},{10,... | collective-permute-start | bytes 786440 | tf_op jit(solution)/shard_map/ppermute | solution.py:264
  110.0 7.1 %collective-permute-start.23 = (bf16[1024,128]{1,0:T(8,128)(2,1)S(1)}, bf16[1024,128]{1,0:T(8,128)(2,1)S(1)}, u32[]{:S(2)}, u32[]{:S(2)}) collective-permute-start(bf16[1024,128]{1,0:T(8,128)(2,1)S(1)} %collective-permute-done.21.refs_6_), channel_id=1, source_target_pairs={{0,14},{1,15},{2,0},{3,1},{4,2},{5,3},{6,4},{7,5},{8,6},{9,7},{10,... | collective-permute-start | bytes 786440 | tf_op jit(solution)/shard_map/ppermute | solution.py:264
  117.1 6.0 %collective-permute-start.24 = (bf16[512,128]{1,0:T(8,128)(2,1)S(1)}, bf16[512,128]{1,0:T(8,128)(2,1)S(1)}, u32[]{:S(2)}, u32[]{:S(2)}) collective-permute-start(bf16[512,128]{1,0:T(8,128)(2,1)S(1)} %slice.22), channel_id=1, source_target_pairs={{0,2},{1,3},{2,4},{3,5},{4,6},{5,7},{6,8},{7,9},{8,10},{9,11},{10,... | collective-permute-start | bytes 393224 | tf_op jit(solution)/shard_map/ppermute | solution.py:264
  118.4 4.8 %collective-permute-start.25 = (bf16[512,128]{1,0:T(8,128)(2,1)S(1)}, bf16[512,128]{1,0:T(8,128)(2,1)S(1)}, u32[]{:S(2)}, u32[]{:S(2)}) collective-permute-start(bf16[512,128]{1,0:T(8,128)(2,1)S(1)} %slice.23), channel_id=1, source_target_pairs={{0,14},{1,15},{2,0},{3,1},{4,2},{5,3},{6,4},{7,5},{8,6},{9,7},{10,... | collective-permute-start | bytes 393224 | tf_op jit(solution)/shard_map/ppermute | solution.py:264
  128.1 18.1 %all-to-all-start.1 = ((s16[8,528,128]{2,1,0:T(8,128)(2,1)}), s16[8,528,128]{2,1,0:T(8,128)(2,1)S(1)}, u32[]{:S(2)}, u32[]{:S(2)}) async-start(s16[8,528,128]{2,1,0:T(8,128)(2,1)} %products.19), calls=%async_computation.1 | async-start | bytes 2162688 | tf_op jit(solution)/shard_map/all_to_all | solution.py:444
  146.5 12.4 %collective-permute-start.26 = (f32[256,128]{1,0:T(8,128)S(1)}, f32[256,128]{1,0:T(8,128)S(1)}, u32[]{:S(2)}, u32[]{:S(2)}) collective-permute-start(f32[256,128]{1,0:T(8,128)S(1)} %get-tuple-element.57), channel_id=1, source_target_pairs={{0,1},{1,0},{2,3},{3,2},{4,5},{5,4},{6,7},{7,6},{8,9},{9,8},{10,11... | collective-permute-start | bytes 393224 | tf_op jit(solution)/shard_map/ppermute | solution.py:264

commit v3 on v1

--- a/solution.py
+++ b/solution.py
@@ -26,11 +26,28 @@
     return pl.BlockSpec(memory_space=SMEM)
 
 
+def anywhere(*_):
+    return pl.BlockSpec(memory_space=pl.ANY)
+
+
+def in_hbm(value):
+    return pltpu.with_memory_space_constraint(value, pltpu.HBM)
+
+
 def params():
-    return pltpu.CompilerParams(vmem_limit_bytes=40 * 1024 * 1024)
-
-
-def column_kernel(source_ref, count_ref, tiles_ref, sums_ref):
+    return pltpu.CompilerParams(vmem_limit_bytes=24 * 1024 * 1024)
+
+
+def column_kernel(source_ref, count_ref, given_ref, sums_ref, tiles_ref, arrived):
+    slots = given_ref.shape[0]
+    chunk = slots // arrived.shape[0]
+    copies = []
+    for c in range(arrived.shape[0]):
+        span = pl.ds(c * chunk, chunk)
+        copies.append(
+            pltpu.make_async_copy(given_ref.at[span], tiles_ref.at[span], arrived.at[c])
+        )
+        copies[c].start()
     sums_ref[...] = jnp.zeros_like(sums_ref)
 
     def slot(k, carry):
@@ -38,7 +55,20 @@
         sums_ref[pl.ds(source_ref[k], 1), :] += column
         return carry
 
-    lax.fori_loop(0, count_ref[0], slot, 0)
+    for c in range(arrived.shape[0]):
+        copies[c].wait()
+        lax.fori_loop(c * chunk, jnp.minimum((c + 1) * chunk, count_ref[0]), slot, 0)
+
+
+def total_kernel(rows, *refs):
+    *piece_refs, out_ref = refs
+    each = out_ref.shape[0]
+    total = jnp.zeros(out_ref.shape, jnp.float32)
+    for piece_ref in piece_refs:
+        code = piece_ref[rows : rows + 3 * each, :].astype(jnp.float32)
+        mantissa = code[each : 2 * each] * 4096.0 + code[2 * each :]
+        total += mantissa * jnp.exp2(code[:each] - 24.0)
+    out_ref[...] = total
 
 
 def seed_kernel(first_ref, ids_ref, counts_ref):
@@ -92,23 +122,40 @@
     lax.while_loop(more, walk, (start, jnp.min(start)))
 
 
-def products(source_ref, target_ref, count_ref, tiles_refs, panel, total, out_ref):
-    unroll = 8
-    slots = tiles_refs[0].shape[0]
-    total[...] = jnp.zeros_like(total)
-    for which, tiles_ref in enumerate(tiles_refs):
-
-        def group(g, carry, which=which, tiles_ref=tiles_ref):
+def fetch(own_ref, sib_ref, tiles, arrived):
+    slots = own_ref.shape[0]
+    copies = [
+        pltpu.make_async_copy(own_ref, tiles.at[pl.ds(0, slots)], arrived.at[0]),
+        pltpu.make_async_copy(sib_ref, tiles.at[pl.ds(slots, slots)], arrived.at[1]),
+    ]
+    for copy in copies:
+        copy.start()
+    return copies
+
+
+def products(facts_refs, copies, tiles, panel, total, out_ref):
+    unroll = 4
+    slots = tiles.shape[0] // 2
+    dummy = total.shape[0] - 1
+    for which, facts_ref in enumerate(facts_refs):
+        copies[which].wait()
+        pairs = facts_ref[3, 0]
+
+        def group(g, carry, base=which * slots, facts_ref=facts_ref, pairs=pairs):
             for u in range(unroll):
-                k = g * unroll + u
-                at = which * slots + k
-                target = target_ref[at]
-                total[target] += jnp.dot(
-                    tiles_ref[k], panel[source_ref[at]], preferred_element_type=jnp.float32
+                pair = g * unroll + u
+                at = 2 * pair
+                target = jnp.where(pair < pairs, facts_ref[2, at], dummy)
+                left = jnp.concatenate(
+                    [tiles[base + facts_ref[0, at]], tiles[base + facts_ref[0, at + 1]]], axis=1
                 )
+                right = jnp.concatenate(
+                    [panel[facts_ref[1, at]], panel[facts_ref[1, at + 1]]], axis=0
+                )
+                total[target] += jnp.dot(left, right, preferred_element_type=jnp.float32)
             return carry
 
-        lax.fori_loop(0, (count_ref[which] + unroll - 1) // unroll, group, 0)
+        lax.fori_loop(0, (pairs + unroll - 1) // unroll, group, 0)
     receivers = out_ref.shape[0]
     per = (out_ref.shape[1] - 16) // TILE
 
@@ -130,10 +177,12 @@
     lax.fori_loop(0, receivers, send, 0)
 
 
-def first_kernel(pieces, source_ref, target_ref, count_ref, chip_ref, sums_ref, own_ref, sib_ref, *refs):
+def first_kernel(pieces, rows, own_facts, sib_facts, chip_ref, sums_ref, own_ref, sib_ref, *refs):
     piece_refs = refs[:pieces]
-    out_ref, inverse_ref, panel, total, ordered = refs[pieces:]
-    per = piece_refs[0].shape[0] // TILE
+    out_ref, inverse_ref, panel, total, tiles, arrived, ordered = refs[pieces:]
+    copies = fetch(own_ref, sib_ref, tiles, arrived)
+    total[...] = jnp.zeros_like(total)
+    per = rows // TILE
     ordered[...] = jnp.zeros_like(ordered)
     for p in range(pieces):
         ordered[p * per : (p + 1) * per, :] = sums_ref[chip_ref[p]]
@@ -146,17 +195,21 @@
             panel[chip_ref[p] * per + t] = (score * column).astype(jnp.bfloat16)
             if p == 0:
                 inverse_ref[t * TILE : (t + 1) * TILE, :] = jnp.broadcast_to(column, (TILE, LANES))
-    products(source_ref, target_ref, count_ref, (own_ref, sib_ref), panel, total, out_ref)
-
-
-def later_kernel(pieces, source_ref, target_ref, count_ref, chip_ref, own_ref, sib_ref, *refs):
+    panel[pieces * per] = jnp.zeros((TILE, LANES), jnp.bfloat16)
+    products((own_facts, sib_facts), copies, tiles, panel, total, out_ref)
+
+
+def later_kernel(pieces, rows, own_facts, sib_facts, chip_ref, own_ref, sib_ref, *refs):
     piece_refs = refs[:pieces]
-    out_ref, panel, total = refs[pieces:]
-    per = piece_refs[0].shape[0] // TILE
+    out_ref, panel, total, tiles, arrived = refs[pieces:]
+    copies = fetch(own_ref, sib_ref, tiles, arrived)
+    total[...] = jnp.zeros_like(total)
+    per = rows // TILE
     for p in range(pieces):
         for t in range(per):
             panel[chip_ref[p] * per + t] = piece_refs[p][t * TILE : (t + 1) * TILE, :]
-    products(source_ref, target_ref, count_ref, (own_ref, sib_ref), panel, total, out_ref)
+    panel[pieces * per] = jnp.zeros((TILE, LANES), jnp.bfloat16)
+    products((own_facts, sib_facts), copies, tiles, panel, total, out_ref)
 
 
 def current_kernel(scaled, parts_ref, restart_ref, inverse_ref, out_ref):
@@ -228,27 +281,52 @@
     block = jnp.where(
         core == 0, jnp.concatenate([mine, theirs]), jnp.concatenate([theirs, mine])
     )
+    sib_tiles = sibling(tile_values)
     sources = tile_cols - row_index * band_tiles
-    targets = tile_rows // band_tiles * per + core * BT + tile_rows % BT
-    targets = jnp.where(jnp.arange(slots) < tile_count[0], targets, grid_rows * per)
-    facts = jnp.stack([sources, targets, jnp.broadcast_to(tile_count, (slots,))])
-    sib_facts = sibling(facts)
-    sib_tiles = sibling(tile_values)
-
     sums = pl.pallas_call(
         column_kernel,
         out_shape=jax.ShapeDtypeStruct((band_tiles, TILE), jnp.float32),
-        in_specs=[smem(), smem(), vmem()],
+        in_specs=[smem(), smem(), anywhere()],
         out_specs=vmem(),
+        scratch_shapes=[VMEM(tile_values.shape, tile_values.dtype), pltpu.SemaphoreType.DMA((4,))],
         compiler_params=params(),
         name="column_sums",
-    )(sources, tile_count, tile_values)
-    sums = sums + sibling(sums)
-    step = 1
-    while step < depth:
-        sums = sums + by_col(sums, lambda y, at, k, step=step: (y, at ^ step, k))
-        step *= 2
-    sums = sums + across(sums)
+    )(sources, tile_count, in_hbm(tile_values))
+
+    part = band_tiles // 2
+    given = sibling(lax.dynamic_slice_in_dim(sums, (1 - core) * part, part, 0))
+    given = given + lax.dynamic_slice_in_dim(sums, core * part, part, 0)
+    exponent = jnp.floor(jnp.log2(jnp.maximum(given, 1e-30))) + 1.0
+    mantissa = (given * jnp.exp2(24.0 - exponent) + 0.5).astype(jnp.int32)
+    tail = jnp.concatenate([exponent.astype(jnp.int32), mantissa >> 12, mantissa & 4095])
+    block = jnp.concatenate([block, tail.astype(jnp.int16)])
+
+    targets = tile_rows // band_tiles * per + core * BT + tile_rows % BT
+    live = jnp.arange(slots) < tile_count[0]
+    target_total = grid_rows * per
+    target_ids = jnp.arange(target_total, dtype=jnp.int32)
+    at_target = (targets[:, None] == target_ids[None, :]) & live[:, None]
+    filled = (jnp.sum(at_target.astype(jnp.int32), axis=0) + 1) // 2 * 2
+    start = jnp.sum(jnp.where(target_ids[:, None] < target_ids[None, :], filled[:, None], 0), axis=0)
+    slot_ids = jnp.arange(slots, dtype=jnp.int32)
+    alike = (targets[:, None] == targets[None, :]) & (slot_ids[None, :] < slot_ids[:, None])
+    place = jnp.sum(alike.astype(jnp.int32), axis=1)
+    place = place + jnp.sum(jnp.where(at_target, start[None, :], 0), axis=1)
+    long = slots + target_total
+    moved = (place[:, None] == jnp.arange(long)[None, :]) & live[:, None]
+
+    def spread(value):
+        return jnp.sum(jnp.where(moved, value[:, None], 0), axis=0)
+
+    facts = jnp.stack(
+        [
+            spread(slot_ids),
+            spread(sources - band_tiles) + band_tiles,
+            spread(targets),
+            jnp.broadcast_to(jnp.sum(filled) // 2, (long,)),
+        ]
+    )
+    sib_facts = sibling(facts)
 
     first_page = (row_index * grid_cols + col_index - core) * own_rows
     ids = lax.dynamic_slice_in_dim(seed_ids, core * half, half, 0).T
@@ -261,40 +339,37 @@
         name="seed_counts",
     )(first_page.reshape(1), ids)
 
-    slot_sources = jnp.concatenate([sources, sib_facts[0]])
-    slot_targets = jnp.concatenate([targets, sib_facts[1]])
-    counts = jnp.concatenate([tile_count, sib_facts[2, :1]])
-
     def multiply(pieces, names, sums):
         order = jnp.stack([(high ^ y) * depth + (z + d) % depth for y, d in names])
         n = len(pieces)
-        parts = jax.ShapeDtypeStruct((grid_rows, per * TILE + 16, half), jnp.int16)
+        rows = per * TILE
+        parts = jax.ShapeDtypeStruct((grid_rows, rows + 16, half), jnp.int16)
         scratch = [
-            VMEM((band_tiles, TILE, half), jnp.bfloat16),
-            VMEM((grid_rows * per + 1, TILE, half), jnp.float32),
+            VMEM((band_tiles + 1, TILE, half), jnp.bfloat16),
+            VMEM((target_total + 1, TILE, half), jnp.float32),
+            VMEM((2 * slots, TILE, TILE), tile_values.dtype),
+            pltpu.SemaphoreType.DMA((2,)),
         ]
+        tiles = (in_hbm(tile_values), in_hbm(sib_tiles))
         if sums is not None:
             return pl.pallas_call(
-                lambda *refs: first_kernel(n, *refs),
-                out_shape=(parts, jax.ShapeDtypeStruct((per * TILE, half), jnp.float32)),
-                in_specs=[smem()] * 4 + [vmem()] * (3 + n),
+                lambda *refs: first_kernel(n, rows, *refs),
+                out_shape=(parts, jax.ShapeDtypeStruct((rows, half), jnp.float32)),
+                in_specs=[smem()] * 3 + [vmem()] + [anywhere()] * 2 + [vmem()] * n,
                 out_specs=(vmem(), vmem()),
                 scratch_shapes=scratch + [VMEM((TILE, TILE), jnp.float32)],
                 compiler_params=params(),
                 name="first_products",
-            )(
-                slot_sources, slot_targets, counts, order,
-                sums.reshape(chips, per, TILE), tile_values, sib_tiles, *pieces,
-            )
+            )(facts, sib_facts, order, sums.reshape(chips, per, TILE), *tiles, *pieces)
         return pl.pallas_call(
-            lambda *refs: later_kernel(n, *refs),
+            lambda *refs: later_kernel(n, rows, *refs),
             out_shape=parts,
-            in_specs=[smem()] * 4 + [vmem()] * (2 + n),
+            in_specs=[smem()] * 3 + [anywhere()] * 2 + [vmem()] * n,
             out_specs=vmem(),
             scratch_shapes=scratch,
             compiler_params=params(),
             name="later_products",
-        )(slot_sources, slot_targets, counts, order, tile_values, sib_tiles, *pieces)
+        )(facts, sib_facts, order, *tiles, *pieces)
 
     def update(parts, inverse, scaled):
         return pl.pallas_call(
@@ -309,6 +384,18 @@
         )(parts, restart, inverse)
 
     pieces, names = gather(block)
+    found = pl.pallas_call(
+        lambda *refs: total_kernel(per * TILE, *refs),
+        out_shape=jax.ShapeDtypeStruct((part, TILE), jnp.float32),
+        in_specs=[vmem()] * len(pieces),
+        out_specs=vmem(),
+        compiler_params=params(),
+        name="column_totals",
+    )(*pieces)
+    other = sibling(found)
+    sums = jnp.where(
+        core == 0, jnp.concatenate([found, other]), jnp.concatenate([other, found])
+    )
     parts, inverse = multiply(pieces, names, sums)
     parts = lax.all_to_all(parts, "row", 0, 0, tiled=True)
     panel = update(parts, inverse, True)

time: 153 us -> 149 us (0.974)
  waiting for transfers between devices: 40.8 us -> 35.7 us
  between operations: 0.89 us -> 3.65 us
  local copies, waits for them, and re-layouts: 6.72 us -> 4.69 us
    ppermute x39 -> x36, waiting for transfers between devices: 26 us -> 19.2 us  [by_col(): return lax.ppermute(value, 'col', pairs)]
    unnamed x15 -> x13, local copies, waits for them, and re-layouts: 5.87 us -> 3.6 us
    all_to_all x2, waiting for transfers between devices: 14.8 us -> 16.5 us  [per_device(): parts = lax.all_to_all(parts, 'row', 0, 0, tiled=True)]
    ppermute x39 -> x36, starting transfers between devices: 61.7 us -> 60.4 us  [by_col(): return lax.ppermute(value, 'col', pairs)]
    pallas_call x2 -> x3, Pallas kernels: 18.9 us -> 17.6 us  [the longest x1 9.35 us: multiply(): pl.pallas_call(lambda *refs: first_kernel(n, rows, *refs), out_shape=(par...]
  transfers between devices with their start and end apart: 41 -> 38, of which waited for: 18 -> 19; matrix products, arithmetic and copies ran while one was open for 2% -> 4% of each run, Pallas kernels for 8% -> 8%
where the time goes in v3:
time: 149 us; the launch traced here: 148 us
  starting transfers between devices  70.2 us (47%)
  waiting for transfers between devices  35.7 us (24%)
  Pallas kernels  30.1 us (20%)
  local copies, waits for them, and re-layouts  4.69 us (3%)
  other arithmetic  3.85 us (3%)
  between operations  3.65 us (2%)
    ppermute x36, starting transfers between devices, by_col(): return lax.ppermute(value, 'col', pairs)  60.4 us
    ppermute x36, waiting for transfers between devices, by_col(): return lax.ppermute(value, 'col', pairs)  19.2 us
    all_to_all x2, waiting for transfers between devices, per_device(): parts = lax.all_to_all(parts, 'row', 0, 0, tiled=True)  16.5 us
    all_to_all x2, starting transfers between devices, per_device(): parts = lax.all_to_all(parts, 'row', 0, 0, tiled=True)  9.79 us
    pallas_call x1, Pallas kernels, multiply(): pl.pallas_call(lambda *refs: first_kernel(n, rows, *refs), out_shape=(par...  9.35 us
    pallas_call x1, Pallas kernels, per_device(): pl.pallas_call(seed_kernel, out_shape=jax.ShapeDtypeStruct((2 * own_rows,...  8.51 us
    pallas_call x1, Pallas kernels, multiply(): pl.pallas_call(lambda *refs: later_kernel(n, rows, *refs), out_shape=part...  8.14 us
    unnamed x13, local copies, waits for them, and re-layouts  3.6 us
  transfers between devices with their start and end apart: 38, of which 19 were waited for; matrix products, arithmetic and copies ran while one was open for 4% of the time, Pallas kernels for 8%

profile of v3, /device:TPU:1, one launch (start us, length us, event | category | flops | bytes accessed | tf_op | source)
XLA Modules:
  0.0 148.1 jit_solution(15609095369346646683)
XLA Ops:
  0.0 3.2 %collective-permute-start.1 = (bf16[96,128,128]{2,1,0:T(8,128)(2,1)}, bf16[96,128,128]{2,1,0:T(8,128)(2,1)}, u32[]{:S(2)}, u32[]{:S(2)}) collective-permute-start(bf16[96,128,128]{2,1,0:T(8,128)(2,1)} %refs_3_.1), channel_id=1, source_target_pairs={{0,1},{1,0},{2,3},{3,2},{4,5},{5,4},{6,7},{7,6},{8,9},{9,8},{10,11... | collective-permute-start | bytes 9437192 | tf_op jit(solution)/shard_map/ppermute | solution.py:251
  3.2 1.0 add_convert_fusion
  5.2 0.7 broadcast_add_fusion
  5.8 3.2 %column_sums.1 = f32[64,128]{1,0:T(8,128)S(1)} custom-call(s32[96]{0:T(128)S(1)} %get-tuple-element.17.source_ref, s32[1]{0:T(128)} %copy.10.count_ref, bf16[96,128,128]{2,1,0:T(8,128)(2,1)} %refs_3_.1), custom_call_target="tpu_custom_call" | custom-call | tf_op jit(solution)/shard_map/column_sums/pallas_call | solution.py:286
  9.3 1.0 collective-permute-done.3
  10.5 2.2 %collective-permute-start.4 = (s16[608,128]{1,0:T(8,128)(2,1)S(1)}, s16[608,128]{1,0:T(8,128)(2,1)S(1)}, u32[]{:S(2)}, u32[]{:S(2)}) collective-permute-start(s16[608,128]{1,0:T(8,128)(2,1)S(1)} %pad_add_fusion.refs_0_.refs_6_), channel_id=1, source_target_pairs={{0,16},{1,17},{2,18},{3,19},{4,20},{5,21},{6,22},{7,23},{8,24},{9,... | collective-permute-start | bytes 466952 | tf_op jit(solution)/shard_map/ppermute | solution.py:251
  12.8 1.3 collective-permute-start.5
  14.1 3.4 %collective-permute-done.4.refs_1_.refs_7_ = s16[608,128]{1,0:T(8,128)(2,1)S(1)} collective-permute-done((s16[608,128]{1,0:T(8,128)(2,1)S(1)}, s16[608,128]{1,0:T(8,128)(2,1)S(1)}, u32[]{:S(2)}, u32[]{:S(2)}) %collective-permute-start.4) | collective-permute-done | bytes 155680 | tf_op jit(solution)/shard_map/ppermute | solution.py:251
  17.5 4.8 %collective-permute-start.8 = (s16[608,128]{1,0:T(8,128)(2,1)S(1)}, s16[608,128]{1,0:T(8,128)(2,1)S(1)}, u32[]{:S(2)}, u32[]{:S(2)}) collective-permute-start(s16[608,128]{1,0:T(8,128)(2,1)S(1)} %collective-permute-done.4.refs_1_.refs_7_), channel_id=1, source_target_pairs={{0,14},{1,15},{2,0},{3,1},{4,2},{5,3},{6,4},{7,5},{8,6},{9,7},{10,... | collective-permute-start | bytes 466952 | tf_op jit(solution)/shard_map/ppermute | solution.py:251
  22.3 0.6 fusion.5
  23.0 1.0 collective-permute-start.6
  24.8 3.4 %collective-permute-start.12 = (s16[608,128]{1,0:T(8,128)(2,1)S(1)}, s16[608,128]{1,0:T(8,128)(2,1)S(1)}, u32[]{:S(2)}, u32[]{:S(2)}) collective-permute-start(s16[608,128]{1,0:T(8,128)(2,1)S(1)} %collective-permute-done.8.refs_5_.refs_11_), channel_id=1, source_target_pairs={{0,14},{1,15},{2,0},{3,1},{4,2},{5,3},{6,4},{7,5},{8,6},{9,7},{10,... | collective-permute-start | bytes 466952 | tf_op jit(solution)/shard_map/ppermute | solution.py:251
  28.4 3.1 %collective-permute-start.10 = (s16[608,128]{1,0:T(8,128)(2,1)S(1)}, s16[608,128]{1,0:T(8,128)(2,1)S(1)}, u32[]{:S(2)}, u32[]{:S(2)}) collective-permute-start(s16[608,128]{1,0:T(8,128)(2,1)S(1)} %collective-permute-done.6.refs_3_.refs_9_), channel_id=1, source_target_pairs={{0,14},{1,15},{2,0},{3,1},{4,2},{5,3},{6,4},{7,5},{8,6},{9,7},{10,... | collective-permute-start | bytes 466952 | tf_op jit(solution)/shard_map/ppermute | solution.py:251
  31.5 1.2 collective-permute-done.9.refs_6_.refs_12_
  32.7 2.7 %collective-permute-start.16 = (s16[608,128]{1,0:T(8,128)(2,1)S(1)}, s16[608,128]{1,0:T(8,128)(2,1)S(1)}, u32[]{:S(2)}, u32[]{:S(2)}) collective-permute-start(s16[608,128]{1,0:T(8,128)(2,1)S(1)} %collective-permute-done.12.refs_9_.refs_15_), channel_id=1, source_target_pairs={{0,14},{1,15},{2,0},{3,1},{4,2},{5,3},{6,4},{7,5},{8,6},{9,7},{10,... | collective-permute-start | bytes 466952 | tf_op jit(solution)/shard_map/ppermute | solution.py:251
  38.8 1.2 collective-permute-start.15
  40.2 2.4 %collective-permute-start.18 = (s16[608,128]{1,0:T(8,128)(2,1)S(1)}, s16[608,128]{1,0:T(8,128)(2,1)S(1)}, u32[]{:S(2)}, u32[]{:S(2)}) collective-permute-start(s16[608,128]{1,0:T(8,128)(2,1)S(1)} %collective-permute-done.16.refs_13_.refs_19_), channel_id=1, source_target_pairs={{0,14},{1,15},{2,0},{3,1},{4,2},{5,3},{6,4},{7,5},{8,6},{9,7},{10,... | collective-permute-start | bytes 466952 | tf_op jit(solution)/shard_map/ppermute | solution.py:251
  42.6 1.4 collective-permute-done.15.refs_12_.refs_18_
  44.1 1.7 %collective-permute-done.17.refs_14_.refs_20_ = s16[608,128]{1,0:T(8,128)(2,1)S(1)} collective-permute-done((s16[608,128]{1,0:T(8,128)(2,1)S(1)}, s16[608,128]{1,0:T(8,128)(2,1)S(1)}, u32[]{:S(2)}, u32[]{:S(2)}) %collective-permute-start.17) | collective-permute-done | bytes 155680 | tf_op jit(solution)/shard_map/ppermute | solution.py:251
  46.8 4.9 %collective-permute-start.19 = (f32[32,128]{1,0:T(8,128)S(1)}, f32[32,128]{1,0:T(8,128)S(1)}, u32[]{:S(2)}, u32[]{:S(2)}) collective-permute-start(f32[32,128]{1,0:T(8,128)S(1)} %column_totals.1), channel_id=1, source_target_pairs={{0,1},{1,0},{2,3},{3,2},{4,5},{5,4},{6,7},{7,6},{8,9},{9,8},{10,11... | collective-permute-start | bytes 49160 | tf_op jit(solution)/shard_map/ppermute | solution.py:251
  53.0 0.9 copy-done.2
  53.9 0.9 copy-done.4
  54.8 9.4 %first_products.1 = (s16[8,528,128]{2,1,0:T(8,128)(2,1)}, f32[512,128]{1,0:T(8,128)S(1)}) custom-call(s32[4,128]{1,0:T(4,128)S(1)} %add_add_fusion.refs_0_, s32[4,128]{1,0:T(4,128)S(1)} %collective-permute-done.refs_1_, s32[16]{0:T(128)S(1)} %stack.97.refs_2_, f32[16,4,128]{2,1,0:T(4,128)S(1)} %bitcast.27, bf16[96,128,128]{2,1,0:T(8,128)(2,1)} %refs_3_.1, ...), custom_call_target="tpu_custom_call" | custom-call | tf_op jit(solution)/shard_map/first_products/pallas_call | solution.py:355
  64.2 6.1 %all-to-all-start = ((s16[8,528,128]{2,1,0:T(8,128)(2,1)}), s16[8,528,128]{2,1,0:T(8,128)(2,1)S(1)}, u32[]{:S(2)}, u32[]{:S(2)}) async-start(s16[8,528,128]{2,1,0:T(8,128)(2,1)} %get-tuple-element.7), calls=%async_computation | async-start | bytes 2162688 | tf_op jit(solution)/shard_map/all_to_all | solution.py:400
  70.3 0.9 constant_dynamic-slice_fusion.1
  71.2 1.2 copy.9
  72.4 8.5 %seed_counts.1.refs_1_ = f32[512,128]{1,0:T(8,128)S(1)} custom-call(s32[1]{0:T(128)} %bitcast.21.first_ref, s32[1024,128]{1,0:T(8,128)S(1)} %bitcast.26), custom_call_target="tpu_custom_call" | custom-call | tf_op jit(solution)/shard_map/seed_counts/pallas_call | solution.py:333
  80.9 6.0 %all-to-all-done.refs_0_ = s16[8,528,128]{2,1,0:T(8,128)(2,1)S(1)} async-done(((s16[8,528,128]{2,1,0:T(8,128)(2,1)}), s16[8,528,128]{2,1,0:T(8,128)(2,1)S(1)}, u32[]{:S(2)}, u32[]{:S(2)}) %all-to-all-start) | async-done | bytes 1081376 | tf_op jit(solution)/shard_map/all_to_all | solution.py:400
  87.3 2.6 %collective-permute-start.20 = (bf16[512,128]{1,0:T(8,128)(2,1)S(1)}, bf16[512,128]{1,0:T(8,128)(2,1)S(1)}, u32[]{:S(2)}, u32[]{:S(2)}) collective-permute-start(bf16[512,128]{1,0:T(8,128)(2,1)S(1)} %current.2.refs_5_), channel_id=1, source_target_pairs={{0,16},{1,17},{2,18},{3,19},{4,20},{5,21},{6,22},{7,23},{8,24},{9,... | collective-permute-start | bytes 393224 | tf_op jit(solution)/shard_map/ppermute | solution.py:251
  89.9 0.8 collective-permute-start.21
  90.7 2.0 %collective-permute-done.20.refs_6_ = bf16[512,128]{1,0:T(8,128)(2,1)S(1)} collective-permute-done((bf16[512,128]{1,0:T(8,128)(2,1)S(1)}, bf16[512,128]{1,0:T(8,128)(2,1)S(1)}, u32[]{:S(2)}, u32[]{:S(2)}) %collective-permute-start.20) | collective-permute-done | bytes 131104 | tf_op jit(solution)/shard_map/ppermute | solution.py:251
  92.7 3.3 %collective-permute-start.24 = (bf16[512,128]{1,0:T(8,128)(2,1)S(1)}, bf16[512,128]{1,0:T(8,128)(2,1)S(1)}, u32[]{:S(2)}, u32[]{:S(2)}) collective-permute-start(bf16[512,128]{1,0:T(8,128)(2,1)S(1)} %collective-permute-done.20.refs_6_), channel_id=1, source_target_pairs={{0,14},{1,15},{2,0},{3,1},{4,2},{5,3},{6,4},{7,5},{8,6},{9,7},{10,... | collective-permute-start | bytes 393224 | tf_op jit(solution)/shard_map/ppermute | solution.py:251
  96.0 1.4 collective-permute-start.23
  98.0 3.1 %collective-permute-start.28 = (bf16[512,128]{1,0:T(8,128)(2,1)S(1)}, bf16[512,128]{1,0:T(8,128)(2,1)S(1)}, u32[]{:S(2)}, u32[]{:S(2)}) collective-permute-start(bf16[512,128]{1,0:T(8,128)(2,1)S(1)} %collective-permute-done.24.refs_10_), channel_id=1, source_target_pairs={{0,14},{1,15},{2,0},{3,1},{4,2},{5,3},{6,4},{7,5},{8,6},{9,7},{10,... | collective-permute-start | bytes 393224 | tf_op jit(solution)/shard_map/ppermute | solution.py:251
  101.0 1.4 collective-permute-start.26
  103.0 0.6 collective-permute-done.28.refs_14_
  103.6 3.1 %collective-permute-start.32 = (bf16[512,128]{1,0:T(8,128)(2,1)S(1)}, bf16[512,128]{1,0:T(8,128)(2,1)S(1)}, u32[]{:S(2)}, u32[]{:S(2)}) collective-permute-start(bf16[512,128]{1,0:T(8,128)(2,1)S(1)} %collective-permute-done.28.refs_14_), channel_id=1, source_target_pairs={{0,14},{1,15},{2,0},{3,1},{4,2},{5,3},{6,4},{7,5},{8,6},{9,7},{10,... | collective-permute-start | bytes 393224 | tf_op jit(solution)/shard_map/ppermute | solution.py:251
  106.8 1.4 collective-permute-start.30
  108.2 0.8 collective-permute-done.29.refs_15_
  109.8 3.4 %collective-permute-start.34 = (bf16[512,128]{1,0:T(8,128)(2,1)S(1)}, bf16[512,128]{1,0:T(8,128)(2,1)S(1)}, u32[]{:S(2)}, u32[]{:S(2)}) collective-permute-start(bf16[512,128]{1,0:T(8,128)(2,1)S(1)} %collective-permute-done.32.refs_18_), channel_id=1, source_target_pairs={{0,14},{1,15},{2,0},{3,1},{4,2},{5,3},{6,4},{7,5},{8,6},{9,7},{10,... | collective-permute-start | bytes 393224 | tf_op jit(solution)/shard_map/ppermute | solution.py:251
  113.2 1.6 %collective-permute-done.31.refs_17_ = bf16[512,128]{1,0:T(8,128)(2,1)S(1)} collective-permute-done((bf16[512,128]{1,0:T(8,128)(2,1)S(1)}, bf16[512,128]{1,0:T(8,128)(2,1)S(1)}, u32[]{:S(2)}, u32[]{:S(2)}) %collective-permute-start.31) | collective-permute-done | bytes 131104 | tf_op jit(solution)/shard_map/ppermute | solution.py:251
  114.9 1.8 %collective-permute-done.33.refs_19_ = bf16[512,128]{1,0:T(8,128)(2,1)S(1)} collective-permute-done((bf16[512,128]{1,0:T(8,128)(2,1)S(1)}, bf16[512,128]{1,0:T(8,128)(2,1)S(1)}, u32[]{:S(2)}, u32[]{:S(2)}) %collective-permute-start.33) | collective-permute-done | bytes 131104 | tf_op jit(solution)/shard_map/ppermute | solution.py:251
  116.6 8.1 %later_products.1 = s16[8,528,128]{2,1,0:T(8,128)(2,1)} custom-call(s32[4,128]{1,0:T(4,128)S(1)} %add_add_fusion.refs_0_, s32[4,128]{1,0:T(4,128)S(1)} %collective-permute-done.refs_1_, s32[16]{0:T(128)S(1)} %stack.97.refs_2_, bf16[96,128,128]{2,1,0:T(8,128)(2,1)} %refs_3_.1, bf16[96,128,128]{2,1,0:T(8,128)(2,1)} %collective-permute-done.1.refs_5_.refs_4_, ...), custom_call_target="tpu_custom_call" | custom-call | tf_op jit(solution)/shard_map/later_products/pallas_call | solution.py:364
  124.8 3.7 %all-to-all-start.1 = ((s16[8,528,128]{2,1,0:T(8,128)(2,1)}), s16[8,528,128]{2,1,0:T(8,128)(2,1)S(1)}, u32[]{:S(2)}, u32[]{:S(2)}) async-start(s16[8,528,128]{2,1,0:T(8,128)(2,1)} %later_products.1), calls=%async_computation.1 | async-start | bytes 2162688 | tf_op jit(solution)/shard_map/all_to_all | solution.py:404
  128.4 10.5 %all-to-all-done.1.refs_0_ = s16[8,528,128]{2,1,0:T(8,128)(2,1)S(1)} async-done(((s16[8,528,128]{2,1,0:T(8,128)(2,1)}), s16[8,528,128]{2,1,0:T(8,128)(2,1)S(1)}, u32[]{:S(2)}, u32[]{:S(2)}) %all-to-all-start.1) | async-done | bytes 1081376 | tf_op jit(solution)/shard_map/all_to_all | solution.py:404
  139.3 7.1 %collective-permute-start.35 = (f32[256,128]{1,0:T(8,128)S(1)}, f32[256,128]{1,0:T(8,128)S(1)}, u32[]{:S(2)}, u32[]{:S(2)}) collective-permute-start(f32[256,128]{1,0:T(8,128)S(1)} %get-tuple-element.19), channel_id=1, source_target_pairs={{0,1},{1,0},{2,3},{3,2},{4,5},{5,4},{6,7},{7,6},{8,9},{9,8},{10,11... | collective-permute-start | bytes 393224 | tf_op jit(solution)/shard_map/ppermute | solution.py:251
  146.4 1.0 collective-permute-done.35
  147.4 0.7 maximum_select_fusion
  (73 shorter events, 7.6 us)
Async XLA Ops:
  0.0 70.3 %copy-start = (s32[256,1024]{1,0:T(8,128)S(1)}, s32[256,1024]{1,0:T(8,128)}, u32[]{:S(2)}) copy-start(s32[256,1024]{1,0:T(8,128)} %param.11) | copy-start | bytes 3145732
  0.0 53.0 %collective-permute-start.1 = (bf16[96,128,128]{2,1,0:T(8,128)(2,1)}, bf16[96,128,128]{2,1,0:T(8,128)(2,1)}, u32[]{:S(2)}, u32[]{:S(2)}) collective-permute-start(bf16[96,128,128]{2,1,0:T(8,128)(2,1)} %refs_3_.1), channel_id=1, source_target_pairs={{0,1},{1,0},{2,3},{3,2},{4,5},{5,4},{6,7},{7,6},{8,9},{9,8},{10,11... | collective-permute-start | bytes 9437192 | tf_op jit(solution)/shard_map/ppermute | solution.py:251
  4.3 6.1 %collective-permute-start.2 = (s16[256,128]{1,0:T(8,128)(2,1)S(1)}, s16[256,128]{1,0:T(8,128)(2,1)S(1)}, u32[]{:S(2)}, u32[]{:S(2)}) collective-permute-start(s16[256,128]{1,0:T(8,128)(2,1)S(1)} %get-tuple-element.21), channel_id=1, source_target_pairs={{0,1},{1,0},{2,3},{3,2},{4,5},{5,4},{6,7},{7,6},{8,9},{9,8},{10,11... | collective-permute-start | bytes 196616 | tf_op jit(solution)/shard_map/ppermute | solution.py:251
  5.8 3.5 %copy-start.5 = (s32[96]{0:T(128)S(1)}, s32[96]{0:T(128)}, u32[]{:S(2)}) copy-start(s32[96]{0:T(128)} %param.8) | copy-start | bytes 1156
  9.1 1.3 collective-permute-start.3
  10.5 7.1 %collective-permute-start.4 = (s16[608,128]{1,0:T(8,128)(2,1)S(1)}, s16[608,128]{1,0:T(8,128)(2,1)S(1)}, u32[]{:S(2)}, u32[]{:S(2)}) collective-permute-start(s16[608,128]{1,0:T(8,128)(2,1)S(1)} %pad_add_fusion.refs_0_.refs_6_), channel_id=1, source_target_pairs={{0,16},{1,17},{2,18},{3,19},{4,20},{5,21},{6,22},{7,23},{8,24},{9,... | collective-permute-start | bytes 466952 | tf_op jit(solution)/shard_map/ppermute | solution.py:251
  12.8 11.6 %collective-permute-start.5 = (s16[608,128]{1,0:T(8,128)(2,1)S(1)}, s16[608,128]{1,0:T(8,128)(2,1)S(1)}, u32[]{:S(2)}, u32[]{:S(2)}) collective-permute-start(s16[608,128]{1,0:T(8,128)(2,1)S(1)} %pad_add_fusion.refs_0_.refs_6_), channel_id=1, source_target_pairs={{0,2},{1,3},{2,4},{3,5},{4,6},{5,7},{6,8},{7,9},{8,10},{9,11},{10,... | collective-permute-start | bytes 466952 | tf_op jit(solution)/shard_map/ppermute | solution.py:251
  17.5 7.2 %collective-permute-start.8 = (s16[608,128]{1,0:T(8,128)(2,1)S(1)}, s16[608,128]{1,0:T(8,128)(2,1)S(1)}, u32[]{:S(2)}, u32[]{:S(2)}) collective-permute-start(s16[608,128]{1,0:T(8,128)(2,1)S(1)} %collective-permute-done.4.refs_1_.refs_7_), channel_id=1, source_target_pairs={{0,14},{1,15},{2,0},{3,1},{4,2},{5,3},{6,4},{7,5},{8,6},{9,7},{10,... | collective-permute-start | bytes 466952 | tf_op jit(solution)/shard_map/ppermute | solution.py:251
  23.0 5.4 %collective-permute-start.6 = (s16[608,128]{1,0:T(8,128)(2,1)S(1)}, s16[608,128]{1,0:T(8,128)(2,1)S(1)}, u32[]{:S(2)}, u32[]{:S(2)}) collective-permute-start(s16[608,128]{1,0:T(8,128)(2,1)S(1)} %pad_add_fusion.refs_0_.refs_6_), channel_id=1, source_target_pairs={{0,14},{1,15},{2,0},{3,1},{4,2},{5,3},{6,4},{7,5},{8,6},{9,7},{10,... | collective-permute-start | bytes 466952 | tf_op jit(solution)/shard_map/ppermute | solution.py:251
  23.9 7.6 %collective-permute-start.7 = (s16[608,128]{1,0:T(8,128)(2,1)S(1)}, s16[608,128]{1,0:T(8,128)(2,1)S(1)}, u32[]{:S(2)}, u32[]{:S(2)}) collective-permute-start(s16[608,128]{1,0:T(8,128)(2,1)S(1)} %collective-permute-done.4.refs_1_.refs_7_), channel_id=1, source_target_pairs={{0,2},{1,3},{2,4},{3,5},{4,6},{5,7},{6,8},{7,9},{8,10},{9,11},{10,... | collective-permute-start | bytes 466952 | tf_op jit(solution)/shard_map/ppermute | solution.py:251
  24.4 8.2 %collective-permute-start.9 = (s16[608,128]{1,0:T(8,128)(2,1)S(1)}, s16[608,128]{1,0:T(8,128)(2,1)S(1)}, u32[]{:S(2)}, u32[]{:S(2)}) collective-permute-start(s16[608,128]{1,0:T(8,128)(2,1)S(1)} %collective-permute-done.5.refs_2_.refs_8_), channel_id=1, source_target_pairs={{0,2},{1,3},{2,4},{3,5},{4,6},{5,7},{6,8},{7,9},{8,10},{9,11},{10,... | collective-permute-start | bytes 466952 | tf_op jit(solution)/shard_map/ppermute | solution.py:251
  24.8 7.9 %collective-permute-start.12 = (s16[608,128]{1,0:T(8,128)(2,1)S(1)}, s16[608,128]{1,0:T(8,128)(2,1)S(1)}, u32[]{:S(2)}, u32[]{:S(2)}) collective-permute-start(s16[608,128]{1,0:T(8,128)(2,1)S(1)} %collective-permute-done.8.refs_5_.refs_11_), channel_id=1, source_target_pairs={{0,14},{1,15},{2,0},{3,1},{4,2},{5,3},{6,4},{7,5},{8,6},{9,7},{10,... | collective-permute-start | bytes 466952 | tf_op jit(solution)/shard_map/ppermute | solution.py:251
  28.4 10.0 %collective-permute-start.10 = (s16[608,128]{1,0:T(8,128)(2,1)S(1)}, s16[608,128]{1,0:T(8,128)(2,1)S(1)}, u32[]{:S(2)}, u32[]{:S(2)}) collective-permute-start(s16[608,128]{1,0:T(8,128)(2,1)S(1)} %collective-permute-done.6.refs_3_.refs_9_), channel_id=1, source_target_pairs={{0,14},{1,15},{2,0},{3,1},{4,2},{5,3},{6,4},{7,5},{8,6},{9,7},{10,... | collective-permute-start | bytes 466952 | tf_op jit(solution)/shard_map/ppermute | solution.py:251
  31.5 7.2 %collective-permute-start.11 = (s16[608,128]{1,0:T(8,128)(2,1)S(1)}, s16[608,128]{1,0:T(8,128)(2,1)S(1)}, u32[]{:S(2)}, u32[]{:S(2)}) collective-permute-start(s16[608,128]{1,0:T(8,128)(2,1)S(1)} %collective-permute-done.7.refs_4_.refs_10_), channel_id=1, source_target_pairs={{0,2},{1,3},{2,4},{3,5},{4,6},{5,7},{6,8},{7,9},{8,10},{9,11},{10,... | collective-permute-start | bytes 466952 | tf_op jit(solution)/shard_map/ppermute | solution.py:251
  32.7 7.2 %collective-permute-start.13 = (s16[608,128]{1,0:T(8,128)(2,1)S(1)}, s16[608,128]{1,0:T(8,128)(2,1)S(1)}, u32[]{:S(2)}, u32[]{:S(2)}) collective-permute-start(s16[608,128]{1,0:T(8,128)(2,1)S(1)} %collective-permute-done.9.refs_6_.refs_12_), channel_id=1, source_target_pairs={{0,2},{1,3},{2,4},{3,5},{4,6},{5,7},{6,8},{7,9},{8,10},{9,11},{10,... | collective-permute-start | bytes 466952 | tf_op jit(solution)/shard_map/ppermute | solution.py:251
  32.7 7.5 %collective-permute-start.16 = (s16[608,128]{1,0:T(8,128)(2,1)S(1)}, s16[608,128]{1,0:T(8,128)(2,1)S(1)}, u32[]{:S(2)}, u32[]{:S(2)}) collective-permute-start(s16[608,128]{1,0:T(8,128)(2,1)S(1)} %collective-permute-done.12.refs_9_.refs_15_), channel_id=1, source_target_pairs={{0,14},{1,15},{2,0},{3,1},{4,2},{5,3},{6,4},{7,5},{8,6},{9,7},{10,... | collective-permute-start | bytes 466952 | tf_op jit(solution)/shard_map/ppermute | solution.py:251
  38.4 4.2 %collective-permute-start.14 = (s16[608,128]{1,0:T(8,128)(2,1)S(1)}, s16[608,128]{1,0:T(8,128)(2,1)S(1)}, u32[]{:S(2)}, u32[]{:S(2)}) collective-permute-start(s16[608,128]{1,0:T(8,128)(2,1)S(1)} %collective-permute-done.10.refs_7_.refs_13_), channel_id=1, source_target_pairs={{0,14},{1,15},{2,0},{3,1},{4,2},{5,3},{6,4},{7,5},{8,6},{9,7},{10,... | collective-permute-start | bytes 466952 | tf_op jit(solution)/shard_map/ppermute | solution.py:251
  38.8 5.3 %collective-permute-start.15 = (s16[608,128]{1,0:T(8,128)(2,1)S(1)}, s16[608,128]{1,0:T(8,128)(2,1)S(1)}, u32[]{:S(2)}, u32[]{:S(2)}) collective-permute-start(s16[608,128]{1,0:T(8,128)(2,1)S(1)} %collective-permute-done.11.refs_8_.refs_14_), channel_id=1, source_target_pairs={{0,2},{1,3},{2,4},{3,5},{4,6},{5,7},{6,8},{7,9},{8,10},{9,11},{10,... | collective-permute-start | bytes 466952 | tf_op jit(solution)/shard_map/ppermute | solution.py:251
  39.9 5.8 %collective-permute-start.17 = (s16[608,128]{1,0:T(8,128)(2,1)S(1)}, s16[608,128]{1,0:T(8,128)(2,1)S(1)}, u32[]{:S(2)}, u32[]{:S(2)}) collective-permute-start(s16[608,128]{1,0:T(8,128)(2,1)S(1)} %collective-permute-done.13.refs_10_.refs_16_), channel_id=1, source_target_pairs={{0,2},{1,3},{2,4},{3,5},{4,6},{5,7},{6,8},{7,9},{8,10},{9,11},{10,... | collective-permute-start | bytes 466952 | tf_op jit(solution)/shard_map/ppermute | solution.py:251
  40.2 6.0 %collective-permute-start.18 = (s16[608,128]{1,0:T(8,128)(2,1)S(1)}, s16[608,128]{1,0:T(8,128)(2,1)S(1)}, u32[]{:S(2)}, u32[]{:S(2)}) collective-permute-start(s16[608,128]{1,0:T(8,128)(2,1)S(1)} %collective-permute-done.16.refs_13_.refs_19_), channel_id=1, source_target_pairs={{0,14},{1,15},{2,0},{3,1},{4,2},{5,3},{6,4},{7,5},{8,6},{9,7},{10,... | collective-permute-start | bytes 466952 | tf_op jit(solution)/shard_map/ppermute | solution.py:251
  45.7 0.7 copy-start.1
  46.2 0.7 copy-start.3
  46.8 5.7 %collective-permute-start.19 = (f32[32,128]{1,0:T(8,128)S(1)}, f32[32,128]{1,0:T(8,128)S(1)}, u32[]{:S(2)}, u32[]{:S(2)}) collective-permute-start(f32[32,128]{1,0:T(8,128)S(1)} %column_totals.1), channel_id=1, source_target_pairs={{0,1},{1,0},{2,3},{3,2},{4,5},{5,4},{6,7},{7,6},{8,9},{9,8},{10,11... | collective-permute-start | bytes 49160 | tf_op jit(solution)/shard_map/ppermute | solution.py:251
  51.8 1.2 collective-permute-start
  53.0 0.9 copy-start.2
  53.9 0.9 copy-start.4
  64.2 22.7 %all-to-all-start = ((s16[8,528,128]{2,1,0:T(8,128)(2,1)}), s16[8,528,128]{2,1,0:T(8,128)(2,1)S(1)}, u32[]{:S(2)}, u32[]{:S(2)}) async-start(s16[8,528,128]{2,1,0:T(8,128)(2,1)} %get-tuple-element.7), calls=%async_computation | async-start | bytes 2162688 | tf_op jit(solution)/shard_map/all_to_all | solution.py:400
  87.3 5.4 %collective-permute-start.20 = (bf16[512,128]{1,0:T(8,128)(2,1)S(1)}, bf16[512,128]{1,0:T(8,128)(2,1)S(1)}, u32[]{:S(2)}, u32[]{:S(2)}) collective-permute-start(bf16[512,128]{1,0:T(8,128)(2,1)S(1)} %current.2.refs_5_), channel_id=1, source_target_pairs={{0,16},{1,17},{2,18},{3,19},{4,20},{5,21},{6,22},{7,23},{8,24},{9,... | collective-permute-start | bytes 393224 | tf_op jit(solution)/shard_map/ppermute | solution.py:251
  89.9 7.6 %collective-permute-start.21 = (bf16[512,128]{1,0:T(8,128)(2,1)S(1)}, bf16[512,128]{1,0:T(8,128)(2,1)S(1)}, u32[]{:S(2)}, u32[]{:S(2)}) collective-permute-start(bf16[512,128]{1,0:T(8,128)(2,1)S(1)} %current.2.refs_5_), channel_id=1, source_target_pairs={{0,2},{1,3},{2,4},{3,5},{4,6},{5,7},{6,8},{7,9},{8,10},{9,11},{10,... | collective-permute-start | bytes 393224 | tf_op jit(solution)/shard_map/ppermute | solution.py:251
  92.7 5.3 %collective-permute-start.24 = (bf16[512,128]{1,0:T(8,128)(2,1)S(1)}, bf16[512,128]{1,0:T(8,128)(2,1)S(1)}, u32[]{:S(2)}, u32[]{:S(2)}) collective-permute-start(bf16[512,128]{1,0:T(8,128)(2,1)S(1)} %collective-permute-done.20.refs_6_), channel_id=1, source_target_pairs={{0,14},{1,15},{2,0},{3,1},{4,2},{5,3},{6,4},{7,5},{8,6},{9,7},{10,... | collective-permute-start | bytes 393224 | tf_op jit(solution)/shard_map/ppermute | solution.py:251
  96.0 5.0 %collective-permute-start.22 = (bf16[512,128]{1,0:T(8,128)(2,1)S(1)}, bf16[512,128]{1,0:T(8,128)(2,1)S(1)}, u32[]{:S(2)}, u32[]{:S(2)}) collective-permute-start(bf16[512,128]{1,0:T(8,128)(2,1)S(1)} %current.2.refs_5_), channel_id=1, source_target_pairs={{0,14},{1,15},{2,0},{3,1},{4,2},{5,3},{6,4},{7,5},{8,6},{9,7},{10,... | collective-permute-start | bytes 393224 | tf_op jit(solution)/shard_map/ppermute | solution.py:251
  96.0 6.4 %collective-permute-start.23 = (bf16[512,128]{1,0:T(8,128)(2,1)S(1)}, bf16[512,128]{1,0:T(8,128)(2,1)S(1)}, u32[]{:S(2)}, u32[]{:S(2)}) collective-permute-start(bf16[512,128]{1,0:T(8,128)(2,1)S(1)} %collective-permute-done.20.refs_6_), channel_id=1, source_target_pairs={{0,2},{1,3},{2,4},{3,5},{4,6},{5,7},{6,8},{7,9},{8,10},{9,11},{10,... | collective-permute-start | bytes 393224 | tf_op jit(solution)/shard_map/ppermute | solution.py:251
  97.5 5.0 %collective-permute-start.25 = (bf16[512,128]{1,0:T(8,128)(2,1)S(1)}, bf16[512,128]{1,0:T(8,128)(2,1)S(1)}, u32[]{:S(2)}, u32[]{:S(2)}) collective-permute-start(bf16[512,128]{1,0:T(8,128)(2,1)S(1)} %collective-permute-done.21.refs_7_), channel_id=1, source_target_pairs={{0,2},{1,3},{2,4},{3,5},{4,6},{5,7},{6,8},{7,9},{8,10},{9,11},{10,... | collective-permute-start | bytes 393224 | tf_op jit(solution)/shard_map/ppermute | solution.py:251
  98.0 5.7 %collective-permute-start.28 = (bf16[512,128]{1,0:T(8,128)(2,1)S(1)}, bf16[512,128]{1,0:T(8,128)(2,1)S(1)}, u32[]{:S(2)}, u32[]{:S(2)}) collective-permute-start(bf16[512,128]{1,0:T(8,128)(2,1)S(1)} %collective-permute-done.24.refs_10_), channel_id=1, source_target_pairs={{0,14},{1,15},{2,0},{3,1},{4,2},{5,3},{6,4},{7,5},{8,6},{9,7},{10,... | collective-permute-start | bytes 393224 | tf_op jit(solution)/shard_map/ppermute | solution.py:251
  101.0 5.7 %collective-permute-start.26 = (bf16[512,128]{1,0:T(8,128)(2,1)S(1)}, bf16[512,128]{1,0:T(8,128)(2,1)S(1)}, u32[]{:S(2)}, u32[]{:S(2)}) collective-permute-start(bf16[512,128]{1,0:T(8,128)(2,1)S(1)} %collective-permute-done.22.refs_8_), channel_id=1, source_target_pairs={{0,14},{1,15},{2,0},{3,1},{4,2},{5,3},{6,4},{7,5},{8,6},{9,7},{10,... | collective-permute-start | bytes 393224 | tf_op jit(solution)/shard_map/ppermute | solution.py:251
  102.5 5.7 %collective-permute-start.27 = (bf16[512,128]{1,0:T(8,128)(2,1)S(1)}, bf16[512,128]{1,0:T(8,128)(2,1)S(1)}, u32[]{:S(2)}, u32[]{:S(2)}) collective-permute-start(bf16[512,128]{1,0:T(8,128)(2,1)S(1)} %collective-permute-done.23.refs_9_), channel_id=1, source_target_pairs={{0,2},{1,3},{2,4},{3,5},{4,6},{5,7},{6,8},{7,9},{8,10},{9,11},{10,... | collective-permute-start | bytes 393224 | tf_op jit(solution)/shard_map/ppermute | solution.py:251
  102.5 6.5 %collective-permute-start.29 = (bf16[512,128]{1,0:T(8,128)(2,1)S(1)}, bf16[512,128]{1,0:T(8,128)(2,1)S(1)}, u32[]{:S(2)}, u32[]{:S(2)}) collective-permute-start(bf16[512,128]{1,0:T(8,128)(2,1)S(1)} %collective-permute-done.25.refs_11_), channel_id=1, source_target_pairs={{0,2},{1,3},{2,4},{3,5},{4,6},{5,7},{6,8},{7,9},{8,10},{9,11},{10,... | collective-permute-start | bytes 393224 | tf_op jit(solution)/shard_map/ppermute | solution.py:251
  103.6 6.2 %collective-permute-start.32 = (bf16[512,128]{1,0:T(8,128)(2,1)S(1)}, bf16[512,128]{1,0:T(8,128)(2,1)S(1)}, u32[]{:S(2)}, u32[]{:S(2)}) collective-permute-start(bf16[512,128]{1,0:T(8,128)(2,1)S(1)} %collective-permute-done.28.refs_14_), channel_id=1, source_target_pairs={{0,14},{1,15},{2,0},{3,1},{4,2},{5,3},{6,4},{7,5},{8,6},{9,7},{10,... | collective-permute-start | bytes 393224 | tf_op jit(solution)/shard_map/ppermute | solution.py:251
  106.8 6.5 %collective-permute-start.30 = (bf16[512,128]{1,0:T(8,128)(2,1)S(1)}, bf16[512,128]{1,0:T(8,128)(2,1)S(1)}, u32[]{:S(2)}, u32[]{:S(2)}) collective-permute-start(bf16[512,128]{1,0:T(8,128)(2,1)S(1)} %collective-permute-done.26.refs_12_), channel_id=1, source_target_pairs={{0,14},{1,15},{2,0},{3,1},{4,2},{5,3},{6,4},{7,5},{8,6},{9,7},{10,... | collective-permute-start | bytes 393224 | tf_op jit(solution)/shard_map/ppermute | solution.py:251
  108.2 6.7 %collective-permute-start.31 = (bf16[512,128]{1,0:T(8,128)(2,1)S(1)}, bf16[512,128]{1,0:T(8,128)(2,1)S(1)}, u32[]{:S(2)}, u32[]{:S(2)}) collective-permute-start(bf16[512,128]{1,0:T(8,128)(2,1)S(1)} %collective-permute-done.27.refs_13_), channel_id=1, source_target_pairs={{0,2},{1,3},{2,4},{3,5},{4,6},{5,7},{6,8},{7,9},{8,10},{9,11},{10,... | collective-permute-start | bytes 393224 | tf_op jit(solution)/shard_map/ppermute | solution.py:251
  109.1 7.6 %collective-permute-start.33 = (bf16[512,128]{1,0:T(8,128)(2,1)S(1)}, bf16[512,128]{1,0:T(8,128)(2,1)S(1)}, u32[]{:S(2)}, u32[]{:S(2)}) collective-permute-start(bf16[512,128]{1,0:T(8,128)(2,1)S(1)} %collective-permute-done.29.refs_15_), channel_id=1, source_target_pairs={{0,2},{1,3},{2,4},{3,5},{4,6},{5,7},{6,8},{7,9},{8,10},{9,11},{10,... | collective-permute-start | bytes 393224 | tf_op jit(solution)/shard_map/ppermute | solution.py:251
  109.8 6.8 %collective-permute-start.34 = (bf16[512,128]{1,0:T(8,128)(2,1)S(1)}, bf16[512,128]{1,0:T(8,128)(2,1)S(1)}, u32[]{:S(2)}, u32[]{:S(2)}) collective-permute-start(bf16[512,128]{1,0:T(8,128)(2,1)S(1)} %collective-permute-done.32.refs_18_), channel_id=1, source_target_pairs={{0,14},{1,15},{2,0},{3,1},{4,2},{5,3},{6,4},{7,5},{8,6},{9,7},{10,... | collective-permute-start | bytes 393224 | tf_op jit(solution)/shard_map/ppermute | solution.py:251
  124.8 14.1 %all-to-all-start.1 = ((s16[8,528,128]{2,1,0:T(8,128)(2,1)}), s16[8,528,128]{2,1,0:T(8,128)(2,1)S(1)}, u32[]{:S(2)}, u32[]{:S(2)}) async-start(s16[8,528,128]{2,1,0:T(8,128)(2,1)} %later_products.1), calls=%async_computation.1 | async-start | bytes 2162688 | tf_op jit(solution)/shard_map/all_to_all | solution.py:404
  139.3 8.1 %collective-permute-start.35 = (f32[256,128]{1,0:T(8,128)S(1)}, f32[256,128]{1,0:T(8,128)S(1)}, u32[]{:S(2)}, u32[]{:S(2)}) collective-permute-start(f32[256,128]{1,0:T(8,128)S(1)} %get-tuple-element.19), channel_id=1, source_target_pairs={{0,1},{1,0},{2,3},{3,2},{4,5},{5,4},{6,7},{7,6},{8,9},{9,8},{10,11... | collective-permute-start | bytes 393224 | tf_op jit(solution)/shard_map/ppermute | solution.py:251

commit v4 on v3

--- a/solution.py
+++ b/solution.py
@@ -34,8 +34,8 @@
     return pltpu.with_memory_space_constraint(value, pltpu.HBM)
 
 
-def params():
-    return pltpu.CompilerParams(vmem_limit_bytes=24 * 1024 * 1024)
+def params(mebibytes):
+    return pltpu.CompilerParams(vmem_limit_bytes=mebibytes * 1024 * 1024)
 
 
 def column_kernel(source_ref, count_ref, given_ref, sums_ref, tiles_ref, arrived):
@@ -50,25 +50,34 @@
         copies[c].start()
     sums_ref[...] = jnp.zeros_like(sums_ref)
 
-    def slot(k, carry):
-        column = jnp.sum(tiles_ref[k].astype(jnp.float32), axis=0, keepdims=True)
-        sums_ref[pl.ds(source_ref[k], 1), :] += column
+    def group(g, carry):
+        columns = [
+            jnp.sum(tiles_ref[8 * g + u].astype(jnp.float32), axis=0, keepdims=True) for u in range(8)
+        ]
+        for u in range(8):
+            k = 8 * g + u
+            live = jnp.where(k < count_ref[0], 1.0, 0.0)
+            sums_ref[pl.ds(source_ref[k], 1), :] += columns[u] * live
         return carry
 
     for c in range(arrived.shape[0]):
         copies[c].wait()
-        lax.fori_loop(c * chunk, jnp.minimum((c + 1) * chunk, count_ref[0]), slot, 0)
-
-
-def total_kernel(rows, *refs):
-    *piece_refs, out_ref = refs
-    each = out_ref.shape[0]
-    total = jnp.zeros(out_ref.shape, jnp.float32)
+        last = jnp.minimum((c + 1) * chunk, count_ref[0])
+        lax.fori_loop(c * chunk // 8, (last + 7) // 8, group, 0)
+
+
+def column_totals(rows, piece_refs, sums_ref):
+    groups, per, lanes = sums_ref.shape
+    each = groups * per
+    total = jnp.zeros((each, lanes), jnp.float32)
     for piece_ref in piece_refs:
-        code = piece_ref[rows : rows + 3 * each, :].astype(jnp.float32)
-        mantissa = code[each : 2 * each] * 4096.0 + code[2 * each :]
-        total += mantissa * jnp.exp2(code[:each] - 24.0)
-    out_ref[...] = total
+        code = piece_ref[rows : rows + 2 * each, :].astype(jnp.int32) + 32768
+        upper, lower = code[:each], code[each:]
+        exponent = (upper >> 8) - 127
+        mantissa = ((upper & 255) * 65536 + lower).astype(jnp.float32)
+        total += mantissa * jnp.exp2((exponent - 24).astype(jnp.float32))
+    for g in range(groups):
+        sums_ref[g] = total[g * per : (g + 1) * per]
 
 
 def seed_kernel(first_ref, ids_ref, counts_ref):
@@ -134,7 +143,7 @@
 
 
 def products(facts_refs, copies, tiles, panel, total, out_ref):
-    unroll = 4
+    unroll = 16
     slots = tiles.shape[0] // 2
     dummy = total.shape[0] - 1
     for which, facts_ref in enumerate(facts_refs):
@@ -177,10 +186,11 @@
     lax.fori_loop(0, receivers, send, 0)
 
 
-def first_kernel(pieces, rows, own_facts, sib_facts, chip_ref, sums_ref, own_ref, sib_ref, *refs):
+def first_kernel(pieces, rows, own_facts, sib_facts, chip_ref, own_ref, sib_ref, *refs):
     piece_refs = refs[:pieces]
-    out_ref, inverse_ref, panel, total, tiles, arrived, ordered = refs[pieces:]
+    out_ref, inverse_ref, panel, total, tiles, arrived, sums_ref, ordered = refs[pieces:]
     copies = fetch(own_ref, sib_ref, tiles, arrived)
+    column_totals(rows, piece_refs, sums_ref)
     total[...] = jnp.zeros_like(total)
     per = rows // TILE
     ordered[...] = jnp.zeros_like(ordered)
@@ -259,7 +269,7 @@
     def across(value):
         return by_col(value, lambda y, at, k: (1 - y, at, k))
 
-    def gather(block):
+    def gather(block, beside=None):
         other = across(block)
         pieces = [block, other]
         names = [(0, 0), (1, 0)]
@@ -269,9 +279,11 @@
             c, d = along(c, 1), along(d, -1)
             pieces += [a, b, c, d]
             names += [(0, -step), (0, step), (1, -step), (1, step)]
+            if step == 1 and beside is not None:
+                a, beside = lax.optimization_barrier((a, beside))
         pieces += [along(a, 1), along(d, -1)]
         names += [(0, depth // 2), (1, depth // 2)]
-        return pieces, names
+        return pieces, names, beside
 
     half = columns // 2
     code = ((scores - LOW) * (STEPS / (HIGH - LOW)) + 0.5).astype(jnp.int32)
@@ -289,16 +301,15 @@
         in_specs=[smem(), smem(), anywhere()],
         out_specs=vmem(),
         scratch_shapes=[VMEM(tile_values.shape, tile_values.dtype), pltpu.SemaphoreType.DMA((4,))],
-        compiler_params=params(),
+        compiler_params=params(8),
         name="column_sums",
     )(sources, tile_count, in_hbm(tile_values))
 
-    part = band_tiles // 2
-    given = sibling(lax.dynamic_slice_in_dim(sums, (1 - core) * part, part, 0))
-    given = given + lax.dynamic_slice_in_dim(sums, core * part, part, 0)
+    given = sums + sibling(sums)
     exponent = jnp.floor(jnp.log2(jnp.maximum(given, 1e-30))) + 1.0
-    mantissa = (given * jnp.exp2(24.0 - exponent) + 0.5).astype(jnp.int32)
-    tail = jnp.concatenate([exponent.astype(jnp.int32), mantissa >> 12, mantissa & 4095])
+    mantissa = jnp.minimum((given * jnp.exp2(24.0 - exponent) + 0.5).astype(jnp.int32), (1 << 24) - 1)
+    upper = (exponent.astype(jnp.int32) + 127) * 256 + (mantissa >> 16)
+    tail = jnp.concatenate([upper, mantissa & 65535]) - 32768
     block = jnp.concatenate([block, tail.astype(jnp.int16)])
 
     targets = tile_rows // band_tiles * per + core * BT + tile_rows % BT
@@ -335,11 +346,11 @@
         out_shape=jax.ShapeDtypeStruct((2 * own_rows, half), jnp.float32),
         in_specs=[smem(), vmem()],
         out_specs=vmem(),
-        compiler_params=params(),
+        compiler_params=params(4),
         name="seed_counts",
     )(first_page.reshape(1), ids)
 
-    def multiply(pieces, names, sums):
+    def multiply(pieces, names, coded):
         order = jnp.stack([(high ^ y) * depth + (z + d) % depth for y, d in names])
         n = len(pieces)
         rows = per * TILE
@@ -351,23 +362,24 @@
             pltpu.SemaphoreType.DMA((2,)),
         ]
         tiles = (in_hbm(tile_values), in_hbm(sib_tiles))
-        if sums is not None:
+        if coded:
             return pl.pallas_call(
                 lambda *refs: first_kernel(n, rows, *refs),
                 out_shape=(parts, jax.ShapeDtypeStruct((rows, half), jnp.float32)),
-                in_specs=[smem()] * 3 + [vmem()] + [anywhere()] * 2 + [vmem()] * n,
+                in_specs=[smem()] * 3 + [anywhere()] * 2 + [vmem()] * n,
                 out_specs=(vmem(), vmem()),
-                scratch_shapes=scratch + [VMEM((TILE, TILE), jnp.float32)],
-                compiler_params=params(),
+                scratch_shapes=scratch
+                + [VMEM((chips, per, TILE), jnp.float32), VMEM((TILE, TILE), jnp.float32)],
+                compiler_params=params(20),
                 name="first_products",
-            )(facts, sib_facts, order, sums.reshape(chips, per, TILE), *tiles, *pieces)
+            )(facts, sib_facts, order, *tiles, *pieces)
         return pl.pallas_call(
             lambda *refs: later_kernel(n, rows, *refs),
             out_shape=parts,
             in_specs=[smem()] * 3 + [anywhere()] * 2 + [vmem()] * n,
             out_specs=vmem(),
             scratch_shapes=scratch,
-            compiler_params=params(),
+            compiler_params=params(20),
             name="later_products",
         )(facts, sib_facts, order, *tiles, *pieces)
 
@@ -379,28 +391,16 @@
             ),
             in_specs=[vmem()] * 3,
             out_specs=vmem(),
-            compiler_params=params(),
+            compiler_params=params(6),
             name="current",
         )(parts, restart, inverse)
 
-    pieces, names = gather(block)
-    found = pl.pallas_call(
-        lambda *refs: total_kernel(per * TILE, *refs),
-        out_shape=jax.ShapeDtypeStruct((part, TILE), jnp.float32),
-        in_specs=[vmem()] * len(pieces),
-        out_specs=vmem(),
-        compiler_params=params(),
-        name="column_totals",
-    )(*pieces)
-    other = sibling(found)
-    sums = jnp.where(
-        core == 0, jnp.concatenate([found, other]), jnp.concatenate([other, found])
-    )
-    parts, inverse = multiply(pieces, names, sums)
+    pieces, names, (sib_facts, sib_tiles) = gather(block, (sib_facts, sib_tiles))
+    parts, inverse = multiply(pieces, names, True)
     parts = lax.all_to_all(parts, "row", 0, 0, tiled=True)
     panel = update(parts, inverse, True)
-    pieces, names = gather(panel)
-    parts = multiply(pieces, names, None)
+    pieces, names, _ = gather(panel)
+    parts = multiply(pieces, names, False)
     parts = lax.all_to_all(parts, "row", 0, 0, tiled=True)
     current = update(parts, inverse, False)
     mine = lax.dynamic_slice_in_dim(current, core * own_rows, own_rows, 0)

time: 149 us -> 144 us (0.966)
  Pallas kernels: 30.1 us -> 27.8 us
  starting transfers between devices: 70.2 us -> 68.7 us
    all_to_all x2, waiting for transfers between devices: 16.5 us -> 10.5 us  [per_device(): parts = lax.all_to_all(parts, 'row', 0, 0, tiled=True)]
    ppermute x36 -> x35, waiting for transfers between devices: 19.2 us -> 23.8 us  [by_col(): return lax.ppermute(value, 'col', pairs)]
    ppermute x36 -> x35, starting transfers between devices: 60.4 us -> 56.6 us  [by_col(): return lax.ppermute(value, 'col', pairs)]
    all_to_all x2, starting transfers between devices: 9.79 us -> 12 us  [per_device(): parts = lax.all_to_all(parts, 'row', 0, 0, tiled=True)]
  transfers between devices with their start and end apart: 38 -> 37, of which waited for: 19 -> 15; matrix products, arithmetic and copies ran while one was open for 4% -> 4% of each run, Pallas kernels for 8% -> 8%
where the time goes in v4:
time: 144 us; the launch traced here: 143 us
  starting transfers between devices  68.7 us (48%)
  waiting for transfers between devices  34.3 us (24%)
  Pallas kernels  27.8 us (19%)
  local copies, waits for them, and re-layouts  5.46 us (4%)
  other arithmetic  3.86 us (3%)
  between operations  3.46 us (2%)
    ppermute x35, starting transfers between devices, by_col(): return lax.ppermute(value, 'col', pairs)  56.6 us
    ppermute x35, waiting for transfers between devices, by_col(): return lax.ppermute(value, 'col', pairs)  23.8 us
    all_to_all x2, starting transfers between devices, per_device(): parts = lax.all_to_all(parts, 'row', 0, 0, tiled=True)  12 us
    all_to_all x2, waiting for transfers between devices, per_device(): parts = lax.all_to_all(parts, 'row', 0, 0, tiled=True)  10.5 us
    pallas_call x1, Pallas kernels, per_device(): pl.pallas_call(seed_kernel, out_shape=jax.ShapeDtypeStruct((2 * own_rows,...  9.05 us
    pallas_call x1, Pallas kernels, multiply(): pl.pallas_call(lambda *refs: first_kernel(n, rows, *refs), out_shape=(par...  8.63 us
    pallas_call x1, Pallas kernels, multiply(): pl.pallas_call(lambda *refs: later_kernel(n, rows, *refs), out_shape=part...  6.69 us
    unnamed x13, local copies, waits for them, and re-layouts  4.38 us
  transfers between devices with their start and end apart: 37, of which 15 were waited for; matrix products, arithmetic and copies ran while one was open for 4% of the time, Pallas kernels for 8%

profile of v4, /device:TPU:1, one launch (start us, length us, event | category | flops | bytes accessed | tf_op | source)
XLA Modules:
  0.0 143.5 jit_solution(14601109498672229853)
XLA Ops:
  0.0 3.2 %collective-permute-start.4 = (bf16[96,128,128]{2,1,0:T(8,128)(2,1)}, bf16[96,128,128]{2,1,0:T(8,128)(2,1)}, u32[]{:S(2)}, u32[]{:S(2)}) collective-permute-start(bf16[96,128,128]{2,1,0:T(8,128)(2,1)} %refs_3_.3), channel_id=1, source_target_pairs={{0,1},{1,0},{2,3},{3,2},{4,5},{5,4},{6,7},{7,6},{8,9},{9,8},{10,11... | collective-permute-start | bytes 9437192 | tf_op jit(solution)/shard_map/ppermute | solution.py:261
  3.2 1.0 add_convert_fusion
  5.2 0.7 broadcast_add_fusion
  5.8 2.6 %column_sums.1 = f32[64,128]{1,0:T(8,128)S(1)} custom-call(s32[96]{0:T(128)S(1)} %get-tuple-element.21.source_ref, s32[1]{0:T(128)} %copy.10.count_ref, bf16[96,128,128]{2,1,0:T(8,128)(2,1)} %refs_3_.3), custom_call_target="tpu_custom_call" | custom-call | tf_op jit(solution)/shard_map/column_sums/pallas_call | solution.py:298
  8.9 0.6 fusion.7
  12.9 1.4 collective-permute-start.5
  14.2 1.6 %collective-permute-start.2 = (s16[640,128]{1,0:T(8,128)(2,1)S(1)}, s16[640,128]{1,0:T(8,128)(2,1)S(1)}, u32[]{:S(2)}, u32[]{:S(2)}) collective-permute-start(s16[640,128]{1,0:T(8,128)(2,1)S(1)} %pad_add_fusion.refs_5_), channel_id=1, source_target_pairs={{0,2},{1,3},{2,4},{3,5},{4,6},{5,7},{6,8},{7,9},{8,10},{9,11},{10,... | collective-permute-start | bytes 491528 | tf_op jit(solution)/shard_map/ppermute | solution.py:261
  15.8 4.2 %collective-permute-done.5.refs_6_ = s16[640,128]{1,0:T(8,128)(2,1)S(1)} collective-permute-done((s16[640,128]{1,0:T(8,128)(2,1)S(1)}, s16[640,128]{1,0:T(8,128)(2,1)S(1)}, u32[]{:S(2)}, u32[]{:S(2)}) %collective-permute-start.5) | collective-permute-done | bytes 163872 | tf_op jit(solution)/shard_map/ppermute | solution.py:261
  20.0 4.3 %collective-permute-start.8 = (s16[640,128]{1,0:T(8,128)(2,1)S(1)}, s16[640,128]{1,0:T(8,128)(2,1)S(1)}, u32[]{:S(2)}, u32[]{:S(2)}) collective-permute-start(s16[640,128]{1,0:T(8,128)(2,1)S(1)} %collective-permute-done.5.refs_6_), channel_id=1, source_target_pairs={{0,14},{1,15},{2,0},{3,1},{4,2},{5,3},{6,4},{7,5},{8,6},{9,7},{10,... | collective-permute-start | bytes 491528 | tf_op jit(solution)/shard_map/ppermute | solution.py:261
  24.4 1.1 collective-permute-start.3
  26.3 0.7 collective-permute-start.7
  27.0 3.4 %collective-permute-start.12 = (s16[640,128]{1,0:T(8,128)(2,1)S(1)}, s16[640,128]{1,0:T(8,128)(2,1)S(1)}, u32[]{:S(2)}, u32[]{:S(2)}) collective-permute-start(s16[640,128]{1,0:T(8,128)(2,1)S(1)} %collective-permute-done.8.refs_10_), channel_id=1, source_target_pairs={{0,14},{1,15},{2,0},{3,1},{4,2},{5,3},{6,4},{7,5},{8,6},{9,7},{10,... | collective-permute-start | bytes 491528 | tf_op jit(solution)/shard_map/ppermute | solution.py:261
  30.4 0.8 collective-permute-done.6.refs_8_
  31.2 2.7 %collective-permute-start.10 = (s16[640,128]{1,0:T(8,128)(2,1)S(1)}, s16[640,128]{1,0:T(8,128)(2,1)S(1)}, u32[]{:S(2)}, u32[]{:S(2)}) collective-permute-start(s16[640,128]{1,0:T(8,128)(2,1)S(1)} %collective-permute-done.6.refs_8_), channel_id=1, source_target_pairs={{0,14},{1,15},{2,0},{3,1},{4,2},{5,3},{6,4},{7,5},{8,6},{9,7},{10,... | collective-permute-start | bytes 491528 | tf_op jit(solution)/shard_map/ppermute | solution.py:261
  33.9 2.8 %collective-permute-start.16 = (s16[640,128]{1,0:T(8,128)(2,1)S(1)}, s16[640,128]{1,0:T(8,128)(2,1)S(1)}, u32[]{:S(2)}, u32[]{:S(2)}) collective-permute-start(s16[640,128]{1,0:T(8,128)(2,1)S(1)} %collective-permute-done.12.refs_14_), channel_id=1, source_target_pairs={{0,14},{1,15},{2,0},{3,1},{4,2},{5,3},{6,4},{7,5},{8,6},{9,7},{10,... | collective-permute-start | bytes 491528 | tf_op jit(solution)/shard_map/ppermute | solution.py:261
  36.7 1.2 collective-permute-done.10.refs_12_
  37.9 3.4 %collective-permute-start.14 = (s16[640,128]{1,0:T(8,128)(2,1)S(1)}, s16[640,128]{1,0:T(8,128)(2,1)S(1)}, u32[]{:S(2)}, u32[]{:S(2)}) collective-permute-start(s16[640,128]{1,0:T(8,128)(2,1)S(1)} %collective-permute-done.10.refs_12_), channel_id=1, source_target_pairs={{0,14},{1,15},{2,0},{3,1},{4,2},{5,3},{6,4},{7,5},{8,6},{9,7},{10,... | collective-permute-start | bytes 491528 | tf_op jit(solution)/shard_map/ppermute | solution.py:261
  41.4 3.4 %collective-permute-start.18 = (s16[640,128]{1,0:T(8,128)(2,1)S(1)}, s16[640,128]{1,0:T(8,128)(2,1)S(1)}, u32[]{:S(2)}, u32[]{:S(2)}) collective-permute-start(s16[640,128]{1,0:T(8,128)(2,1)S(1)} %collective-permute-done.16.refs_18_), channel_id=1, source_target_pairs={{0,14},{1,15},{2,0},{3,1},{4,2},{5,3},{6,4},{7,5},{8,6},{9,7},{10,... | collective-permute-start | bytes 491528 | tf_op jit(solution)/shard_map/ppermute | solution.py:261
  44.9 2.7 %collective-permute-done.15.refs_17_ = s16[640,128]{1,0:T(8,128)(2,1)S(1)} collective-permute-done((s16[640,128]{1,0:T(8,128)(2,1)S(1)}, s16[640,128]{1,0:T(8,128)(2,1)S(1)}, u32[]{:S(2)}, u32[]{:S(2)}) %collective-permute-start.15) | collective-permute-done | bytes 163872 | tf_op jit(solution)/shard_map/ppermute | solution.py:261
  47.6 0.7 copy-done.1
  48.9 2.2 %collective-permute-done.17.refs_19_ = s16[640,128]{1,0:T(8,128)(2,1)} collective-permute-done((s16[640,128]{1,0:T(8,128)(2,1)S(1)}, s16[640,128]{1,0:T(8,128)(2,1)}, u32[]{:S(2)}, u32[]{:S(2)}) %collective-permute-start.17) | collective-permute-done | bytes 163872 | tf_op jit(solution)/shard_map/ppermute | solution.py:261
  51.2 0.9 copy-done.2
  52.1 0.9 copy-done.4
  53.0 8.6 %first_products.1 = (s16[8,528,128]{2,1,0:T(8,128)(2,1)}, f32[512,128]{1,0:T(8,128)S(1)}) custom-call(s32[4,128]{1,0:T(4,128)S(1)} %add_add_fusion.1.refs_0_, s32[4,128]{1,0:T(4,128)S(1)} %collective-permute-done.3.refs_1_, s32[16]{0:T(128)S(1)} %stack.97.refs_2_, bf16[96,128,128]{2,1,0:T(8,128)(2,1)} %refs_3_.3, ...), custom_call_target="tpu_custom_call" | custom-call | tf_op jit(solution)/shard_map/first_products/pallas_call | solution.py:366
  61.6 5.2 %all-to-all-start = ((s16[8,528,128]{2,1,0:T(8,128)(2,1)}), s16[8,528,128]{2,1,0:T(8,128)(2,1)S(1)}, u32[]{:S(2)}, u32[]{:S(2)}) async-start(s16[8,528,128]{2,1,0:T(8,128)(2,1)} %get-tuple-element.13), calls=%async_computation | async-start | bytes 2162688 | tf_op jit(solution)/shard_map/all_to_all | solution.py:400
  66.8 0.9 constant_dynamic-slice_fusion.2
  67.7 1.2 copy.9
  69.0 9.0 %seed_counts.1.refs_1_ = f32[512,128]{1,0:T(8,128)S(1)} custom-call(s32[1]{0:T(128)} %bitcast.20.first_ref, s32[1024,128]{1,0:T(8,128)S(1)} %bitcast.25), custom_call_target="tpu_custom_call" | custom-call | tf_op jit(solution)/shard_map/seed_counts/pallas_call | solution.py:344
  78.4 2.9 %collective-permute-start.19 = (bf16[512,128]{1,0:T(8,128)(2,1)S(1)}, bf16[512,128]{1,0:T(8,128)(2,1)S(1)}, u32[]{:S(2)}, u32[]{:S(2)}) collective-permute-start(bf16[512,128]{1,0:T(8,128)(2,1)S(1)} %current.2.refs_5_), channel_id=1, source_target_pairs={{0,16},{1,17},{2,18},{3,19},{4,20},{5,21},{6,22},{7,23},{8,24},{9,... | collective-permute-start | bytes 393224 | tf_op jit(solution)/shard_map/ppermute | solution.py:261
  81.4 3.9 %collective-permute-done.19.refs_6_ = bf16[512,128]{1,0:T(8,128)(2,1)S(1)} collective-permute-done((bf16[512,128]{1,0:T(8,128)(2,1)S(1)}, bf16[512,128]{1,0:T(8,128)(2,1)S(1)}, u32[]{:S(2)}, u32[]{:S(2)}) %collective-permute-start.19) | collective-permute-done | bytes 131104 | tf_op jit(solution)/shard_map/ppermute | solution.py:261
  85.3 1.0 collective-permute-start.23
  86.4 1.4 collective-permute-start.22
  88.2 1.2 collective-permute-done.23.refs_10_
  89.4 2.0 %collective-permute-start.27 = (bf16[512,128]{1,0:T(8,128)(2,1)S(1)}, bf16[512,128]{1,0:T(8,128)(2,1)S(1)}, u32[]{:S(2)}, u32[]{:S(2)}) collective-permute-start(bf16[512,128]{1,0:T(8,128)(2,1)S(1)} %collective-permute-done.23.refs_10_), channel_id=1, source_target_pairs={{0,14},{1,15},{2,0},{3,1},{4,2},{5,3},{6,4},{7,5},{8,6},{9,7},{10,... | collective-permute-start | bytes 393224 | tf_op jit(solution)/shard_map/ppermute | solution.py:261
  91.4 1.4 collective-permute-start.25
  93.2 1.1 collective-permute-done.24.refs_11_
  94.6 2.9 %collective-permute-start.31 = (bf16[512,128]{1,0:T(8,128)(2,1)S(1)}, bf16[512,128]{1,0:T(8,128)(2,1)S(1)}, u32[]{:S(2)}, u32[]{:S(2)}) collective-permute-start(bf16[512,128]{1,0:T(8,128)(2,1)S(1)} %collective-permute-done.27.refs_14_), channel_id=1, source_target_pairs={{0,14},{1,15},{2,0},{3,1},{4,2},{5,3},{6,4},{7,5},{8,6},{9,7},{10,... | collective-permute-start | bytes 393224 | tf_op jit(solution)/shard_map/ppermute | solution.py:261
  97.5 2.8 %collective-permute-start.29 = (bf16[512,128]{1,0:T(8,128)(2,1)S(1)}, bf16[512,128]{1,0:T(8,128)(2,1)S(1)}, u32[]{:S(2)}, u32[]{:S(2)}) collective-permute-start(bf16[512,128]{1,0:T(8,128)(2,1)S(1)} %collective-permute-done.25.refs_12_), channel_id=1, source_target_pairs={{0,14},{1,15},{2,0},{3,1},{4,2},{5,3},{6,4},{7,5},{8,6},{9,7},{10,... | collective-permute-start | bytes 393224 | tf_op jit(solution)/shard_map/ppermute | solution.py:261
  100.3 1.1 collective-permute-done.28.refs_15_
  101.5 2.7 %collective-permute-start.33 = (bf16[512,128]{1,0:T(8,128)(2,1)S(1)}, bf16[512,128]{1,0:T(8,128)(2,1)S(1)}, u32[]{:S(2)}, u32[]{:S(2)}) collective-permute-start(bf16[512,128]{1,0:T(8,128)(2,1)S(1)} %collective-permute-done.31.refs_18_), channel_id=1, source_target_pairs={{0,14},{1,15},{2,0},{3,1},{4,2},{5,3},{6,4},{7,5},{8,6},{9,7},{10,... | collective-permute-start | bytes 393224 | tf_op jit(solution)/shard_map/ppermute | solution.py:261
  104.2 1.2 collective-permute-done.30.refs_17_
  105.4 2.7 %collective-permute-done.32.refs_19_ = bf16[512,128]{1,0:T(8,128)(2,1)S(1)} collective-permute-done((bf16[512,128]{1,0:T(8,128)(2,1)S(1)}, bf16[512,128]{1,0:T(8,128)(2,1)S(1)}, u32[]{:S(2)}, u32[]{:S(2)}) %collective-permute-start.32) | collective-permute-done | bytes 131104 | tf_op jit(solution)/shard_map/ppermute | solution.py:261
  108.1 6.7 %later_products.1 = s16[8,528,128]{2,1,0:T(8,128)(2,1)} custom-call(s32[4,128]{1,0:T(4,128)S(1)} %add_add_fusion.1.refs_0_, s32[4,128]{1,0:T(4,128)S(1)} %collective-permute-done.3.refs_1_, s32[16]{0:T(128)S(1)} %stack.97.refs_2_, bf16[96,128,128]{2,1,0:T(8,128)(2,1)} %refs_3_.3, bf16[96,128,128]{2,1,0:T(8,128)(2,1)} %collective-permute-done.4.refs_4_, ...), custom_call_target="tpu_custom_call" | custom-call | tf_op jit(solution)/shard_map/later_products/pallas_call | solution.py:376
  114.8 6.8 %all-to-all-start.1 = ((s16[8,528,128]{2,1,0:T(8,128)(2,1)}), s16[8,528,128]{2,1,0:T(8,128)(2,1)S(1)}, u32[]{:S(2)}, u32[]{:S(2)}) async-start(s16[8,528,128]{2,1,0:T(8,128)(2,1)} %later_products.1), calls=%async_computation.1 | async-start | bytes 2162688 | tf_op jit(solution)/shard_map/all_to_all | solution.py:404
  121.7 10.4 %all-to-all-done.1.refs_0_ = s16[8,528,128]{2,1,0:T(8,128)(2,1)S(1)} async-done(((s16[8,528,128]{2,1,0:T(8,128)(2,1)}), s16[8,528,128]{2,1,0:T(8,128)(2,1)S(1)}, u32[]{:S(2)}, u32[]{:S(2)}) %all-to-all-start.1) | async-done | bytes 1081376 | tf_op jit(solution)/shard_map/all_to_all | solution.py:404
  132.5 9.2 %collective-permute-start.34 = (f32[256,128]{1,0:T(8,128)S(1)}, f32[256,128]{1,0:T(8,128)S(1)}, u32[]{:S(2)}, u32[]{:S(2)}) collective-permute-start(f32[256,128]{1,0:T(8,128)S(1)} %get-tuple-element.23), channel_id=1, source_target_pairs={{0,1},{1,0},{2,3},{3,2},{4,5},{5,4},{6,7},{7,6},{8,9},{9,8},{10,11... | collective-permute-start | bytes 393224 | tf_op jit(solution)/shard_map/ppermute | solution.py:261
  141.8 1.0 collective-permute-done.34
  142.8 0.7 maximum_select_fusion
  (68 shorter events, 5.1 us)
Async XLA Ops:
  0.0 66.8 %copy-start = (s32[256,1024]{1,0:T(8,128)S(1)}, s32[256,1024]{1,0:T(8,128)}, u32[]{:S(2)}) copy-start(s32[256,1024]{1,0:T(8,128)} %param.11) | copy-start | bytes 3145732
  0.0 30.4 %collective-permute-start.4 = (bf16[96,128,128]{2,1,0:T(8,128)(2,1)}, bf16[96,128,128]{2,1,0:T(8,128)(2,1)}, u32[]{:S(2)}, u32[]{:S(2)}) collective-permute-start(bf16[96,128,128]{2,1,0:T(8,128)(2,1)} %refs_3_.3), channel_id=1, source_target_pairs={{0,1},{1,0},{2,3},{3,2},{4,5},{5,4},{6,7},{7,6},{8,9},{9,8},{10,11... | collective-permute-start | bytes 9437192 | tf_op jit(solution)/shard_map/ppermute | solution.py:261
  4.3 8.5 %collective-permute-start = (s16[256,128]{1,0:T(8,128)(2,1)S(1)}, s16[256,128]{1,0:T(8,128)(2,1)S(1)}, u32[]{:S(2)}, u32[]{:S(2)}) collective-permute-start(s16[256,128]{1,0:T(8,128)(2,1)S(1)} %get-tuple-element.25), channel_id=1, source_target_pairs={{0,1},{1,0},{2,3},{3,2},{4,5},{5,4},{6,7},{7,6},{8,9},{9,8},{10,11... | collective-permute-start | bytes 196616 | tf_op jit(solution)/shard_map/ppermute | solution.py:261
  5.8 2.9 %copy-start.5 = (s32[96]{0:T(128)S(1)}, s32[96]{0:T(128)}, u32[]{:S(2)}) copy-start(s32[96]{0:T(128)} %param.8) | copy-start | bytes 1156
  8.4 4.3 %collective-permute-start.1 = (f32[64,128]{1,0:T(8,128)S(1)}, f32[64,128]{1,0:T(8,128)S(1)}, u32[]{:S(2)}, u32[]{:S(2)}) collective-permute-start(f32[64,128]{1,0:T(8,128)S(1)} %column_sums.1), channel_id=1, source_target_pairs={{0,1},{1,0},{2,3},{3,2},{4,5},{5,4},{6,7},{7,6},{8,9},{9,8},{10,11... | collective-permute-start | bytes 98312 | tf_op jit(solution)/shard_map/ppermute | solution.py:261
  12.9 7.1 %collective-permute-start.5 = (s16[640,128]{1,0:T(8,128)(2,1)S(1)}, s16[640,128]{1,0:T(8,128)(2,1)S(1)}, u32[]{:S(2)}, u32[]{:S(2)}) collective-permute-start(s16[640,128]{1,0:T(8,128)(2,1)S(1)} %pad_add_fusion.refs_5_), channel_id=1, source_target_pairs={{0,16},{1,17},{2,18},{3,19},{4,20},{5,21},{6,22},{7,23},{8,24},{9,... | collective-permute-start | bytes 491528 | tf_op jit(solution)/shard_map/ppermute | solution.py:261
  14.2 16.1 %collective-permute-start.2 = (s16[640,128]{1,0:T(8,128)(2,1)S(1)}, s16[640,128]{1,0:T(8,128)(2,1)S(1)}, u32[]{:S(2)}, u32[]{:S(2)}) collective-permute-start(s16[640,128]{1,0:T(8,128)(2,1)S(1)} %pad_add_fusion.refs_5_), channel_id=1, source_target_pairs={{0,2},{1,3},{2,4},{3,5},{4,6},{5,7},{6,8},{7,9},{8,10},{9,11},{10,... | collective-permute-start | bytes 491528 | tf_op jit(solution)/shard_map/ppermute | solution.py:261
  20.0 7.0 %collective-permute-start.8 = (s16[640,128]{1,0:T(8,128)(2,1)S(1)}, s16[640,128]{1,0:T(8,128)(2,1)S(1)}, u32[]{:S(2)}, u32[]{:S(2)}) collective-permute-start(s16[640,128]{1,0:T(8,128)(2,1)S(1)} %collective-permute-done.5.refs_6_), channel_id=1, source_target_pairs={{0,14},{1,15},{2,0},{3,1},{4,2},{5,3},{6,4},{7,5},{8,6},{9,7},{10,... | collective-permute-start | bytes 491528 | tf_op jit(solution)/shard_map/ppermute | solution.py:261
  24.4 2.0 %collective-permute-start.3 = (s32[4,128]{1,0:T(4,128)S(1)}, s32[4,128]{1,0:T(4,128)S(1)}, u32[]{:S(2)}, u32[]{:S(2)}) collective-permute-start(s32[4,128]{1,0:T(4,128)S(1)} %add_add_fusion.1.refs_0_), channel_id=1, source_target_pairs={{0,1},{1,0},{2,3},{3,2},{4,5},{5,4},{6,7},{7,6},{8,9},{9,8},{10,11... | collective-permute-start | bytes 6152 | tf_op jit(solution)/shard_map/ppermute | solution.py:261
  25.5 5.8 %collective-permute-start.6 = (s16[640,128]{1,0:T(8,128)(2,1)S(1)}, s16[640,128]{1,0:T(8,128)(2,1)S(1)}, u32[]{:S(2)}, u32[]{:S(2)}) collective-permute-start(s16[640,128]{1,0:T(8,128)(2,1)S(1)} %pad_add_fusion.refs_5_), channel_id=1, source_target_pairs={{0,14},{1,15},{2,0},{3,1},{4,2},{5,3},{6,4},{7,5},{8,6},{9,7},{10,... | collective-permute-start | bytes 491528 | tf_op jit(solution)/shard_map/ppermute | solution.py:261
  26.3 7.6 %collective-permute-start.7 = (s16[640,128]{1,0:T(8,128)(2,1)S(1)}, s16[640,128]{1,0:T(8,128)(2,1)S(1)}, u32[]{:S(2)}, u32[]{:S(2)}) collective-permute-start(s16[640,128]{1,0:T(8,128)(2,1)S(1)} %collective-permute-done.5.refs_6_), channel_id=1, source_target_pairs={{0,2},{1,3},{2,4},{3,5},{4,6},{5,7},{6,8},{7,9},{8,10},{9,11},{10,... | collective-permute-start | bytes 491528 | tf_op jit(solution)/shard_map/ppermute | solution.py:261
  27.0 6.9 %collective-permute-start.12 = (s16[640,128]{1,0:T(8,128)(2,1)S(1)}, s16[640,128]{1,0:T(8,128)(2,1)S(1)}, u32[]{:S(2)}, u32[]{:S(2)}) collective-permute-start(s16[640,128]{1,0:T(8,128)(2,1)S(1)} %collective-permute-done.8.refs_10_), channel_id=1, source_target_pairs={{0,14},{1,15},{2,0},{3,1},{4,2},{5,3},{6,4},{7,5},{8,6},{9,7},{10,... | collective-permute-start | bytes 491528 | tf_op jit(solution)/shard_map/ppermute | solution.py:261
  30.4 6.3 %collective-permute-start.9 = (s16[640,128]{1,0:T(8,128)(2,1)S(1)}, s16[640,128]{1,0:T(8,128)(2,1)S(1)}, u32[]{:S(2)}, u32[]{:S(2)}) collective-permute-start(s16[640,128]{1,0:T(8,128)(2,1)S(1)} %collective-permute-done.2.refs_7_), channel_id=1, source_target_pairs={{0,2},{1,3},{2,4},{3,5},{4,6},{5,7},{6,8},{7,9},{8,10},{9,11},{10,... | collective-permute-start | bytes 491528 | tf_op jit(solution)/shard_map/ppermute | solution.py:261
  31.2 6.7 %collective-permute-start.10 = (s16[640,128]{1,0:T(8,128)(2,1)S(1)}, s16[640,128]{1,0:T(8,128)(2,1)S(1)}, u32[]{:S(2)}, u32[]{:S(2)}) collective-permute-start(s16[640,128]{1,0:T(8,128)(2,1)S(1)} %collective-permute-done.6.refs_8_), channel_id=1, source_target_pairs={{0,14},{1,15},{2,0},{3,1},{4,2},{5,3},{6,4},{7,5},{8,6},{9,7},{10,... | collective-permute-start | bytes 491528 | tf_op jit(solution)/shard_map/ppermute | solution.py:261
  33.9 7.4 %collective-permute-start.11 = (s16[640,128]{1,0:T(8,128)(2,1)S(1)}, s16[640,128]{1,0:T(8,128)(2,1)S(1)}, u32[]{:S(2)}, u32[]{:S(2)}) collective-permute-start(s16[640,128]{1,0:T(8,128)(2,1)S(1)} %collective-permute-done.7.refs_9_), channel_id=1, source_target_pairs={{0,2},{1,3},{2,4},{3,5},{4,6},{5,7},{6,8},{7,9},{8,10},{9,11},{10,... | collective-permute-start | bytes 491528 | tf_op jit(solution)/shard_map/ppermute | solution.py:261
  33.9 7.5 %collective-permute-start.16 = (s16[640,128]{1,0:T(8,128)(2,1)S(1)}, s16[640,128]{1,0:T(8,128)(2,1)S(1)}, u32[]{:S(2)}, u32[]{:S(2)}) collective-permute-start(s16[640,128]{1,0:T(8,128)(2,1)S(1)} %collective-permute-done.12.refs_14_), channel_id=1, source_target_pairs={{0,14},{1,15},{2,0},{3,1},{4,2},{5,3},{6,4},{7,5},{8,6},{9,7},{10,... | collective-permute-start | bytes 491528 | tf_op jit(solution)/shard_map/ppermute | solution.py:261
  36.7 8.1 %collective-permute-start.13 = (s16[640,128]{1,0:T(8,128)(2,1)S(1)}, s16[640,128]{1,0:T(8,128)(2,1)S(1)}, u32[]{:S(2)}, u32[]{:S(2)}) collective-permute-start(s16[640,128]{1,0:T(8,128)(2,1)S(1)} %collective-permute-done.9.refs_11_), channel_id=1, source_target_pairs={{0,2},{1,3},{2,4},{3,5},{4,6},{5,7},{6,8},{7,9},{8,10},{9,11},{10,... | collective-permute-start | bytes 491528 | tf_op jit(solution)/shard_map/ppermute | solution.py:261
  37.9 7.0 %collective-permute-start.14 = (s16[640,128]{1,0:T(8,128)(2,1)S(1)}, s16[640,128]{1,0:T(8,128)(2,1)S(1)}, u32[]{:S(2)}, u32[]{:S(2)}) collective-permute-start(s16[640,128]{1,0:T(8,128)(2,1)S(1)} %collective-permute-done.10.refs_12_), channel_id=1, source_target_pairs={{0,14},{1,15},{2,0},{3,1},{4,2},{5,3},{6,4},{7,5},{8,6},{9,7},{10,... | collective-permute-start | bytes 491528 | tf_op jit(solution)/shard_map/ppermute | solution.py:261
  41.3 6.3 %collective-permute-start.15 = (s16[640,128]{1,0:T(8,128)(2,1)S(1)}, s16[640,128]{1,0:T(8,128)(2,1)S(1)}, u32[]{:S(2)}, u32[]{:S(2)}) collective-permute-start(s16[640,128]{1,0:T(8,128)(2,1)S(1)} %collective-permute-done.11.refs_13_), channel_id=1, source_target_pairs={{0,2},{1,3},{2,4},{3,5},{4,6},{5,7},{6,8},{7,9},{8,10},{9,11},{10,... | collective-permute-start | bytes 491528 | tf_op jit(solution)/shard_map/ppermute | solution.py:261
  41.4 6.9 %collective-permute-start.18 = (s16[640,128]{1,0:T(8,128)(2,1)S(1)}, s16[640,128]{1,0:T(8,128)(2,1)S(1)}, u32[]{:S(2)}, u32[]{:S(2)}) collective-permute-start(s16[640,128]{1,0:T(8,128)(2,1)S(1)} %collective-permute-done.16.refs_18_), channel_id=1, source_target_pairs={{0,14},{1,15},{2,0},{3,1},{4,2},{5,3},{6,4},{7,5},{8,6},{9,7},{10,... | collective-permute-start | bytes 491528 | tf_op jit(solution)/shard_map/ppermute | solution.py:261
  44.8 6.4 %collective-permute-start.17 = (s16[640,128]{1,0:T(8,128)(2,1)S(1)}, s16[640,128]{1,0:T(8,128)(2,1)}, u32[]{:S(2)}, u32[]{:S(2)}) collective-permute-start(s16[640,128]{1,0:T(8,128)(2,1)S(1)} %collective-permute-done.13.refs_15_), channel_id=1, source_target_pairs={{0,2},{1,3},{2,4},{3,5},{4,6},{5,7},{6,8},{7,9},{8,10},{9,11},{10,... | collective-permute-start | bytes 491528 | tf_op jit(solution)/shard_map/ppermute | solution.py:261
  47.6 0.7 copy-start.1
  48.3 0.6 copy-start.3
  51.2 0.9 copy-start.2
  52.1 0.9 copy-start.4
  61.6 16.4 %all-to-all-start = ((s16[8,528,128]{2,1,0:T(8,128)(2,1)}), s16[8,528,128]{2,1,0:T(8,128)(2,1)S(1)}, u32[]{:S(2)}, u32[]{:S(2)}) async-start(s16[8,528,128]{2,1,0:T(8,128)(2,1)} %get-tuple-element.13), calls=%async_computation | async-start | bytes 2162688 | tf_op jit(solution)/shard_map/all_to_all | solution.py:400
  78.4 6.9 %collective-permute-start.19 = (bf16[512,128]{1,0:T(8,128)(2,1)S(1)}, bf16[512,128]{1,0:T(8,128)(2,1)S(1)}, u32[]{:S(2)}, u32[]{:S(2)}) collective-permute-start(bf16[512,128]{1,0:T(8,128)(2,1)S(1)} %current.2.refs_5_), channel_id=1, source_target_pairs={{0,16},{1,17},{2,18},{3,19},{4,20},{5,21},{6,22},{7,23},{8,24},{9,... | collective-permute-start | bytes 393224 | tf_op jit(solution)/shard_map/ppermute | solution.py:261
  81.4 6.4 %collective-permute-start.20 = (bf16[512,128]{1,0:T(8,128)(2,1)S(1)}, bf16[512,128]{1,0:T(8,128)(2,1)S(1)}, u32[]{:S(2)}, u32[]{:S(2)}) collective-permute-start(bf16[512,128]{1,0:T(8,128)(2,1)S(1)} %current.2.refs_5_), channel_id=1, source_target_pairs={{0,2},{1,3},{2,4},{3,5},{4,6},{5,7},{6,8},{7,9},{8,10},{9,11},{10,... | collective-permute-start | bytes 393224 | tf_op jit(solution)/shard_map/ppermute | solution.py:261
  85.3 4.1 %collective-permute-start.23 = (bf16[512,128]{1,0:T(8,128)(2,1)S(1)}, bf16[512,128]{1,0:T(8,128)(2,1)S(1)}, u32[]{:S(2)}, u32[]{:S(2)}) collective-permute-start(bf16[512,128]{1,0:T(8,128)(2,1)S(1)} %collective-permute-done.19.refs_6_), channel_id=1, source_target_pairs={{0,14},{1,15},{2,0},{3,1},{4,2},{5,3},{6,4},{7,5},{8,6},{9,7},{10,... | collective-permute-start | bytes 393224 | tf_op jit(solution)/shard_map/ppermute | solution.py:261
  86.3 5.0 %collective-permute-start.21 = (bf16[512,128]{1,0:T(8,128)(2,1)S(1)}, bf16[512,128]{1,0:T(8,128)(2,1)S(1)}, u32[]{:S(2)}, u32[]{:S(2)}) collective-permute-start(bf16[512,128]{1,0:T(8,128)(2,1)S(1)} %current.2.refs_5_), channel_id=1, source_target_pairs={{0,14},{1,15},{2,0},{3,1},{4,2},{5,3},{6,4},{7,5},{8,6},{9,7},{10,... | collective-permute-start | bytes 393224 | tf_op jit(solution)/shard_map/ppermute | solution.py:261
  86.4 6.4 %collective-permute-start.22 = (bf16[512,128]{1,0:T(8,128)(2,1)S(1)}, bf16[512,128]{1,0:T(8,128)(2,1)S(1)}, u32[]{:S(2)}, u32[]{:S(2)}) collective-permute-start(bf16[512,128]{1,0:T(8,128)(2,1)S(1)} %collective-permute-done.19.refs_6_), channel_id=1, source_target_pairs={{0,2},{1,3},{2,4},{3,5},{4,6},{5,7},{6,8},{7,9},{8,10},{9,11},{10,... | collective-permute-start | bytes 393224 | tf_op jit(solution)/shard_map/ppermute | solution.py:261
  87.8 6.6 %collective-permute-start.24 = (bf16[512,128]{1,0:T(8,128)(2,1)S(1)}, bf16[512,128]{1,0:T(8,128)(2,1)S(1)}, u32[]{:S(2)}, u32[]{:S(2)}) collective-permute-start(bf16[512,128]{1,0:T(8,128)(2,1)S(1)} %collective-permute-done.20.refs_7_), channel_id=1, source_target_pairs={{0,2},{1,3},{2,4},{3,5},{4,6},{5,7},{6,8},{7,9},{8,10},{9,11},{10,... | collective-permute-start | bytes 393224 | tf_op jit(solution)/shard_map/ppermute | solution.py:261
  89.4 5.2 %collective-permute-start.27 = (bf16[512,128]{1,0:T(8,128)(2,1)S(1)}, bf16[512,128]{1,0:T(8,128)(2,1)S(1)}, u32[]{:S(2)}, u32[]{:S(2)}) collective-permute-start(bf16[512,128]{1,0:T(8,128)(2,1)S(1)} %collective-permute-done.23.refs_10_), channel_id=1, source_target_pairs={{0,14},{1,15},{2,0},{3,1},{4,2},{5,3},{6,4},{7,5},{8,6},{9,7},{10,... | collective-permute-start | bytes 393224 | tf_op jit(solution)/shard_map/ppermute | solution.py:261
  91.4 6.2 %collective-permute-start.25 = (bf16[512,128]{1,0:T(8,128)(2,1)S(1)}, bf16[512,128]{1,0:T(8,128)(2,1)S(1)}, u32[]{:S(2)}, u32[]{:S(2)}) collective-permute-start(bf16[512,128]{1,0:T(8,128)(2,1)S(1)} %collective-permute-done.21.refs_8_), channel_id=1, source_target_pairs={{0,14},{1,15},{2,0},{3,1},{4,2},{5,3},{6,4},{7,5},{8,6},{9,7},{10,... | collective-permute-start | bytes 393224 | tf_op jit(solution)/shard_map/ppermute | solution.py:261
  92.8 7.6 %collective-permute-start.26 = (bf16[512,128]{1,0:T(8,128)(2,1)S(1)}, bf16[512,128]{1,0:T(8,128)(2,1)S(1)}, u32[]{:S(2)}, u32[]{:S(2)}) collective-permute-start(bf16[512,128]{1,0:T(8,128)(2,1)S(1)} %collective-permute-done.22.refs_9_), channel_id=1, source_target_pairs={{0,2},{1,3},{2,4},{3,5},{4,6},{5,7},{6,8},{7,9},{8,10},{9,11},{10,... | collective-permute-start | bytes 393224 | tf_op jit(solution)/shard_map/ppermute | solution.py:261
  94.4 7.1 %collective-permute-start.28 = (bf16[512,128]{1,0:T(8,128)(2,1)S(1)}, bf16[512,128]{1,0:T(8,128)(2,1)S(1)}, u32[]{:S(2)}, u32[]{:S(2)}) collective-permute-start(bf16[512,128]{1,0:T(8,128)(2,1)S(1)} %collective-permute-done.24.refs_11_), channel_id=1, source_target_pairs={{0,2},{1,3},{2,4},{3,5},{4,6},{5,7},{6,8},{7,9},{8,10},{9,11},{10,... | collective-permute-start | bytes 393224 | tf_op jit(solution)/shard_map/ppermute | solution.py:261
  94.6 6.9 %collective-permute-start.31 = (bf16[512,128]{1,0:T(8,128)(2,1)S(1)}, bf16[512,128]{1,0:T(8,128)(2,1)S(1)}, u32[]{:S(2)}, u32[]{:S(2)}) collective-permute-start(bf16[512,128]{1,0:T(8,128)(2,1)S(1)} %collective-permute-done.27.refs_14_), channel_id=1, source_target_pairs={{0,14},{1,15},{2,0},{3,1},{4,2},{5,3},{6,4},{7,5},{8,6},{9,7},{10,... | collective-permute-start | bytes 393224 | tf_op jit(solution)/shard_map/ppermute | solution.py:261
  97.5 6.7 %collective-permute-start.29 = (bf16[512,128]{1,0:T(8,128)(2,1)S(1)}, bf16[512,128]{1,0:T(8,128)(2,1)S(1)}, u32[]{:S(2)}, u32[]{:S(2)}) collective-permute-start(bf16[512,128]{1,0:T(8,128)(2,1)S(1)} %collective-permute-done.25.refs_12_), channel_id=1, source_target_pairs={{0,14},{1,15},{2,0},{3,1},{4,2},{5,3},{6,4},{7,5},{8,6},{9,7},{10,... | collective-permute-start | bytes 393224 | tf_op jit(solution)/shard_map/ppermute | solution.py:261
  100.3 5.0 %collective-permute-start.30 = (bf16[512,128]{1,0:T(8,128)(2,1)S(1)}, bf16[512,128]{1,0:T(8,128)(2,1)S(1)}, u32[]{:S(2)}, u32[]{:S(2)}) collective-permute-start(bf16[512,128]{1,0:T(8,128)(2,1)S(1)} %collective-permute-done.26.refs_13_), channel_id=1, source_target_pairs={{0,2},{1,3},{2,4},{3,5},{4,6},{5,7},{6,8},{7,9},{8,10},{9,11},{10,... | collective-permute-start | bytes 393224 | tf_op jit(solution)/shard_map/ppermute | solution.py:261
  101.5 6.6 %collective-permute-start.32 = (bf16[512,128]{1,0:T(8,128)(2,1)S(1)}, bf16[512,128]{1,0:T(8,128)(2,1)S(1)}, u32[]{:S(2)}, u32[]{:S(2)}) collective-permute-start(bf16[512,128]{1,0:T(8,128)(2,1)S(1)} %collective-permute-done.28.refs_15_), channel_id=1, source_target_pairs={{0,2},{1,3},{2,4},{3,5},{4,6},{5,7},{6,8},{7,9},{8,10},{9,11},{10,... | collective-permute-start | bytes 393224 | tf_op jit(solution)/shard_map/ppermute | solution.py:261
  101.5 6.6 %collective-permute-start.33 = (bf16[512,128]{1,0:T(8,128)(2,1)S(1)}, bf16[512,128]{1,0:T(8,128)(2,1)S(1)}, u32[]{:S(2)}, u32[]{:S(2)}) collective-permute-start(bf16[512,128]{1,0:T(8,128)(2,1)S(1)} %collective-permute-done.31.refs_18_), channel_id=1, source_target_pairs={{0,14},{1,15},{2,0},{3,1},{4,2},{5,3},{6,4},{7,5},{8,6},{9,7},{10,... | collective-permute-start | bytes 393224 | tf_op jit(solution)/shard_map/ppermute | solution.py:261
  114.8 17.3 %all-to-all-start.1 = ((s16[8,528,128]{2,1,0:T(8,128)(2,1)}), s16[8,528,128]{2,1,0:T(8,128)(2,1)S(1)}, u32[]{:S(2)}, u32[]{:S(2)}) async-start(s16[8,528,128]{2,1,0:T(8,128)(2,1)} %later_products.1), calls=%async_computation.1 | async-start | bytes 2162688 | tf_op jit(solution)/shard_map/all_to_all | solution.py:404
  132.5 10.2 %collective-permute-start.34 = (f32[256,128]{1,0:T(8,128)S(1)}, f32[256,128]{1,0:T(8,128)S(1)}, u32[]{:S(2)}, u32[]{:S(2)}) collective-permute-start(f32[256,128]{1,0:T(8,128)S(1)} %get-tuple-element.23), channel_id=1, source_target_pairs={{0,1},{1,0},{2,3},{3,2},{4,5},{5,4},{6,7},{7,6},{8,9},{9,8},{10,11... | collective-permute-start | bytes 393224 | tf_op jit(solution)/shard_map/ppermute | solution.py:261

commit v5 on v4

--- a/solution.py
+++ b/solution.py
@@ -57,13 +57,29 @@
         for u in range(8):
             k = 8 * g + u
             live = jnp.where(k < count_ref[0], 1.0, 0.0)
-            sums_ref[pl.ds(source_ref[k], 1), :] += columns[u] * live
+            sums_ref[pl.ds(source_ref[k] % sums_ref.shape[0], 1), :] += columns[u] * live
         return carry
 
     for c in range(arrived.shape[0]):
         copies[c].wait()
         last = jnp.minimum((c + 1) * chunk, count_ref[0])
         lax.fori_loop(c * chunk // 8, (last + 7) // 8, group, 0)
+
+
+def encode(value):
+    exponent = jnp.floor(jnp.log2(jnp.maximum(value, 1e-30))) + 1.0
+    mantissa = (value * jnp.exp2(24.0 - exponent) + 0.5).astype(jnp.int32)
+    mantissa = jnp.minimum(mantissa, (1 << 24) - 1)
+    upper = (exponent.astype(jnp.int32) + 127) * 256 + (mantissa >> 16)
+    return (jnp.concatenate([upper, mantissa & 65535]) - 32768).astype(jnp.int16)
+
+
+def decode(code):
+    code = code.astype(jnp.int32) + 32768
+    each = code.shape[0] // 2
+    upper, lower = code[:each], code[each:]
+    mantissa = ((upper & 255) * 65536 + lower).astype(jnp.float32)
+    return mantissa * jnp.exp2(((upper >> 8) - (127 + 24)).astype(jnp.float32))
 
 
 def column_totals(rows, piece_refs, sums_ref):
@@ -71,11 +87,8 @@
     each = groups * per
     total = jnp.zeros((each, lanes), jnp.float32)
     for piece_ref in piece_refs:
-        code = piece_ref[rows : rows + 2 * each, :].astype(jnp.int32) + 32768
-        upper, lower = code[:each], code[each:]
-        exponent = (upper >> 8) - 127
-        mantissa = ((upper & 255) * 65536 + lower).astype(jnp.float32)
-        total += mantissa * jnp.exp2((exponent - 24).astype(jnp.float32))
+        if piece_ref.shape[0] > rows:
+            total += decode(piece_ref[rows : rows + 2 * each, :])
     for g in range(groups):
         sums_ref[g] = total[g * per : (g + 1) * per]
 
@@ -269,18 +282,30 @@
     def across(value):
         return by_col(value, lambda y, at, k: (1 - y, at, k))
 
-    def gather(block, beside=None):
-        other = across(block)
-        pieces = [block, other]
-        names = [(0, 0), (1, 0)]
-        a, b, c, d = block, block, other, other
+    tie = lax.optimization_barrier
+
+    def gather(block, sums=None, later=None):
+        rows = block.shape[0]
+        a, b = along(block, 1), along(block, -1)
+        if sums is None:
+            other = across(block)
+        else:
+            other = across(jnp.concatenate([block, encode(sums)]))
+            sums = sums + decode(other[rows:])
+            other = jnp.concatenate([other[:rows], encode(sums)])
+        pieces, names, beside = [block, other], [(0, 0), (1, 0)], None
+        c, d = other, other
         for step in range(1, depth // 2):
-            a, b = along(a, 1), along(b, -1)
+            if step > 1:
+                a, b = along(a, 1), along(b, -1)
             c, d = along(c, 1), along(d, -1)
+            if later is not None and step == 1:
+                a, raw = tie((a, (tile_rows, tile_cols, tile_count)))
+                beside = later(*raw)
+            if later is not None and step == 2:
+                a, beside = tie((a, beside))
             pieces += [a, b, c, d]
             names += [(0, -step), (0, step), (1, -step), (1, step)]
-            if step == 1 and beside is not None:
-                a, beside = lax.optimization_barrier((a, beside))
         pieces += [along(a, 1), along(d, -1)]
         names += [(0, depth // 2), (1, depth // 2)]
         return pieces, names, beside
@@ -294,7 +319,6 @@
         core == 0, jnp.concatenate([mine, theirs]), jnp.concatenate([theirs, mine])
     )
     sib_tiles = sibling(tile_values)
-    sources = tile_cols - row_index * band_tiles
     sums = pl.pallas_call(
         column_kernel,
         out_shape=jax.ShapeDtypeStruct((band_tiles, TILE), jnp.float32),
@@ -303,41 +327,40 @@
         scratch_shapes=[VMEM(tile_values.shape, tile_values.dtype), pltpu.SemaphoreType.DMA((4,))],
         compiler_params=params(8),
         name="column_sums",
-    )(sources, tile_count, in_hbm(tile_values))
-
-    given = sums + sibling(sums)
-    exponent = jnp.floor(jnp.log2(jnp.maximum(given, 1e-30))) + 1.0
-    mantissa = jnp.minimum((given * jnp.exp2(24.0 - exponent) + 0.5).astype(jnp.int32), (1 << 24) - 1)
-    upper = (exponent.astype(jnp.int32) + 127) * 256 + (mantissa >> 16)
-    tail = jnp.concatenate([upper, mantissa & 65535]) - 32768
-    block = jnp.concatenate([block, tail.astype(jnp.int16)])
-
-    targets = tile_rows // band_tiles * per + core * BT + tile_rows % BT
-    live = jnp.arange(slots) < tile_count[0]
+    )(tile_cols, tile_count, in_hbm(tile_values))
+
+    sums = sums + sibling(sums)
+
     target_total = grid_rows * per
-    target_ids = jnp.arange(target_total, dtype=jnp.int32)
-    at_target = (targets[:, None] == target_ids[None, :]) & live[:, None]
-    filled = (jnp.sum(at_target.astype(jnp.int32), axis=0) + 1) // 2 * 2
-    start = jnp.sum(jnp.where(target_ids[:, None] < target_ids[None, :], filled[:, None], 0), axis=0)
-    slot_ids = jnp.arange(slots, dtype=jnp.int32)
-    alike = (targets[:, None] == targets[None, :]) & (slot_ids[None, :] < slot_ids[:, None])
-    place = jnp.sum(alike.astype(jnp.int32), axis=1)
-    place = place + jnp.sum(jnp.where(at_target, start[None, :], 0), axis=1)
-    long = slots + target_total
-    moved = (place[:, None] == jnp.arange(long)[None, :]) & live[:, None]
-
-    def spread(value):
-        return jnp.sum(jnp.where(moved, value[:, None], 0), axis=0)
-
-    facts = jnp.stack(
-        [
-            spread(slot_ids),
-            spread(sources - band_tiles) + band_tiles,
-            spread(targets),
-            jnp.broadcast_to(jnp.sum(filled) // 2, (long,)),
-        ]
-    )
-    sib_facts = sibling(facts)
+
+    def order_tiles(tile_rows, tile_cols, tile_count):
+        sources = tile_cols - row_index * band_tiles
+        targets = tile_rows // band_tiles * per + core * BT + tile_rows % BT
+        slot_ids = jnp.arange(slots, dtype=jnp.int32)
+        live = slot_ids < tile_count[0]
+        target_ids = jnp.arange(target_total, dtype=jnp.int32)
+        at_target = (targets[:, None] == target_ids[None, :]) & live[:, None]
+        filled = (jnp.sum(at_target.astype(jnp.int32), axis=0) + 1) // 2 * 2
+        before = target_ids[:, None] < target_ids[None, :]
+        start = jnp.sum(jnp.where(before, filled[:, None], 0), axis=0)
+        alike = (targets[:, None] == targets[None, :]) & (slot_ids[None, :] < slot_ids[:, None])
+        place = jnp.sum(alike.astype(jnp.int32), axis=1)
+        place = place + jnp.sum(jnp.where(at_target, start[None, :], 0), axis=1)
+        long = slots + target_total
+        moved = (place[:, None] == jnp.arange(long)[None, :]) & live[:, None]
+
+        def spread(value):
+            return jnp.sum(jnp.where(moved, value[:, None], 0), axis=0)
+
+        facts = jnp.stack(
+            [
+                spread(slot_ids),
+                spread(sources - band_tiles) + band_tiles,
+                spread(targets),
+                jnp.broadcast_to(jnp.sum(filled) // 2, (long,)),
+            ]
+        )
+        return facts, sibling(facts), sib_tiles
 
     first_page = (row_index * grid_cols + col_index - core) * own_rows
     ids = lax.dynamic_slice_in_dim(seed_ids, core * half, half, 0).T
@@ -350,7 +373,7 @@
         name="seed_counts",
     )(first_page.reshape(1), ids)
 
-    def multiply(pieces, names, coded):
+    def multiply(pieces, names, coded, facts, sib_facts, sib_tiles):
         order = jnp.stack([(high ^ y) * depth + (z + d) % depth for y, d in names])
         n = len(pieces)
         rows = per * TILE
@@ -395,12 +418,12 @@
             name="current",
         )(parts, restart, inverse)
 
-    pieces, names, (sib_facts, sib_tiles) = gather(block, (sib_facts, sib_tiles))
-    parts, inverse = multiply(pieces, names, True)
+    pieces, names, tile_facts = gather(block, sums, order_tiles)
+    parts, inverse = multiply(pieces, names, True, *tile_facts)
     parts = lax.all_to_all(parts, "row", 0, 0, tiled=True)
     panel = update(parts, inverse, True)
     pieces, names, _ = gather(panel)
-    parts = multiply(pieces, names, False)
+    parts = multiply(pieces, names, False, *tile_facts)
     parts = lax.all_to_all(parts, "row", 0, 0, tiled=True)
     current = update(parts, inverse, False)
     mine = lax.dynamic_slice_in_dim(current, core * own_rows, own_rows, 0)

time: 144 us -> 145 us (level)
  starting transfers between devices: 68.7 us -> 70.9 us
  Pallas kernels: 27.8 us -> 26.3 us
    ppermute x35, starting transfers between devices: 56.6 us -> 60.1 us  [by_col(): return lax.ppermute(value, 'col', pairs)]
    ppermute x35, waiting for transfers between devices: 23.8 us -> 21 us  [by_col(): return lax.ppermute(value, 'col', pairs)]
    all_to_all x2, waiting for transfers between devices: 10.5 us -> 12.4 us  [per_device(): parts = lax.all_to_all(parts, 'row', 0, 0, tiled=True)]
    unnamed x13 -> x17, local copies, waits for them, and re-layouts: 4.38 us -> 5 us
  transfers between devices with their start and end apart: 37 -> 37, of which waited for: 15 -> 18; matrix products, arithmetic and copies ran while one was open for 4% -> 3% of each run, Pallas kernels for 8% -> 8%
where the time goes in v5:
time: 145 us; the launch traced here: 144 us
  starting transfers between devices  70.9 us (49%)
  waiting for transfers between devices  33.4 us (23%)
  Pallas kernels  26.3 us (18%)
  local copies, waits for them, and re-layouts  6.08 us (4%)
  between operations  3.55 us (2%)
  other arithmetic  3.42 us (2%)
    ppermute x35, starting transfers between devices, by_col(): return lax.ppermute(value, 'col', pairs)  60.1 us
    ppermute x35, waiting for transfers between devices, by_col(): return lax.ppermute(value, 'col', pairs)  21 us
    all_to_all x2, waiting for transfers between devices, per_device(): parts = lax.all_to_all(parts, 'row', 0, 0, tiled=True)  12.4 us
    all_to_all x2, starting transfers between devices, per_device(): parts = lax.all_to_all(parts, 'row', 0, 0, tiled=True)  10.8 us
    pallas_call x1, Pallas kernels, per_device(): pl.pallas_call(seed_kernel, out_shape=jax.ShapeDtypeStruct((2 * own_rows,...  9.05 us
    pallas_call x1, Pallas kernels, multiply(): pl.pallas_call(lambda *refs: first_kernel(n, rows, *refs), out_shape=(par...  7.7 us
    pallas_call x1, Pallas kernels, multiply(): pl.pallas_call(lambda *refs: later_kernel(n, rows, *refs), out_shape=part...  6.32 us
    unnamed x17, local copies, waits for them, and re-layouts  5 us
  transfers between devices with their start and end apart: 37, of which 18 were waited for; matrix products, arithmetic and copies ran while one was open for 3% of the time, Pallas kernels for 8%

profile of v5, /device:TPU:1, one launch (start us, length us, event | category | flops | bytes accessed | tf_op | source)
XLA Modules:
  0.0 143.6 jit_solution(8869043403623768525)
XLA Ops:
  0.0 1.1 add_convert_fusion
  1.2 3.3 %collective-permute-start = (s16[256,128]{1,0:T(8,128)(2,1)S(1)}, s16[256,128]{1,0:T(8,128)(2,1)S(1)}, u32[]{:S(2)}, u32[]{:S(2)}) collective-permute-start(s16[256,128]{1,0:T(8,128)(2,1)S(1)} %get-tuple-element.35), channel_id=1, source_target_pairs={{0,1},{1,0},{2,3},{3,2},{4,5},{5,4},{6,7},{7,6},{8,9},{9,8},{10,11... | collective-permute-start | bytes 196616 | tf_op jit(solution)/shard_map/ppermute | solution.py:274
  5.3 0.6 copy-done.5
  5.9 2.4 %column_sums.1 = f32[64,128]{1,0:T(8,128)S(1)} custom-call(s32[96]{0:T(128)S(1)} %copy-done.5, s32[1]{0:T(128)} %copy.10.count_ref, bf16[96,128,128]{2,1,0:T(8,128)(2,1)} %refs_3_.3), custom_call_target="tpu_custom_call" | custom-call | tf_op jit(solution)/shard_map/column_sums/pallas_call | solution.py:322
  8.8 1.4 collective-permute-done.5
  10.5 3.9 %collective-permute-start.7 = (s16[512,128]{1,0:T(8,128)(2,1)S(1)}, s16[512,128]{1,0:T(8,128)(2,1)S(1)}, u32[]{:S(2)}, u32[]{:S(2)}) collective-permute-start(s16[512,128]{1,0:T(8,128)(2,1)S(1)} %add_select_fusion.refs_5_), channel_id=1, source_target_pairs={{0,14},{1,15},{2,0},{3,1},{4,2},{5,3},{6,4},{7,5},{8,6},{9,7},{10,... | collective-permute-start | bytes 393224 | tf_op jit(solution)/shard_map/ppermute | solution.py:274
  14.4 3.0 %collective-permute-start.6 = (s16[640,128]{1,0:T(8,128)(2,1)S(1)}, s16[640,128]{1,0:T(8,128)(2,1)S(1)}, u32[]{:S(2)}, u32[]{:S(2)}) collective-permute-start(s16[640,128]{1,0:T(8,128)(2,1)S(1)} %pad_add_fusion), channel_id=1, source_target_pairs={{0,16},{1,17},{2,18},{3,19},{4,20},{5,21},{6,22},{7,23},{8,24},{9,... | collective-permute-start | bytes 491528 | tf_op jit(solution)/shard_map/ppermute | solution.py:274
  18.1 0.6 fusion.12
  21.8 2.7 %collective-permute-start.9 = (s16[640,128]{1,0:T(8,128)(2,1)S(1)}, s16[640,128]{1,0:T(8,128)(2,1)S(1)}, u32[]{:S(2)}, u32[]{:S(2)}) collective-permute-start(s16[640,128]{1,0:T(8,128)(2,1)S(1)} %pad_add_fusion.1.refs_6_), channel_id=1, source_target_pairs={{0,14},{1,15},{2,0},{3,1},{4,2},{5,3},{6,4},{7,5},{8,6},{9,7},{10,... | collective-permute-start | bytes 491528 | tf_op jit(solution)/shard_map/ppermute | solution.py:274
  25.0 2.1 %collective-permute-done.9.refs_10_ = s16[640,128]{1,0:T(8,128)(2,1)S(1)} collective-permute-done((s16[640,128]{1,0:T(8,128)(2,1)S(1)}, s16[640,128]{1,0:T(8,128)(2,1)S(1)}, u32[]{:S(2)}, u32[]{:S(2)}) %collective-permute-start.9) | collective-permute-done | bytes 163872 | tf_op jit(solution)/shard_map/ppermute | solution.py:274
  27.1 3.4 %collective-permute-start.12 = (s16[640,128]{1,0:T(8,128)(2,1)S(1)}, s16[640,128]{1,0:T(8,128)(2,1)S(1)}, u32[]{:S(2)}, u32[]{:S(2)}) collective-permute-start(s16[640,128]{1,0:T(8,128)(2,1)S(1)} %collective-permute-done.9.refs_10_), channel_id=1, source_target_pairs={{0,14},{1,15},{2,0},{3,1},{4,2},{5,3},{6,4},{7,5},{8,6},{9,7},{10,... | collective-permute-start | bytes 491528 | tf_op jit(solution)/shard_map/ppermute | solution.py:274
  30.5 2.3 %collective-permute-done.12.refs_14_ = s16[640,128]{1,0:T(8,128)(2,1)S(1)} collective-permute-done((s16[640,128]{1,0:T(8,128)(2,1)S(1)}, s16[640,128]{1,0:T(8,128)(2,1)S(1)}, u32[]{:S(2)}, u32[]{:S(2)}) %collective-permute-start.12) | collective-permute-done | bytes 163872 | tf_op jit(solution)/shard_map/ppermute | solution.py:274
  32.7 3.1 %collective-permute-start.16 = (s16[640,128]{1,0:T(8,128)(2,1)S(1)}, s16[640,128]{1,0:T(8,128)(2,1)S(1)}, u32[]{:S(2)}, u32[]{:S(2)}) collective-permute-start(s16[640,128]{1,0:T(8,128)(2,1)S(1)} %collective-permute-done.12.refs_14_), channel_id=1, source_target_pairs={{0,14},{1,15},{2,0},{3,1},{4,2},{5,3},{6,4},{7,5},{8,6},{9,7},{10,... | collective-permute-start | bytes 491528 | tf_op jit(solution)/shard_map/ppermute | solution.py:274
  35.9 3.4 %collective-permute-start.3 = (s32[4,128]{1,0:T(4,128)S(1)}, s32[4,128]{1,0:T(4,128)S(1)}, u32[]{:S(2)}, u32[]{:S(2)}) collective-permute-start(s32[4,128]{1,0:T(4,128)S(1)} %add_add_fusion.2.refs_0_), channel_id=1, source_target_pairs={{0,1},{1,0},{2,3},{3,2},{4,5},{5,4},{6,7},{7,6},{8,9},{9,8},{10,11... | collective-permute-start | bytes 6152 | tf_op jit(solution)/shard_map/ppermute | solution.py:274
  39.3 0.8 collective-permute-done.3.refs_1_
  40.1 1.5 %collective-permute-start.13 = (s16[512,128]{1,0:T(8,128)(2,1)S(1)}, s16[512,128]{1,0:T(8,128)(2,1)S(1)}, u32[]{:S(2)}, u32[]{:S(2)}) collective-permute-start(s16[512,128]{1,0:T(8,128)(2,1)S(1)} %collective-permute-done.2.refs_11_), channel_id=1, source_target_pairs={{0,2},{1,3},{2,4},{3,5},{4,6},{5,7},{6,8},{7,9},{8,10},{9,11},{10,... | collective-permute-start | bytes 393224 | tf_op jit(solution)/shard_map/ppermute | solution.py:274
  41.9 2.4 %collective-permute-start.18 = (s16[640,128]{1,0:T(8,128)(2,1)S(1)}, s16[640,128]{1,0:T(8,128)(2,1)S(1)}, u32[]{:S(2)}, u32[]{:S(2)}) collective-permute-start(s16[640,128]{1,0:T(8,128)(2,1)S(1)} %collective-permute-done.16.refs_18_), channel_id=1, source_target_pairs={{0,14},{1,15},{2,0},{3,1},{4,2},{5,3},{6,4},{7,5},{8,6},{9,7},{10,... | collective-permute-start | bytes 491528 | tf_op jit(solution)/shard_map/ppermute | solution.py:274
  44.9 1.9 %collective-permute-start.14 = (s16[512,128]{1,0:T(8,128)(2,1)S(1)}, s16[512,128]{1,0:T(8,128)(2,1)S(1)}, u32[]{:S(2)}, u32[]{:S(2)}) collective-permute-start(s16[512,128]{1,0:T(8,128)(2,1)S(1)} %collective-permute-done.10.refs_12_), channel_id=1, source_target_pairs={{0,14},{1,15},{2,0},{3,1},{4,2},{5,3},{6,4},{7,5},{8,6},{9,7},{10,... | collective-permute-start | bytes 393224 | tf_op jit(solution)/shard_map/ppermute | solution.py:274
  46.9 4.2 %collective-permute-done.14.refs_16_ = s16[512,128]{1,0:T(8,128)(2,1)S(1)} collective-permute-done((s16[512,128]{1,0:T(8,128)(2,1)S(1)}, s16[512,128]{1,0:T(8,128)(2,1)S(1)}, u32[]{:S(2)}, u32[]{:S(2)}) %collective-permute-start.14) | collective-permute-done | bytes 131104 | tf_op jit(solution)/shard_map/ppermute | solution.py:274
  51.1 0.7 copy-done.1
  52.5 0.9 copy-done.2
  53.4 0.9 copy-done.4
  54.3 7.7 %first_products.1 = (s16[8,528,128]{2,1,0:T(8,128)(2,1)}, f32[512,128]{1,0:T(8,128)S(1)}) custom-call(s32[4,128]{1,0:T(4,128)S(1)} %add_add_fusion.2.refs_0_, s32[4,128]{1,0:T(4,128)S(1)} %collective-permute-done.3.refs_1_, s32[16]{0:T(128)S(1)} %stack.97.refs_2_, bf16[96,128,128]{2,1,0:T(8,128)(2,1)} %refs_3_.3, ...), custom_call_target="tpu_custom_call" | custom-call | tf_op jit(solution)/shard_map/first_products/pallas_call | solution.py:389
  62.0 6.3 %all-to-all-start = ((s16[8,528,128]{2,1,0:T(8,128)(2,1)}), s16[8,528,128]{2,1,0:T(8,128)(2,1)S(1)}, u32[]{:S(2)}, u32[]{:S(2)}) async-start(s16[8,528,128]{2,1,0:T(8,128)(2,1)} %get-tuple-element.23), calls=%async_computation | async-start | bytes 2162688 | tf_op jit(solution)/shard_map/all_to_all | solution.py:423
  68.3 0.9 constant_dynamic-slice_fusion.2
  69.2 1.2 copy.9
  70.4 9.0 %seed_counts.1.refs_1_ = f32[512,128]{1,0:T(8,128)S(1)} custom-call(s32[1]{0:T(128)} %bitcast.20.first_ref, s32[1024,128]{1,0:T(8,128)S(1)} %bitcast.25), custom_call_target="tpu_custom_call" | custom-call | tf_op jit(solution)/shard_map/seed_counts/pallas_call | solution.py:367
  79.5 1.9 %all-to-all-done.refs_0_ = s16[8,528,128]{2,1,0:T(8,128)(2,1)S(1)} async-done(((s16[8,528,128]{2,1,0:T(8,128)(2,1)}), s16[8,528,128]{2,1,0:T(8,128)(2,1)S(1)}, u32[]{:S(2)}, u32[]{:S(2)}) %all-to-all-start) | async-done | bytes 1081376 | tf_op jit(solution)/shard_map/all_to_all | solution.py:423
  81.8 2.0 %collective-permute-start.19 = (bf16[512,128]{1,0:T(8,128)(2,1)S(1)}, bf16[512,128]{1,0:T(8,128)(2,1)S(1)}, u32[]{:S(2)}, u32[]{:S(2)}) collective-permute-start(bf16[512,128]{1,0:T(8,128)(2,1)S(1)} %current.2.refs_5_), channel_id=1, source_target_pairs={{0,16},{1,17},{2,18},{3,19},{4,20},{5,21},{6,22},{7,23},{8,24},{9,... | collective-permute-start | bytes 393224 | tf_op jit(solution)/shard_map/ppermute | solution.py:274
  83.8 2.7 %collective-permute-start.20 = (bf16[512,128]{1,0:T(8,128)(2,1)S(1)}, bf16[512,128]{1,0:T(8,128)(2,1)S(1)}, u32[]{:S(2)}, u32[]{:S(2)}) collective-permute-start(bf16[512,128]{1,0:T(8,128)(2,1)S(1)} %current.2.refs_5_), channel_id=1, source_target_pairs={{0,2},{1,3},{2,4},{3,5},{4,6},{5,7},{6,8},{7,9},{8,10},{9,11},{10,... | collective-permute-start | bytes 393224 | tf_op jit(solution)/shard_map/ppermute | solution.py:274
  86.4 0.8 collective-permute-done.19.refs_6_
  87.2 2.7 %collective-permute-start.23 = (bf16[512,128]{1,0:T(8,128)(2,1)S(1)}, bf16[512,128]{1,0:T(8,128)(2,1)S(1)}, u32[]{:S(2)}, u32[]{:S(2)}) collective-permute-start(bf16[512,128]{1,0:T(8,128)(2,1)S(1)} %collective-permute-done.19.refs_6_), channel_id=1, source_target_pairs={{0,14},{1,15},{2,0},{3,1},{4,2},{5,3},{6,4},{7,5},{8,6},{9,7},{10,... | collective-permute-start | bytes 393224 | tf_op jit(solution)/shard_map/ppermute | solution.py:274
  89.9 1.5 %collective-permute-start.21 = (bf16[512,128]{1,0:T(8,128)(2,1)S(1)}, bf16[512,128]{1,0:T(8,128)(2,1)S(1)}, u32[]{:S(2)}, u32[]{:S(2)}) collective-permute-start(bf16[512,128]{1,0:T(8,128)(2,1)S(1)} %current.2.refs_5_), channel_id=1, source_target_pairs={{0,14},{1,15},{2,0},{3,1},{4,2},{5,3},{6,4},{7,5},{8,6},{9,7},{10,... | collective-permute-start | bytes 393224 | tf_op jit(solution)/shard_map/ppermute | solution.py:274
  91.8 3.1 %collective-permute-start.27 = (bf16[512,128]{1,0:T(8,128)(2,1)S(1)}, bf16[512,128]{1,0:T(8,128)(2,1)S(1)}, u32[]{:S(2)}, u32[]{:S(2)}) collective-permute-start(bf16[512,128]{1,0:T(8,128)(2,1)S(1)} %collective-permute-done.23.refs_10_), channel_id=1, source_target_pairs={{0,14},{1,15},{2,0},{3,1},{4,2},{5,3},{6,4},{7,5},{8,6},{9,7},{10,... | collective-permute-start | bytes 393224 | tf_op jit(solution)/shard_map/ppermute | solution.py:274
  94.9 1.5 %collective-permute-start.25 = (bf16[512,128]{1,0:T(8,128)(2,1)S(1)}, bf16[512,128]{1,0:T(8,128)(2,1)S(1)}, u32[]{:S(2)}, u32[]{:S(2)}) collective-permute-start(bf16[512,128]{1,0:T(8,128)(2,1)S(1)} %collective-permute-done.21.refs_8_), channel_id=1, source_target_pairs={{0,14},{1,15},{2,0},{3,1},{4,2},{5,3},{6,4},{7,5},{8,6},{9,7},{10,... | collective-permute-start | bytes 393224 | tf_op jit(solution)/shard_map/ppermute | solution.py:274
  96.4 1.4 collective-permute-done.24.refs_11_
  98.1 3.4 %collective-permute-start.31 = (bf16[512,128]{1,0:T(8,128)(2,1)S(1)}, bf16[512,128]{1,0:T(8,128)(2,1)S(1)}, u32[]{:S(2)}, u32[]{:S(2)}) collective-permute-start(bf16[512,128]{1,0:T(8,128)(2,1)S(1)} %collective-permute-done.27.refs_14_), channel_id=1, source_target_pairs={{0,14},{1,15},{2,0},{3,1},{4,2},{5,3},{6,4},{7,5},{8,6},{9,7},{10,... | collective-permute-start | bytes 393224 | tf_op jit(solution)/shard_map/ppermute | solution.py:274
  101.6 2.1 %collective-permute-start.29 = (bf16[512,128]{1,0:T(8,128)(2,1)S(1)}, bf16[512,128]{1,0:T(8,128)(2,1)S(1)}, u32[]{:S(2)}, u32[]{:S(2)}) collective-permute-start(bf16[512,128]{1,0:T(8,128)(2,1)S(1)} %collective-permute-done.25.refs_12_), channel_id=1, source_target_pairs={{0,14},{1,15},{2,0},{3,1},{4,2},{5,3},{6,4},{7,5},{8,6},{9,7},{10,... | collective-permute-start | bytes 393224 | tf_op jit(solution)/shard_map/ppermute | solution.py:274
  103.7 1.1 collective-permute-done.28.refs_15_
  104.8 3.4 %collective-permute-start.33 = (bf16[512,128]{1,0:T(8,128)(2,1)S(1)}, bf16[512,128]{1,0:T(8,128)(2,1)S(1)}, u32[]{:S(2)}, u32[]{:S(2)}) collective-permute-start(bf16[512,128]{1,0:T(8,128)(2,1)S(1)} %collective-permute-done.31.refs_18_), channel_id=1, source_target_pairs={{0,14},{1,15},{2,0},{3,1},{4,2},{5,3},{6,4},{7,5},{8,6},{9,7},{10,... | collective-permute-start | bytes 393224 | tf_op jit(solution)/shard_map/ppermute | solution.py:274
  108.2 1.1 collective-permute-done.30.refs_17_
  109.4 2.8 %collective-permute-done.32.refs_19_ = bf16[512,128]{1,0:T(8,128)(2,1)S(1)} collective-permute-done((bf16[512,128]{1,0:T(8,128)(2,1)S(1)}, bf16[512,128]{1,0:T(8,128)(2,1)S(1)}, u32[]{:S(2)}, u32[]{:S(2)}) %collective-permute-start.32) | collective-permute-done | bytes 131104 | tf_op jit(solution)/shard_map/ppermute | solution.py:274
  112.2 6.3 %later_products.1 = s16[8,528,128]{2,1,0:T(8,128)(2,1)} custom-call(s32[4,128]{1,0:T(4,128)S(1)} %add_add_fusion.2.refs_0_, s32[4,128]{1,0:T(4,128)S(1)} %collective-permute-done.3.refs_1_, s32[16]{0:T(128)S(1)} %stack.97.refs_2_, bf16[96,128,128]{2,1,0:T(8,128)(2,1)} %refs_3_.3, bf16[96,128,128]{2,1,0:T(8,128)(2,1)} %collective-permute-done.4.refs_4_, ...), custom_call_target="tpu_custom_call" | custom-call | tf_op jit(solution)/shard_map/later_products/pallas_call | solution.py:399
  118.5 4.5 %all-to-all-start.1 = ((s16[8,528,128]{2,1,0:T(8,128)(2,1)}), s16[8,528,128]{2,1,0:T(8,128)(2,1)S(1)}, u32[]{:S(2)}, u32[]{:S(2)}) async-start(s16[8,528,128]{2,1,0:T(8,128)(2,1)} %later_products.1), calls=%async_computation.1 | async-start | bytes 2162688 | tf_op jit(solution)/shard_map/all_to_all | solution.py:427
  123.0 10.4 %all-to-all-done.1.refs_0_ = s16[8,528,128]{2,1,0:T(8,128)(2,1)S(1)} async-done(((s16[8,528,128]{2,1,0:T(8,128)(2,1)}), s16[8,528,128]{2,1,0:T(8,128)(2,1)S(1)}, u32[]{:S(2)}, u32[]{:S(2)}) %all-to-all-start.1) | async-done | bytes 1081376 | tf_op jit(solution)/shard_map/all_to_all | solution.py:427
  133.9 8.0 %collective-permute-start.34 = (f32[256,128]{1,0:T(8,128)S(1)}, f32[256,128]{1,0:T(8,128)S(1)}, u32[]{:S(2)}, u32[]{:S(2)}) collective-permute-start(f32[256,128]{1,0:T(8,128)S(1)} %get-tuple-element.33), channel_id=1, source_target_pairs={{0,1},{1,0},{2,3},{3,2},{4,5},{5,4},{6,7},{7,6},{8,9},{9,8},{10,11... | collective-permute-start | bytes 393224 | tf_op jit(solution)/shard_map/ppermute | solution.py:274
  141.9 1.0 collective-permute-done.34
  142.9 0.7 maximum_select_fusion
  (78 shorter events, 5.8 us)
Async XLA Ops:
  0.0 68.3 %copy-start = (s32[256,1024]{1,0:T(8,128)S(1)}, s32[256,1024]{1,0:T(8,128)}, u32[]{:S(2)}) copy-start(s32[256,1024]{1,0:T(8,128)} %param.11) | copy-start | bytes 3145732
  1.2 9.1 %collective-permute-start = (s16[256,128]{1,0:T(8,128)(2,1)S(1)}, s16[256,128]{1,0:T(8,128)(2,1)S(1)}, u32[]{:S(2)}, u32[]{:S(2)}) collective-permute-start(s16[256,128]{1,0:T(8,128)(2,1)S(1)} %get-tuple-element.35), channel_id=1, source_target_pairs={{0,1},{1,0},{2,3},{3,2},{4,5},{5,4},{6,7},{7,6},{8,9},{9,8},{10,11... | collective-permute-start | bytes 196616 | tf_op jit(solution)/shard_map/ppermute | solution.py:274
  4.5 35.6 %collective-permute-start.4 = (bf16[96,128,128]{2,1,0:T(8,128)(2,1)}, bf16[96,128,128]{2,1,0:T(8,128)(2,1)}, u32[]{:S(2)}, u32[]{:S(2)}) collective-permute-start(bf16[96,128,128]{2,1,0:T(8,128)(2,1)} %refs_3_.3), channel_id=1, source_target_pairs={{0,1},{1,0},{2,3},{3,2},{4,5},{5,4},{6,7},{7,6},{8,9},{9,8},{10,11... | collective-permute-start | bytes 9437192 | tf_op jit(solution)/shard_map/ppermute | solution.py:274
  5.3 0.7 copy-start.5
  5.9 12.1 %copy-start.7 = (s32[96]{0:T(128)S(1)}, s32[96]{0:T(128)}, u32[]{:S(2)}) copy-start(s32[96]{0:T(128)} %param.8) | copy-start | bytes 1156
  5.9 15.6 %copy-start.6 = (s32[96]{0:T(128)S(1)}, s32[96]{0:T(128)}, u32[]{:S(2)}) copy-start(s32[96]{0:T(128)} %source_ref.1) | copy-start | bytes 1156
  8.3 1.9 %collective-permute-start.5 = (f32[64,128]{1,0:T(8,128)S(1)}, f32[64,128]{1,0:T(8,128)S(1)}, u32[]{:S(2)}, u32[]{:S(2)}) collective-permute-start(f32[64,128]{1,0:T(8,128)S(1)} %column_sums.1), channel_id=1, source_target_pairs={{0,1},{1,0},{2,3},{3,2},{4,5},{5,4},{6,7},{7,6},{8,9},{9,8},{10,11... | collective-permute-start | bytes 98312 | tf_op jit(solution)/shard_map/ppermute | solution.py:274
  10.3 7.7 %collective-permute-start.1 = (s16[512,128]{1,0:T(8,128)(2,1)S(1)}, s16[512,128]{1,0:T(8,128)(2,1)S(1)}, u32[]{:S(2)}, u32[]{:S(2)}) collective-permute-start(s16[512,128]{1,0:T(8,128)(2,1)S(1)} %add_select_fusion.refs_5_), channel_id=1, source_target_pairs={{0,2},{1,3},{2,4},{3,5},{4,6},{5,7},{6,8},{7,9},{8,10},{9,11},{10,... | collective-permute-start | bytes 393224 | tf_op jit(solution)/shard_map/ppermute | solution.py:274
  10.5 25.5 %collective-permute-start.7 = (s16[512,128]{1,0:T(8,128)(2,1)S(1)}, s16[512,128]{1,0:T(8,128)(2,1)S(1)}, u32[]{:S(2)}, u32[]{:S(2)}) collective-permute-start(s16[512,128]{1,0:T(8,128)(2,1)S(1)} %add_select_fusion.refs_5_), channel_id=1, source_target_pairs={{0,14},{1,15},{2,0},{3,1},{4,2},{5,3},{6,4},{7,5},{8,6},{9,7},{10,... | collective-permute-start | bytes 393224 | tf_op jit(solution)/shard_map/ppermute | solution.py:274
  14.4 7.3 %collective-permute-start.6 = (s16[640,128]{1,0:T(8,128)(2,1)S(1)}, s16[640,128]{1,0:T(8,128)(2,1)S(1)}, u32[]{:S(2)}, u32[]{:S(2)}) collective-permute-start(s16[640,128]{1,0:T(8,128)(2,1)S(1)} %pad_add_fusion), channel_id=1, source_target_pairs={{0,16},{1,17},{2,18},{3,19},{4,20},{5,21},{6,22},{7,23},{8,24},{9,... | collective-permute-start | bytes 491528 | tf_op jit(solution)/shard_map/ppermute | solution.py:274
  21.5 18.7 %collective-permute-start.2 = (s16[512,128]{1,0:T(8,128)(2,1)S(1)}, s16[512,128]{1,0:T(8,128)(2,1)S(1)}, u32[]{:S(2)}, u32[]{:S(2)}) collective-permute-start(s16[512,128]{1,0:T(8,128)(2,1)S(1)} %collective-permute-done.1.refs_7_), channel_id=1, source_target_pairs={{0,2},{1,3},{2,4},{3,5},{4,6},{5,7},{6,8},{7,9},{8,10},{9,11},{10,... | collective-permute-start | bytes 393224 | tf_op jit(solution)/shard_map/ppermute | solution.py:274
  21.8 5.2 %collective-permute-start.9 = (s16[640,128]{1,0:T(8,128)(2,1)S(1)}, s16[640,128]{1,0:T(8,128)(2,1)S(1)}, u32[]{:S(2)}, u32[]{:S(2)}) collective-permute-start(s16[640,128]{1,0:T(8,128)(2,1)S(1)} %pad_add_fusion.1.refs_6_), channel_id=1, source_target_pairs={{0,14},{1,15},{2,0},{3,1},{4,2},{5,3},{6,4},{7,5},{8,6},{9,7},{10,... | collective-permute-start | bytes 491528 | tf_op jit(solution)/shard_map/ppermute | solution.py:274
  24.9 5.6 %collective-permute-start.8 = (s16[640,128]{1,0:T(8,128)(2,1)S(1)}, s16[640,128]{1,0:T(8,128)(2,1)S(1)}, u32[]{:S(2)}, u32[]{:S(2)}) collective-permute-start(s16[640,128]{1,0:T(8,128)(2,1)S(1)} %pad_add_fusion.1.refs_6_), channel_id=1, source_target_pairs={{0,2},{1,3},{2,4},{3,5},{4,6},{5,7},{6,8},{7,9},{8,10},{9,11},{10,... | collective-permute-start | bytes 491528 | tf_op jit(solution)/shard_map/ppermute | solution.py:274
  27.1 5.7 %collective-permute-start.12 = (s16[640,128]{1,0:T(8,128)(2,1)S(1)}, s16[640,128]{1,0:T(8,128)(2,1)S(1)}, u32[]{:S(2)}, u32[]{:S(2)}) collective-permute-start(s16[640,128]{1,0:T(8,128)(2,1)S(1)} %collective-permute-done.9.refs_10_), channel_id=1, source_target_pairs={{0,14},{1,15},{2,0},{3,1},{4,2},{5,3},{6,4},{7,5},{8,6},{9,7},{10,... | collective-permute-start | bytes 491528 | tf_op jit(solution)/shard_map/ppermute | solution.py:274
  30.5 11.1 %collective-permute-start.11 = (s16[640,128]{1,0:T(8,128)(2,1)S(1)}, s16[640,128]{1,0:T(8,128)(2,1)S(1)}, u32[]{:S(2)}, u32[]{:S(2)}) collective-permute-start(s16[640,128]{1,0:T(8,128)(2,1)S(1)} %collective-permute-done.8.refs_9_), channel_id=1, source_target_pairs={{0,2},{1,3},{2,4},{3,5},{4,6},{5,7},{6,8},{7,9},{8,10},{9,11},{10,... | collective-permute-start | bytes 491528 | tf_op jit(solution)/shard_map/ppermute | solution.py:274
  32.7 9.1 %collective-permute-start.16 = (s16[640,128]{1,0:T(8,128)(2,1)S(1)}, s16[640,128]{1,0:T(8,128)(2,1)S(1)}, u32[]{:S(2)}, u32[]{:S(2)}) collective-permute-start(s16[640,128]{1,0:T(8,128)(2,1)S(1)} %collective-permute-done.12.refs_14_), channel_id=1, source_target_pairs={{0,14},{1,15},{2,0},{3,1},{4,2},{5,3},{6,4},{7,5},{8,6},{9,7},{10,... | collective-permute-start | bytes 491528 | tf_op jit(solution)/shard_map/ppermute | solution.py:274
  35.9 4.2 %collective-permute-start.3 = (s32[4,128]{1,0:T(4,128)S(1)}, s32[4,128]{1,0:T(4,128)S(1)}, u32[]{:S(2)}, u32[]{:S(2)}) collective-permute-start(s32[4,128]{1,0:T(4,128)S(1)} %add_add_fusion.2.refs_0_), channel_id=1, source_target_pairs={{0,1},{1,0},{2,3},{3,2},{4,5},{5,4},{6,7},{7,6},{8,9},{9,8},{10,11... | collective-permute-start | bytes 6152 | tf_op jit(solution)/shard_map/ppermute | solution.py:274
  40.1 4.7 %collective-permute-start.10 = (s16[512,128]{1,0:T(8,128)(2,1)S(1)}, s16[512,128]{1,0:T(8,128)(2,1)S(1)}, u32[]{:S(2)}, u32[]{:S(2)}) collective-permute-start(s16[512,128]{1,0:T(8,128)(2,1)S(1)} %collective-permute-done.7.refs_8_), channel_id=1, source_target_pairs={{0,14},{1,15},{2,0},{3,1},{4,2},{5,3},{6,4},{7,5},{8,6},{9,7},{10,... | collective-permute-start | bytes 393224 | tf_op jit(solution)/shard_map/ppermute | solution.py:274
  40.1 6.7 %collective-permute-start.13 = (s16[512,128]{1,0:T(8,128)(2,1)S(1)}, s16[512,128]{1,0:T(8,128)(2,1)S(1)}, u32[]{:S(2)}, u32[]{:S(2)}) collective-permute-start(s16[512,128]{1,0:T(8,128)(2,1)S(1)} %collective-permute-done.2.refs_11_), channel_id=1, source_target_pairs={{0,2},{1,3},{2,4},{3,5},{4,6},{5,7},{6,8},{7,9},{8,10},{9,11},{10,... | collective-permute-start | bytes 393224 | tf_op jit(solution)/shard_map/ppermute | solution.py:274
  41.6 10.1 %collective-permute-start.15 = (s16[640,128]{1,0:T(8,128)(2,1)S(1)}, s16[640,128]{1,0:T(8,128)(2,1)S(1)}, u32[]{:S(2)}, u32[]{:S(2)}) collective-permute-start(s16[640,128]{1,0:T(8,128)(2,1)S(1)} %collective-permute-done.11.refs_13_), channel_id=1, source_target_pairs={{0,2},{1,3},{2,4},{3,5},{4,6},{5,7},{6,8},{7,9},{8,10},{9,11},{10,... | collective-permute-start | bytes 491528 | tf_op jit(solution)/shard_map/ppermute | solution.py:274
  41.9 9.9 %collective-permute-start.18 = (s16[640,128]{1,0:T(8,128)(2,1)S(1)}, s16[640,128]{1,0:T(8,128)(2,1)S(1)}, u32[]{:S(2)}, u32[]{:S(2)}) collective-permute-start(s16[640,128]{1,0:T(8,128)(2,1)S(1)} %collective-permute-done.16.refs_18_), channel_id=1, source_target_pairs={{0,14},{1,15},{2,0},{3,1},{4,2},{5,3},{6,4},{7,5},{8,6},{9,7},{10,... | collective-permute-start | bytes 491528 | tf_op jit(solution)/shard_map/ppermute | solution.py:274
  44.9 6.2 %collective-permute-start.14 = (s16[512,128]{1,0:T(8,128)(2,1)S(1)}, s16[512,128]{1,0:T(8,128)(2,1)S(1)}, u32[]{:S(2)}, u32[]{:S(2)}) collective-permute-start(s16[512,128]{1,0:T(8,128)(2,1)S(1)} %collective-permute-done.10.refs_12_), channel_id=1, source_target_pairs={{0,14},{1,15},{2,0},{3,1},{4,2},{5,3},{6,4},{7,5},{8,6},{9,7},{10,... | collective-permute-start | bytes 393224 | tf_op jit(solution)/shard_map/ppermute | solution.py:274
  46.8 5.0 %collective-permute-start.17 = (s16[512,128]{1,0:T(8,128)(2,1)S(1)}, s16[512,128]{1,0:T(8,128)(2,1)S(1)}, u32[]{:S(2)}, u32[]{:S(2)}) collective-permute-start(s16[512,128]{1,0:T(8,128)(2,1)S(1)} %collective-permute-done.13.refs_15_), channel_id=1, source_target_pairs={{0,2},{1,3},{2,4},{3,5},{4,6},{5,7},{6,8},{7,9},{8,10},{9,11},{10,... | collective-permute-start | bytes 393224 | tf_op jit(solution)/shard_map/ppermute | solution.py:274
  51.1 0.7 copy-start.1
  51.9 0.6 copy-start.3
  52.5 0.9 copy-start.2
  53.4 0.9 copy-start.4
  62.0 19.4 %all-to-all-start = ((s16[8,528,128]{2,1,0:T(8,128)(2,1)}), s16[8,528,128]{2,1,0:T(8,128)(2,1)S(1)}, u32[]{:S(2)}, u32[]{:S(2)}) async-start(s16[8,528,128]{2,1,0:T(8,128)(2,1)} %get-tuple-element.23), calls=%async_computation | async-start | bytes 2162688 | tf_op jit(solution)/shard_map/all_to_all | solution.py:423
  81.8 5.4 %collective-permute-start.19 = (bf16[512,128]{1,0:T(8,128)(2,1)S(1)}, bf16[512,128]{1,0:T(8,128)(2,1)S(1)}, u32[]{:S(2)}, u32[]{:S(2)}) collective-permute-start(bf16[512,128]{1,0:T(8,128)(2,1)S(1)} %current.2.refs_5_), channel_id=1, source_target_pairs={{0,16},{1,17},{2,18},{3,19},{4,20},{5,21},{6,22},{7,23},{8,24},{9,... | collective-permute-start | bytes 393224 | tf_op jit(solution)/shard_map/ppermute | solution.py:274
  83.8 7.6 %collective-permute-start.20 = (bf16[512,128]{1,0:T(8,128)(2,1)S(1)}, bf16[512,128]{1,0:T(8,128)(2,1)S(1)}, u32[]{:S(2)}, u32[]{:S(2)}) collective-permute-start(bf16[512,128]{1,0:T(8,128)(2,1)S(1)} %current.2.refs_5_), channel_id=1, source_target_pairs={{0,2},{1,3},{2,4},{3,5},{4,6},{5,7},{6,8},{7,9},{8,10},{9,11},{10,... | collective-permute-start | bytes 393224 | tf_op jit(solution)/shard_map/ppermute | solution.py:274
  87.2 4.6 %collective-permute-start.23 = (bf16[512,128]{1,0:T(8,128)(2,1)S(1)}, bf16[512,128]{1,0:T(8,128)(2,1)S(1)}, u32[]{:S(2)}, u32[]{:S(2)}) collective-permute-start(bf16[512,128]{1,0:T(8,128)(2,1)S(1)} %collective-permute-done.19.refs_6_), channel_id=1, source_target_pairs={{0,14},{1,15},{2,0},{3,1},{4,2},{5,3},{6,4},{7,5},{8,6},{9,7},{10,... | collective-permute-start | bytes 393224 | tf_op jit(solution)/shard_map/ppermute | solution.py:274
  89.9 5.0 %collective-permute-start.21 = (bf16[512,128]{1,0:T(8,128)(2,1)S(1)}, bf16[512,128]{1,0:T(8,128)(2,1)S(1)}, u32[]{:S(2)}, u32[]{:S(2)}) collective-permute-start(bf16[512,128]{1,0:T(8,128)(2,1)S(1)} %current.2.refs_5_), channel_id=1, source_target_pairs={{0,14},{1,15},{2,0},{3,1},{4,2},{5,3},{6,4},{7,5},{8,6},{9,7},{10,... | collective-permute-start | bytes 393224 | tf_op jit(solution)/shard_map/ppermute | solution.py:274
  91.4 5.0 %collective-permute-start.22 = (bf16[512,128]{1,0:T(8,128)(2,1)S(1)}, bf16[512,128]{1,0:T(8,128)(2,1)S(1)}, u32[]{:S(2)}, u32[]{:S(2)}) collective-permute-start(bf16[512,128]{1,0:T(8,128)(2,1)S(1)} %collective-permute-done.19.refs_6_), channel_id=1, source_target_pairs={{0,2},{1,3},{2,4},{3,5},{4,6},{5,7},{6,8},{7,9},{8,10},{9,11},{10,... | collective-permute-start | bytes 393224 | tf_op jit(solution)/shard_map/ppermute | solution.py:274
  91.4 6.4 %collective-permute-start.24 = (bf16[512,128]{1,0:T(8,128)(2,1)S(1)}, bf16[512,128]{1,0:T(8,128)(2,1)S(1)}, u32[]{:S(2)}, u32[]{:S(2)}) collective-permute-start(bf16[512,128]{1,0:T(8,128)(2,1)S(1)} %collective-permute-done.20.refs_7_), channel_id=1, source_target_pairs={{0,2},{1,3},{2,4},{3,5},{4,6},{5,7},{6,8},{7,9},{8,10},{9,11},{10,... | collective-permute-start | bytes 393224 | tf_op jit(solution)/shard_map/ppermute | solution.py:274
  91.8 6.3 %collective-permute-start.27 = (bf16[512,128]{1,0:T(8,128)(2,1)S(1)}, bf16[512,128]{1,0:T(8,128)(2,1)S(1)}, u32[]{:S(2)}, u32[]{:S(2)}) collective-permute-start(bf16[512,128]{1,0:T(8,128)(2,1)S(1)} %collective-permute-done.23.refs_10_), channel_id=1, source_target_pairs={{0,14},{1,15},{2,0},{3,1},{4,2},{5,3},{6,4},{7,5},{8,6},{9,7},{10,... | collective-permute-start | bytes 393224 | tf_op jit(solution)/shard_map/ppermute | solution.py:274
  94.9 6.6 %collective-permute-start.25 = (bf16[512,128]{1,0:T(8,128)(2,1)S(1)}, bf16[512,128]{1,0:T(8,128)(2,1)S(1)}, u32[]{:S(2)}, u32[]{:S(2)}) collective-permute-start(bf16[512,128]{1,0:T(8,128)(2,1)S(1)} %collective-permute-done.21.refs_8_), channel_id=1, source_target_pairs={{0,14},{1,15},{2,0},{3,1},{4,2},{5,3},{6,4},{7,5},{8,6},{9,7},{10,... | collective-permute-start | bytes 393224 | tf_op jit(solution)/shard_map/ppermute | solution.py:274
  96.4 7.3 %collective-permute-start.26 = (bf16[512,128]{1,0:T(8,128)(2,1)S(1)}, bf16[512,128]{1,0:T(8,128)(2,1)S(1)}, u32[]{:S(2)}, u32[]{:S(2)}) collective-permute-start(bf16[512,128]{1,0:T(8,128)(2,1)S(1)} %collective-permute-done.22.refs_9_), channel_id=1, source_target_pairs={{0,2},{1,3},{2,4},{3,5},{4,6},{5,7},{6,8},{7,9},{8,10},{9,11},{10,... | collective-permute-start | bytes 393224 | tf_op jit(solution)/shard_map/ppermute | solution.py:274
  97.8 7.0 %collective-permute-start.28 = (bf16[512,128]{1,0:T(8,128)(2,1)S(1)}, bf16[512,128]{1,0:T(8,128)(2,1)S(1)}, u32[]{:S(2)}, u32[]{:S(2)}) collective-permute-start(bf16[512,128]{1,0:T(8,128)(2,1)S(1)} %collective-permute-done.24.refs_11_), channel_id=1, source_target_pairs={{0,2},{1,3},{2,4},{3,5},{4,6},{5,7},{6,8},{7,9},{8,10},{9,11},{10,... | collective-permute-start | bytes 393224 | tf_op jit(solution)/shard_map/ppermute | solution.py:274
  98.1 6.7 %collective-permute-start.31 = (bf16[512,128]{1,0:T(8,128)(2,1)S(1)}, bf16[512,128]{1,0:T(8,128)(2,1)S(1)}, u32[]{:S(2)}, u32[]{:S(2)}) collective-permute-start(bf16[512,128]{1,0:T(8,128)(2,1)S(1)} %collective-permute-done.27.refs_14_), channel_id=1, source_target_pairs={{0,14},{1,15},{2,0},{3,1},{4,2},{5,3},{6,4},{7,5},{8,6},{9,7},{10,... | collective-permute-start | bytes 393224 | tf_op jit(solution)/shard_map/ppermute | solution.py:274
  101.6 6.7 %collective-permute-start.29 = (bf16[512,128]{1,0:T(8,128)(2,1)S(1)}, bf16[512,128]{1,0:T(8,128)(2,1)S(1)}, u32[]{:S(2)}, u32[]{:S(2)}) collective-permute-start(bf16[512,128]{1,0:T(8,128)(2,1)S(1)} %collective-permute-done.25.refs_12_), channel_id=1, source_target_pairs={{0,14},{1,15},{2,0},{3,1},{4,2},{5,3},{6,4},{7,5},{8,6},{9,7},{10,... | collective-permute-start | bytes 393224 | tf_op jit(solution)/shard_map/ppermute | solution.py:274
  103.7 5.7 %collective-permute-start.30 = (bf16[512,128]{1,0:T(8,128)(2,1)S(1)}, bf16[512,128]{1,0:T(8,128)(2,1)S(1)}, u32[]{:S(2)}, u32[]{:S(2)}) collective-permute-start(bf16[512,128]{1,0:T(8,128)(2,1)S(1)} %collective-permute-done.26.refs_13_), channel_id=1, source_target_pairs={{0,2},{1,3},{2,4},{3,5},{4,6},{5,7},{6,8},{7,9},{8,10},{9,11},{10,... | collective-permute-start | bytes 393224 | tf_op jit(solution)/shard_map/ppermute | solution.py:274
  104.8 7.4 %collective-permute-start.32 = (bf16[512,128]{1,0:T(8,128)(2,1)S(1)}, bf16[512,128]{1,0:T(8,128)(2,1)S(1)}, u32[]{:S(2)}, u32[]{:S(2)}) collective-permute-start(bf16[512,128]{1,0:T(8,128)(2,1)S(1)} %collective-permute-done.28.refs_15_), channel_id=1, source_target_pairs={{0,2},{1,3},{2,4},{3,5},{4,6},{5,7},{6,8},{7,9},{8,10},{9,11},{10,... | collective-permute-start | bytes 393224 | tf_op jit(solution)/shard_map/ppermute | solution.py:274
  104.8 7.4 %collective-permute-start.33 = (bf16[512,128]{1,0:T(8,128)(2,1)S(1)}, bf16[512,128]{1,0:T(8,128)(2,1)S(1)}, u32[]{:S(2)}, u32[]{:S(2)}) collective-permute-start(bf16[512,128]{1,0:T(8,128)(2,1)S(1)} %collective-permute-done.31.refs_18_), channel_id=1, source_target_pairs={{0,14},{1,15},{2,0},{3,1},{4,2},{5,3},{6,4},{7,5},{8,6},{9,7},{10,... | collective-permute-start | bytes 393224 | tf_op jit(solution)/shard_map/ppermute | solution.py:274
  118.5 14.9 %all-to-all-start.1 = ((s16[8,528,128]{2,1,0:T(8,128)(2,1)}), s16[8,528,128]{2,1,0:T(8,128)(2,1)S(1)}, u32[]{:S(2)}, u32[]{:S(2)}) async-start(s16[8,528,128]{2,1,0:T(8,128)(2,1)} %later_products.1), calls=%async_computation.1 | async-start | bytes 2162688 | tf_op jit(solution)/shard_map/all_to_all | solution.py:427
  133.9 9.0 %collective-permute-start.34 = (f32[256,128]{1,0:T(8,128)S(1)}, f32[256,128]{1,0:T(8,128)S(1)}, u32[]{:S(2)}, u32[]{:S(2)}) collective-permute-start(f32[256,128]{1,0:T(8,128)S(1)} %get-tuple-element.33), channel_id=1, source_target_pairs={{0,1},{1,0},{2,3},{3,2},{4,5},{5,4},{6,7},{7,6},{8,9},{9,8},{10,11... | collective-permute-start | bytes 393224 | tf_op jit(solution)/shard_map/ppermute | solution.py:274

commit v6 on v5

--- a/solution.py
+++ b/solution.py
@@ -82,32 +82,35 @@
     return mantissa * jnp.exp2(((upper >> 8) - (127 + 24)).astype(jnp.float32))
 
 
-def column_totals(rows, piece_refs, sums_ref):
-    groups, per, lanes = sums_ref.shape
-    each = groups * per
-    total = jnp.zeros((each, lanes), jnp.float32)
+def column_totals(rows, each, piece_refs):
+    total = jnp.zeros((each, LANES), jnp.float32)
     for piece_ref in piece_refs:
         if piece_ref.shape[0] > rows:
             total += decode(piece_ref[rows : rows + 2 * each, :])
-    for g in range(groups):
-        sums_ref[g] = total[g * per : (g + 1) * per]
-
-
-def seed_kernel(first_ref, ids_ref, counts_ref):
+    return total
+
+
+def seed_kernel(first_ref, ids_ref, counts_ref, pages_ref):
     total, lanes = ids_ref.shape
     pages = counts_ref.shape[0]
     first = first_ref[0]
-    chunk = 64
+    chunk = 256
     counts_ref[...] = jnp.zeros_like(counts_ref)
 
-    def above(low):
-        def step(i, best):
-            page = ids_ref[pl.ds(pl.multiple_of(i * chunk, chunk), chunk), :] - first
-            found = jnp.where(page > low, page, FAR).reshape(chunk // 8, 8, lanes)
-            return jnp.minimum(best, jnp.min(found, axis=0))
-
-        best = lax.fori_loop(0, total // chunk, step, jnp.full((8, lanes), FAR, jnp.int32))
-        return jnp.min(best, axis=0, keepdims=True)
+    def fold(value, reduce):
+        parts = [value[i : i + 8] for i in range(0, value.shape[0], 8)]
+        while len(parts) > 1:
+            parts = [reduce(p, q) for p, q in zip(parts[::2], parts[1::2])]
+        return parts[0]
+
+    def rows(i):
+        return pl.ds(pl.multiple_of(i * chunk, chunk), chunk)
+
+    def prepare(i, best):
+        page = ids_ref[rows(i), :] - first
+        page = jnp.where((page >= 0) & (page < pages), page, FAR)
+        pages_ref[rows(i), :] = page
+        return jnp.minimum(best, fold(page, jnp.minimum))
 
     def more(carry):
         return carry[1] < pages
@@ -117,30 +120,26 @@
 
         def step(i, inner):
             best, seen = inner
-            page = ids_ref[pl.ds(pl.multiple_of(i * chunk, chunk), chunk), :] - first
-            found = jnp.where(page > page_now, page, FAR).reshape(chunk // 8, 8, lanes)
-            same = jnp.where(page == page_now, 1.0, 0.0).reshape(chunk // 8, 8, lanes)
-            return jnp.minimum(best, jnp.min(found, axis=0)), seen + jnp.sum(same, axis=0)
-
-        best, seen = lax.fori_loop(
-            0,
-            total // chunk,
-            step,
-            (jnp.full((8, lanes), FAR, jnp.int32), jnp.zeros((8, lanes), jnp.float32)),
-        )
+            page = pages_ref[rows(i), :]
+            found = jnp.where(page > page_now, page, FAR)
+            same = jnp.where(page == page_now, 1.0, 0.0)
+            return jnp.minimum(best, fold(found, jnp.minimum)), seen + fold(same, jnp.add)
+
+        best, seen = lax.fori_loop(0, total // chunk, step, (far, jnp.zeros((8, lanes), jnp.float32)))
         seen = jnp.sum(seen, axis=0, keepdims=True)
 
         def place(i, inner):
-            rows = pl.ds(pl.multiple_of(i * chunk, chunk), chunk)
             here = lax.broadcasted_iota(jnp.int32, (chunk, lanes), 0) + i * chunk
-            counts_ref[rows, :] += jnp.where(here == page_now, seen, 0.0)
+            counts_ref[rows(i), :] += jnp.where(here == page_now, seen, 0.0)
             return inner
 
         lax.fori_loop(0, pages // chunk, place, 0)
         later = jnp.min(best, axis=0, keepdims=True)
         return later, jnp.min(later)
 
-    start = above(jnp.full((1, lanes), -1, jnp.int32))
+    far = jnp.full((8, lanes), FAR, jnp.int32)
+    best = lax.fori_loop(0, total // chunk, prepare, far)
+    start = jnp.min(best, axis=0, keepdims=True)
     lax.while_loop(more, walk, (start, jnp.min(start)))
 
 
@@ -199,13 +198,24 @@
     lax.fori_loop(0, receivers, send, 0)
 
 
-def first_kernel(pieces, rows, own_facts, sib_facts, chip_ref, own_ref, sib_ref, *refs):
-    piece_refs = refs[:pieces]
-    out_ref, inverse_ref, panel, total, tiles, arrived, sums_ref, ordered = refs[pieces:]
+def first_kernel(pieces, far, rows, own_facts, sib_facts, chip_ref, own_ref, sib_ref, *refs):
+    piece_refs = list(refs[:pieces])
+    out_ref, inverse_ref, panel, total, tiles, arrived, sums_ref, ordered, brought, near = refs[pieces:]
+    brings = []
+    for i, piece_ref in enumerate(piece_refs[pieces - far :]):
+        inside = brought.at[i, pl.ds(0, piece_ref.shape[0])]
+        brings.append(pltpu.make_async_copy(piece_ref, inside, near.at[i]))
+        brings[i].start()
+        piece_refs[pieces - far + i] = inside
     copies = fetch(own_ref, sib_ref, tiles, arrived)
-    column_totals(rows, piece_refs, sums_ref)
     total[...] = jnp.zeros_like(total)
-    per = rows // TILE
+    groups, per, _ = sums_ref.shape
+    sums = column_totals(rows, groups * per, piece_refs[: pieces - far])
+    for bring in brings:
+        bring.wait()
+    sums = sums + column_totals(rows, groups * per, piece_refs[pieces - far :])
+    for g in range(groups):
+        sums_ref[g] = sums[g * per : (g + 1) * per]
     ordered[...] = jnp.zeros_like(ordered)
     for p in range(pieces):
         ordered[p * per : (p + 1) * per, :] = sums_ref[chip_ref[p]]
@@ -291,6 +301,7 @@
             other = across(block)
         else:
             other = across(jnp.concatenate([block, encode(sums)]))
+            a, b, other = tie((a, b, other))
             sums = sums + decode(other[rows:])
             other = jnp.concatenate([other[:rows], encode(sums)])
         pieces, names, beside = [block, other], [(0, 0), (1, 0)], None
@@ -299,11 +310,9 @@
             if step > 1:
                 a, b = along(a, 1), along(b, -1)
             c, d = along(c, 1), along(d, -1)
-            if later is not None and step == 1:
-                a, raw = tie((a, (tile_rows, tile_cols, tile_count)))
+            if later is not None and step == depth // 2 - 1:
+                c, raw = tie((c, (tile_rows, tile_cols, tile_count)))
                 beside = later(*raw)
-            if later is not None and step == 2:
-                a, beside = tie((a, beside))
             pieces += [a, b, c, d]
             names += [(0, -step), (0, step), (1, -step), (1, step)]
         pieces += [along(a, 1), along(d, -1)]
@@ -313,6 +322,7 @@
     half = columns // 2
     code = ((scores - LOW) * (STEPS / (HIGH - LOW)) + 0.5).astype(jnp.int32)
     code = (jnp.clip(code, 0, 65535) - 32768).astype(jnp.int16)
+    code, count = tie((code, tile_count))
     mine = lax.dynamic_slice_in_dim(code, core * half, half, 1)
     theirs = sibling(lax.dynamic_slice_in_dim(code, (1 - core) * half, half, 1))
     block = jnp.where(
@@ -327,7 +337,7 @@
         scratch_shapes=[VMEM(tile_values.shape, tile_values.dtype), pltpu.SemaphoreType.DMA((4,))],
         compiler_params=params(8),
         name="column_sums",
-    )(tile_cols, tile_count, in_hbm(tile_values))
+    )(tile_cols, count, in_hbm(tile_values))
 
     sums = sums + sibling(sums)
 
@@ -369,6 +379,7 @@
         out_shape=jax.ShapeDtypeStruct((2 * own_rows, half), jnp.float32),
         in_specs=[smem(), vmem()],
         out_specs=vmem(),
+        scratch_shapes=[VMEM(ids.shape, jnp.int32)],
         compiler_params=params(4),
         name="seed_counts",
     )(first_page.reshape(1), ids)
@@ -386,13 +397,24 @@
         ]
         tiles = (in_hbm(tile_values), in_hbm(sib_tiles))
         if coded:
+            far = 6
+            pieces = pieces[: n - far] + [in_hbm(piece) for piece in pieces[n - far :]]
+            longest = max(piece.shape[0] for piece in pieces)
             return pl.pallas_call(
-                lambda *refs: first_kernel(n, rows, *refs),
+                lambda *refs: first_kernel(n, far, rows, *refs),
                 out_shape=(parts, jax.ShapeDtypeStruct((rows, half), jnp.float32)),
-                in_specs=[smem()] * 3 + [anywhere()] * 2 + [vmem()] * n,
+                in_specs=[smem()] * 3
+                + [anywhere()] * 2
+                + [vmem()] * (n - far)
+                + [anywhere()] * far,
                 out_specs=(vmem(), vmem()),
                 scratch_shapes=scratch
-                + [VMEM((chips, per, TILE), jnp.float32), VMEM((TILE, TILE), jnp.float32)],
+                + [
+                    VMEM((chips, per, TILE), jnp.float32),
+                    VMEM((TILE, TILE), jnp.float32),
+                    VMEM((far, longest, half), jnp.int16),
+                    pltpu.SemaphoreType.DMA((far,)),
+                ],
                 compiler_params=params(20),
                 name="first_products",
             )(facts, sib_facts, order, *tiles, *pieces)

time: 145 us -> 144 us (level)
  waiting for transfers between devices: 33.4 us -> 45.8 us
  starting transfers between devices: 70.9 us -> 63.9 us
  local copies, waits for them, and re-layouts: 6.08 us -> 3.63 us
  Pallas kernels: 26.3 us -> 24.3 us
    ppermute x35, waiting for transfers between devices: 21 us -> 28.9 us  [by_col(): return lax.ppermute(value, 'col', pairs)]
    all_to_all x2, waiting for transfers between devices: 12.4 us -> 16.9 us  [per_device(): parts = lax.all_to_all(parts, 'row', 0, 0, tiled=True)]
    ppermute x35, starting transfers between devices: 60.1 us -> 55.7 us  [by_col(): return lax.ppermute(value, 'col', pairs)]
    pallas_call x1, Pallas kernels: 9.05 us -> 5.96 us  [per_device(): pl.pallas_call(seed_kernel, out_shape=jax.ShapeDtypeStruct((2 * own_rows,...]
    all_to_all x2, starting transfers between devices: 10.8 us -> 8.18 us  [per_device(): parts = lax.all_to_all(parts, 'row', 0, 0, tiled=True)]
    unnamed x17 -> x23, local copies, waits for them, and re-layouts: 5 us -> 2.54 us
  transfers between devices with their start and end apart: 37 -> 37, of which waited for: 18 -> 21; matrix products, arithmetic and copies ran while one was open for 3% -> 3% of each run, Pallas kernels for 8% -> 6%
where the time goes in v6:
time: 144 us; the launch traced here: 143 us
  starting transfers between devices  63.9 us (44%)
  waiting for transfers between devices  45.8 us (32%)
  Pallas kernels  24.3 us (17%)
  local copies, waits for them, and re-layouts  3.63 us (3%)
  between operations  3.49 us (2%)
  other arithmetic  2.38 us (2%)
    ppermute x35, starting transfers between devices, by_col(): return lax.ppermute(value, 'col', pairs)  55.7 us
    ppermute x35, waiting for transfers between devices, by_col(): return lax.ppermute(value, 'col', pairs)  28.9 us
    all_to_all x2, waiting for transfers between devices, per_device(): parts = lax.all_to_all(parts, 'row', 0, 0, tiled=True)  16.9 us
    all_to_all x2, starting transfers between devices, per_device(): parts = lax.all_to_all(parts, 'row', 0, 0, tiled=True)  8.18 us
    pallas_call x1, Pallas kernels, multiply(): pl.pallas_call(lambda *refs: first_kernel(n, far, rows, *refs), out_shape...  8 us
    pallas_call x1, Pallas kernels, multiply(): pl.pallas_call(lambda *refs: later_kernel(n, rows, *refs), out_shape=part...  7.15 us
    pallas_call x1, Pallas kernels, per_device(): pl.pallas_call(seed_kernel, out_shape=jax.ShapeDtypeStruct((2 * own_rows,...  5.96 us
  transfers between devices with their start and end apart: 37, of which 21 were waited for; matrix products, arithmetic and copies ran while one was open for 3% of the time, Pallas kernels for 6%

profile of v6, /device:TPU:1, one launch (start us, length us, event | category | flops | bytes accessed | tf_op | source)
XLA Modules:
  0.0 143.5 jit_solution(10460012367862315612)
XLA Ops:
  0.0 3.2 %collective-permute-start.9 = (bf16[96,128,128]{2,1,0:T(8,128)(2,1)}, bf16[96,128,128]{2,1,0:T(8,128)(2,1)}, u32[]{:S(2)}, u32[]{:S(2)}) collective-permute-start(bf16[96,128,128]{2,1,0:T(8,128)(2,1)} %refs_3_.3), channel_id=1, source_target_pairs={{0,1},{1,0},{2,3},{3,2},{4,5},{5,4},{6,7},{7,6},{8,9},{9,8},{10,11... | collective-permute-start | bytes 9437192 | tf_op jit(solution)/shard_map/ppermute | solution.py:284
  3.9 0.6 copy-done.1
  4.6 2.4 %column_sums.1 = f32[64,128]{1,0:T(8,128)S(1)} custom-call(s32[96]{0:T(128)S(1)} %copy-done.1, s32[1]{0:T(128)} %copy.10.count_ref, bf16[96,128,128]{2,1,0:T(8,128)(2,1)} %refs_3_.3), custom_call_target="tpu_custom_call" | custom-call | tf_op jit(solution)/shard_map/column_sums/pallas_call | solution.py:332
  7.8 0.7 collective-permute-done.3
  8.8 1.4 collective-permute-start.4
  10.2 1.6 %collective-permute-start.1 = (s16[512,128]{1,0:T(8,128)(2,1)S(1)}, s16[512,128]{1,0:T(8,128)(2,1)S(1)}, u32[]{:S(2)}, u32[]{:S(2)}) collective-permute-start(s16[512,128]{1,0:T(8,128)(2,1)S(1)} %add_select_fusion.refs_5_), channel_id=1, source_target_pairs={{0,2},{1,3},{2,4},{3,5},{4,6},{5,7},{6,8},{7,9},{8,10},{9,11},{10,... | collective-permute-start | bytes 393224 | tf_op jit(solution)/shard_map/ppermute | solution.py:284
  11.8 3.8 %collective-permute-start.2 = (s16[512,128]{1,0:T(8,128)(2,1)S(1)}, s16[512,128]{1,0:T(8,128)(2,1)S(1)}, u32[]{:S(2)}, u32[]{:S(2)}) collective-permute-start(s16[512,128]{1,0:T(8,128)(2,1)S(1)} %add_select_fusion.refs_5_), channel_id=1, source_target_pairs={{0,14},{1,15},{2,0},{3,1},{4,2},{5,3},{6,4},{7,5},{8,6},{9,7},{10,... | collective-permute-start | bytes 393224 | tf_op jit(solution)/shard_map/ppermute | solution.py:284
  15.6 3.3 %collective-permute-done.1.refs_7_ = s16[512,128]{1,0:T(8,128)(2,1)S(1)} collective-permute-done((s16[512,128]{1,0:T(8,128)(2,1)S(1)}, s16[512,128]{1,0:T(8,128)(2,1)S(1)}, u32[]{:S(2)}, u32[]{:S(2)}) %collective-permute-start.1) | collective-permute-done | bytes 131104 | tf_op jit(solution)/shard_map/ppermute | solution.py:284
  19.1 2.7 %collective-permute-start.10 = (s16[640,128]{1,0:T(8,128)(2,1)S(1)}, s16[640,128]{1,0:T(8,128)(2,1)S(1)}, u32[]{:S(2)}, u32[]{:S(2)}) collective-permute-start(s16[640,128]{1,0:T(8,128)(2,1)S(1)} %pad_add_fusion.1.refs_6_), channel_id=1, source_target_pairs={{0,14},{1,15},{2,0},{3,1},{4,2},{5,3},{6,4},{7,5},{8,6},{9,7},{10,... | collective-permute-start | bytes 491528 | tf_op jit(solution)/shard_map/ppermute | solution.py:284
  21.8 3.0 %collective-permute-done.5.refs_9_ = s16[640,128]{1,0:T(8,128)(2,1)S(1)} collective-permute-done((s16[640,128]{1,0:T(8,128)(2,1)S(1)}, s16[640,128]{1,0:T(8,128)(2,1)S(1)}, u32[]{:S(2)}, u32[]{:S(2)}) %collective-permute-start.5) | collective-permute-done | bytes 163872 | tf_op jit(solution)/shard_map/ppermute | solution.py:284
  25.4 2.1 %collective-permute-start.13 = (s16[640,128]{1,0:T(8,128)(2,1)S(1)}, s16[640,128]{1,0:T(8,128)(2,1)S(1)}, u32[]{:S(2)}, u32[]{:S(2)}) collective-permute-start(s16[640,128]{1,0:T(8,128)(2,1)S(1)} %collective-permute-done.10.refs_10_), channel_id=1, source_target_pairs={{0,14},{1,15},{2,0},{3,1},{4,2},{5,3},{6,4},{7,5},{8,6},{9,7},{10,... | collective-permute-start | bytes 491528 | tf_op jit(solution)/shard_map/ppermute | solution.py:284
  27.5 2.7 %collective-permute-done.6.refs_13_ = s16[640,128]{1,0:T(8,128)(2,1)S(1)} collective-permute-done((s16[640,128]{1,0:T(8,128)(2,1)S(1)}, s16[640,128]{1,0:T(8,128)(2,1)S(1)}, u32[]{:S(2)}, u32[]{:S(2)}) %collective-permute-start.6) | collective-permute-done | bytes 163872 | tf_op jit(solution)/shard_map/ppermute | solution.py:284
  30.2 2.7 %collective-permute-start.12 = (s16[512,128]{1,0:T(8,128)(2,1)S(1)}, s16[512,128]{1,0:T(8,128)(2,1)S(1)}, u32[]{:S(2)}, u32[]{:S(2)}) collective-permute-start(s16[512,128]{1,0:T(8,128)(2,1)S(1)} %collective-permute-done.2.refs_8_), channel_id=1, source_target_pairs={{0,14},{1,15},{2,0},{3,1},{4,2},{5,3},{6,4},{7,5},{8,6},{9,7},{10,... | collective-permute-start | bytes 393224 | tf_op jit(solution)/shard_map/ppermute | solution.py:284
  32.9 2.8 %collective-permute-done.12.refs_12_ = s16[512,128]{1,0:T(8,128)(2,1)S(1)} collective-permute-done((s16[512,128]{1,0:T(8,128)(2,1)S(1)}, s16[512,128]{1,0:T(8,128)(2,1)S(1)}, u32[]{:S(2)}, u32[]{:S(2)}) %collective-permute-start.12) | collective-permute-done | bytes 131104 | tf_op jit(solution)/shard_map/ppermute | solution.py:284
  35.7 2.2 %collective-permute-start.15 = (s16[512,128]{1,0:T(8,128)(2,1)S(1)}, s16[512,128]{1,0:T(8,128)(2,1)S(1)}, u32[]{:S(2)}, u32[]{:S(2)}) collective-permute-start(s16[512,128]{1,0:T(8,128)(2,1)S(1)} %collective-permute-done.12.refs_12_), channel_id=1, source_target_pairs={{0,14},{1,15},{2,0},{3,1},{4,2},{5,3},{6,4},{7,5},{8,6},{9,7},{10,... | collective-permute-start | bytes 393224 | tf_op jit(solution)/shard_map/ppermute | solution.py:284
  37.9 2.7 %collective-permute-start.16 = (s16[640,128]{1,0:T(8,128)(2,1)S(1)}, s16[640,128]{1,0:T(8,128)(2,1)S(1)}, u32[]{:S(2)}, u32[]{:S(2)}) collective-permute-start(s16[640,128]{1,0:T(8,128)(2,1)S(1)} %collective-permute-done.13.refs_14_), channel_id=1, source_target_pairs={{0,14},{1,15},{2,0},{3,1},{4,2},{5,3},{6,4},{7,5},{8,6},{9,7},{10,... | collective-permute-start | bytes 491528 | tf_op jit(solution)/shard_map/ppermute | solution.py:284
  41.0 0.7 fusion.12
  44.4 1.6 %collective-permute-start.18 = (s16[640,128]{1,0:T(8,128)(2,1)S(1)}, s16[640,128]{1,0:T(8,128)(2,1)S(1)}, u32[]{:S(2)}, u32[]{:S(2)}) collective-permute-start(s16[640,128]{1,0:T(8,128)(2,1)S(1)} %collective-permute-done.16.refs_18_), channel_id=1, source_target_pairs={{0,14},{1,15},{2,0},{3,1},{4,2},{5,3},{6,4},{7,5},{8,6},{9,7},{10,... | collective-permute-start | bytes 491528 | tf_op jit(solution)/shard_map/ppermute | solution.py:284
  46.2 8.5 %collective-permute-start.8 = (s32[4,128]{1,0:T(4,128)S(1)}, s32[4,128]{1,0:T(4,128)S(1)}, u32[]{:S(2)}, u32[]{:S(2)}) collective-permute-start(s32[4,128]{1,0:T(4,128)S(1)} %add_add_fusion.2.refs_0_), channel_id=1, source_target_pairs={{0,1},{1,0},{2,3},{3,2},{4,5},{5,4},{6,7},{7,6},{8,9},{9,8},{10,11... | collective-permute-start | bytes 6152 | tf_op jit(solution)/shard_map/ppermute | solution.py:284
  54.9 0.7 collective-permute-done.8.refs_1_
  55.6 0.6 copy-done.6
  56.2 8.0 %first_products.1 = (s16[8,528,128]{2,1,0:T(8,128)(2,1)}, f32[512,128]{1,0:T(8,128)S(1)}) custom-call(s32[4,128]{1,0:T(4,128)S(1)} %add_add_fusion.2.refs_0_, s32[4,128]{1,0:T(4,128)S(1)} %collective-permute-done.8.refs_1_, s32[16]{0:T(128)S(1)} %stack.97.refs_2_, bf16[96,128,128]{2,1,0:T(8,128)(2,1)} %refs_3_.3, ...), custom_call_target="tpu_custom_call" | custom-call | tf_op jit(solution)/shard_map/first_products/pallas_call | solution.py:403
  64.2 4.5 %all-to-all-start = ((s16[8,528,128]{2,1,0:T(8,128)(2,1)}), s16[8,528,128]{2,1,0:T(8,128)(2,1)S(1)}, u32[]{:S(2)}, u32[]{:S(2)}) async-start(s16[8,528,128]{2,1,0:T(8,128)(2,1)} %get-tuple-element.25), calls=%async_computation | async-start | bytes 2162688 | tf_op jit(solution)/shard_map/all_to_all | solution.py:445
  68.7 0.9 constant_dynamic-slice_fusion.2
  69.6 1.2 copy.9
  70.8 6.0 %seed_counts.1.refs_1_ = f32[512,128]{1,0:T(8,128)S(1)} custom-call(s32[1]{0:T(128)} %bitcast.20.first_ref, s32[1024,128]{1,0:T(8,128)S(1)} %bitcast.25), custom_call_target="tpu_custom_call" | custom-call | tf_op jit(solution)/shard_map/seed_counts/pallas_call | solution.py:377
  76.8 6.4 %all-to-all-done.refs_0_ = s16[8,528,128]{2,1,0:T(8,128)(2,1)S(1)} async-done(((s16[8,528,128]{2,1,0:T(8,128)(2,1)}), s16[8,528,128]{2,1,0:T(8,128)(2,1)S(1)}, u32[]{:S(2)}, u32[]{:S(2)}) %all-to-all-start) | async-done | bytes 1081376 | tf_op jit(solution)/shard_map/all_to_all | solution.py:445
  83.6 1.7 %collective-permute-start.19 = (bf16[512,128]{1,0:T(8,128)(2,1)S(1)}, bf16[512,128]{1,0:T(8,128)(2,1)S(1)}, u32[]{:S(2)}, u32[]{:S(2)}) collective-permute-start(bf16[512,128]{1,0:T(8,128)(2,1)S(1)} %current.2.refs_5_), channel_id=1, source_target_pairs={{0,16},{1,17},{2,18},{3,19},{4,20},{5,21},{6,22},{7,23},{8,24},{9,... | collective-permute-start | bytes 393224 | tf_op jit(solution)/shard_map/ppermute | solution.py:284
  85.3 3.7 %collective-permute-done.19.refs_6_ = bf16[512,128]{1,0:T(8,128)(2,1)S(1)} collective-permute-done((bf16[512,128]{1,0:T(8,128)(2,1)S(1)}, bf16[512,128]{1,0:T(8,128)(2,1)S(1)}, u32[]{:S(2)}, u32[]{:S(2)}) %collective-permute-start.19) | collective-permute-done | bytes 131104 | tf_op jit(solution)/shard_map/ppermute | solution.py:284
  89.0 1.5 %collective-permute-start.22 = (bf16[512,128]{1,0:T(8,128)(2,1)S(1)}, bf16[512,128]{1,0:T(8,128)(2,1)S(1)}, u32[]{:S(2)}, u32[]{:S(2)}) collective-permute-start(bf16[512,128]{1,0:T(8,128)(2,1)S(1)} %collective-permute-done.19.refs_6_), channel_id=1, source_target_pairs={{0,2},{1,3},{2,4},{3,5},{4,6},{5,7},{6,8},{7,9},{8,10},{9,11},{10,... | collective-permute-start | bytes 393224 | tf_op jit(solution)/shard_map/ppermute | solution.py:284
  90.5 1.4 collective-permute-start.24
  91.9 1.2 collective-permute-done.23.refs_10_
  93.1 0.9 collective-permute-start.27
  94.5 0.9 collective-permute-start.25
  96.3 2.3 %collective-permute-done.27.refs_14_ = bf16[512,128]{1,0:T(8,128)(2,1)S(1)} collective-permute-done((bf16[512,128]{1,0:T(8,128)(2,1)S(1)}, bf16[512,128]{1,0:T(8,128)(2,1)S(1)}, u32[]{:S(2)}, u32[]{:S(2)}) %collective-permute-start.27) | collective-permute-done | bytes 131104 | tf_op jit(solution)/shard_map/ppermute | solution.py:284
  98.6 2.1 %collective-permute-start.31 = (bf16[512,128]{1,0:T(8,128)(2,1)S(1)}, bf16[512,128]{1,0:T(8,128)(2,1)S(1)}, u32[]{:S(2)}, u32[]{:S(2)}) collective-permute-start(bf16[512,128]{1,0:T(8,128)(2,1)S(1)} %collective-permute-done.27.refs_14_), channel_id=1, source_target_pairs={{0,14},{1,15},{2,0},{3,1},{4,2},{5,3},{6,4},{7,5},{8,6},{9,7},{10,... | collective-permute-start | bytes 393224 | tf_op jit(solution)/shard_map/ppermute | solution.py:284
  100.8 0.6 collective-permute-done.25.refs_12_
  101.4 0.9 collective-permute-start.29
  102.3 0.6 collective-permute-start.30
  103.4 2.6 %collective-permute-start.33 = (bf16[512,128]{1,0:T(8,128)(2,1)S(1)}, bf16[512,128]{1,0:T(8,128)(2,1)S(1)}, u32[]{:S(2)}, u32[]{:S(2)}) collective-permute-start(bf16[512,128]{1,0:T(8,128)(2,1)S(1)} %collective-permute-done.31.refs_18_), channel_id=1, source_target_pairs={{0,14},{1,15},{2,0},{3,1},{4,2},{5,3},{6,4},{7,5},{8,6},{9,7},{10,... | collective-permute-start | bytes 393224 | tf_op jit(solution)/shard_map/ppermute | solution.py:284
  106.3 2.3 %collective-permute-done.30.refs_17_ = bf16[512,128]{1,0:T(8,128)(2,1)S(1)} collective-permute-done((bf16[512,128]{1,0:T(8,128)(2,1)S(1)}, bf16[512,128]{1,0:T(8,128)(2,1)S(1)}, u32[]{:S(2)}, u32[]{:S(2)}) %collective-permute-start.30) | collective-permute-done | bytes 131104 | tf_op jit(solution)/shard_map/ppermute | solution.py:284
  108.7 2.8 %collective-permute-done.32.refs_19_ = bf16[512,128]{1,0:T(8,128)(2,1)S(1)} collective-permute-done((bf16[512,128]{1,0:T(8,128)(2,1)S(1)}, bf16[512,128]{1,0:T(8,128)(2,1)S(1)}, u32[]{:S(2)}, u32[]{:S(2)}) %collective-permute-start.32) | collective-permute-done | bytes 131104 | tf_op jit(solution)/shard_map/ppermute | solution.py:284
  111.5 7.1 %later_products.1 = s16[8,528,128]{2,1,0:T(8,128)(2,1)} custom-call(s32[4,128]{1,0:T(4,128)S(1)} %add_add_fusion.2.refs_0_, s32[4,128]{1,0:T(4,128)S(1)} %collective-permute-done.8.refs_1_, s32[16]{0:T(128)S(1)} %stack.97.refs_2_, bf16[96,128,128]{2,1,0:T(8,128)(2,1)} %refs_3_.3, bf16[96,128,128]{2,1,0:T(8,128)(2,1)} %collective-permute-done.9.refs_4_, ...), custom_call_target="tpu_custom_call" | custom-call | tf_op jit(solution)/shard_map/later_products/pallas_call | solution.py:421
  118.6 3.7 %all-to-all-start.1 = ((s16[8,528,128]{2,1,0:T(8,128)(2,1)}), s16[8,528,128]{2,1,0:T(8,128)(2,1)S(1)}, u32[]{:S(2)}, u32[]{:S(2)}) async-start(s16[8,528,128]{2,1,0:T(8,128)(2,1)} %later_products.1), calls=%async_computation.1 | async-start | bytes 2162688 | tf_op jit(solution)/shard_map/all_to_all | solution.py:449
  122.4 10.4 %all-to-all-done.1.refs_0_ = s16[8,528,128]{2,1,0:T(8,128)(2,1)S(1)} async-done(((s16[8,528,128]{2,1,0:T(8,128)(2,1)}), s16[8,528,128]{2,1,0:T(8,128)(2,1)S(1)}, u32[]{:S(2)}, u32[]{:S(2)}) %all-to-all-start.1) | async-done | bytes 1081376 | tf_op jit(solution)/shard_map/all_to_all | solution.py:449
  133.2 8.5 %collective-permute-start.34 = (f32[256,128]{1,0:T(8,128)S(1)}, f32[256,128]{1,0:T(8,128)S(1)}, u32[]{:S(2)}, u32[]{:S(2)}) collective-permute-start(f32[256,128]{1,0:T(8,128)S(1)} %get-tuple-element.35), channel_id=1, source_target_pairs={{0,1},{1,0},{2,3},{3,2},{4,5},{5,4},{6,7},{7,6},{8,9},{9,8},{10,11... | collective-permute-start | bytes 393224 | tf_op jit(solution)/shard_map/ppermute | solution.py:284
  141.8 1.0 collective-permute-done.34
  142.7 0.7 maximum_select_fusion
  (83 shorter events, 5.8 us)
Async XLA Ops:
  0.0 68.7 %copy-start = (s32[256,1024]{1,0:T(8,128)S(1)}, s32[256,1024]{1,0:T(8,128)}, u32[]{:S(2)}) copy-start(s32[256,1024]{1,0:T(8,128)} %param.11) | copy-start | bytes 3145732
  0.0 55.6 %collective-permute-start.9 = (bf16[96,128,128]{2,1,0:T(8,128)(2,1)}, bf16[96,128,128]{2,1,0:T(8,128)(2,1)}, u32[]{:S(2)}, u32[]{:S(2)}) collective-permute-start(bf16[96,128,128]{2,1,0:T(8,128)(2,1)} %refs_3_.3), channel_id=1, source_target_pairs={{0,1},{1,0},{2,3},{3,2},{4,5},{5,4},{6,7},{7,6},{8,9},{9,8},{10,11... | collective-permute-start | bytes 9437192 | tf_op jit(solution)/shard_map/ppermute | solution.py:284
  3.9 0.7 copy-start.1
  4.6 2.6 %copy-start.3 = (f32[256,256]{1,0:T(8,128)S(1)}, f32[256,256]{1,0:T(8,128)}, u32[]{:S(2)}) copy-start(f32[256,256]{1,0:T(8,128)} %param.6) | copy-start | bytes 786436
  7.0 1.6 %collective-permute-start.3 = (f32[64,128]{1,0:T(8,128)S(1)}, f32[64,128]{1,0:T(8,128)S(1)}, u32[]{:S(2)}, u32[]{:S(2)}) collective-permute-start(f32[64,128]{1,0:T(8,128)S(1)} %column_sums.1), channel_id=1, source_target_pairs={{0,1},{1,0},{2,3},{3,2},{4,5},{5,4},{6,7},{7,6},{8,9},{9,8},{10,11... | collective-permute-start | bytes 98312 | tf_op jit(solution)/shard_map/ppermute | solution.py:284
  7.3 33.3 %copy-start.2 = (s32[96]{0:T(128)S(1)}, s32[96]{0:T(128)}, u32[]{:S(2)}) copy-start(s32[96]{0:T(128)} %source_ref.1) | copy-start | bytes 1156
  7.3 33.3 %copy-start.10 = (s32[96]{0:T(128)S(1)}, s32[96]{0:T(128)}, u32[]{:S(2)}) copy-start(s32[96]{0:T(128)} %param.8) | copy-start | bytes 1156
  7.3 1.4 collective-permute-start
  8.8 10.1 %collective-permute-start.4 = (s16[640,128]{1,0:T(8,128)(2,1)S(1)}, s16[640,128]{1,0:T(8,128)(2,1)S(1)}, u32[]{:S(2)}, u32[]{:S(2)}) collective-permute-start(s16[640,128]{1,0:T(8,128)(2,1)S(1)} %pad_add_fusion), channel_id=1, source_target_pairs={{0,16},{1,17},{2,18},{3,19},{4,20},{5,21},{6,22},{7,23},{8,24},{9,... | collective-permute-start | bytes 491528 | tf_op jit(solution)/shard_map/ppermute | solution.py:284
  10.2 8.7 %collective-permute-start.1 = (s16[512,128]{1,0:T(8,128)(2,1)S(1)}, s16[512,128]{1,0:T(8,128)(2,1)S(1)}, u32[]{:S(2)}, u32[]{:S(2)}) collective-permute-start(s16[512,128]{1,0:T(8,128)(2,1)S(1)} %add_select_fusion.refs_5_), channel_id=1, source_target_pairs={{0,2},{1,3},{2,4},{3,5},{4,6},{5,7},{6,8},{7,9},{8,10},{9,11},{10,... | collective-permute-start | bytes 393224 | tf_op jit(solution)/shard_map/ppermute | solution.py:284
  11.8 7.1 %collective-permute-start.2 = (s16[512,128]{1,0:T(8,128)(2,1)S(1)}, s16[512,128]{1,0:T(8,128)(2,1)S(1)}, u32[]{:S(2)}, u32[]{:S(2)}) collective-permute-start(s16[512,128]{1,0:T(8,128)(2,1)S(1)} %add_select_fusion.refs_5_), channel_id=1, source_target_pairs={{0,14},{1,15},{2,0},{3,1},{4,2},{5,3},{6,4},{7,5},{8,6},{9,7},{10,... | collective-permute-start | bytes 393224 | tf_op jit(solution)/shard_map/ppermute | solution.py:284
  19.0 5.8 %collective-permute-start.5 = (s16[640,128]{1,0:T(8,128)(2,1)S(1)}, s16[640,128]{1,0:T(8,128)(2,1)S(1)}, u32[]{:S(2)}, u32[]{:S(2)}) collective-permute-start(s16[640,128]{1,0:T(8,128)(2,1)S(1)} %pad_add_fusion.1.refs_6_), channel_id=1, source_target_pairs={{0,2},{1,3},{2,4},{3,5},{4,6},{5,7},{6,8},{7,9},{8,10},{9,11},{10,... | collective-permute-start | bytes 491528 | tf_op jit(solution)/shard_map/ppermute | solution.py:284
  19.1 6.3 %collective-permute-start.10 = (s16[640,128]{1,0:T(8,128)(2,1)S(1)}, s16[640,128]{1,0:T(8,128)(2,1)S(1)}, u32[]{:S(2)}, u32[]{:S(2)}) collective-permute-start(s16[640,128]{1,0:T(8,128)(2,1)S(1)} %pad_add_fusion.1.refs_6_), channel_id=1, source_target_pairs={{0,14},{1,15},{2,0},{3,1},{4,2},{5,3},{6,4},{7,5},{8,6},{9,7},{10,... | collective-permute-start | bytes 491528 | tf_op jit(solution)/shard_map/ppermute | solution.py:284
  24.8 5.4 %collective-permute-start.6 = (s16[640,128]{1,0:T(8,128)(2,1)S(1)}, s16[640,128]{1,0:T(8,128)(2,1)S(1)}, u32[]{:S(2)}, u32[]{:S(2)}) collective-permute-start(s16[640,128]{1,0:T(8,128)(2,1)S(1)} %collective-permute-done.5.refs_9_), channel_id=1, source_target_pairs={{0,2},{1,3},{2,4},{3,5},{4,6},{5,7},{6,8},{7,9},{8,10},{9,11},{10,... | collective-permute-start | bytes 491528 | tf_op jit(solution)/shard_map/ppermute | solution.py:284
  24.8 8.1 %collective-permute-start.11 = (s16[512,128]{1,0:T(8,128)(2,1)S(1)}, s16[512,128]{1,0:T(8,128)(2,1)S(1)}, u32[]{:S(2)}, u32[]{:S(2)}) collective-permute-start(s16[512,128]{1,0:T(8,128)(2,1)S(1)} %collective-permute-done.1.refs_7_), channel_id=1, source_target_pairs={{0,2},{1,3},{2,4},{3,5},{4,6},{5,7},{6,8},{7,9},{8,10},{9,11},{10,... | collective-permute-start | bytes 393224 | tf_op jit(solution)/shard_map/ppermute | solution.py:284
  25.4 12.5 %collective-permute-start.13 = (s16[640,128]{1,0:T(8,128)(2,1)S(1)}, s16[640,128]{1,0:T(8,128)(2,1)S(1)}, u32[]{:S(2)}, u32[]{:S(2)}) collective-permute-start(s16[640,128]{1,0:T(8,128)(2,1)S(1)} %collective-permute-done.10.refs_10_), channel_id=1, source_target_pairs={{0,14},{1,15},{2,0},{3,1},{4,2},{5,3},{6,4},{7,5},{8,6},{9,7},{10,... | collective-permute-start | bytes 491528 | tf_op jit(solution)/shard_map/ppermute | solution.py:284
  30.2 10.4 %collective-permute-start.7 = (s16[640,128]{1,0:T(8,128)(2,1)S(1)}, s16[640,128]{1,0:T(8,128)(2,1)S(1)}, u32[]{:S(2)}, u32[]{:S(2)}) collective-permute-start(s16[640,128]{1,0:T(8,128)(2,1)S(1)} %collective-permute-done.6.refs_13_), channel_id=1, source_target_pairs={{0,2},{1,3},{2,4},{3,5},{4,6},{5,7},{6,8},{7,9},{8,10},{9,11},{10,... | collective-permute-start | bytes 491528 | tf_op jit(solution)/shard_map/ppermute | solution.py:284
  30.2 5.5 %collective-permute-start.12 = (s16[512,128]{1,0:T(8,128)(2,1)S(1)}, s16[512,128]{1,0:T(8,128)(2,1)S(1)}, u32[]{:S(2)}, u32[]{:S(2)}) collective-permute-start(s16[512,128]{1,0:T(8,128)(2,1)S(1)} %collective-permute-done.2.refs_8_), channel_id=1, source_target_pairs={{0,14},{1,15},{2,0},{3,1},{4,2},{5,3},{6,4},{7,5},{8,6},{9,7},{10,... | collective-permute-start | bytes 393224 | tf_op jit(solution)/shard_map/ppermute | solution.py:284
  32.9 5.0 %collective-permute-start.14 = (s16[512,128]{1,0:T(8,128)(2,1)S(1)}, s16[512,128]{1,0:T(8,128)(2,1)S(1)}, u32[]{:S(2)}, u32[]{:S(2)}) collective-permute-start(s16[512,128]{1,0:T(8,128)(2,1)S(1)} %collective-permute-done.11.refs_11_), channel_id=1, source_target_pairs={{0,2},{1,3},{2,4},{3,5},{4,6},{5,7},{6,8},{7,9},{8,10},{9,11},{10,... | collective-permute-start | bytes 393224 | tf_op jit(solution)/shard_map/ppermute | solution.py:284
  35.7 19.1 %collective-permute-start.15 = (s16[512,128]{1,0:T(8,128)(2,1)S(1)}, s16[512,128]{1,0:T(8,128)(2,1)S(1)}, u32[]{:S(2)}, u32[]{:S(2)}) collective-permute-start(s16[512,128]{1,0:T(8,128)(2,1)S(1)} %collective-permute-done.12.refs_12_), channel_id=1, source_target_pairs={{0,14},{1,15},{2,0},{3,1},{4,2},{5,3},{6,4},{7,5},{8,6},{9,7},{10,... | collective-permute-start | bytes 393224 | tf_op jit(solution)/shard_map/ppermute | solution.py:284
  37.9 17.6 %copy-start.7 = (s16[512,128]{1,0:T(8,128)(2,1)}, s16[512,128]{1,0:T(8,128)(2,1)S(1)}, u32[]{:S(2)}) copy-start(s16[512,128]{1,0:T(8,128)(2,1)S(1)} %collective-permute-done.14.refs_15_) | copy-start | bytes 393220
  37.9 16.9 %collective-permute-start.17 = (s16[512,128]{1,0:T(8,128)(2,1)S(1)}, s16[512,128]{1,0:T(8,128)(2,1)S(1)}, u32[]{:S(2)}, u32[]{:S(2)}) collective-permute-start(s16[512,128]{1,0:T(8,128)(2,1)S(1)} %collective-permute-done.14.refs_15_), channel_id=1, source_target_pairs={{0,2},{1,3},{2,4},{3,5},{4,6},{5,7},{6,8},{7,9},{8,10},{9,11},{10,... | collective-permute-start | bytes 393224 | tf_op jit(solution)/shard_map/ppermute | solution.py:284
  37.9 6.4 %collective-permute-start.16 = (s16[640,128]{1,0:T(8,128)(2,1)S(1)}, s16[640,128]{1,0:T(8,128)(2,1)S(1)}, u32[]{:S(2)}, u32[]{:S(2)}) collective-permute-start(s16[640,128]{1,0:T(8,128)(2,1)S(1)} %collective-permute-done.13.refs_14_), channel_id=1, source_target_pairs={{0,14},{1,15},{2,0},{3,1},{4,2},{5,3},{6,4},{7,5},{8,6},{9,7},{10,... | collective-permute-start | bytes 491528 | tf_op jit(solution)/shard_map/ppermute | solution.py:284
  40.6 14.9 %copy-start.4 = (s16[640,128]{1,0:T(8,128)(2,1)}, s16[640,128]{1,0:T(8,128)(2,1)S(1)}, u32[]{:S(2)}) copy-start(s16[640,128]{1,0:T(8,128)(2,1)S(1)} %collective-permute-done.7.refs_17_) | copy-start | bytes 491524
  44.4 11.2 %copy-start.5 = (s16[640,128]{1,0:T(8,128)(2,1)}, s16[640,128]{1,0:T(8,128)(2,1)S(1)}, u32[]{:S(2)}) copy-start(s16[640,128]{1,0:T(8,128)(2,1)S(1)} %collective-permute-done.16.refs_18_) | copy-start | bytes 491524
  44.4 11.2 %collective-permute-start.18 = (s16[640,128]{1,0:T(8,128)(2,1)S(1)}, s16[640,128]{1,0:T(8,128)(2,1)S(1)}, u32[]{:S(2)}, u32[]{:S(2)}) collective-permute-start(s16[640,128]{1,0:T(8,128)(2,1)S(1)} %collective-permute-done.16.refs_18_), channel_id=1, source_target_pairs={{0,14},{1,15},{2,0},{3,1},{4,2},{5,3},{6,4},{7,5},{8,6},{9,7},{10,... | collective-permute-start | bytes 491528 | tf_op jit(solution)/shard_map/ppermute | solution.py:284
  46.2 9.3 %collective-permute-start.8 = (s32[4,128]{1,0:T(4,128)S(1)}, s32[4,128]{1,0:T(4,128)S(1)}, u32[]{:S(2)}, u32[]{:S(2)}) collective-permute-start(s32[4,128]{1,0:T(4,128)S(1)} %add_add_fusion.2.refs_0_), channel_id=1, source_target_pairs={{0,1},{1,0},{2,3},{3,2},{4,5},{5,4},{6,7},{7,6},{8,9},{9,8},{10,11... | collective-permute-start | bytes 6152 | tf_op jit(solution)/shard_map/ppermute | solution.py:284
  54.8 0.8 copy-start.8
  54.9 0.7 copy-start.9
  55.6 0.7 copy-start.6
  64.2 19.0 %all-to-all-start = ((s16[8,528,128]{2,1,0:T(8,128)(2,1)}), s16[8,528,128]{2,1,0:T(8,128)(2,1)S(1)}, u32[]{:S(2)}, u32[]{:S(2)}) async-start(s16[8,528,128]{2,1,0:T(8,128)(2,1)} %get-tuple-element.25), calls=%async_computation | async-start | bytes 2162688 | tf_op jit(solution)/shard_map/all_to_all | solution.py:445
  83.6 5.4 %collective-permute-start.19 = (bf16[512,128]{1,0:T(8,128)(2,1)S(1)}, bf16[512,128]{1,0:T(8,128)(2,1)S(1)}, u32[]{:S(2)}, u32[]{:S(2)}) collective-permute-start(bf16[512,128]{1,0:T(8,128)(2,1)S(1)} %current.2.refs_5_), channel_id=1, source_target_pairs={{0,16},{1,17},{2,18},{3,19},{4,20},{5,21},{6,22},{7,23},{8,24},{9,... | collective-permute-start | bytes 393224 | tf_op jit(solution)/shard_map/ppermute | solution.py:284
  85.3 5.2 %collective-permute-start.20 = (bf16[512,128]{1,0:T(8,128)(2,1)S(1)}, bf16[512,128]{1,0:T(8,128)(2,1)S(1)}, u32[]{:S(2)}, u32[]{:S(2)}) collective-permute-start(bf16[512,128]{1,0:T(8,128)(2,1)S(1)} %current.2.refs_5_), channel_id=1, source_target_pairs={{0,2},{1,3},{2,4},{3,5},{4,6},{5,7},{6,8},{7,9},{8,10},{9,11},{10,... | collective-permute-start | bytes 393224 | tf_op jit(solution)/shard_map/ppermute | solution.py:284
  89.0 4.1 %collective-permute-start.23 = (bf16[512,128]{1,0:T(8,128)(2,1)S(1)}, bf16[512,128]{1,0:T(8,128)(2,1)S(1)}, u32[]{:S(2)}, u32[]{:S(2)}) collective-permute-start(bf16[512,128]{1,0:T(8,128)(2,1)S(1)} %collective-permute-done.19.refs_6_), channel_id=1, source_target_pairs={{0,14},{1,15},{2,0},{3,1},{4,2},{5,3},{6,4},{7,5},{8,6},{9,7},{10,... | collective-permute-start | bytes 393224 | tf_op jit(solution)/shard_map/ppermute | solution.py:284
  89.0 5.5 %collective-permute-start.21 = (bf16[512,128]{1,0:T(8,128)(2,1)S(1)}, bf16[512,128]{1,0:T(8,128)(2,1)S(1)}, u32[]{:S(2)}, u32[]{:S(2)}) collective-permute-start(bf16[512,128]{1,0:T(8,128)(2,1)S(1)} %current.2.refs_5_), channel_id=1, source_target_pairs={{0,14},{1,15},{2,0},{3,1},{4,2},{5,3},{6,4},{7,5},{8,6},{9,7},{10,... | collective-permute-start | bytes 393224 | tf_op jit(solution)/shard_map/ppermute | solution.py:284
  89.0 6.4 %collective-permute-start.22 = (bf16[512,128]{1,0:T(8,128)(2,1)S(1)}, bf16[512,128]{1,0:T(8,128)(2,1)S(1)}, u32[]{:S(2)}, u32[]{:S(2)}) collective-permute-start(bf16[512,128]{1,0:T(8,128)(2,1)S(1)} %collective-permute-done.19.refs_6_), channel_id=1, source_target_pairs={{0,2},{1,3},{2,4},{3,5},{4,6},{5,7},{6,8},{7,9},{8,10},{9,11},{10,... | collective-permute-start | bytes 393224 | tf_op jit(solution)/shard_map/ppermute | solution.py:284
  90.5 5.8 %collective-permute-start.24 = (bf16[512,128]{1,0:T(8,128)(2,1)S(1)}, bf16[512,128]{1,0:T(8,128)(2,1)S(1)}, u32[]{:S(2)}, u32[]{:S(2)}) collective-permute-start(bf16[512,128]{1,0:T(8,128)(2,1)S(1)} %collective-permute-done.20.refs_7_), channel_id=1, source_target_pairs={{0,2},{1,3},{2,4},{3,5},{4,6},{5,7},{6,8},{7,9},{8,10},{9,11},{10,... | collective-permute-start | bytes 393224 | tf_op jit(solution)/shard_map/ppermute | solution.py:284
  93.1 5.5 %collective-permute-start.27 = (bf16[512,128]{1,0:T(8,128)(2,1)S(1)}, bf16[512,128]{1,0:T(8,128)(2,1)S(1)}, u32[]{:S(2)}, u32[]{:S(2)}) collective-permute-start(bf16[512,128]{1,0:T(8,128)(2,1)S(1)} %collective-permute-done.23.refs_10_), channel_id=1, source_target_pairs={{0,14},{1,15},{2,0},{3,1},{4,2},{5,3},{6,4},{7,5},{8,6},{9,7},{10,... | collective-permute-start | bytes 393224 | tf_op jit(solution)/shard_map/ppermute | solution.py:284
  94.5 6.9 %collective-permute-start.25 = (bf16[512,128]{1,0:T(8,128)(2,1)S(1)}, bf16[512,128]{1,0:T(8,128)(2,1)S(1)}, u32[]{:S(2)}, u32[]{:S(2)}) collective-permute-start(bf16[512,128]{1,0:T(8,128)(2,1)S(1)} %collective-permute-done.21.refs_8_), channel_id=1, source_target_pairs={{0,14},{1,15},{2,0},{3,1},{4,2},{5,3},{6,4},{7,5},{8,6},{9,7},{10,... | collective-permute-start | bytes 393224 | tf_op jit(solution)/shard_map/ppermute | solution.py:284
  95.4 6.8 %collective-permute-start.26 = (bf16[512,128]{1,0:T(8,128)(2,1)S(1)}, bf16[512,128]{1,0:T(8,128)(2,1)S(1)}, u32[]{:S(2)}, u32[]{:S(2)}) collective-permute-start(bf16[512,128]{1,0:T(8,128)(2,1)S(1)} %collective-permute-done.22.refs_9_), channel_id=1, source_target_pairs={{0,2},{1,3},{2,4},{3,5},{4,6},{5,7},{6,8},{7,9},{8,10},{9,11},{10,... | collective-permute-start | bytes 393224 | tf_op jit(solution)/shard_map/ppermute | solution.py:284
  96.3 7.0 %collective-permute-start.28 = (bf16[512,128]{1,0:T(8,128)(2,1)S(1)}, bf16[512,128]{1,0:T(8,128)(2,1)S(1)}, u32[]{:S(2)}, u32[]{:S(2)}) collective-permute-start(bf16[512,128]{1,0:T(8,128)(2,1)S(1)} %collective-permute-done.24.refs_11_), channel_id=1, source_target_pairs={{0,2},{1,3},{2,4},{3,5},{4,6},{5,7},{6,8},{7,9},{8,10},{9,11},{10,... | collective-permute-start | bytes 393224 | tf_op jit(solution)/shard_map/ppermute | solution.py:284
  98.6 4.8 %collective-permute-start.31 = (bf16[512,128]{1,0:T(8,128)(2,1)S(1)}, bf16[512,128]{1,0:T(8,128)(2,1)S(1)}, u32[]{:S(2)}, u32[]{:S(2)}) collective-permute-start(bf16[512,128]{1,0:T(8,128)(2,1)S(1)} %collective-permute-done.27.refs_14_), channel_id=1, source_target_pairs={{0,14},{1,15},{2,0},{3,1},{4,2},{5,3},{6,4},{7,5},{8,6},{9,7},{10,... | collective-permute-start | bytes 393224 | tf_op jit(solution)/shard_map/ppermute | solution.py:284
  101.4 5.0 %collective-permute-start.29 = (bf16[512,128]{1,0:T(8,128)(2,1)S(1)}, bf16[512,128]{1,0:T(8,128)(2,1)S(1)}, u32[]{:S(2)}, u32[]{:S(2)}) collective-permute-start(bf16[512,128]{1,0:T(8,128)(2,1)S(1)} %collective-permute-done.25.refs_12_), channel_id=1, source_target_pairs={{0,14},{1,15},{2,0},{3,1},{4,2},{5,3},{6,4},{7,5},{8,6},{9,7},{10,... | collective-permute-start | bytes 393224 | tf_op jit(solution)/shard_map/ppermute | solution.py:284
  102.3 6.4 %collective-permute-start.30 = (bf16[512,128]{1,0:T(8,128)(2,1)S(1)}, bf16[512,128]{1,0:T(8,128)(2,1)S(1)}, u32[]{:S(2)}, u32[]{:S(2)}) collective-permute-start(bf16[512,128]{1,0:T(8,128)(2,1)S(1)} %collective-permute-done.26.refs_13_), channel_id=1, source_target_pairs={{0,2},{1,3},{2,4},{3,5},{4,6},{5,7},{6,8},{7,9},{8,10},{9,11},{10,... | collective-permute-start | bytes 393224 | tf_op jit(solution)/shard_map/ppermute | solution.py:284
  103.3 8.2 %collective-permute-start.32 = (bf16[512,128]{1,0:T(8,128)(2,1)S(1)}, bf16[512,128]{1,0:T(8,128)(2,1)S(1)}, u32[]{:S(2)}, u32[]{:S(2)}) collective-permute-start(bf16[512,128]{1,0:T(8,128)(2,1)S(1)} %collective-permute-done.28.refs_15_), channel_id=1, source_target_pairs={{0,2},{1,3},{2,4},{3,5},{4,6},{5,7},{6,8},{7,9},{8,10},{9,11},{10,... | collective-permute-start | bytes 393224 | tf_op jit(solution)/shard_map/ppermute | solution.py:284
  103.4 8.0 %collective-permute-start.33 = (bf16[512,128]{1,0:T(8,128)(2,1)S(1)}, bf16[512,128]{1,0:T(8,128)(2,1)S(1)}, u32[]{:S(2)}, u32[]{:S(2)}) collective-permute-start(bf16[512,128]{1,0:T(8,128)(2,1)S(1)} %collective-permute-done.31.refs_18_), channel_id=1, source_target_pairs={{0,14},{1,15},{2,0},{3,1},{4,2},{5,3},{6,4},{7,5},{8,6},{9,7},{10,... | collective-permute-start | bytes 393224 | tf_op jit(solution)/shard_map/ppermute | solution.py:284
  118.6 14.2 %all-to-all-start.1 = ((s16[8,528,128]{2,1,0:T(8,128)(2,1)}), s16[8,528,128]{2,1,0:T(8,128)(2,1)S(1)}, u32[]{:S(2)}, u32[]{:S(2)}) async-start(s16[8,528,128]{2,1,0:T(8,128)(2,1)} %later_products.1), calls=%async_computation.1 | async-start | bytes 2162688 | tf_op jit(solution)/shard_map/all_to_all | solution.py:449
  133.2 9.5 %collective-permute-start.34 = (f32[256,128]{1,0:T(8,128)S(1)}, f32[256,128]{1,0:T(8,128)S(1)}, u32[]{:S(2)}, u32[]{:S(2)}) collective-permute-start(f32[256,128]{1,0:T(8,128)S(1)} %get-tuple-element.35), channel_id=1, source_target_pairs={{0,1},{1,0},{2,3},{3,2},{4,5},{5,4},{6,7},{7,6},{8,9},{9,8},{10,11... | collective-permute-start | bytes 393224 | tf_op jit(solution)/shard_map/ppermute | solution.py:284

commit v7 on v6

--- a/solution.py
+++ b/solution.py
@@ -82,14 +82,6 @@
     return mantissa * jnp.exp2(((upper >> 8) - (127 + 24)).astype(jnp.float32))
 
 
-def column_totals(rows, each, piece_refs):
-    total = jnp.zeros((each, LANES), jnp.float32)
-    for piece_ref in piece_refs:
-        if piece_ref.shape[0] > rows:
-            total += decode(piece_ref[rows : rows + 2 * each, :])
-    return total
-
-
 def seed_kernel(first_ref, ids_ref, counts_ref, pages_ref):
     total, lanes = ids_ref.shape
     pages = counts_ref.shape[0]
@@ -154,7 +146,7 @@
     return copies
 
 
-def products(facts_refs, copies, tiles, panel, total, out_ref):
+def products(facts_refs, copies, tiles, panel, total):
     unroll = 16
     slots = tiles.shape[0] // 2
     dummy = total.shape[0] - 1
@@ -177,6 +169,35 @@
             return carry
 
         lax.fori_loop(0, (pairs + unroll - 1) // unroll, group, 0)
+
+
+def single_products(slot_refs, count_ref, core_ref, copies, tiles, panel, total):
+    unroll = 16
+    slots = tiles.shape[0] // 2
+    dummy = total.shape[0] - 1
+    per = 2 * BT
+    band = panel.shape[0] - 1
+    for which in range(2):
+        copies[which].wait()
+        rows_ref, cols_ref = slot_refs[2 * which : 2 * which + 2]
+        owner = core_ref[0] if which == 0 else 1 - core_ref[0]
+
+        def group(g, carry, which=which, rows_ref=rows_ref, cols_ref=cols_ref, owner=owner):
+            for u in range(unroll):
+                k = g * unroll + u
+                target = rows_ref[k] // band * per + owner * BT + rows_ref[k] % BT
+                target = jnp.where(k < count_ref[which], target, dummy)
+                total[target] += jnp.dot(
+                    tiles[which * slots + k],
+                    panel[cols_ref[k] % band],
+                    preferred_element_type=jnp.float32,
+                )
+            return carry
+
+        lax.fori_loop(0, (count_ref[which] + unroll - 1) // unroll, group, 0)
+
+
+def round_parts(total, out_ref):
     receivers = out_ref.shape[0]
     per = (out_ref.shape[1] - 16) // TILE
 
@@ -198,29 +219,27 @@
     lax.fori_loop(0, receivers, send, 0)
 
 
-def first_kernel(pieces, far, rows, own_facts, sib_facts, chip_ref, own_ref, sib_ref, *refs):
-    piece_refs = list(refs[:pieces])
-    out_ref, inverse_ref, panel, total, tiles, arrived, sums_ref, ordered, brought, near = refs[pieces:]
-    brings = []
-    for i, piece_ref in enumerate(piece_refs[pieces - far :]):
-        inside = brought.at[i, pl.ds(0, piece_ref.shape[0])]
-        brings.append(pltpu.make_async_copy(piece_ref, inside, near.at[i]))
-        brings[i].start()
-        piece_refs[pieces - far + i] = inside
+def first_kernel(pieces, far, *refs):
+    slot_refs, (count_ref, core_ref, chip_ref, sums_ref, own_ref, sib_ref) = refs[:4], refs[4:10]
+    piece_refs = list(refs[10 : 10 + pieces])
+    out_ref, inverse_ref, panel, total, tiles, arrived, ordered, brought, near = refs[10 + pieces :]
+    brings = {}
+    for i in range(far):
+        p = pieces - far + i
+        inside = brought.at[i, pl.ds(0, piece_refs[p].shape[0])]
+        brings[p] = pltpu.make_async_copy(piece_refs[p], inside, near.at[i])
+        brings[p].start()
+        piece_refs[p] = inside
     copies = fetch(own_ref, sib_ref, tiles, arrived)
     total[...] = jnp.zeros_like(total)
     groups, per, _ = sums_ref.shape
-    sums = column_totals(rows, groups * per, piece_refs[: pieces - far])
-    for bring in brings:
-        bring.wait()
-    sums = sums + column_totals(rows, groups * per, piece_refs[pieces - far :])
-    for g in range(groups):
-        sums_ref[g] = sums[g * per : (g + 1) * per]
     ordered[...] = jnp.zeros_like(ordered)
     for p in range(pieces):
         ordered[p * per : (p + 1) * per, :] = sums_ref[chip_ref[p]]
     inverse = (1.0 / jnp.maximum(ordered[...], 1.0)).T
     for p in range(pieces):
+        if p in brings:
+            brings[p].wait()
         for t in range(per):
             column = inverse[:, p * per + t : p * per + t + 1]
             code = piece_refs[p][t * TILE : (t + 1) * TILE, :].astype(jnp.float32)
@@ -228,8 +247,8 @@
             panel[chip_ref[p] * per + t] = (score * column).astype(jnp.bfloat16)
             if p == 0:
                 inverse_ref[t * TILE : (t + 1) * TILE, :] = jnp.broadcast_to(column, (TILE, LANES))
-    panel[pieces * per] = jnp.zeros((TILE, LANES), jnp.bfloat16)
-    products((own_facts, sib_facts), copies, tiles, panel, total, out_ref)
+    single_products(slot_refs, count_ref, core_ref, copies, tiles, panel, total)
+    round_parts(total, out_ref)
 
 
 def later_kernel(pieces, rows, own_facts, sib_facts, chip_ref, own_ref, sib_ref, *refs):
@@ -242,7 +261,8 @@
         for t in range(per):
             panel[chip_ref[p] * per + t] = piece_refs[p][t * TILE : (t + 1) * TILE, :]
     panel[pieces * per] = jnp.zeros((TILE, LANES), jnp.bfloat16)
-    products((own_facts, sib_facts), copies, tiles, panel, total, out_ref)
+    products((own_facts, sib_facts), copies, tiles, panel, total)
+    round_parts(total, out_ref)
 
 
 def current_kernel(scaled, parts_ref, restart_ref, inverse_ref, out_ref):
@@ -294,40 +314,37 @@
 
     tie = lax.optimization_barrier
 
-    def gather(block, sums=None, later=None):
+    def gather(block, sums=None):
         rows = block.shape[0]
-        a, b = along(block, 1), along(block, -1)
-        if sums is None:
-            other = across(block)
-        else:
-            other = across(jnp.concatenate([block, encode(sums)]))
-            a, b, other = tie((a, b, other))
-            sums = sums + decode(other[rows:])
-            other = jnp.concatenate([other[:rows], encode(sums)])
-        pieces, names, beside = [block, other], [(0, 0), (1, 0)], None
-        c, d = other, other
+        other = across(block)
+        if sums is not None:
+            block = jnp.concatenate([block, encode(sums)])
+        pieces, names = [block, other], [(0, 0), (1, 0)]
+        a, b, c, d = block, block, other, other
         for step in range(1, depth // 2):
-            if step > 1:
-                a, b = along(a, 1), along(b, -1)
+            a, b = along(a, 1), along(b, -1)
             c, d = along(c, 1), along(d, -1)
-            if later is not None and step == depth // 2 - 1:
-                c, raw = tie((c, (tile_rows, tile_cols, tile_count)))
-                beside = later(*raw)
             pieces += [a, b, c, d]
             names += [(0, -step), (0, step), (1, -step), (1, step)]
-        pieces += [along(a, 1), along(d, -1)]
+        a = along(a, 1)
+        if sums is not None:
+            plane = [p for p, (y, _) in zip(pieces, names) if y == 0] + [a]
+            found = sum(decode(p[rows:]) for p in plane[1:]) + sums
+            sums = found + across(found)
+        pieces += [a, along(d, -1)]
         names += [(0, depth // 2), (1, depth // 2)]
-        return pieces, names, beside
+        return pieces, names, sums
 
     half = columns // 2
     code = ((scores - LOW) * (STEPS / (HIGH - LOW)) + 0.5).astype(jnp.int32)
     code = (jnp.clip(code, 0, 65535) - 32768).astype(jnp.int16)
-    code, count = tie((code, tile_count))
     mine = lax.dynamic_slice_in_dim(code, core * half, half, 1)
     theirs = sibling(lax.dynamic_slice_in_dim(code, (1 - core) * half, half, 1))
     block = jnp.where(
         core == 0, jnp.concatenate([mine, theirs]), jnp.concatenate([theirs, mine])
     )
+    slots_here = jnp.stack([tile_rows, tile_cols, jnp.broadcast_to(tile_count, (slots,))])
+    slots_there = sibling(slots_here)
     sib_tiles = sibling(tile_values)
     sums = pl.pallas_call(
         column_kernel,
@@ -337,7 +354,7 @@
         scratch_shapes=[VMEM(tile_values.shape, tile_values.dtype), pltpu.SemaphoreType.DMA((4,))],
         compiler_params=params(8),
         name="column_sums",
-    )(tile_cols, count, in_hbm(tile_values))
+    )(tile_cols, tile_count, in_hbm(tile_values))
 
     sums = sums + sibling(sums)
 
@@ -370,7 +387,7 @@
                 jnp.broadcast_to(jnp.sum(filled) // 2, (long,)),
             ]
         )
-        return facts, sibling(facts), sib_tiles
+        return facts
 
     first_page = (row_index * grid_cols + col_index - core) * own_rows
     ids = lax.dynamic_slice_in_dim(seed_ids, core * half, half, 0).T
@@ -384,7 +401,7 @@
         name="seed_counts",
     )(first_page.reshape(1), ids)
 
-    def multiply(pieces, names, coded, facts, sib_facts, sib_tiles):
+    def multiply(pieces, names, sums, facts):
         order = jnp.stack([(high ^ y) * depth + (z + d) % depth for y, d in names])
         n = len(pieces)
         rows = per * TILE
@@ -396,28 +413,32 @@
             pltpu.SemaphoreType.DMA((2,)),
         ]
         tiles = (in_hbm(tile_values), in_hbm(sib_tiles))
-        if coded:
+        if sums is not None:
             far = 6
             pieces = pieces[: n - far] + [in_hbm(piece) for piece in pieces[n - far :]]
             longest = max(piece.shape[0] for piece in pieces)
+            counts = jnp.concatenate([tile_count, slots_there[2, :1]])
             return pl.pallas_call(
-                lambda *refs: first_kernel(n, far, rows, *refs),
+                lambda *refs: first_kernel(n, far, *refs),
                 out_shape=(parts, jax.ShapeDtypeStruct((rows, half), jnp.float32)),
-                in_specs=[smem()] * 3
+                in_specs=[smem()] * 7
+                + [vmem()]
                 + [anywhere()] * 2
                 + [vmem()] * (n - far)
                 + [anywhere()] * far,
                 out_specs=(vmem(), vmem()),
                 scratch_shapes=scratch
                 + [
-                    VMEM((chips, per, TILE), jnp.float32),
                     VMEM((TILE, TILE), jnp.float32),
                     VMEM((far, longest, half), jnp.int16),
                     pltpu.SemaphoreType.DMA((far,)),
                 ],
                 compiler_params=params(20),
                 name="first_products",
-            )(facts, sib_facts, order, *tiles, *pieces)
+            )(
+                tile_rows, tile_cols, slots_there[0], slots_there[1], counts, core.reshape(1),
+                order, sums.reshape(chips, per, TILE), *tiles, *pieces,
+            )
         return pl.pallas_call(
             lambda *refs: later_kernel(n, rows, *refs),
             out_shape=parts,
@@ -426,7 +447,7 @@
             scratch_shapes=scratch,
             compiler_params=params(20),
             name="later_products",
-        )(facts, sib_facts, order, *tiles, *pieces)
+        )(*facts, order, *tiles, *pieces)
 
     def update(parts, inverse, scaled):
         return pl.pallas_call(
@@ -440,12 +461,16 @@
             name="current",
         )(parts, restart, inverse)
 
-    pieces, names, tile_facts = gather(block, sums, order_tiles)
-    parts, inverse = multiply(pieces, names, True, *tile_facts)
+    pieces, names, sums = gather(block, sums)
+    parts, inverse = multiply(pieces, names, sums, None)
+    parts, raw = tie((parts, (tile_rows, tile_cols, tile_count)))
+    facts = order_tiles(*raw)
     parts = lax.all_to_all(parts, "row", 0, 0, tiled=True)
+    parts, facts = tie((parts, facts))
+    facts = (facts, sibling(facts))
     panel = update(parts, inverse, True)
     pieces, names, _ = gather(panel)
-    parts = multiply(pieces, names, False, *tile_facts)
+    parts = multiply(pieces, names, None, facts)
     parts = lax.all_to_all(parts, "row", 0, 0, tiled=True)
     current = update(parts, inverse, False)
     mine = lax.dynamic_slice_in_dim(current, core * own_rows, own_rows, 0)

time: 144 us -> 149 us (1.035)
  Pallas kernels: 24.3 us -> 27.4 us
  starting transfers between devices: 63.9 us -> 66.7 us
  other arithmetic: 2.38 us -> 4.23 us
    ppermute x35 -> x37, waiting for transfers between devices: 28.9 us -> 22.4 us  [by_col(): return lax.ppermute(value, 'col', pairs)]
    all_to_all x2, waiting for transfers between devices: 16.9 us -> 22.3 us  [per_device(): parts = lax.all_to_all(parts, 'row', 0, 0, tiled=True)]
    all_to_all x2, starting transfers between devices: 8.18 us -> 12.8 us  [per_device(): parts = lax.all_to_all(parts, 'row', 0, 0, tiled=True)]
    pallas_call x1, Pallas kernels: 8 us -> 9.79 us  [multiply(): pl.pallas_call(lambda *refs: first_kernel(n, far, *refs), out_shape=(part...]
    ppermute x35 -> x37, starting transfers between devices: 55.7 us -> 54 us  [by_col(): return lax.ppermute(value, 'col', pairs)]
  transfers between devices with their start and end apart: 37 -> 39, of which waited for: 21 -> 15; matrix products, arithmetic and copies ran while one was open for 3% -> 2% of each run, Pallas kernels for 6% -> 6%
where the time goes in v7:
time: 149 us
  starting transfers between devices  66.7 us (45%)
  waiting for transfers between devices  44.7 us (30%)
  Pallas kernels  27.4 us (18%)
  other arithmetic  4.23 us (3%)
  between operations  3.87 us (3%)
  local copies, waits for them, and re-layouts  2.35 us (2%)
    ppermute x37, starting transfers between devices, by_col(): return lax.ppermute(value, 'col', pairs)  54 us
    ppermute x37, waiting for transfers between devices, by_col(): return lax.ppermute(value, 'col', pairs)  22.4 us
    all_to_all x2, waiting for transfers between devices, per_device(): parts = lax.all_to_all(parts, 'row', 0, 0, tiled=True)  22.3 us
    all_to_all x2, starting transfers between devices, per_device(): parts = lax.all_to_all(parts, 'row', 0, 0, tiled=True)  12.8 us
    pallas_call x1, Pallas kernels, multiply(): pl.pallas_call(lambda *refs: first_kernel(n, far, *refs), out_shape=(part...  9.79 us
    pallas_call x1, Pallas kernels, multiply(): pl.pallas_call(lambda *refs: later_kernel(n, rows, *refs), out_shape=part...  7.23 us
    pallas_call x1, Pallas kernels, per_device(): pl.pallas_call(seed_kernel, out_shape=jax.ShapeDtypeStruct((2 * own_rows,...  7.16 us
  transfers between devices with their start and end apart: 39, of which 15 were waited for; matrix products, arithmetic and copies ran while one was open for 2% of the time, Pallas kernels for 6%

profile of v7, /device:TPU:1, one launch (start us, length us, event | category | flops | bytes accessed | tf_op | source)
XLA Modules:
  0.0 149.3 jit_solution(1787649366232312438)
XLA Ops:
  0.0 1.1 add_convert_fusion
  1.2 3.3 %collective-permute-start.1 = (s16[256,128]{1,0:T(8,128)(2,1)S(1)}, s16[256,128]{1,0:T(8,128)(2,1)S(1)}, u32[]{:S(2)}, u32[]{:S(2)}) collective-permute-start(s16[256,128]{1,0:T(8,128)(2,1)S(1)} %get-tuple-element.31), channel_id=1, source_target_pairs={{0,1},{1,0},{2,3},{3,2},{4,5},{5,4},{6,7},{7,6},{8,9},{9,8},{10,11... | collective-permute-start | bytes 196616 | tf_op jit(solution)/shard_map/ppermute | solution.py:304
  5.3 0.6 copy-done.1
  5.9 2.4 %column_sums.1 = f32[64,128]{1,0:T(8,128)S(1)} custom-call(s32[96]{0:T(128)S(1)} %copy-done.1, s32[1]{0:T(128)} %copy.10.count_ref, bf16[96,128,128]{2,1,0:T(8,128)(2,1)} %refs_3_.1), custom_call_target="tpu_custom_call" | custom-call | tf_op jit(solution)/shard_map/column_sums/pallas_call | solution.py:349
  8.3 0.7 collective-permute-start.2
  9.7 7.2 %seed_counts.1.refs_1_ = f32[512,128]{1,0:T(8,128)S(1)} custom-call(s32[1]{0:T(128)} %bitcast.28.first_ref, s32[1024,128]{1,0:T(8,128)S(1)} %bitcast.35), custom_call_target="tpu_custom_call" | custom-call | tf_op jit(solution)/shard_map/seed_counts/pallas_call | solution.py:394
  17.0 0.5 slice.74
  17.7 3.2 %collective-permute-start.4 = (s16[640,128]{1,0:T(8,128)(2,1)S(1)}, s16[640,128]{1,0:T(8,128)(2,1)S(1)}, u32[]{:S(2)}, u32[]{:S(2)}) collective-permute-start(s16[640,128]{1,0:T(8,128)(2,1)S(1)} %pad_add_fusion.refs_10_), channel_id=1, source_target_pairs={{0,14},{1,15},{2,0},{3,1},{4,2},{5,3},{6,4},{7,5},{8,6},{9,7},{10,... | collective-permute-start | bytes 491528 | tf_op jit(solution)/shard_map/ppermute | solution.py:304
  20.9 2.5 %collective-permute-start.12 = (s16[512,128]{1,0:T(8,128)(2,1)S(1)}, s16[512,128]{1,0:T(8,128)(2,1)S(1)}, u32[]{:S(2)}, u32[]{:S(2)}) collective-permute-start(s16[512,128]{1,0:T(8,128)(2,1)S(1)} %add_select_fusion), channel_id=1, source_target_pairs={{0,16},{1,17},{2,18},{3,19},{4,20},{5,21},{6,22},{7,23},{8,24},{9,... | collective-permute-start | bytes 393224 | tf_op jit(solution)/shard_map/ppermute | solution.py:304
  23.4 2.8 %collective-permute-done.12.refs_11_ = s16[512,128]{1,0:T(8,128)(2,1)S(1)} collective-permute-done((s16[512,128]{1,0:T(8,128)(2,1)S(1)}, s16[512,128]{1,0:T(8,128)(2,1)S(1)}, u32[]{:S(2)}, u32[]{:S(2)}) %collective-permute-start.12) | collective-permute-done | bytes 131104 | tf_op jit(solution)/shard_map/ppermute | solution.py:304
  26.3 1.4 collective-permute-start.14
  27.8 2.7 %collective-permute-start.6 = (s16[640,128]{1,0:T(8,128)(2,1)S(1)}, s16[640,128]{1,0:T(8,128)(2,1)S(1)}, u32[]{:S(2)}, u32[]{:S(2)}) collective-permute-start(s16[640,128]{1,0:T(8,128)(2,1)S(1)} %collective-permute-done.4.refs_13_), channel_id=1, source_target_pairs={{0,14},{1,15},{2,0},{3,1},{4,2},{5,3},{6,4},{7,5},{8,6},{9,7},{10,... | collective-permute-start | bytes 491528 | tf_op jit(solution)/shard_map/ppermute | solution.py:304
  30.5 2.2 %collective-permute-start.16 = (s16[512,128]{1,0:T(8,128)(2,1)S(1)}, s16[512,128]{1,0:T(8,128)(2,1)S(1)}, u32[]{:S(2)}, u32[]{:S(2)}) collective-permute-start(s16[512,128]{1,0:T(8,128)(2,1)S(1)} %collective-permute-done.14.refs_15_), channel_id=1, source_target_pairs={{0,14},{1,15},{2,0},{3,1},{4,2},{5,3},{6,4},{7,5},{8,6},{9,7},{10,... | collective-permute-start | bytes 393224 | tf_op jit(solution)/shard_map/ppermute | solution.py:304
  32.7 1.7 %collective-permute-done.5.refs_16_ = s16[640,128]{1,0:T(8,128)(2,1)S(1)} collective-permute-done((s16[640,128]{1,0:T(8,128)(2,1)S(1)}, s16[640,128]{1,0:T(8,128)(2,1)S(1)}, u32[]{:S(2)}, u32[]{:S(2)}) %collective-permute-start.5) | collective-permute-done | bytes 163872 | tf_op jit(solution)/shard_map/ppermute | solution.py:304
  34.5 3.0 %collective-permute-start.8 = (s16[640,128]{1,0:T(8,128)(2,1)S(1)}, s16[640,128]{1,0:T(8,128)(2,1)S(1)}, u32[]{:S(2)}, u32[]{:S(2)}) collective-permute-start(s16[640,128]{1,0:T(8,128)(2,1)S(1)} %collective-permute-done.6.refs_17_), channel_id=1, source_target_pairs={{0,14},{1,15},{2,0},{3,1},{4,2},{5,3},{6,4},{7,5},{8,6},{9,7},{10,... | collective-permute-start | bytes 491528 | tf_op jit(solution)/shard_map/ppermute | solution.py:304
  37.5 2.1 %collective-permute-start.18 = (s16[512,128]{1,0:T(8,128)(2,1)S(1)}, s16[512,128]{1,0:T(8,128)(2,1)S(1)}, u32[]{:S(2)}, u32[]{:S(2)}) collective-permute-start(s16[512,128]{1,0:T(8,128)(2,1)S(1)} %collective-permute-done.16.refs_19_), channel_id=1, source_target_pairs={{0,14},{1,15},{2,0},{3,1},{4,2},{5,3},{6,4},{7,5},{8,6},{9,7},{10,... | collective-permute-start | bytes 393224 | tf_op jit(solution)/shard_map/ppermute | solution.py:304
  39.6 1.6 %collective-permute-done.7.refs_20_ = s16[640,128]{1,0:T(8,128)(2,1)S(1)} collective-permute-done((s16[640,128]{1,0:T(8,128)(2,1)S(1)}, s16[640,128]{1,0:T(8,128)(2,1)S(1)}, u32[]{:S(2)}, u32[]{:S(2)}) %collective-permute-start.7) | collective-permute-done | bytes 163872 | tf_op jit(solution)/shard_map/ppermute | solution.py:304
  41.2 1.3 collective-permute-done.18.refs_23_
  42.5 3.1 %collective-permute-start.19 = (s16[512,128]{1,0:T(8,128)(2,1)S(1)}, s16[512,128]{1,0:T(8,128)(2,1)S(1)}, u32[]{:S(2)}, u32[]{:S(2)}) collective-permute-start(s16[512,128]{1,0:T(8,128)(2,1)S(1)} %collective-permute-done.18.refs_23_), channel_id=1, source_target_pairs={{0,14},{1,15},{2,0},{3,1},{4,2},{5,3},{6,4},{7,5},{8,6},{9,7},{10,... | collective-permute-start | bytes 393224 | tf_op jit(solution)/shard_map/ppermute | solution.py:304
  45.6 3.1 %collective-permute-done.9.refs_24_ = s16[640,128]{1,0:T(8,128)(2,1)S(1)} collective-permute-done((s16[640,128]{1,0:T(8,128)(2,1)S(1)}, s16[640,128]{1,0:T(8,128)(2,1)S(1)}, u32[]{:S(2)}, u32[]{:S(2)}) %collective-permute-start.9) | collective-permute-done | bytes 163872 | tf_op jit(solution)/shard_map/ppermute | solution.py:304
  48.8 3.4 %collective-permute-start.10 = (f32[64,128]{1,0:T(8,128)S(1)}, f32[64,128]{1,0:T(8,128)S(1)}, u32[]{:S(2)}, u32[]{:S(2)}) collective-permute-start(f32[64,128]{1,0:T(8,128)S(1)} %fusion.6), channel_id=1, source_target_pairs={{0,16},{1,17},{2,18},{3,19},{4,20},{5,21},{6,22},{7,23},{8,24},{9,... | collective-permute-start | bytes 98312 | tf_op jit(solution)/shard_map/ppermute | solution.py:304
  52.2 0.6 pad_add_fusion.1.refs_4_
  52.8 0.7 collective-permute-done.10
  53.6 0.6 copy-done.8
  54.2 9.8 %first_products.1 = (s16[8,528,128]{2,1,0:T(8,128)(2,1)}, f32[512,128]{1,0:T(8,128)S(1)}) custom-call(s32[96]{0:T(128)S(1)} %copy-done.3, s32[96]{0:T(128)S(1)} %copy-done.2, s32[96]{0:T(128)S(1)} %get-tuple-element.33.refs_2_, s32[96]{0:T(128)S(1)} %get-tuple-element.32.refs_3_, s32[2]{0:T(128)S(1)} %pad_add_fusion.1.refs_4_, s32[1]{0:T(128)} %bitcast.6.refs_5_, ...), custom_call_target="tpu_custom_call" | custom-call | tf_op jit(solution)/shard_map/first_products/pallas_call | solution.py:421
  64.0 9.2 %all-to-all-start = ((s16[8,528,128]{2,1,0:T(8,128)(2,1)}), s16[8,528,128]{2,1,0:T(8,128)(2,1)S(1)}, u32[]{:S(2)}, u32[]{:S(2)}) async-start(s16[8,528,128]{2,1,0:T(8,128)(2,1)} %get-tuple-element.14), calls=%async_computation | async-start | bytes 2162688 | tf_op jit(solution)/shard_map/all_to_all | solution.py:468
  73.3 0.6 fusion.28
  77.2 7.9 %all-to-all-done.refs_0_ = s16[8,528,128]{2,1,0:T(8,128)(2,1)S(1)} async-done(((s16[8,528,128]{2,1,0:T(8,128)(2,1)}), s16[8,528,128]{2,1,0:T(8,128)(2,1)S(1)}, u32[]{:S(2)}, u32[]{:S(2)}) %all-to-all-start) | async-done | bytes 1081376 | tf_op jit(solution)/shard_map/all_to_all | solution.py:468
  85.7 5.2 %collective-permute-done.21.refs_6_ = bf16[512,128]{1,0:T(8,128)(2,1)S(1)} collective-permute-done((bf16[512,128]{1,0:T(8,128)(2,1)S(1)}, bf16[512,128]{1,0:T(8,128)(2,1)S(1)}, u32[]{:S(2)}, u32[]{:S(2)}) %collective-permute-start.21) | collective-permute-done | bytes 131104 | tf_op jit(solution)/shard_map/ppermute | solution.py:304
  90.9 1.5 %collective-permute-start.24 = (bf16[512,128]{1,0:T(8,128)(2,1)S(1)}, bf16[512,128]{1,0:T(8,128)(2,1)S(1)}, u32[]{:S(2)}, u32[]{:S(2)}) collective-permute-start(bf16[512,128]{1,0:T(8,128)(2,1)S(1)} %collective-permute-done.21.refs_6_), channel_id=1, source_target_pairs={{0,2},{1,3},{2,4},{3,5},{4,6},{5,7},{6,8},{7,9},{8,10},{9,11},{10,... | collective-permute-start | bytes 393224 | tf_op jit(solution)/shard_map/ppermute | solution.py:304
  92.4 1.4 collective-permute-start.26
  93.9 0.9 collective-permute-done.25.refs_10_
  94.8 1.5 collective-permute-start.29
  96.5 0.9 collective-permute-start.27
  97.4 0.5 collective-permute-start.28
  97.9 1.1 collective-permute-done.26.refs_11_
  99.0 3.0 %collective-permute-start.33 = (bf16[512,128]{1,0:T(8,128)(2,1)S(1)}, bf16[512,128]{1,0:T(8,128)(2,1)S(1)}, u32[]{:S(2)}, u32[]{:S(2)}) collective-permute-start(bf16[512,128]{1,0:T(8,128)(2,1)S(1)} %collective-permute-done.29.refs_14_), channel_id=1, source_target_pairs={{0,14},{1,15},{2,0},{3,1},{4,2},{5,3},{6,4},{7,5},{8,6},{9,7},{10,... | collective-permute-start | bytes 393224 | tf_op jit(solution)/shard_map/ppermute | solution.py:304
  102.0 2.8 %collective-permute-start.31 = (bf16[512,128]{1,0:T(8,128)(2,1)S(1)}, bf16[512,128]{1,0:T(8,128)(2,1)S(1)}, u32[]{:S(2)}, u32[]{:S(2)}) collective-permute-start(bf16[512,128]{1,0:T(8,128)(2,1)S(1)} %collective-permute-done.27.refs_12_), channel_id=1, source_target_pairs={{0,14},{1,15},{2,0},{3,1},{4,2},{5,3},{6,4},{7,5},{8,6},{9,7},{10,... | collective-permute-start | bytes 393224 | tf_op jit(solution)/shard_map/ppermute | solution.py:304
  104.8 2.0 %collective-permute-done.30.refs_15_ = bf16[512,128]{1,0:T(8,128)(2,1)S(1)} collective-permute-done((bf16[512,128]{1,0:T(8,128)(2,1)S(1)}, bf16[512,128]{1,0:T(8,128)(2,1)S(1)}, u32[]{:S(2)}, u32[]{:S(2)}) %collective-permute-start.30) | collective-permute-done | bytes 131104 | tf_op jit(solution)/shard_map/ppermute | solution.py:304
  106.8 2.7 %collective-permute-start.35 = (bf16[512,128]{1,0:T(8,128)(2,1)S(1)}, bf16[512,128]{1,0:T(8,128)(2,1)S(1)}, u32[]{:S(2)}, u32[]{:S(2)}) collective-permute-start(bf16[512,128]{1,0:T(8,128)(2,1)S(1)} %collective-permute-done.33.refs_18_), channel_id=1, source_target_pairs={{0,14},{1,15},{2,0},{3,1},{4,2},{5,3},{6,4},{7,5},{8,6},{9,7},{10,... | collective-permute-start | bytes 393224 | tf_op jit(solution)/shard_map/ppermute | solution.py:304
  109.4 9.1 %collective-permute-start.20 = (s32[4,128]{1,0:T(4,128)S(1)}, s32[4,128]{1,0:T(4,128)S(1)}, u32[]{:S(2)}, u32[]{:S(2)}) collective-permute-start(s32[4,128]{1,0:T(4,128)S(1)} %add_add_fusion.2.refs_0_), channel_id=1, source_target_pairs={{0,1},{1,0},{2,3},{3,2},{4,5},{5,4},{6,7},{7,6},{8,9},{9,8},{10,11... | collective-permute-start | bytes 6152 | tf_op jit(solution)/shard_map/ppermute | solution.py:304
  118.5 0.8 collective-permute-done.20.refs_1_
  119.4 7.2 %later_products.1 = s16[8,528,128]{2,1,0:T(8,128)(2,1)} custom-call(s32[4,128]{1,0:T(4,128)S(1)} %add_add_fusion.2.refs_0_, s32[4,128]{1,0:T(4,128)S(1)} %collective-permute-done.20.refs_1_, s32[16]{0:T(128)S(1)} %stack.106.refs_6_.refs_2_, bf16[96,128,128]{2,1,0:T(8,128)(2,1)} %refs_3_.1, bf16[96,128,128]{2,1,0:T(8,128)(2,1)} %collective-permute-done.11.refs_9_.refs_4_, ...), custom_call_target="tpu_custom_call" | custom-call | tf_op jit(solution)/shard_map/later_products/pallas_call | solution.py:442
  126.6 3.6 %all-to-all-start.1 = ((s16[8,528,128]{2,1,0:T(8,128)(2,1)}), s16[8,528,128]{2,1,0:T(8,128)(2,1)S(1)}, u32[]{:S(2)}, u32[]{:S(2)}) async-start(s16[8,528,128]{2,1,0:T(8,128)(2,1)} %later_products.1), calls=%async_computation.1 | async-start | bytes 2162688 | tf_op jit(solution)/shard_map/all_to_all | solution.py:474
  130.2 14.4 %all-to-all-done.1.refs_0_ = s16[8,528,128]{2,1,0:T(8,128)(2,1)S(1)} async-done(((s16[8,528,128]{2,1,0:T(8,128)(2,1)}), s16[8,528,128]{2,1,0:T(8,128)(2,1)S(1)}, u32[]{:S(2)}, u32[]{:S(2)}) %all-to-all-start.1) | async-done | bytes 1081376 | tf_op jit(solution)/shard_map/all_to_all | solution.py:474
  145.0 2.5 %collective-permute-start.36 = (f32[256,128]{1,0:T(8,128)S(1)}, f32[256,128]{1,0:T(8,128)S(1)}, u32[]{:S(2)}, u32[]{:S(2)}) collective-permute-start(f32[256,128]{1,0:T(8,128)S(1)} %get-tuple-element.29), channel_id=1, source_target_pairs={{0,1},{1,0},{2,3},{3,2},{4,5},{5,4},{6,7},{7,6},{8,9},{9,8},{10,11... | collective-permute-start | bytes 393224 | tf_op jit(solution)/shard_map/ppermute | solution.py:304
  147.5 1.0 collective-permute-done.36
  148.5 0.7 maximum_select_fusion
  (94 shorter events, 3.3 us)
Async XLA Ops:
  0.0 9.2 %copy-start = (s32[256,1024]{1,0:T(8,128)S(1)}, s32[256,1024]{1,0:T(8,128)}, u32[]{:S(2)}) copy-start(s32[256,1024]{1,0:T(8,128)} %param.11) | copy-start | bytes 3145732
  1.2 16.4 %collective-permute-start.1 = (s16[256,128]{1,0:T(8,128)(2,1)S(1)}, s16[256,128]{1,0:T(8,128)(2,1)S(1)}, u32[]{:S(2)}, u32[]{:S(2)}) collective-permute-start(s16[256,128]{1,0:T(8,128)(2,1)S(1)} %get-tuple-element.31), channel_id=1, source_target_pairs={{0,1},{1,0},{2,3},{3,2},{4,5},{5,4},{6,7},{7,6},{8,9},{9,8},{10,11... | collective-permute-start | bytes 196616 | tf_op jit(solution)/shard_map/ppermute | solution.py:304
  4.5 49.0 %collective-permute-start.11 = (bf16[96,128,128]{2,1,0:T(8,128)(2,1)}, bf16[96,128,128]{2,1,0:T(8,128)(2,1)}, u32[]{:S(2)}, u32[]{:S(2)}) collective-permute-start(bf16[96,128,128]{2,1,0:T(8,128)(2,1)} %refs_3_.1), channel_id=1, source_target_pairs={{0,1},{1,0},{2,3},{3,2},{4,5},{5,4},{6,7},{7,6},{8,9},{9,8},{10,11... | collective-permute-start | bytes 9437192 | tf_op jit(solution)/shard_map/ppermute | solution.py:304
  5.3 0.7 copy-start.1
  5.9 3.2 %copy-start.3 = (s32[96]{0:T(128)S(1)}, s32[96]{0:T(128)}, u32[]{:S(2)}) copy-start(s32[96]{0:T(128)} %refs_0_.1) | copy-start | bytes 1156
  8.3 9.1 %collective-permute-start.2 = (f32[64,128]{1,0:T(8,128)S(1)}, f32[64,128]{1,0:T(8,128)S(1)}, u32[]{:S(2)}, u32[]{:S(2)}) collective-permute-start(f32[64,128]{1,0:T(8,128)S(1)} %column_sums.1), channel_id=1, source_target_pairs={{0,1},{1,0},{2,3},{3,2},{4,5},{5,4},{6,7},{7,6},{8,9},{9,8},{10,11... | collective-permute-start | bytes 98312 | tf_op jit(solution)/shard_map/ppermute | solution.py:304
  9.2 7.8 %collective-permute-start = (s32[3,96]{1,0:T(4,128)S(1)}, s32[3,96]{1,0:T(4,128)S(1)}, u32[]{:S(2)}, u32[]{:S(2)}) collective-permute-start(s32[3,96]{1,0:T(4,128)S(1)} %add_add_fusion.1), channel_id=1, source_target_pairs={{0,1},{1,0},{2,3},{3,2},{4,5},{5,4},{6,7},{7,6},{8,9},{9,8},{10,11... | collective-permute-start | bytes 3464 | tf_op jit(solution)/shard_map/ppermute | solution.py:304
  17.5 36.7 %copy-start.2 = (s32[96]{0:T(128)S(1)}, s32[96]{0:T(128)}, u32[]{:S(2)}) copy-start(s32[96]{0:T(128)} %refs_1_.1) | copy-start | bytes 1156
  17.7 10.1 %collective-permute-start.3 = (s16[640,128]{1,0:T(8,128)(2,1)S(1)}, s16[640,128]{1,0:T(8,128)(2,1)S(1)}, u32[]{:S(2)}, u32[]{:S(2)}) collective-permute-start(s16[640,128]{1,0:T(8,128)(2,1)S(1)} %pad_add_fusion.refs_10_), channel_id=1, source_target_pairs={{0,2},{1,3},{2,4},{3,5},{4,6},{5,7},{6,8},{7,9},{8,10},{9,11},{10,... | collective-permute-start | bytes 491528 | tf_op jit(solution)/shard_map/ppermute | solution.py:304
  17.7 10.0 %collective-permute-start.4 = (s16[640,128]{1,0:T(8,128)(2,1)S(1)}, s16[640,128]{1,0:T(8,128)(2,1)S(1)}, u32[]{:S(2)}, u32[]{:S(2)}) collective-permute-start(s16[640,128]{1,0:T(8,128)(2,1)S(1)} %pad_add_fusion.refs_10_), channel_id=1, source_target_pairs={{0,14},{1,15},{2,0},{3,1},{4,2},{5,3},{6,4},{7,5},{8,6},{9,7},{10,... | collective-permute-start | bytes 491528 | tf_op jit(solution)/shard_map/ppermute | solution.py:304
  20.9 5.3 %collective-permute-start.12 = (s16[512,128]{1,0:T(8,128)(2,1)S(1)}, s16[512,128]{1,0:T(8,128)(2,1)S(1)}, u32[]{:S(2)}, u32[]{:S(2)}) collective-permute-start(s16[512,128]{1,0:T(8,128)(2,1)S(1)} %add_select_fusion), channel_id=1, source_target_pairs={{0,16},{1,17},{2,18},{3,19},{4,20},{5,21},{6,22},{7,23},{8,24},{9,... | collective-permute-start | bytes 393224 | tf_op jit(solution)/shard_map/ppermute | solution.py:304
  26.3 4.2 %collective-permute-start.14 = (s16[512,128]{1,0:T(8,128)(2,1)S(1)}, s16[512,128]{1,0:T(8,128)(2,1)S(1)}, u32[]{:S(2)}, u32[]{:S(2)}) collective-permute-start(s16[512,128]{1,0:T(8,128)(2,1)S(1)} %collective-permute-done.12.refs_11_), channel_id=1, source_target_pairs={{0,14},{1,15},{2,0},{3,1},{4,2},{5,3},{6,4},{7,5},{8,6},{9,7},{10,... | collective-permute-start | bytes 393224 | tf_op jit(solution)/shard_map/ppermute | solution.py:304
  27.7 5.0 %collective-permute-start.13 = (s16[512,128]{1,0:T(8,128)(2,1)S(1)}, s16[512,128]{1,0:T(8,128)(2,1)S(1)}, u32[]{:S(2)}, u32[]{:S(2)}) collective-permute-start(s16[512,128]{1,0:T(8,128)(2,1)S(1)} %collective-permute-done.12.refs_11_), channel_id=1, source_target_pairs={{0,2},{1,3},{2,4},{3,5},{4,6},{5,7},{6,8},{7,9},{8,10},{9,11},{10,... | collective-permute-start | bytes 393224 | tf_op jit(solution)/shard_map/ppermute | solution.py:304
  27.7 6.7 %collective-permute-start.5 = (s16[640,128]{1,0:T(8,128)(2,1)S(1)}, s16[640,128]{1,0:T(8,128)(2,1)S(1)}, u32[]{:S(2)}, u32[]{:S(2)}) collective-permute-start(s16[640,128]{1,0:T(8,128)(2,1)S(1)} %collective-permute-done.3.refs_12_), channel_id=1, source_target_pairs={{0,2},{1,3},{2,4},{3,5},{4,6},{5,7},{6,8},{7,9},{8,10},{9,11},{10,... | collective-permute-start | bytes 491528 | tf_op jit(solution)/shard_map/ppermute | solution.py:304
  27.8 6.7 %collective-permute-start.6 = (s16[640,128]{1,0:T(8,128)(2,1)S(1)}, s16[640,128]{1,0:T(8,128)(2,1)S(1)}, u32[]{:S(2)}, u32[]{:S(2)}) collective-permute-start(s16[640,128]{1,0:T(8,128)(2,1)S(1)} %collective-permute-done.4.refs_13_), channel_id=1, source_target_pairs={{0,14},{1,15},{2,0},{3,1},{4,2},{5,3},{6,4},{7,5},{8,6},{9,7},{10,... | collective-permute-start | bytes 491528 | tf_op jit(solution)/shard_map/ppermute | solution.py:304
  30.5 7.0 %collective-permute-start.16 = (s16[512,128]{1,0:T(8,128)(2,1)S(1)}, s16[512,128]{1,0:T(8,128)(2,1)S(1)}, u32[]{:S(2)}, u32[]{:S(2)}) collective-permute-start(s16[512,128]{1,0:T(8,128)(2,1)S(1)} %collective-permute-done.14.refs_15_), channel_id=1, source_target_pairs={{0,14},{1,15},{2,0},{3,1},{4,2},{5,3},{6,4},{7,5},{8,6},{9,7},{10,... | collective-permute-start | bytes 393224 | tf_op jit(solution)/shard_map/ppermute | solution.py:304
  32.7 6.9 %collective-permute-start.15 = (s16[512,128]{1,0:T(8,128)(2,1)S(1)}, s16[512,128]{1,0:T(8,128)(2,1)S(1)}, u32[]{:S(2)}, u32[]{:S(2)}) collective-permute-start(s16[512,128]{1,0:T(8,128)(2,1)S(1)} %collective-permute-done.13.refs_14_), channel_id=1, source_target_pairs={{0,2},{1,3},{2,4},{3,5},{4,6},{5,7},{6,8},{7,9},{8,10},{9,11},{10,... | collective-permute-start | bytes 393224 | tf_op jit(solution)/shard_map/ppermute | solution.py:304
  34.4 6.7 %collective-permute-start.7 = (s16[640,128]{1,0:T(8,128)(2,1)S(1)}, s16[640,128]{1,0:T(8,128)(2,1)S(1)}, u32[]{:S(2)}, u32[]{:S(2)}) collective-permute-start(s16[640,128]{1,0:T(8,128)(2,1)S(1)} %collective-permute-done.5.refs_16_), channel_id=1, source_target_pairs={{0,2},{1,3},{2,4},{3,5},{4,6},{5,7},{6,8},{7,9},{8,10},{9,11},{10,... | collective-permute-start | bytes 491528 | tf_op jit(solution)/shard_map/ppermute | solution.py:304
  34.5 6.7 %collective-permute-start.8 = (s16[640,128]{1,0:T(8,128)(2,1)S(1)}, s16[640,128]{1,0:T(8,128)(2,1)S(1)}, u32[]{:S(2)}, u32[]{:S(2)}) collective-permute-start(s16[640,128]{1,0:T(8,128)(2,1)S(1)} %collective-permute-done.6.refs_17_), channel_id=1, source_target_pairs={{0,14},{1,15},{2,0},{3,1},{4,2},{5,3},{6,4},{7,5},{8,6},{9,7},{10,... | collective-permute-start | bytes 491528 | tf_op jit(solution)/shard_map/ppermute | solution.py:304
  37.5 5.0 %collective-permute-start.18 = (s16[512,128]{1,0:T(8,128)(2,1)S(1)}, s16[512,128]{1,0:T(8,128)(2,1)S(1)}, u32[]{:S(2)}, u32[]{:S(2)}) collective-permute-start(s16[512,128]{1,0:T(8,128)(2,1)S(1)} %collective-permute-done.16.refs_19_), channel_id=1, source_target_pairs={{0,14},{1,15},{2,0},{3,1},{4,2},{5,3},{6,4},{7,5},{8,6},{9,7},{10,... | collective-permute-start | bytes 393224 | tf_op jit(solution)/shard_map/ppermute | solution.py:304
  39.6 13.9 %collective-permute-start.17 = (s16[512,128]{1,0:T(8,128)(2,1)S(1)}, s16[512,128]{1,0:T(8,128)(2,1)S(1)}, u32[]{:S(2)}, u32[]{:S(2)}) collective-permute-start(s16[512,128]{1,0:T(8,128)(2,1)S(1)} %collective-permute-done.15.refs_18_), channel_id=1, source_target_pairs={{0,2},{1,3},{2,4},{3,5},{4,6},{5,7},{6,8},{7,9},{8,10},{9,11},{10,... | collective-permute-start | bytes 393224 | tf_op jit(solution)/shard_map/ppermute | solution.py:304
  41.2 12.4 %copy-start.4 = (s16[640,128]{1,0:T(8,128)(2,1)}, s16[640,128]{1,0:T(8,128)(2,1)S(1)}, u32[]{:S(2)}) copy-start(s16[640,128]{1,0:T(8,128)(2,1)S(1)} %collective-permute-done.7.refs_20_) | copy-start | bytes 491524
  41.2 7.5 %collective-permute-start.9 = (s16[640,128]{1,0:T(8,128)(2,1)S(1)}, s16[640,128]{1,0:T(8,128)(2,1)S(1)}, u32[]{:S(2)}, u32[]{:S(2)}) collective-permute-start(s16[640,128]{1,0:T(8,128)(2,1)S(1)} %collective-permute-done.7.refs_20_), channel_id=1, source_target_pairs={{0,2},{1,3},{2,4},{3,5},{4,6},{5,7},{6,8},{7,9},{8,10},{9,11},{10,... | collective-permute-start | bytes 491528 | tf_op jit(solution)/shard_map/ppermute | solution.py:304
  41.2 12.3 %copy-start.5 = (s16[640,128]{1,0:T(8,128)(2,1)}, s16[640,128]{1,0:T(8,128)(2,1)S(1)}, u32[]{:S(2)}) copy-start(s16[640,128]{1,0:T(8,128)(2,1)S(1)} %collective-permute-done.8.refs_21_) | copy-start | bytes 491524
  42.5 11.0 %copy-start.7 = (s16[512,128]{1,0:T(8,128)(2,1)}, s16[512,128]{1,0:T(8,128)(2,1)S(1)}, u32[]{:S(2)}) copy-start(s16[512,128]{1,0:T(8,128)(2,1)S(1)} %collective-permute-done.18.refs_23_) | copy-start | bytes 393220
  42.5 11.0 %collective-permute-start.19 = (s16[512,128]{1,0:T(8,128)(2,1)S(1)}, s16[512,128]{1,0:T(8,128)(2,1)S(1)}, u32[]{:S(2)}, u32[]{:S(2)}) collective-permute-start(s16[512,128]{1,0:T(8,128)(2,1)S(1)} %collective-permute-done.18.refs_23_), channel_id=1, source_target_pairs={{0,14},{1,15},{2,0},{3,1},{4,2},{5,3},{6,4},{7,5},{8,6},{9,7},{10,... | collective-permute-start | bytes 393224 | tf_op jit(solution)/shard_map/ppermute | solution.py:304
  48.7 4.9 %copy-start.6 = (s16[640,128]{1,0:T(8,128)(2,1)}, s16[640,128]{1,0:T(8,128)(2,1)S(1)}, u32[]{:S(2)}) copy-start(s16[640,128]{1,0:T(8,128)(2,1)S(1)} %collective-permute-done.9.refs_24_) | copy-start | bytes 491524
  48.8 4.7 %collective-permute-start.10 = (f32[64,128]{1,0:T(8,128)S(1)}, f32[64,128]{1,0:T(8,128)S(1)}, u32[]{:S(2)}, u32[]{:S(2)}) collective-permute-start(f32[64,128]{1,0:T(8,128)S(1)} %fusion.6), channel_id=1, source_target_pairs={{0,16},{1,17},{2,18},{3,19},{4,20},{5,21},{6,22},{7,23},{8,24},{9,... | collective-permute-start | bytes 98312 | tf_op jit(solution)/shard_map/ppermute | solution.py:304
  53.5 0.7 copy-start.9
  64.0 21.1 %all-to-all-start = ((s16[8,528,128]{2,1,0:T(8,128)(2,1)}), s16[8,528,128]{2,1,0:T(8,128)(2,1)S(1)}, u32[]{:S(2)}, u32[]{:S(2)}) async-start(s16[8,528,128]{2,1,0:T(8,128)(2,1)} %get-tuple-element.14), calls=%async_computation | async-start | bytes 2162688 | tf_op jit(solution)/shard_map/all_to_all | solution.py:468
  85.5 5.4 %collective-permute-start.21 = (bf16[512,128]{1,0:T(8,128)(2,1)S(1)}, bf16[512,128]{1,0:T(8,128)(2,1)S(1)}, u32[]{:S(2)}, u32[]{:S(2)}) collective-permute-start(bf16[512,128]{1,0:T(8,128)(2,1)S(1)} %current.2.refs_5_), channel_id=1, source_target_pairs={{0,16},{1,17},{2,18},{3,19},{4,20},{5,21},{6,22},{7,23},{8,24},{9,... | collective-permute-start | bytes 393224 | tf_op jit(solution)/shard_map/ppermute | solution.py:304
  85.6 6.8 %collective-permute-start.22 = (bf16[512,128]{1,0:T(8,128)(2,1)S(1)}, bf16[512,128]{1,0:T(8,128)(2,1)S(1)}, u32[]{:S(2)}, u32[]{:S(2)}) collective-permute-start(bf16[512,128]{1,0:T(8,128)(2,1)S(1)} %current.2.refs_5_), channel_id=1, source_target_pairs={{0,2},{1,3},{2,4},{3,5},{4,6},{5,7},{6,8},{7,9},{8,10},{9,11},{10,... | collective-permute-start | bytes 393224 | tf_op jit(solution)/shard_map/ppermute | solution.py:304
  90.9 3.8 %collective-permute-start.25 = (bf16[512,128]{1,0:T(8,128)(2,1)S(1)}, bf16[512,128]{1,0:T(8,128)(2,1)S(1)}, u32[]{:S(2)}, u32[]{:S(2)}) collective-permute-start(bf16[512,128]{1,0:T(8,128)(2,1)S(1)} %collective-permute-done.21.refs_6_), channel_id=1, source_target_pairs={{0,14},{1,15},{2,0},{3,1},{4,2},{5,3},{6,4},{7,5},{8,6},{9,7},{10,... | collective-permute-start | bytes 393224 | tf_op jit(solution)/shard_map/ppermute | solution.py:304
  90.9 5.5 %collective-permute-start.23 = (bf16[512,128]{1,0:T(8,128)(2,1)S(1)}, bf16[512,128]{1,0:T(8,128)(2,1)S(1)}, u32[]{:S(2)}, u32[]{:S(2)}) collective-permute-start(bf16[512,128]{1,0:T(8,128)(2,1)S(1)} %current.2.refs_5_), channel_id=1, source_target_pairs={{0,14},{1,15},{2,0},{3,1},{4,2},{5,3},{6,4},{7,5},{8,6},{9,7},{10,... | collective-permute-start | bytes 393224 | tf_op jit(solution)/shard_map/ppermute | solution.py:304
  90.9 6.4 %collective-permute-start.24 = (bf16[512,128]{1,0:T(8,128)(2,1)S(1)}, bf16[512,128]{1,0:T(8,128)(2,1)S(1)}, u32[]{:S(2)}, u32[]{:S(2)}) collective-permute-start(bf16[512,128]{1,0:T(8,128)(2,1)S(1)} %collective-permute-done.21.refs_6_), channel_id=1, source_target_pairs={{0,2},{1,3},{2,4},{3,5},{4,6},{5,7},{6,8},{7,9},{8,10},{9,11},{10,... | collective-permute-start | bytes 393224 | tf_op jit(solution)/shard_map/ppermute | solution.py:304
  92.4 6.5 %collective-permute-start.26 = (bf16[512,128]{1,0:T(8,128)(2,1)S(1)}, bf16[512,128]{1,0:T(8,128)(2,1)S(1)}, u32[]{:S(2)}, u32[]{:S(2)}) collective-permute-start(bf16[512,128]{1,0:T(8,128)(2,1)S(1)} %collective-permute-done.22.refs_7_), channel_id=1, source_target_pairs={{0,2},{1,3},{2,4},{3,5},{4,6},{5,7},{6,8},{7,9},{8,10},{9,11},{10,... | collective-permute-start | bytes 393224 | tf_op jit(solution)/shard_map/ppermute | solution.py:304
  94.8 4.2 %collective-permute-start.29 = (bf16[512,128]{1,0:T(8,128)(2,1)S(1)}, bf16[512,128]{1,0:T(8,128)(2,1)S(1)}, u32[]{:S(2)}, u32[]{:S(2)}) collective-permute-start(bf16[512,128]{1,0:T(8,128)(2,1)S(1)} %collective-permute-done.25.refs_10_), channel_id=1, source_target_pairs={{0,14},{1,15},{2,0},{3,1},{4,2},{5,3},{6,4},{7,5},{8,6},{9,7},{10,... | collective-permute-start | bytes 393224 | tf_op jit(solution)/shard_map/ppermute | solution.py:304
  96.5 5.5 %collective-permute-start.27 = (bf16[512,128]{1,0:T(8,128)(2,1)S(1)}, bf16[512,128]{1,0:T(8,128)(2,1)S(1)}, u32[]{:S(2)}, u32[]{:S(2)}) collective-permute-start(bf16[512,128]{1,0:T(8,128)(2,1)S(1)} %collective-permute-done.23.refs_8_), channel_id=1, source_target_pairs={{0,14},{1,15},{2,0},{3,1},{4,2},{5,3},{6,4},{7,5},{8,6},{9,7},{10,... | collective-permute-start | bytes 393224 | tf_op jit(solution)/shard_map/ppermute | solution.py:304
  97.4 7.4 %collective-permute-start.28 = (bf16[512,128]{1,0:T(8,128)(2,1)S(1)}, bf16[512,128]{1,0:T(8,128)(2,1)S(1)}, u32[]{:S(2)}, u32[]{:S(2)}) collective-permute-start(bf16[512,128]{1,0:T(8,128)(2,1)S(1)} %collective-permute-done.24.refs_9_), channel_id=1, source_target_pairs={{0,2},{1,3},{2,4},{3,5},{4,6},{5,7},{6,8},{7,9},{8,10},{9,11},{10,... | collective-permute-start | bytes 393224 | tf_op jit(solution)/shard_map/ppermute | solution.py:304
  99.0 7.8 %collective-permute-start.30 = (bf16[512,128]{1,0:T(8,128)(2,1)S(1)}, bf16[512,128]{1,0:T(8,128)(2,1)S(1)}, u32[]{:S(2)}, u32[]{:S(2)}) collective-permute-start(bf16[512,128]{1,0:T(8,128)(2,1)S(1)} %collective-permute-done.26.refs_11_), channel_id=1, source_target_pairs={{0,2},{1,3},{2,4},{3,5},{4,6},{5,7},{6,8},{7,9},{8,10},{9,11},{10,... | collective-permute-start | bytes 393224 | tf_op jit(solution)/shard_map/ppermute | solution.py:304
  99.0 7.8 %collective-permute-start.33 = (bf16[512,128]{1,0:T(8,128)(2,1)S(1)}, bf16[512,128]{1,0:T(8,128)(2,1)S(1)}, u32[]{:S(2)}, u32[]{:S(2)}) collective-permute-start(bf16[512,128]{1,0:T(8,128)(2,1)S(1)} %collective-permute-done.29.refs_14_), channel_id=1, source_target_pairs={{0,14},{1,15},{2,0},{3,1},{4,2},{5,3},{6,4},{7,5},{8,6},{9,7},{10,... | collective-permute-start | bytes 393224 | tf_op jit(solution)/shard_map/ppermute | solution.py:304
  102.0 17.4 %collective-permute-start.31 = (bf16[512,128]{1,0:T(8,128)(2,1)S(1)}, bf16[512,128]{1,0:T(8,128)(2,1)S(1)}, u32[]{:S(2)}, u32[]{:S(2)}) collective-permute-start(bf16[512,128]{1,0:T(8,128)(2,1)S(1)} %collective-permute-done.27.refs_12_), channel_id=1, source_target_pairs={{0,14},{1,15},{2,0},{3,1},{4,2},{5,3},{6,4},{7,5},{8,6},{9,7},{10,... | collective-permute-start | bytes 393224 | tf_op jit(solution)/shard_map/ppermute | solution.py:304
  104.8 14.6 %collective-permute-start.32 = (bf16[512,128]{1,0:T(8,128)(2,1)S(1)}, bf16[512,128]{1,0:T(8,128)(2,1)S(1)}, u32[]{:S(2)}, u32[]{:S(2)}) collective-permute-start(bf16[512,128]{1,0:T(8,128)(2,1)S(1)} %collective-permute-done.28.refs_13_), channel_id=1, source_target_pairs={{0,2},{1,3},{2,4},{3,5},{4,6},{5,7},{6,8},{7,9},{8,10},{9,11},{10,... | collective-permute-start | bytes 393224 | tf_op jit(solution)/shard_map/ppermute | solution.py:304
  106.7 12.6 %collective-permute-start.34 = (bf16[512,128]{1,0:T(8,128)(2,1)S(1)}, bf16[512,128]{1,0:T(8,128)(2,1)S(1)}, u32[]{:S(2)}, u32[]{:S(2)}) collective-permute-start(bf16[512,128]{1,0:T(8,128)(2,1)S(1)} %collective-permute-done.30.refs_15_), channel_id=1, source_target_pairs={{0,2},{1,3},{2,4},{3,5},{4,6},{5,7},{6,8},{7,9},{8,10},{9,11},{10,... | collective-permute-start | bytes 393224 | tf_op jit(solution)/shard_map/ppermute | solution.py:304
  106.8 12.6 %collective-permute-start.35 = (bf16[512,128]{1,0:T(8,128)(2,1)S(1)}, bf16[512,128]{1,0:T(8,128)(2,1)S(1)}, u32[]{:S(2)}, u32[]{:S(2)}) collective-permute-start(bf16[512,128]{1,0:T(8,128)(2,1)S(1)} %collective-permute-done.33.refs_18_), channel_id=1, source_target_pairs={{0,14},{1,15},{2,0},{3,1},{4,2},{5,3},{6,4},{7,5},{8,6},{9,7},{10,... | collective-permute-start | bytes 393224 | tf_op jit(solution)/shard_map/ppermute | solution.py:304
  109.4 9.9 %collective-permute-start.20 = (s32[4,128]{1,0:T(4,128)S(1)}, s32[4,128]{1,0:T(4,128)S(1)}, u32[]{:S(2)}, u32[]{:S(2)}) collective-permute-start(s32[4,128]{1,0:T(4,128)S(1)} %add_add_fusion.2.refs_0_), channel_id=1, source_target_pairs={{0,1},{1,0},{2,3},{3,2},{4,5},{5,4},{6,7},{7,6},{8,9},{9,8},{10,11... | collective-permute-start | bytes 6152 | tf_op jit(solution)/shard_map/ppermute | solution.py:304
  126.6 18.0 %all-to-all-start.1 = ((s16[8,528,128]{2,1,0:T(8,128)(2,1)}), s16[8,528,128]{2,1,0:T(8,128)(2,1)S(1)}, u32[]{:S(2)}, u32[]{:S(2)}) async-start(s16[8,528,128]{2,1,0:T(8,128)(2,1)} %later_products.1), calls=%async_computation.1 | async-start | bytes 2162688 | tf_op jit(solution)/shard_map/all_to_all | solution.py:474
  145.0 3.5 %collective-permute-start.36 = (f32[256,128]{1,0:T(8,128)S(1)}, f32[256,128]{1,0:T(8,128)S(1)}, u32[]{:S(2)}, u32[]{:S(2)}) collective-permute-start(f32[256,128]{1,0:T(8,128)S(1)} %get-tuple-element.29), channel_id=1, source_target_pairs={{0,1},{1,0},{2,3},{3,2},{4,5},{5,4},{6,7},{7,6},{8,9},{9,8},{10,11... | collective-permute-start | bytes 393224 | tf_op jit(solution)/shard_map/ppermute | solution.py:304
  (1 other events, 0.6 us)

commit v8 on v7

--- a/solution.py
+++ b/solution.py
@@ -82,10 +82,13 @@
     return mantissa * jnp.exp2(((upper >> 8) - (127 + 24)).astype(jnp.float32))
 
 
-def seed_kernel(first_ref, ids_ref, counts_ref, pages_ref):
-    total, lanes = ids_ref.shape
+def seed_kernel(where_ref, all_ref, counts_ref, ids_ref, pages_ref, arrived):
+    total, lanes = pages_ref.shape
     pages = counts_ref.shape[0]
-    first = first_ref[0]
+    first = where_ref[0]
+    mine = pl.ds(pl.multiple_of(where_ref[1] * lanes, lanes), lanes)
+    copy = pltpu.make_async_copy(all_ref.at[mine], ids_ref, arrived)
+    copy.start()
     chunk = 256
     counts_ref[...] = jnp.zeros_like(counts_ref)
 
@@ -97,12 +100,6 @@
 
     def rows(i):
         return pl.ds(pl.multiple_of(i * chunk, chunk), chunk)
-
-    def prepare(i, best):
-        page = ids_ref[rows(i), :] - first
-        page = jnp.where((page >= 0) & (page < pages), page, FAR)
-        pages_ref[rows(i), :] = page
-        return jnp.minimum(best, fold(page, jnp.minimum))
 
     def more(carry):
         return carry[1] < pages
@@ -130,7 +127,14 @@
         return later, jnp.min(later)
 
     far = jnp.full((8, lanes), FAR, jnp.int32)
-    best = lax.fori_loop(0, total // chunk, prepare, far)
+    best = far
+    copy.wait()
+    for i in range(0, total, lanes):
+        page = ids_ref[:, i : i + lanes] - first
+        page = jnp.where((page >= 0) & (page < pages), page, FAR)
+        page = page.astype(jnp.float32).T.astype(jnp.int32)
+        pages_ref[i : i + lanes, :] = page
+        best = jnp.minimum(best, fold(page, jnp.minimum))
     start = jnp.min(best, axis=0, keepdims=True)
     lax.while_loop(more, walk, (start, jnp.min(start)))
 
@@ -316,23 +320,29 @@
 
     def gather(block, sums=None):
         rows = block.shape[0]
-        other = across(block)
-        if sums is not None:
-            block = jnp.concatenate([block, encode(sums)])
+        a, b = along(block, 1), along(block, -1)
+        if sums is None:
+            other = across(block)
+        else:
+            other = across(jnp.concatenate([block, encode(sums)]))
+            a, other = tie((a, other))
+            sums = sums + decode(other[rows:])
+            other = jnp.concatenate([other[:rows], encode(sums)])
         pieces, names = [block, other], [(0, 0), (1, 0)]
-        a, b, c, d = block, block, other, other
+        c, d = other, other
         for step in range(1, depth // 2):
-            a, b = along(a, 1), along(b, -1)
+            if step > 1:
+                a, b = along(a, 1), along(b, -1)
             c, d = along(c, 1), along(d, -1)
             pieces += [a, b, c, d]
             names += [(0, -step), (0, step), (1, -step), (1, step)]
-        a = along(a, 1)
+            if sums is not None:
+                sums = sums + (decode(c[rows:]) + decode(d[rows:]))
+        a, d = along(a, 1), along(d, -1)
+        pieces += [a, d]
+        names += [(0, depth // 2), (1, depth // 2)]
         if sums is not None:
-            plane = [p for p, (y, _) in zip(pieces, names) if y == 0] + [a]
-            found = sum(decode(p[rows:]) for p in plane[1:]) + sums
-            sums = found + across(found)
-        pieces += [a, along(d, -1)]
-        names += [(0, depth // 2), (1, depth // 2)]
+            sums = sums + decode(d[rows:])
         return pieces, names, sums
 
     half = columns // 2
@@ -356,7 +366,9 @@
         name="column_sums",
     )(tile_cols, tile_count, in_hbm(tile_values))
 
-    sums = sums + sibling(sums)
+    part = band_tiles // 2
+    given = sibling(lax.dynamic_slice_in_dim(sums, (1 - core) * part, part, 0))
+    sums = given + lax.dynamic_slice_in_dim(sums, core * part, part, 0)
 
     target_total = grid_rows * per
 
@@ -389,17 +401,21 @@
         )
         return facts
 
-    first_page = (row_index * grid_cols + col_index - core) * own_rows
-    ids = lax.dynamic_slice_in_dim(seed_ids, core * half, half, 0).T
-    restart = pl.pallas_call(
-        seed_kernel,
-        out_shape=jax.ShapeDtypeStruct((2 * own_rows, half), jnp.float32),
-        in_specs=[smem(), vmem()],
-        out_specs=vmem(),
-        scratch_shapes=[VMEM(ids.shape, jnp.int32)],
-        compiler_params=params(4),
-        name="seed_counts",
-    )(first_page.reshape(1), ids)
+    def count_seeds(seed_ids):
+        first_page = (row_index * grid_cols + col_index - core) * own_rows
+        return pl.pallas_call(
+            seed_kernel,
+            out_shape=jax.ShapeDtypeStruct((2 * own_rows, half), jnp.float32),
+            in_specs=[smem(), anywhere()],
+            out_specs=vmem(),
+            scratch_shapes=[
+                VMEM((half, seed_total), jnp.int32),
+                VMEM((seed_total, half), jnp.int32),
+                pltpu.SemaphoreType.DMA,
+            ],
+            compiler_params=params(6),
+            name="seed_counts",
+        )(jnp.stack([first_page, core]), seed_ids)
 
     def multiply(pieces, names, sums, facts):
         order = jnp.stack([(high ^ y) * depth + (z + d) % depth for y, d in names])
@@ -449,7 +465,7 @@
             name="later_products",
         )(*facts, order, *tiles, *pieces)
 
-    def update(parts, inverse, scaled):
+    def update(parts, restart, inverse, scaled):
         return pl.pallas_call(
             lambda *refs: current_kernel(scaled, *refs),
             out_shape=jax.ShapeDtypeStruct(
@@ -461,18 +477,23 @@
             name="current",
         )(parts, restart, inverse)
 
-    pieces, names, sums = gather(block, sums)
+    pieces, names, found = gather(block, sums)
+    other = sibling(found)
+    sums = jnp.where(
+        core == 0, jnp.concatenate([found, other]), jnp.concatenate([other, found])
+    )
     parts, inverse = multiply(pieces, names, sums, None)
-    parts, raw = tie((parts, (tile_rows, tile_cols, tile_count)))
+    parts, raw, lists = tie((parts, (tile_rows, tile_cols, tile_count), seed_ids))
+    restart = count_seeds(lists)
     facts = order_tiles(*raw)
     parts = lax.all_to_all(parts, "row", 0, 0, tiled=True)
-    parts, facts = tie((parts, facts))
+    parts, restart, facts = tie((parts, restart, facts))
     facts = (facts, sibling(facts))
-    panel = update(parts, inverse, True)
+    panel = update(parts, restart, inverse, True)
     pieces, names, _ = gather(panel)
     parts = multiply(pieces, names, None, facts)
     parts = lax.all_to_all(parts, "row", 0, 0, tiled=True)
-    current = update(parts, inverse, False)
+    current = update(parts, restart, inverse, False)
     mine = lax.dynamic_slice_in_dim(current, core * own_rows, own_rows, 0)
     theirs = sibling(lax.dynamic_slice_in_dim(current, (1 - core) * own_rows, own_rows, 0))
     return jnp.where(

time: 149 us -> 152 us (1.020)
  starting transfers between devices: 66.7 us -> 73.2 us
  waiting for transfers between devices: 44.7 us -> 40.2 us
  Pallas kernels: 27.4 us -> 29.4 us
    ppermute x37, starting transfers between devices: 54 us -> 64.9 us  [by_col(): return lax.ppermute(value, 'col', pairs)]
    all_to_all x2, starting transfers between devices: 12.8 us -> 8.37 us  [per_device(): parts = lax.all_to_all(parts, 'row', 0, 0, tiled=True)]
    all_to_all x2, waiting for transfers between devices: 22.3 us -> 18.3 us  [per_device(): parts = lax.all_to_all(parts, 'row', 0, 0, tiled=True)]
  transfers between devices with their start and end apart: 39 -> 39, of which waited for: 15 -> 18; matrix products, arithmetic and copies ran while one was open for 2% -> 2% of each run, Pallas kernels for 6% -> 7%
where the time goes in v8:
time: 152 us; the launch traced here: 153 us
  starting transfers between devices  73.2 us (48%)
  waiting for transfers between devices  40.2 us (26%)
  Pallas kernels  29.4 us (19%)
  other arithmetic  3.93 us (3%)
  between operations  3.7 us (2%)
  local copies, waits for them, and re-layouts  2.13 us (1%)
    ppermute x37, starting transfers between devices, by_col(): return lax.ppermute(value, 'col', pairs)  64.9 us
    ppermute x37, waiting for transfers between devices, by_col(): return lax.ppermute(value, 'col', pairs)  21.9 us
    all_to_all x2, waiting for transfers between devices, per_device(): parts = lax.all_to_all(parts, 'row', 0, 0, tiled=True)  18.3 us
    pallas_call x1, Pallas kernels, multiply(): pl.pallas_call(lambda *refs: first_kernel(n, far, *refs), out_shape=(part...  10.1 us
    all_to_all x2, starting transfers between devices, per_device(): parts = lax.all_to_all(parts, 'row', 0, 0, tiled=True)  8.37 us
    pallas_call x1, Pallas kernels, count_seeds(): pl.pallas_call(seed_kernel, out_shape=jax.ShapeDtypeStruct((2 * own_rows,...  8.22 us
    pallas_call x1, Pallas kernels, multiply(): pl.pallas_call(lambda *refs: later_kernel(n, rows, *refs), out_shape=part...  7.63 us
  transfers between devices with their start and end apart: 39, of which 18 were waited for; matrix products, arithmetic and copies ran while one was open for 2% of the time, Pallas kernels for 7%

profile of v8, /device:TPU:1, one launch (start us, length us, event | category | flops | bytes accessed | tf_op | source)
XLA Modules:
  0.0 152.6 jit_solution(5449543637140078112)
XLA Ops:
  0.7 0.7 add_add_fusion.2
  1.5 3.3 %collective-permute-start = (s32[3,96]{1,0:T(4,128)S(1)}, s32[3,96]{1,0:T(4,128)S(1)}, u32[]{:S(2)}, u32[]{:S(2)}) collective-permute-start(s32[3,96]{1,0:T(4,128)S(1)} %add_add_fusion.2), channel_id=1, source_target_pairs={{0,1},{1,0},{2,3},{3,2},{4,5},{5,4},{6,7},{7,6},{8,9},{9,8},{10,11... | collective-permute-start | bytes 3464 | tf_op jit(solution)/shard_map/ppermute | solution.py:308
  4.8 0.7 copy-done.1
  5.5 2.6 %column_sums.1 = f32[64,128]{1,0:T(8,128)S(1)} custom-call(s32[96]{0:T(128)S(1)} %copy-done.1, s32[1]{0:T(128)} %copy.7.count_ref, bf16[96,128,128]{2,1,0:T(8,128)(2,1)} %refs_3_.1), custom_call_target="tpu_custom_call" | custom-call | tf_op jit(solution)/shard_map/column_sums/pallas_call | solution.py:359
  9.0 1.5 collective-permute-done.1
  10.6 3.9 %collective-permute-start.14 = (s16[512,128]{1,0:T(8,128)(2,1)S(1)}, s16[512,128]{1,0:T(8,128)(2,1)S(1)}, u32[]{:S(2)}, u32[]{:S(2)}) collective-permute-start(s16[512,128]{1,0:T(8,128)(2,1)S(1)} %add_select_fusion.refs_10_), channel_id=1, source_target_pairs={{0,14},{1,15},{2,0},{3,1},{4,2},{5,3},{6,4},{7,5},{8,6},{9,7},{10,... | collective-permute-start | bytes 393224 | tf_op jit(solution)/shard_map/ppermute | solution.py:308
  14.5 3.0 %collective-permute-start.4 = (s16[576,128]{1,0:T(8,128)(2,1)S(1)}, s16[576,128]{1,0:T(8,128)(2,1)S(1)}, u32[]{:S(2)}, u32[]{:S(2)}) collective-permute-start(s16[576,128]{1,0:T(8,128)(2,1)S(1)} %pad_add_fusion), channel_id=1, source_target_pairs={{0,16},{1,17},{2,18},{3,19},{4,20},{5,21},{6,22},{7,23},{8,24},{9,... | collective-permute-start | bytes 442376 | tf_op jit(solution)/shard_map/ppermute | solution.py:308
  17.7 0.5 slice.86
  18.2 2.7 %collective-permute-start.16 = (s16[512,128]{1,0:T(8,128)(2,1)S(1)}, s16[512,128]{1,0:T(8,128)(2,1)S(1)}, u32[]{:S(2)}, u32[]{:S(2)}) collective-permute-start(s16[512,128]{1,0:T(8,128)(2,1)S(1)} %collective-permute-done.14.refs_13_), channel_id=1, source_target_pairs={{0,14},{1,15},{2,0},{3,1},{4,2},{5,3},{6,4},{7,5},{8,6},{9,7},{10,... | collective-permute-start | bytes 393224 | tf_op jit(solution)/shard_map/ppermute | solution.py:308
  21.2 2.4 %collective-permute-start.6 = (s16[576,128]{1,0:T(8,128)(2,1)S(1)}, s16[576,128]{1,0:T(8,128)(2,1)S(1)}, u32[]{:S(2)}, u32[]{:S(2)}) collective-permute-start(s16[576,128]{1,0:T(8,128)(2,1)S(1)} %pad_add_fusion.1.refs_11_), channel_id=1, source_target_pairs={{0,14},{1,15},{2,0},{3,1},{4,2},{5,3},{6,4},{7,5},{8,6},{9,7},{10,... | collective-permute-start | bytes 442376 | tf_op jit(solution)/shard_map/ppermute | solution.py:308
  23.7 2.8 %collective-permute-start.18 = (s16[512,128]{1,0:T(8,128)(2,1)S(1)}, s16[512,128]{1,0:T(8,128)(2,1)S(1)}, u32[]{:S(2)}, u32[]{:S(2)}) collective-permute-start(s16[512,128]{1,0:T(8,128)(2,1)S(1)} %collective-permute-done.16.refs_17_), channel_id=1, source_target_pairs={{0,14},{1,15},{2,0},{3,1},{4,2},{5,3},{6,4},{7,5},{8,6},{9,7},{10,... | collective-permute-start | bytes 393224 | tf_op jit(solution)/shard_map/ppermute | solution.py:308
  26.4 4.7 %collective-permute-done.15.refs_16_ = s16[512,128]{1,0:T(8,128)(2,1)S(1)} collective-permute-done((s16[512,128]{1,0:T(8,128)(2,1)S(1)}, s16[512,128]{1,0:T(8,128)(2,1)S(1)}, u32[]{:S(2)}, u32[]{:S(2)}) %collective-permute-start.15) | collective-permute-done | bytes 131104 | tf_op jit(solution)/shard_map/ppermute | solution.py:308
  31.2 2.7 %collective-permute-start.8 = (s16[576,128]{1,0:T(8,128)(2,1)S(1)}, s16[576,128]{1,0:T(8,128)(2,1)S(1)}, u32[]{:S(2)}, u32[]{:S(2)}) collective-permute-start(s16[576,128]{1,0:T(8,128)(2,1)S(1)} %collective-permute-done.6.refs_15_), channel_id=1, source_target_pairs={{0,14},{1,15},{2,0},{3,1},{4,2},{5,3},{6,4},{7,5},{8,6},{9,7},{10,... | collective-permute-start | bytes 442376 | tf_op jit(solution)/shard_map/ppermute | solution.py:308
  33.9 2.3 %collective-permute-done.17.refs_20_ = s16[512,128]{1,0:T(8,128)(2,1)S(1)} collective-permute-done((s16[512,128]{1,0:T(8,128)(2,1)S(1)}, s16[512,128]{1,0:T(8,128)(2,1)S(1)}, u32[]{:S(2)}, u32[]{:S(2)}) %collective-permute-start.17) | collective-permute-done | bytes 131104 | tf_op jit(solution)/shard_map/ppermute | solution.py:308
  36.2 2.8 %collective-permute-start.10 = (s16[576,128]{1,0:T(8,128)(2,1)S(1)}, s16[576,128]{1,0:T(8,128)(2,1)S(1)}, u32[]{:S(2)}, u32[]{:S(2)}) collective-permute-start(s16[576,128]{1,0:T(8,128)(2,1)S(1)} %collective-permute-done.8.refs_19_), channel_id=1, source_target_pairs={{0,14},{1,15},{2,0},{3,1},{4,2},{5,3},{6,4},{7,5},{8,6},{9,7},{10,... | collective-permute-start | bytes 442376 | tf_op jit(solution)/shard_map/ppermute | solution.py:308
  39.0 1.4 collective-permute-done.7.refs_18_
  40.5 0.6 collective-permute-done.10.refs_23_
  41.1 3.1 %collective-permute-start.11 = (s16[576,128]{1,0:T(8,128)(2,1)S(1)}, s16[576,128]{1,0:T(8,128)(2,1)S(1)}, u32[]{:S(2)}, u32[]{:S(2)}) collective-permute-start(s16[576,128]{1,0:T(8,128)(2,1)S(1)} %collective-permute-done.10.refs_23_), channel_id=1, source_target_pairs={{0,14},{1,15},{2,0},{3,1},{4,2},{5,3},{6,4},{7,5},{8,6},{9,7},{10,... | collective-permute-start | bytes 442376 | tf_op jit(solution)/shard_map/ppermute | solution.py:308
  44.3 1.8 %collective-permute-done.9.refs_22_ = s16[576,128]{1,0:T(8,128)(2,1)S(1)} collective-permute-done((s16[576,128]{1,0:T(8,128)(2,1)S(1)}, s16[576,128]{1,0:T(8,128)(2,1)S(1)}, u32[]{:S(2)}, u32[]{:S(2)}) %collective-permute-start.9) | collective-permute-done | bytes 147488 | tf_op jit(solution)/shard_map/ppermute | solution.py:308
  46.0 1.3 collective-permute-done.11.refs_25_
  47.4 7.4 %collective-permute-start.12 = (f32[32,128]{1,0:T(8,128)S(1)}, f32[32,128]{1,0:T(8,128)S(1)}, u32[]{:S(2)}, u32[]{:S(2)}) collective-permute-start(f32[32,128]{1,0:T(8,128)S(1)} %fusion.6), channel_id=1, source_target_pairs={{0,1},{1,0},{2,3},{3,2},{4,5},{5,4},{6,7},{7,6},{8,9},{9,8},{10,11... | collective-permute-start | bytes 49160 | tf_op jit(solution)/shard_map/ppermute | solution.py:308
  54.8 0.6 pad_add_fusion.2.refs_4_
  55.8 0.6 copy-done.8
  56.4 10.1 %first_products.1 = (s16[8,528,128]{2,1,0:T(8,128)(2,1)}, f32[512,128]{1,0:T(8,128)S(1)}) custom-call(s32[96]{0:T(128)S(1)} %copy-done.3, s32[96]{0:T(128)S(1)} %copy-done.2, s32[96]{0:T(128)S(1)} %get-tuple-element.43.refs_2_, s32[96]{0:T(128)S(1)} %get-tuple-element.42.refs_3_, s32[2]{0:T(128)S(1)} %pad_add_fusion.2.refs_4_, s32[1]{0:T(128)} %bitcast.6.refs_5_, ...), custom_call_target="tpu_custom_call" | custom-call | tf_op jit(solution)/shard_map/first_products/pallas_call | solution.py:437
  66.6 4.8 %all-to-all-start = ((s16[8,528,128]{2,1,0:T(8,128)(2,1)}), s16[8,528,128]{2,1,0:T(8,128)(2,1)S(1)}, u32[]{:S(2)}, u32[]{:S(2)}) async-start(s16[8,528,128]{2,1,0:T(8,128)(2,1)} %get-tuple-element.20), calls=%async_computation | async-start | bytes 2162688 | tf_op jit(solution)/shard_map/all_to_all | solution.py:489
  71.5 0.6 fusion.33
  75.2 8.2 %seed_counts.1.refs_1_ = f32[512,128]{1,0:T(8,128)S(1)} custom-call(s32[2]{0:T(128)S(1)} %pad_add_fusion.3.where_ref, s32[256,1024]{1,0:T(8,128)S(1)} %copy-done), custom_call_target="tpu_custom_call" | custom-call | tf_op jit(solution)/shard_map/seed_counts/pallas_call | solution.py:406
  83.6 4.0 %all-to-all-done.refs_0_ = s16[8,528,128]{2,1,0:T(8,128)(2,1)S(1)} async-done(((s16[8,528,128]{2,1,0:T(8,128)(2,1)}), s16[8,528,128]{2,1,0:T(8,128)(2,1)S(1)}, u32[]{:S(2)}, u32[]{:S(2)}) %all-to-all-start) | async-done | bytes 1081376 | tf_op jit(solution)/shard_map/all_to_all | solution.py:489
  88.0 2.3 %collective-permute-start.21 = (bf16[512,128]{1,0:T(8,128)(2,1)S(1)}, bf16[512,128]{1,0:T(8,128)(2,1)S(1)}, u32[]{:S(2)}, u32[]{:S(2)}) collective-permute-start(bf16[512,128]{1,0:T(8,128)(2,1)S(1)} %current.2.refs_5_), channel_id=1, source_target_pairs={{0,16},{1,17},{2,18},{3,19},{4,20},{5,21},{6,22},{7,23},{8,24},{9,... | collective-permute-start | bytes 393224 | tf_op jit(solution)/shard_map/ppermute | solution.py:308
  90.3 3.1 %collective-permute-done.21.refs_6_ = bf16[512,128]{1,0:T(8,128)(2,1)S(1)} collective-permute-done((bf16[512,128]{1,0:T(8,128)(2,1)S(1)}, bf16[512,128]{1,0:T(8,128)(2,1)S(1)}, u32[]{:S(2)}, u32[]{:S(2)}) %collective-permute-start.21) | collective-permute-done | bytes 131104 | tf_op jit(solution)/shard_map/ppermute | solution.py:308
  93.4 3.8 %collective-permute-start.25 = (bf16[512,128]{1,0:T(8,128)(2,1)S(1)}, bf16[512,128]{1,0:T(8,128)(2,1)S(1)}, u32[]{:S(2)}, u32[]{:S(2)}) collective-permute-start(bf16[512,128]{1,0:T(8,128)(2,1)S(1)} %collective-permute-done.21.refs_6_), channel_id=1, source_target_pairs={{0,14},{1,15},{2,0},{3,1},{4,2},{5,3},{6,4},{7,5},{8,6},{9,7},{10,... | collective-permute-start | bytes 393224 | tf_op jit(solution)/shard_map/ppermute | solution.py:308
  97.2 1.4 collective-permute-start.26
  99.1 3.1 %collective-permute-start.29 = (bf16[512,128]{1,0:T(8,128)(2,1)S(1)}, bf16[512,128]{1,0:T(8,128)(2,1)S(1)}, u32[]{:S(2)}, u32[]{:S(2)}) collective-permute-start(bf16[512,128]{1,0:T(8,128)(2,1)S(1)} %collective-permute-done.25.refs_10_), channel_id=1, source_target_pairs={{0,14},{1,15},{2,0},{3,1},{4,2},{5,3},{6,4},{7,5},{8,6},{9,7},{10,... | collective-permute-start | bytes 393224 | tf_op jit(solution)/shard_map/ppermute | solution.py:308
  102.2 1.4 collective-permute-start.27
  103.9 1.1 collective-permute-done.29.refs_14_
  104.9 3.1 %collective-permute-start.33 = (bf16[512,128]{1,0:T(8,128)(2,1)S(1)}, bf16[512,128]{1,0:T(8,128)(2,1)S(1)}, u32[]{:S(2)}, u32[]{:S(2)}) collective-permute-start(bf16[512,128]{1,0:T(8,128)(2,1)S(1)} %collective-permute-done.29.refs_14_), channel_id=1, source_target_pairs={{0,14},{1,15},{2,0},{3,1},{4,2},{5,3},{6,4},{7,5},{8,6},{9,7},{10,... | collective-permute-start | bytes 393224 | tf_op jit(solution)/shard_map/ppermute | solution.py:308
  108.1 1.4 collective-permute-start.31
  109.5 0.8 collective-permute-done.28.refs_13_
  110.4 0.6 collective-permute-done.33.refs_18_
  110.9 3.4 %collective-permute-start.35 = (bf16[512,128]{1,0:T(8,128)(2,1)S(1)}, bf16[512,128]{1,0:T(8,128)(2,1)S(1)}, u32[]{:S(2)}, u32[]{:S(2)}) collective-permute-start(bf16[512,128]{1,0:T(8,128)(2,1)S(1)} %collective-permute-done.33.refs_18_), channel_id=1, source_target_pairs={{0,14},{1,15},{2,0},{3,1},{4,2},{5,3},{6,4},{7,5},{8,6},{9,7},{10,... | collective-permute-start | bytes 393224 | tf_op jit(solution)/shard_map/ppermute | solution.py:308
  114.4 7.1 %collective-permute-start.20 = (s32[4,128]{1,0:T(4,128)S(1)}, s32[4,128]{1,0:T(4,128)S(1)}, u32[]{:S(2)}, u32[]{:S(2)}) collective-permute-start(s32[4,128]{1,0:T(4,128)S(1)} %add_add_fusion.3.refs_0_), channel_id=1, source_target_pairs={{0,1},{1,0},{2,3},{3,2},{4,5},{5,4},{6,7},{7,6},{8,9},{9,8},{10,11... | collective-permute-start | bytes 6152 | tf_op jit(solution)/shard_map/ppermute | solution.py:308
  121.4 0.8 collective-permute-done.20.refs_1_
  122.3 7.6 %later_products.1 = s16[8,528,128]{2,1,0:T(8,128)(2,1)} custom-call(s32[4,128]{1,0:T(4,128)S(1)} %add_add_fusion.3.refs_0_, s32[4,128]{1,0:T(4,128)S(1)} %collective-permute-done.20.refs_1_, s32[16]{0:T(128)S(1)} %stack.113.refs_6_.refs_2_, bf16[96,128,128]{2,1,0:T(8,128)(2,1)} %refs_3_.1, bf16[96,128,128]{2,1,0:T(8,128)(2,1)} %collective-permute-done.13.refs_9_.refs_4_, ...), custom_call_target="tpu_custom_call" | custom-call | tf_op jit(solution)/shard_map/later_products/pallas_call | solution.py:458
  129.9 3.6 %all-to-all-start.1 = ((s16[8,528,128]{2,1,0:T(8,128)(2,1)}), s16[8,528,128]{2,1,0:T(8,128)(2,1)S(1)}, u32[]{:S(2)}, u32[]{:S(2)}) async-start(s16[8,528,128]{2,1,0:T(8,128)(2,1)} %later_products.1), calls=%async_computation.1 | async-start | bytes 2162688 | tf_op jit(solution)/shard_map/all_to_all | solution.py:495
  133.5 14.4 %all-to-all-done.1.refs_0_ = s16[8,528,128]{2,1,0:T(8,128)(2,1)S(1)} async-done(((s16[8,528,128]{2,1,0:T(8,128)(2,1)}), s16[8,528,128]{2,1,0:T(8,128)(2,1)S(1)}, u32[]{:S(2)}, u32[]{:S(2)}) %all-to-all-start.1) | async-done | bytes 1081376 | tf_op jit(solution)/shard_map/all_to_all | solution.py:495
  148.3 2.6 %collective-permute-start.36 = (f32[256,128]{1,0:T(8,128)S(1)}, f32[256,128]{1,0:T(8,128)S(1)}, u32[]{:S(2)}, u32[]{:S(2)}) collective-permute-start(f32[256,128]{1,0:T(8,128)S(1)} %get-tuple-element.39), channel_id=1, source_target_pairs={{0,1},{1,0},{2,3},{3,2},{4,5},{5,4},{6,7},{7,6},{8,9},{9,8},{10,11... | collective-permute-start | bytes 393224 | tf_op jit(solution)/shard_map/ppermute | solution.py:308
  150.8 1.0 collective-permute-done.36
  151.8 0.7 maximum_select_fusion
  (102 shorter events, 4.5 us)
Async XLA Ops:
  1.5 16.2 %collective-permute-start = (s32[3,96]{1,0:T(4,128)S(1)}, s32[3,96]{1,0:T(4,128)S(1)}, u32[]{:S(2)}, u32[]{:S(2)}) collective-permute-start(s32[3,96]{1,0:T(4,128)S(1)} %add_add_fusion.2), channel_id=1, source_target_pairs={{0,1},{1,0},{2,3},{3,2},{4,5},{5,4},{6,7},{7,6},{8,9},{9,8},{10,11... | collective-permute-start | bytes 3464 | tf_op jit(solution)/shard_map/ppermute | solution.py:308
  4.7 51.0 %collective-permute-start.13 = (bf16[96,128,128]{2,1,0:T(8,128)(2,1)}, bf16[96,128,128]{2,1,0:T(8,128)(2,1)}, u32[]{:S(2)}, u32[]{:S(2)}) collective-permute-start(bf16[96,128,128]{2,1,0:T(8,128)(2,1)} %refs_3_.1), channel_id=1, source_target_pairs={{0,1},{1,0},{2,3},{3,2},{4,5},{5,4},{6,7},{7,6},{8,9},{9,8},{10,11... | collective-permute-start | bytes 9437192 | tf_op jit(solution)/shard_map/ppermute | solution.py:308
  5.5 3.0 %copy-start.4 = (f32[256,256]{1,0:T(8,128)S(1)}, f32[256,256]{1,0:T(8,128)}, u32[]{:S(2)}) copy-start(f32[256,256]{1,0:T(8,128)} %param.6) | copy-start | bytes 786436
  8.1 2.3 %collective-permute-start.1 = (f32[32,128]{1,0:T(8,128)S(1)}, f32[32,128]{1,0:T(8,128)S(1)}, u32[]{:S(2)}, u32[]{:S(2)}) collective-permute-start(f32[32,128]{1,0:T(8,128)S(1)} %constant_dynamic-slice_fusion.4), channel_id=1, source_target_pairs={{0,1},{1,0},{2,3},{3,2},{4,5},{5,4},{6,7},{7,6},{8,9},{9,8},{10,11... | collective-permute-start | bytes 49160 | tf_op jit(solution)/shard_map/ppermute | solution.py:308
  8.6 1.9 %collective-permute-start.2 = (s16[256,128]{1,0:T(8,128)(2,1)S(1)}, s16[256,128]{1,0:T(8,128)(2,1)S(1)}, u32[]{:S(2)}, u32[]{:S(2)}) collective-permute-start(s16[256,128]{1,0:T(8,128)(2,1)S(1)} %get-tuple-element.41), channel_id=1, source_target_pairs={{0,1},{1,0},{2,3},{3,2},{4,5},{5,4},{6,7},{7,6},{8,9},{9,8},{10,11... | collective-permute-start | bytes 196616 | tf_op jit(solution)/shard_map/ppermute | solution.py:308
  10.5 45.9 %copy-start.2 = (s32[96]{0:T(128)S(1)}, s32[96]{0:T(128)}, u32[]{:S(2)}) copy-start(s32[96]{0:T(128)} %refs_1_.1) | copy-start | bytes 1156
  10.6 45.8 %copy-start.3 = (s32[96]{0:T(128)S(1)}, s32[96]{0:T(128)}, u32[]{:S(2)}) copy-start(s32[96]{0:T(128)} %refs_0_.1) | copy-start | bytes 1156
  10.6 7.6 %collective-permute-start.14 = (s16[512,128]{1,0:T(8,128)(2,1)S(1)}, s16[512,128]{1,0:T(8,128)(2,1)S(1)}, u32[]{:S(2)}, u32[]{:S(2)}) collective-permute-start(s16[512,128]{1,0:T(8,128)(2,1)S(1)} %add_select_fusion.refs_10_), channel_id=1, source_target_pairs={{0,14},{1,15},{2,0},{3,1},{4,2},{5,3},{6,4},{7,5},{8,6},{9,7},{10,... | collective-permute-start | bytes 393224 | tf_op jit(solution)/shard_map/ppermute | solution.py:308
  14.5 6.4 %collective-permute-start.3 = (s16[512,128]{1,0:T(8,128)(2,1)S(1)}, s16[512,128]{1,0:T(8,128)(2,1)S(1)}, u32[]{:S(2)}, u32[]{:S(2)}) collective-permute-start(s16[512,128]{1,0:T(8,128)(2,1)S(1)} %add_select_fusion.refs_10_), channel_id=1, source_target_pairs={{0,2},{1,3},{2,4},{3,5},{4,6},{5,7},{6,8},{7,9},{8,10},{9,11},{10,... | collective-permute-start | bytes 393224 | tf_op jit(solution)/shard_map/ppermute | solution.py:308
  14.5 6.6 %collective-permute-start.4 = (s16[576,128]{1,0:T(8,128)(2,1)S(1)}, s16[576,128]{1,0:T(8,128)(2,1)S(1)}, u32[]{:S(2)}, u32[]{:S(2)}) collective-permute-start(s16[576,128]{1,0:T(8,128)(2,1)S(1)} %pad_add_fusion), channel_id=1, source_target_pairs={{0,16},{1,17},{2,18},{3,19},{4,20},{5,21},{6,22},{7,23},{8,24},{9,... | collective-permute-start | bytes 442376 | tf_op jit(solution)/shard_map/ppermute | solution.py:308
  18.2 5.5 %collective-permute-start.16 = (s16[512,128]{1,0:T(8,128)(2,1)S(1)}, s16[512,128]{1,0:T(8,128)(2,1)S(1)}, u32[]{:S(2)}, u32[]{:S(2)}) collective-permute-start(s16[512,128]{1,0:T(8,128)(2,1)S(1)} %collective-permute-done.14.refs_13_), channel_id=1, source_target_pairs={{0,14},{1,15},{2,0},{3,1},{4,2},{5,3},{6,4},{7,5},{8,6},{9,7},{10,... | collective-permute-start | bytes 393224 | tf_op jit(solution)/shard_map/ppermute | solution.py:308
  21.2 9.9 %collective-permute-start.6 = (s16[576,128]{1,0:T(8,128)(2,1)S(1)}, s16[576,128]{1,0:T(8,128)(2,1)S(1)}, u32[]{:S(2)}, u32[]{:S(2)}) collective-permute-start(s16[576,128]{1,0:T(8,128)(2,1)S(1)} %pad_add_fusion.1.refs_11_), channel_id=1, source_target_pairs={{0,14},{1,15},{2,0},{3,1},{4,2},{5,3},{6,4},{7,5},{8,6},{9,7},{10,... | collective-permute-start | bytes 442376 | tf_op jit(solution)/shard_map/ppermute | solution.py:308
  23.7 10.2 %collective-permute-start.5 = (s16[576,128]{1,0:T(8,128)(2,1)S(1)}, s16[576,128]{1,0:T(8,128)(2,1)S(1)}, u32[]{:S(2)}, u32[]{:S(2)}) collective-permute-start(s16[576,128]{1,0:T(8,128)(2,1)S(1)} %pad_add_fusion.1.refs_11_), channel_id=1, source_target_pairs={{0,2},{1,3},{2,4},{3,5},{4,6},{5,7},{6,8},{7,9},{8,10},{9,11},{10,... | collective-permute-start | bytes 442376 | tf_op jit(solution)/shard_map/ppermute | solution.py:308
  23.7 7.5 %collective-permute-start.15 = (s16[512,128]{1,0:T(8,128)(2,1)S(1)}, s16[512,128]{1,0:T(8,128)(2,1)S(1)}, u32[]{:S(2)}, u32[]{:S(2)}) collective-permute-start(s16[512,128]{1,0:T(8,128)(2,1)S(1)} %collective-permute-done.3.refs_12_), channel_id=1, source_target_pairs={{0,2},{1,3},{2,4},{3,5},{4,6},{5,7},{6,8},{7,9},{8,10},{9,11},{10,... | collective-permute-start | bytes 393224 | tf_op jit(solution)/shard_map/ppermute | solution.py:308
  23.7 32.0 %collective-permute-start.18 = (s16[512,128]{1,0:T(8,128)(2,1)S(1)}, s16[512,128]{1,0:T(8,128)(2,1)S(1)}, u32[]{:S(2)}, u32[]{:S(2)}) collective-permute-start(s16[512,128]{1,0:T(8,128)(2,1)S(1)} %collective-permute-done.16.refs_17_), channel_id=1, source_target_pairs={{0,14},{1,15},{2,0},{3,1},{4,2},{5,3},{6,4},{7,5},{8,6},{9,7},{10,... | collective-permute-start | bytes 393224 | tf_op jit(solution)/shard_map/ppermute | solution.py:308
  31.2 5.0 %collective-permute-start.17 = (s16[512,128]{1,0:T(8,128)(2,1)S(1)}, s16[512,128]{1,0:T(8,128)(2,1)S(1)}, u32[]{:S(2)}, u32[]{:S(2)}) collective-permute-start(s16[512,128]{1,0:T(8,128)(2,1)S(1)} %collective-permute-done.15.refs_16_), channel_id=1, source_target_pairs={{0,2},{1,3},{2,4},{3,5},{4,6},{5,7},{6,8},{7,9},{8,10},{9,11},{10,... | collective-permute-start | bytes 393224 | tf_op jit(solution)/shard_map/ppermute | solution.py:308
  31.2 5.0 %collective-permute-start.8 = (s16[576,128]{1,0:T(8,128)(2,1)S(1)}, s16[576,128]{1,0:T(8,128)(2,1)S(1)}, u32[]{:S(2)}, u32[]{:S(2)}) collective-permute-start(s16[576,128]{1,0:T(8,128)(2,1)S(1)} %collective-permute-done.6.refs_15_), channel_id=1, source_target_pairs={{0,14},{1,15},{2,0},{3,1},{4,2},{5,3},{6,4},{7,5},{8,6},{9,7},{10,... | collective-permute-start | bytes 442376 | tf_op jit(solution)/shard_map/ppermute | solution.py:308
  33.8 6.6 %collective-permute-start.7 = (s16[576,128]{1,0:T(8,128)(2,1)S(1)}, s16[576,128]{1,0:T(8,128)(2,1)S(1)}, u32[]{:S(2)}, u32[]{:S(2)}) collective-permute-start(s16[576,128]{1,0:T(8,128)(2,1)S(1)} %collective-permute-done.5.refs_14_), channel_id=1, source_target_pairs={{0,2},{1,3},{2,4},{3,5},{4,6},{5,7},{6,8},{7,9},{8,10},{9,11},{10,... | collective-permute-start | bytes 442376 | tf_op jit(solution)/shard_map/ppermute | solution.py:308
  36.2 19.6 %copy-start.9 = (s16[512,128]{1,0:T(8,128)(2,1)}, s16[512,128]{1,0:T(8,128)(2,1)S(1)}, u32[]{:S(2)}) copy-start(s16[512,128]{1,0:T(8,128)(2,1)S(1)} %collective-permute-done.17.refs_20_) | copy-start | bytes 393220
  36.2 19.5 %collective-permute-start.19 = (s16[512,128]{1,0:T(8,128)(2,1)S(1)}, s16[512,128]{1,0:T(8,128)(2,1)S(1)}, u32[]{:S(2)}, u32[]{:S(2)}) collective-permute-start(s16[512,128]{1,0:T(8,128)(2,1)S(1)} %collective-permute-done.17.refs_20_), channel_id=1, source_target_pairs={{0,2},{1,3},{2,4},{3,5},{4,6},{5,7},{6,8},{7,9},{8,10},{9,11},{10,... | collective-permute-start | bytes 393224 | tf_op jit(solution)/shard_map/ppermute | solution.py:308
  36.2 4.9 %collective-permute-start.10 = (s16[576,128]{1,0:T(8,128)(2,1)S(1)}, s16[576,128]{1,0:T(8,128)(2,1)S(1)}, u32[]{:S(2)}, u32[]{:S(2)}) collective-permute-start(s16[576,128]{1,0:T(8,128)(2,1)S(1)} %collective-permute-done.8.refs_19_), channel_id=1, source_target_pairs={{0,14},{1,15},{2,0},{3,1},{4,2},{5,3},{6,4},{7,5},{8,6},{9,7},{10,... | collective-permute-start | bytes 442376 | tf_op jit(solution)/shard_map/ppermute | solution.py:308
  40.5 5.6 %collective-permute-start.9 = (s16[576,128]{1,0:T(8,128)(2,1)S(1)}, s16[576,128]{1,0:T(8,128)(2,1)S(1)}, u32[]{:S(2)}, u32[]{:S(2)}) collective-permute-start(s16[576,128]{1,0:T(8,128)(2,1)S(1)} %collective-permute-done.7.refs_18_), channel_id=1, source_target_pairs={{0,2},{1,3},{2,4},{3,5},{4,6},{5,7},{6,8},{7,9},{8,10},{9,11},{10,... | collective-permute-start | bytes 442376 | tf_op jit(solution)/shard_map/ppermute | solution.py:308
  41.1 14.6 %copy-start.5 = (s16[576,128]{1,0:T(8,128)(2,1)}, s16[576,128]{1,0:T(8,128)(2,1)S(1)}, u32[]{:S(2)}) copy-start(s16[576,128]{1,0:T(8,128)(2,1)S(1)} %collective-permute-done.10.refs_23_) | copy-start | bytes 442372
  41.1 6.2 %collective-permute-start.11 = (s16[576,128]{1,0:T(8,128)(2,1)S(1)}, s16[576,128]{1,0:T(8,128)(2,1)S(1)}, u32[]{:S(2)}, u32[]{:S(2)}) collective-permute-start(s16[576,128]{1,0:T(8,128)(2,1)S(1)} %collective-permute-done.10.refs_23_), channel_id=1, source_target_pairs={{0,14},{1,15},{2,0},{3,1},{4,2},{5,3},{6,4},{7,5},{8,6},{9,7},{10,... | collective-permute-start | bytes 442376 | tf_op jit(solution)/shard_map/ppermute | solution.py:308
  46.0 9.7 %copy-start.6 = (s16[576,128]{1,0:T(8,128)(2,1)}, s16[576,128]{1,0:T(8,128)(2,1)S(1)}, u32[]{:S(2)}) copy-start(s16[576,128]{1,0:T(8,128)(2,1)S(1)} %collective-permute-done.9.refs_22_) | copy-start | bytes 442372
  47.3 8.4 %copy-start.7 = (s16[576,128]{1,0:T(8,128)(2,1)}, s16[576,128]{1,0:T(8,128)(2,1)S(1)}, u32[]{:S(2)}) copy-start(s16[576,128]{1,0:T(8,128)(2,1)S(1)} %collective-permute-done.11.refs_25_) | copy-start | bytes 442372
  47.4 8.3 %collective-permute-start.12 = (f32[32,128]{1,0:T(8,128)S(1)}, f32[32,128]{1,0:T(8,128)S(1)}, u32[]{:S(2)}, u32[]{:S(2)}) collective-permute-start(f32[32,128]{1,0:T(8,128)S(1)} %fusion.6), channel_id=1, source_target_pairs={{0,1},{1,0},{2,3},{3,2},{4,5},{5,4},{6,7},{7,6},{8,9},{9,8},{10,11... | collective-permute-start | bytes 49160 | tf_op jit(solution)/shard_map/ppermute | solution.py:308
  55.7 0.7 copy-start.10
  66.6 8.6 %copy-start = (s32[256,1024]{1,0:T(8,128)S(1)}, s32[256,1024]{1,0:T(8,128)}, u32[]{:S(2)}) copy-start(s32[256,1024]{1,0:T(8,128)} %all_ref) | copy-start | bytes 3145732
  66.6 21.0 %all-to-all-start = ((s16[8,528,128]{2,1,0:T(8,128)(2,1)}), s16[8,528,128]{2,1,0:T(8,128)(2,1)S(1)}, u32[]{:S(2)}, u32[]{:S(2)}) async-start(s16[8,528,128]{2,1,0:T(8,128)(2,1)} %get-tuple-element.20), calls=%async_computation | async-start | bytes 2162688 | tf_op jit(solution)/shard_map/all_to_all | solution.py:489
  88.0 5.4 %collective-permute-start.21 = (bf16[512,128]{1,0:T(8,128)(2,1)S(1)}, bf16[512,128]{1,0:T(8,128)(2,1)S(1)}, u32[]{:S(2)}, u32[]{:S(2)}) collective-permute-start(bf16[512,128]{1,0:T(8,128)(2,1)S(1)} %current.2.refs_5_), channel_id=1, source_target_pairs={{0,16},{1,17},{2,18},{3,19},{4,20},{5,21},{6,22},{7,23},{8,24},{9,... | collective-permute-start | bytes 393224 | tf_op jit(solution)/shard_map/ppermute | solution.py:308
  90.3 6.9 %collective-permute-start.22 = (bf16[512,128]{1,0:T(8,128)(2,1)S(1)}, bf16[512,128]{1,0:T(8,128)(2,1)S(1)}, u32[]{:S(2)}, u32[]{:S(2)}) collective-permute-start(bf16[512,128]{1,0:T(8,128)(2,1)S(1)} %current.2.refs_5_), channel_id=1, source_target_pairs={{0,2},{1,3},{2,4},{3,5},{4,6},{5,7},{6,8},{7,9},{8,10},{9,11},{10,... | collective-permute-start | bytes 393224 | tf_op jit(solution)/shard_map/ppermute | solution.py:308
  93.4 5.7 %collective-permute-start.25 = (bf16[512,128]{1,0:T(8,128)(2,1)S(1)}, bf16[512,128]{1,0:T(8,128)(2,1)S(1)}, u32[]{:S(2)}, u32[]{:S(2)}) collective-permute-start(bf16[512,128]{1,0:T(8,128)(2,1)S(1)} %collective-permute-done.21.refs_6_), channel_id=1, source_target_pairs={{0,14},{1,15},{2,0},{3,1},{4,2},{5,3},{6,4},{7,5},{8,6},{9,7},{10,... | collective-permute-start | bytes 393224 | tf_op jit(solution)/shard_map/ppermute | solution.py:308
  97.2 5.0 %collective-permute-start.23 = (bf16[512,128]{1,0:T(8,128)(2,1)S(1)}, bf16[512,128]{1,0:T(8,128)(2,1)S(1)}, u32[]{:S(2)}, u32[]{:S(2)}) collective-permute-start(bf16[512,128]{1,0:T(8,128)(2,1)S(1)} %current.2.refs_5_), channel_id=1, source_target_pairs={{0,14},{1,15},{2,0},{3,1},{4,2},{5,3},{6,4},{7,5},{8,6},{9,7},{10,... | collective-permute-start | bytes 393224 | tf_op jit(solution)/shard_map/ppermute | solution.py:308
  97.2 6.4 %collective-permute-start.26 = (bf16[512,128]{1,0:T(8,128)(2,1)S(1)}, bf16[512,128]{1,0:T(8,128)(2,1)S(1)}, u32[]{:S(2)}, u32[]{:S(2)}) collective-permute-start(bf16[512,128]{1,0:T(8,128)(2,1)S(1)} %collective-permute-done.22.refs_7_), channel_id=1, source_target_pairs={{0,2},{1,3},{2,4},{3,5},{4,6},{5,7},{6,8},{7,9},{8,10},{9,11},{10,... | collective-permute-start | bytes 393224 | tf_op jit(solution)/shard_map/ppermute | solution.py:308
  98.6 5.0 %collective-permute-start.24 = (bf16[512,128]{1,0:T(8,128)(2,1)S(1)}, bf16[512,128]{1,0:T(8,128)(2,1)S(1)}, u32[]{:S(2)}, u32[]{:S(2)}) collective-permute-start(bf16[512,128]{1,0:T(8,128)(2,1)S(1)} %collective-permute-done.21.refs_6_), channel_id=1, source_target_pairs={{0,2},{1,3},{2,4},{3,5},{4,6},{5,7},{6,8},{7,9},{8,10},{9,11},{10,... | collective-permute-start | bytes 393224 | tf_op jit(solution)/shard_map/ppermute | solution.py:308
  99.1 5.8 %collective-permute-start.29 = (bf16[512,128]{1,0:T(8,128)(2,1)S(1)}, bf16[512,128]{1,0:T(8,128)(2,1)S(1)}, u32[]{:S(2)}, u32[]{:S(2)}) collective-permute-start(bf16[512,128]{1,0:T(8,128)(2,1)S(1)} %collective-permute-done.25.refs_10_), channel_id=1, source_target_pairs={{0,14},{1,15},{2,0},{3,1},{4,2},{5,3},{6,4},{7,5},{8,6},{9,7},{10,... | collective-permute-start | bytes 393224 | tf_op jit(solution)/shard_map/ppermute | solution.py:308
  102.2 5.8 %collective-permute-start.27 = (bf16[512,128]{1,0:T(8,128)(2,1)S(1)}, bf16[512,128]{1,0:T(8,128)(2,1)S(1)}, u32[]{:S(2)}, u32[]{:S(2)}) collective-permute-start(bf16[512,128]{1,0:T(8,128)(2,1)S(1)} %collective-permute-done.23.refs_8_), channel_id=1, source_target_pairs={{0,14},{1,15},{2,0},{3,1},{4,2},{5,3},{6,4},{7,5},{8,6},{9,7},{10,... | collective-permute-start | bytes 393224 | tf_op jit(solution)/shard_map/ppermute | solution.py:308
  103.6 5.8 %collective-permute-start.30 = (bf16[512,128]{1,0:T(8,128)(2,1)S(1)}, bf16[512,128]{1,0:T(8,128)(2,1)S(1)}, u32[]{:S(2)}, u32[]{:S(2)}) collective-permute-start(bf16[512,128]{1,0:T(8,128)(2,1)S(1)} %collective-permute-done.26.refs_11_), channel_id=1, source_target_pairs={{0,2},{1,3},{2,4},{3,5},{4,6},{5,7},{6,8},{7,9},{8,10},{9,11},{10,... | collective-permute-start | bytes 393224 | tf_op jit(solution)/shard_map/ppermute | solution.py:308
  103.7 6.7 %collective-permute-start.28 = (bf16[512,128]{1,0:T(8,128)(2,1)S(1)}, bf16[512,128]{1,0:T(8,128)(2,1)S(1)}, u32[]{:S(2)}, u32[]{:S(2)}) collective-permute-start(bf16[512,128]{1,0:T(8,128)(2,1)S(1)} %collective-permute-done.24.refs_9_), channel_id=1, source_target_pairs={{0,2},{1,3},{2,4},{3,5},{4,6},{5,7},{6,8},{7,9},{8,10},{9,11},{10,... | collective-permute-start | bytes 393224 | tf_op jit(solution)/shard_map/ppermute | solution.py:308
  104.9 6.0 %collective-permute-start.33 = (bf16[512,128]{1,0:T(8,128)(2,1)S(1)}, bf16[512,128]{1,0:T(8,128)(2,1)S(1)}, u32[]{:S(2)}, u32[]{:S(2)}) collective-permute-start(bf16[512,128]{1,0:T(8,128)(2,1)S(1)} %collective-permute-done.29.refs_14_), channel_id=1, source_target_pairs={{0,14},{1,15},{2,0},{3,1},{4,2},{5,3},{6,4},{7,5},{8,6},{9,7},{10,... | collective-permute-start | bytes 393224 | tf_op jit(solution)/shard_map/ppermute | solution.py:308
  108.1 14.2 %collective-permute-start.31 = (bf16[512,128]{1,0:T(8,128)(2,1)S(1)}, bf16[512,128]{1,0:T(8,128)(2,1)S(1)}, u32[]{:S(2)}, u32[]{:S(2)}) collective-permute-start(bf16[512,128]{1,0:T(8,128)(2,1)S(1)} %collective-permute-done.27.refs_12_), channel_id=1, source_target_pairs={{0,14},{1,15},{2,0},{3,1},{4,2},{5,3},{6,4},{7,5},{8,6},{9,7},{10,... | collective-permute-start | bytes 393224 | tf_op jit(solution)/shard_map/ppermute | solution.py:308
  109.5 12.8 %collective-permute-start.34 = (bf16[512,128]{1,0:T(8,128)(2,1)S(1)}, bf16[512,128]{1,0:T(8,128)(2,1)S(1)}, u32[]{:S(2)}, u32[]{:S(2)}) collective-permute-start(bf16[512,128]{1,0:T(8,128)(2,1)S(1)} %collective-permute-done.30.refs_15_), channel_id=1, source_target_pairs={{0,2},{1,3},{2,4},{3,5},{4,6},{5,7},{6,8},{7,9},{8,10},{9,11},{10,... | collective-permute-start | bytes 393224 | tf_op jit(solution)/shard_map/ppermute | solution.py:308
  110.4 11.9 %collective-permute-start.32 = (bf16[512,128]{1,0:T(8,128)(2,1)S(1)}, bf16[512,128]{1,0:T(8,128)(2,1)S(1)}, u32[]{:S(2)}, u32[]{:S(2)}) collective-permute-start(bf16[512,128]{1,0:T(8,128)(2,1)S(1)} %collective-permute-done.28.refs_13_), channel_id=1, source_target_pairs={{0,2},{1,3},{2,4},{3,5},{4,6},{5,7},{6,8},{7,9},{8,10},{9,11},{10,... | collective-permute-start | bytes 393224 | tf_op jit(solution)/shard_map/ppermute | solution.py:308
  110.9 11.3 %collective-permute-start.35 = (bf16[512,128]{1,0:T(8,128)(2,1)S(1)}, bf16[512,128]{1,0:T(8,128)(2,1)S(1)}, u32[]{:S(2)}, u32[]{:S(2)}) collective-permute-start(bf16[512,128]{1,0:T(8,128)(2,1)S(1)} %collective-permute-done.33.refs_18_), channel_id=1, source_target_pairs={{0,14},{1,15},{2,0},{3,1},{4,2},{5,3},{6,4},{7,5},{8,6},{9,7},{10,... | collective-permute-start | bytes 393224 | tf_op jit(solution)/shard_map/ppermute | solution.py:308
  114.4 7.9 %collective-permute-start.20 = (s32[4,128]{1,0:T(4,128)S(1)}, s32[4,128]{1,0:T(4,128)S(1)}, u32[]{:S(2)}, u32[]{:S(2)}) collective-permute-start(s32[4,128]{1,0:T(4,128)S(1)} %add_add_fusion.3.refs_0_), channel_id=1, source_target_pairs={{0,1},{1,0},{2,3},{3,2},{4,5},{5,4},{6,7},{7,6},{8,9},{9,8},{10,11... | collective-permute-start | bytes 6152 | tf_op jit(solution)/shard_map/ppermute | solution.py:308
  129.9 18.0 %all-to-all-start.1 = ((s16[8,528,128]{2,1,0:T(8,128)(2,1)}), s16[8,528,128]{2,1,0:T(8,128)(2,1)S(1)}, u32[]{:S(2)}, u32[]{:S(2)}) async-start(s16[8,528,128]{2,1,0:T(8,128)(2,1)} %later_products.1), calls=%async_computation.1 | async-start | bytes 2162688 | tf_op jit(solution)/shard_map/all_to_all | solution.py:495
  148.3 3.5 %collective-permute-start.36 = (f32[256,128]{1,0:T(8,128)S(1)}, f32[256,128]{1,0:T(8,128)S(1)}, u32[]{:S(2)}, u32[]{:S(2)}) collective-permute-start(f32[256,128]{1,0:T(8,128)S(1)} %get-tuple-element.39), channel_id=1, source_target_pairs={{0,1},{1,0},{2,3},{3,2},{4,5},{5,4},{6,7},{7,6},{8,9},{9,8},{10,11... | collective-permute-start | bytes 393224 | tf_op jit(solution)/shard_map/ppermute | solution.py:308
  (2 other events, 1.3 us)

commit v9 on v8

--- a/solution.py
+++ b/solution.py
@@ -173,32 +173,6 @@
             return carry
 
         lax.fori_loop(0, (pairs + unroll - 1) // unroll, group, 0)
-
-
-def single_products(slot_refs, count_ref, core_ref, copies, tiles, panel, total):
-    unroll = 16
-    slots = tiles.shape[0] // 2
-    dummy = total.shape[0] - 1
-    per = 2 * BT
-    band = panel.shape[0] - 1
-    for which in range(2):
-        copies[which].wait()
-        rows_ref, cols_ref = slot_refs[2 * which : 2 * which + 2]
-        owner = core_ref[0] if which == 0 else 1 - core_ref[0]
-
-        def group(g, carry, which=which, rows_ref=rows_ref, cols_ref=cols_ref, owner=owner):
-            for u in range(unroll):
-                k = g * unroll + u
-                target = rows_ref[k] // band * per + owner * BT + rows_ref[k] % BT
-                target = jnp.where(k < count_ref[which], target, dummy)
-                total[target] += jnp.dot(
-                    tiles[which * slots + k],
-                    panel[cols_ref[k] % band],
-                    preferred_element_type=jnp.float32,
-                )
-            return carry
-
-        lax.fori_loop(0, (count_ref[which] + unroll - 1) // unroll, group, 0)
 
 
 def round_parts(total, out_ref):
@@ -224,9 +198,9 @@
 
 
 def first_kernel(pieces, far, *refs):
-    slot_refs, (count_ref, core_ref, chip_ref, sums_ref, own_ref, sib_ref) = refs[:4], refs[4:10]
-    piece_refs = list(refs[10 : 10 + pieces])
-    out_ref, inverse_ref, panel, total, tiles, arrived, ordered, brought, near = refs[10 + pieces :]
+    own_facts, sib_facts, chip_ref, sums_ref, own_ref, sib_ref = refs[:6]
+    piece_refs = list(refs[6 : 6 + pieces])
+    out_ref, inverse_ref, panel, total, tiles, arrived, ordered, brought, near = refs[6 + pieces :]
     brings = {}
     for i in range(far):
         p = pieces - far + i
@@ -251,7 +225,8 @@
             panel[chip_ref[p] * per + t] = (score * column).astype(jnp.bfloat16)
             if p == 0:
                 inverse_ref[t * TILE : (t + 1) * TILE, :] = jnp.broadcast_to(column, (TILE, LANES))
-    single_products(slot_refs, count_ref, core_ref, copies, tiles, panel, total)
+    panel[pieces * per] = jnp.zeros((TILE, LANES), jnp.bfloat16)
+    products((own_facts, sib_facts), copies, tiles, panel, total)
     round_parts(total, out_ref)
 
 
@@ -318,32 +293,28 @@
 
     tie = lax.optimization_barrier
 
-    def gather(block, sums=None):
+    def gather(block, sums=None, later=None):
         rows = block.shape[0]
-        a, b = along(block, 1), along(block, -1)
-        if sums is None:
-            other = across(block)
-        else:
-            other = across(jnp.concatenate([block, encode(sums)]))
-            a, other = tie((a, other))
-            sums = sums + decode(other[rows:])
-            other = jnp.concatenate([other[:rows], encode(sums)])
+        beside = None
+        if sums is not None:
+            block = jnp.concatenate([block, encode(sums)])
+        other = across(block)
         pieces, names = [block, other], [(0, 0), (1, 0)]
-        c, d = other, other
+        a, b, c, d = block, block, other, other
         for step in range(1, depth // 2):
-            if step > 1:
-                a, b = along(a, 1), along(b, -1)
+            a, b = along(a, 1), along(b, -1)
             c, d = along(c, 1), along(d, -1)
+            if later is not None and step == depth // 2 - 1:
+                a, d, raw = tie((a, d, (tile_rows, tile_cols, tile_count)))
+                beside = later(*raw)
             pieces += [a, b, c, d]
             names += [(0, -step), (0, step), (1, -step), (1, step)]
-            if sums is not None:
-                sums = sums + (decode(c[rows:]) + decode(d[rows:]))
-        a, d = along(a, 1), along(d, -1)
-        pieces += [a, d]
+        pieces += [along(a, 1), along(d, -1)]
         names += [(0, depth // 2), (1, depth // 2)]
         if sums is not None:
-            sums = sums + decode(d[rows:])
-        return pieces, names, sums
+            for piece in pieces[1:]:
+                sums = sums + decode(piece[rows:])
+        return pieces, names, sums, beside
 
     half = columns // 2
     code = ((scores - LOW) * (STEPS / (HIGH - LOW)) + 0.5).astype(jnp.int32)
@@ -353,8 +324,6 @@
     block = jnp.where(
         core == 0, jnp.concatenate([mine, theirs]), jnp.concatenate([theirs, mine])
     )
-    slots_here = jnp.stack([tile_rows, tile_cols, jnp.broadcast_to(tile_count, (slots,))])
-    slots_there = sibling(slots_here)
     sib_tiles = sibling(tile_values)
     sums = pl.pallas_call(
         column_kernel,
@@ -433,11 +402,10 @@
             far = 6
             pieces = pieces[: n - far] + [in_hbm(piece) for piece in pieces[n - far :]]
             longest = max(piece.shape[0] for piece in pieces)
-            counts = jnp.concatenate([tile_count, slots_there[2, :1]])
             return pl.pallas_call(
                 lambda *refs: first_kernel(n, far, *refs),
                 out_shape=(parts, jax.ShapeDtypeStruct((rows, half), jnp.float32)),
-                in_specs=[smem()] * 7
+                in_specs=[smem()] * 3
                 + [vmem()]
                 + [anywhere()] * 2
                 + [vmem()] * (n - far)
@@ -452,8 +420,7 @@
                 compiler_params=params(20),
                 name="first_products",
             )(
-                tile_rows, tile_cols, slots_there[0], slots_there[1], counts, core.reshape(1),
-                order, sums.reshape(chips, per, TILE), *tiles, *pieces,
+                *facts, order, sums.reshape(chips, per, TILE), *tiles, *pieces
             )
         return pl.pallas_call(
             lambda *refs: later_kernel(n, rows, *refs),
@@ -477,20 +444,18 @@
             name="current",
         )(parts, restart, inverse)
 
-    pieces, names, found = gather(block, sums)
+    pieces, names, found, facts = gather(block, sums, order_tiles)
+    facts = (facts, sibling(facts))
     other = sibling(found)
     sums = jnp.where(
         core == 0, jnp.concatenate([found, other]), jnp.concatenate([other, found])
     )
-    parts, inverse = multiply(pieces, names, sums, None)
-    parts, raw, lists = tie((parts, (tile_rows, tile_cols, tile_count), seed_ids))
+    parts, inverse = multiply(pieces, names, sums, facts)
+    parts, lists = tie((parts, seed_ids))
     restart = count_seeds(lists)
-    facts = order_tiles(*raw)
     parts = lax.all_to_all(parts, "row", 0, 0, tiled=True)
-    parts, restart, facts = tie((parts, restart, facts))
-    facts = (facts, sibling(facts))
     panel = update(parts, restart, inverse, True)
-    pieces, names, _ = gather(panel)
+    pieces, names, _, _ = gather(panel)
     parts = multiply(pieces, names, None, facts)
     parts = lax.all_to_all(parts, "row", 0, 0, tiled=True)
     current = update(parts, restart, inverse, False)

time: 152 us -> 145 us (0.954)
  starting transfers between devices: 73.2 us -> 69.7 us
    ppermute x37 -> x36, starting transfers between devices: 64.9 us -> 61.3 us  [by_col(): return lax.ppermute(value, 'col', pairs)]
    ppermute x37 -> x36, waiting for transfers between devices: 21.9 us -> 20.7 us  [by_col(): return lax.ppermute(value, 'col', pairs)]
  transfers between devices with their start and end apart: 39 -> 38, of which waited for: 18 -> 23; matrix products, arithmetic and copies ran while one was open for 2% -> 1% of each run, Pallas kernels for 7% -> 6%
where the time goes in v9:
time: 145 us
  starting transfers between devices  69.7 us (48%)
  waiting for transfers between devices  39.4 us (27%)
  Pallas kernels  28.4 us (20%)
  between operations  3.64 us (3%)
  other arithmetic  2.6 us (2%)
    ppermute x36, starting transfers between devices, by_col(): return lax.ppermute(value, 'col', pairs)  61.3 us
    ppermute x36, waiting for transfers between devices, by_col(): return lax.ppermute(value, 'col', pairs)  20.7 us
    all_to_all x2, waiting for transfers between devices, per_device(): parts = lax.all_to_all(parts, 'row', 0, 0, tiled=True)  18.7 us
    pallas_call x1, Pallas kernels, multiply(): pl.pallas_call(lambda *refs: first_kernel(n, far, *refs), out_shape=(part...  9.22 us
    all_to_all x2, starting transfers between devices, per_device(): parts = lax.all_to_all(parts, 'row', 0, 0, tiled=True)  8.43 us
    pallas_call x1, Pallas kernels, count_seeds(): pl.pallas_call(seed_kernel, out_shape=jax.ShapeDtypeStruct((2 * own_rows,...  8.22 us
    pallas_call x1, Pallas kernels, multiply(): pl.pallas_call(lambda *refs: later_kernel(n, rows, *refs), out_shape=part...  7.59 us
  transfers between devices with their start and end apart: 38, of which 23 were waited for; matrix products, arithmetic and copies ran while one was open for 1% of the time, Pallas kernels for 6%

profile of v9, /device:TPU:1, one launch (start us, length us, event | category | flops | bytes accessed | tf_op | source)
XLA Modules:
  0.0 144.7 jit_solution(8938861832721918730)
XLA Ops:
  0.7 0.6 copy-done.1
  1.3 2.6 %column_sums.1 = f32[64,128]{1,0:T(8,128)S(1)} custom-call(s32[96]{0:T(128)S(1)} %copy-done.1, s32[1]{0:T(128)} %copy.7.count_ref, bf16[96,128,128]{2,1,0:T(8,128)(2,1)} %refs_3_.1), custom_call_target="tpu_custom_call" | custom-call | tf_op jit(solution)/shard_map/column_sums/pallas_call | solution.py:328
  4.0 3.2 %collective-permute-start.1 = (f32[32,128]{1,0:T(8,128)S(1)}, f32[32,128]{1,0:T(8,128)S(1)}, u32[]{:S(2)}, u32[]{:S(2)}) collective-permute-start(f32[32,128]{1,0:T(8,128)S(1)} %constant_dynamic-slice_fusion.2), channel_id=1, source_target_pairs={{0,1},{1,0},{2,3},{3,2},{4,5},{5,4},{6,7},{7,6},{8,9},{9,8},{10,11... | collective-permute-start | bytes 49160 | tf_op jit(solution)/shard_map/ppermute | solution.py:283
  7.4 0.6 collective-permute-done.1
  8.1 0.6 collective-permute-done
  8.7 3.9 %collective-permute-start.11 = (s16[576,128]{1,0:T(8,128)(2,1)S(1)}, s16[576,128]{1,0:T(8,128)(2,1)S(1)}, u32[]{:S(2)}, u32[]{:S(2)}) collective-permute-start(s16[576,128]{1,0:T(8,128)(2,1)S(1)} %pad_add_fusion.refs_6_), channel_id=1, source_target_pairs={{0,14},{1,15},{2,0},{3,1},{4,2},{5,3},{6,4},{7,5},{8,6},{9,7},{10,... | collective-permute-start | bytes 442376 | tf_op jit(solution)/shard_map/ppermute | solution.py:283
  12.6 0.4 collective-permute-start.10
  13.2 2.9 %collective-permute-start.5 = (s16[576,128]{1,0:T(8,128)(2,1)S(1)}, s16[576,128]{1,0:T(8,128)(2,1)S(1)}, u32[]{:S(2)}, u32[]{:S(2)}) collective-permute-start(s16[576,128]{1,0:T(8,128)(2,1)S(1)} %pad_add_fusion.refs_6_), channel_id=1, source_target_pairs={{0,16},{1,17},{2,18},{3,19},{4,20},{5,21},{6,22},{7,23},{8,24},{9,... | collective-permute-start | bytes 442376 | tf_op jit(solution)/shard_map/ppermute | solution.py:283
  16.1 3.0 %collective-permute-start.13 = (s16[576,128]{1,0:T(8,128)(2,1)S(1)}, s16[576,128]{1,0:T(8,128)(2,1)S(1)}, u32[]{:S(2)}, u32[]{:S(2)}) collective-permute-start(s16[576,128]{1,0:T(8,128)(2,1)S(1)} %collective-permute-done.11.refs_9_), channel_id=1, source_target_pairs={{0,14},{1,15},{2,0},{3,1},{4,2},{5,3},{6,4},{7,5},{8,6},{9,7},{10,... | collective-permute-start | bytes 442376 | tf_op jit(solution)/shard_map/ppermute | solution.py:283
  19.1 1.0 collective-permute-done.5.refs_7_
  20.1 2.7 %collective-permute-start.6 = (s16[576,128]{1,0:T(8,128)(2,1)S(1)}, s16[576,128]{1,0:T(8,128)(2,1)S(1)}, u32[]{:S(2)}, u32[]{:S(2)}) collective-permute-start(s16[576,128]{1,0:T(8,128)(2,1)S(1)} %collective-permute-done.5.refs_7_), channel_id=1, source_target_pairs={{0,14},{1,15},{2,0},{3,1},{4,2},{5,3},{6,4},{7,5},{8,6},{9,7},{10,... | collective-permute-start | bytes 442376 | tf_op jit(solution)/shard_map/ppermute | solution.py:283
  22.9 2.7 %collective-permute-start.15 = (s16[576,128]{1,0:T(8,128)(2,1)S(1)}, s16[576,128]{1,0:T(8,128)(2,1)S(1)}, u32[]{:S(2)}, u32[]{:S(2)}) collective-permute-start(s16[576,128]{1,0:T(8,128)(2,1)S(1)} %collective-permute-done.13.refs_13_), channel_id=1, source_target_pairs={{0,14},{1,15},{2,0},{3,1},{4,2},{5,3},{6,4},{7,5},{8,6},{9,7},{10,... | collective-permute-start | bytes 442376 | tf_op jit(solution)/shard_map/ppermute | solution.py:283
  25.9 2.7 %collective-permute-start.7 = (s16[576,128]{1,0:T(8,128)(2,1)S(1)}, s16[576,128]{1,0:T(8,128)(2,1)S(1)}, u32[]{:S(2)}, u32[]{:S(2)}) collective-permute-start(s16[576,128]{1,0:T(8,128)(2,1)S(1)} %collective-permute-done.6.refs_11_), channel_id=1, source_target_pairs={{0,14},{1,15},{2,0},{3,1},{4,2},{5,3},{6,4},{7,5},{8,6},{9,7},{10,... | collective-permute-start | bytes 442376 | tf_op jit(solution)/shard_map/ppermute | solution.py:283
  28.8 2.8 %collective-permute-done.14.refs_14_ = s16[576,128]{1,0:T(8,128)(2,1)S(1)} collective-permute-done((s16[576,128]{1,0:T(8,128)(2,1)S(1)}, s16[576,128]{1,0:T(8,128)(2,1)S(1)}, u32[]{:S(2)}, u32[]{:S(2)}) %collective-permute-start.14) | collective-permute-done | bytes 147488 | tf_op jit(solution)/shard_map/ppermute | solution.py:283
  31.7 2.9 %collective-permute-start.8 = (s16[576,128]{1,0:T(8,128)(2,1)S(1)}, s16[576,128]{1,0:T(8,128)(2,1)S(1)}, u32[]{:S(2)}, u32[]{:S(2)}) collective-permute-start(s16[576,128]{1,0:T(8,128)(2,1)S(1)} %collective-permute-done.7.refs_15_), channel_id=1, source_target_pairs={{0,14},{1,15},{2,0},{3,1},{4,2},{5,3},{6,4},{7,5},{8,6},{9,7},{10,... | collective-permute-start | bytes 442376 | tf_op jit(solution)/shard_map/ppermute | solution.py:283
  34.7 0.5 collective-permute-done.4.refs_16_
  35.2 1.5 %collective-permute-done.8.refs_19_ = s16[576,128]{1,0:T(8,128)(2,1)S(1)} collective-permute-done((s16[576,128]{1,0:T(8,128)(2,1)S(1)}, s16[576,128]{1,0:T(8,128)(2,1)S(1)}, u32[]{:S(2)}, u32[]{:S(2)}) %collective-permute-start.8) | collective-permute-done | bytes 147488 | tf_op jit(solution)/shard_map/ppermute | solution.py:283
  36.9 0.7 fusion.52
  40.2 3.2 %collective-permute-start.18 = (s16[576,128]{1,0:T(8,128)(2,1)S(1)}, s16[576,128]{1,0:T(8,128)(2,1)S(1)}, u32[]{:S(2)}, u32[]{:S(2)}) collective-permute-start(s16[576,128]{1,0:T(8,128)(2,1)S(1)} %collective-permute-done.8.refs_19_), channel_id=1, source_target_pairs={{0,14},{1,15},{2,0},{3,1},{4,2},{5,3},{6,4},{7,5},{8,6},{9,7},{10,... | collective-permute-start | bytes 442376 | tf_op jit(solution)/shard_map/ppermute | solution.py:283
  44.0 1.8 %collective-permute-done.17.refs_20_ = s16[576,128]{1,0:T(8,128)(2,1)S(1)} collective-permute-done((s16[576,128]{1,0:T(8,128)(2,1)S(1)}, s16[576,128]{1,0:T(8,128)(2,1)S(1)}, u32[]{:S(2)}, u32[]{:S(2)}) %collective-permute-start.17) | collective-permute-done | bytes 147488 | tf_op jit(solution)/shard_map/ppermute | solution.py:283
  46.0 6.2 %collective-permute-start.19 = (f32[32,128]{1,0:T(8,128)S(1)}, f32[32,128]{1,0:T(8,128)S(1)}, u32[]{:S(2)}, u32[]{:S(2)}) collective-permute-start(f32[32,128]{1,0:T(8,128)S(1)} %fusion.5), channel_id=1, source_target_pairs={{0,1},{1,0},{2,3},{3,2},{4,5},{5,4},{6,7},{7,6},{8,9},{9,8},{10,11... | collective-permute-start | bytes 49160 | tf_op jit(solution)/shard_map/ppermute | solution.py:283
  52.4 0.7 collective-permute-done.19
  53.1 0.4 collective-permute-done.9.refs_1_
  53.5 9.2 %first_products.1 = (s16[8,528,128]{2,1,0:T(8,128)(2,1)}, f32[512,128]{1,0:T(8,128)S(1)}) custom-call(s32[4,128]{1,0:T(4,128)S(1)} %add_add_fusion.1.refs_0_, s32[4,128]{1,0:T(4,128)S(1)} %collective-permute-done.9.refs_1_, s32[16]{0:T(128)S(1)} %stack.106.refs_2_, f32[16,4,128]{2,1,0:T(4,128)S(1)} %bitcast.26, bf16[96,128,128]{2,1,0:T(8,128)(2,1)} %refs_3_.1, ...), custom_call_target="tpu_custom_call" | custom-call | tf_op jit(solution)/shard_map/first_products/pallas_call | solution.py:405
  62.8 4.9 %all-to-all-start = ((s16[8,528,128]{2,1,0:T(8,128)(2,1)}), s16[8,528,128]{2,1,0:T(8,128)(2,1)S(1)}, u32[]{:S(2)}, u32[]{:S(2)}) async-start(s16[8,528,128]{2,1,0:T(8,128)(2,1)} %get-tuple-element.20), calls=%async_computation | async-start | bytes 2162688 | tf_op jit(solution)/shard_map/all_to_all | solution.py:456
  67.7 8.2 %seed_counts.1.refs_1_ = f32[512,128]{1,0:T(8,128)S(1)} custom-call(s32[2]{0:T(128)S(1)} %pad_add_fusion.1.where_ref, s32[256,1024]{1,0:T(8,128)S(1)} %copy-done), custom_call_target="tpu_custom_call" | custom-call | tf_op jit(solution)/shard_map/seed_counts/pallas_call | solution.py:375
  75.9 8.3 %all-to-all-done.refs_0_ = s16[8,528,128]{2,1,0:T(8,128)(2,1)S(1)} async-done(((s16[8,528,128]{2,1,0:T(8,128)(2,1)}), s16[8,528,128]{2,1,0:T(8,128)(2,1)S(1)}, u32[]{:S(2)}, u32[]{:S(2)}) %all-to-all-start) | async-done | bytes 1081376 | tf_op jit(solution)/shard_map/all_to_all | solution.py:456
  84.7 2.7 %collective-permute-start.20 = (bf16[512,128]{1,0:T(8,128)(2,1)S(1)}, bf16[512,128]{1,0:T(8,128)(2,1)S(1)}, u32[]{:S(2)}, u32[]{:S(2)}) collective-permute-start(bf16[512,128]{1,0:T(8,128)(2,1)S(1)} %current.2.refs_5_), channel_id=1, source_target_pairs={{0,16},{1,17},{2,18},{3,19},{4,20},{5,21},{6,22},{7,23},{8,24},{9,... | collective-permute-start | bytes 393224 | tf_op jit(solution)/shard_map/ppermute | solution.py:283
  87.4 2.7 %collective-permute-done.20.refs_6_ = bf16[512,128]{1,0:T(8,128)(2,1)S(1)} collective-permute-done((bf16[512,128]{1,0:T(8,128)(2,1)S(1)}, bf16[512,128]{1,0:T(8,128)(2,1)S(1)}, u32[]{:S(2)}, u32[]{:S(2)}) %collective-permute-start.20) | collective-permute-done | bytes 131104 | tf_op jit(solution)/shard_map/ppermute | solution.py:283
  90.1 3.0 %collective-permute-start.24 = (bf16[512,128]{1,0:T(8,128)(2,1)S(1)}, bf16[512,128]{1,0:T(8,128)(2,1)S(1)}, u32[]{:S(2)}, u32[]{:S(2)}) collective-permute-start(bf16[512,128]{1,0:T(8,128)(2,1)S(1)} %collective-permute-done.20.refs_6_), channel_id=1, source_target_pairs={{0,14},{1,15},{2,0},{3,1},{4,2},{5,3},{6,4},{7,5},{8,6},{9,7},{10,... | collective-permute-start | bytes 393224 | tf_op jit(solution)/shard_map/ppermute | solution.py:283
  93.1 0.9 collective-permute-start.22
  94.0 0.6 collective-permute-start.25
  94.6 0.4 collective-permute-done.24.refs_10_
  95.0 3.1 %collective-permute-start.28 = (bf16[512,128]{1,0:T(8,128)(2,1)S(1)}, bf16[512,128]{1,0:T(8,128)(2,1)S(1)}, u32[]{:S(2)}, u32[]{:S(2)}) collective-permute-start(bf16[512,128]{1,0:T(8,128)(2,1)S(1)} %collective-permute-done.24.refs_10_), channel_id=1, source_target_pairs={{0,14},{1,15},{2,0},{3,1},{4,2},{5,3},{6,4},{7,5},{8,6},{9,7},{10,... | collective-permute-start | bytes 393224 | tf_op jit(solution)/shard_map/ppermute | solution.py:283
  98.4 1.1 collective-permute-start.26
  99.9 0.5 collective-permute-done.23.refs_9_
  100.8 3.1 %collective-permute-start.32 = (bf16[512,128]{1,0:T(8,128)(2,1)S(1)}, bf16[512,128]{1,0:T(8,128)(2,1)S(1)}, u32[]{:S(2)}, u32[]{:S(2)}) collective-permute-start(bf16[512,128]{1,0:T(8,128)(2,1)S(1)} %collective-permute-done.28.refs_14_), channel_id=1, source_target_pairs={{0,14},{1,15},{2,0},{3,1},{4,2},{5,3},{6,4},{7,5},{8,6},{9,7},{10,... | collective-permute-start | bytes 393224 | tf_op jit(solution)/shard_map/ppermute | solution.py:283
  103.8 1.4 collective-permute-start.30
  105.3 1.4 collective-permute-done.27.refs_13_
  106.9 3.4 %collective-permute-start.34 = (bf16[512,128]{1,0:T(8,128)(2,1)S(1)}, bf16[512,128]{1,0:T(8,128)(2,1)S(1)}, u32[]{:S(2)}, u32[]{:S(2)}) collective-permute-start(bf16[512,128]{1,0:T(8,128)(2,1)S(1)} %collective-permute-done.32.refs_18_), channel_id=1, source_target_pairs={{0,14},{1,15},{2,0},{3,1},{4,2},{5,3},{6,4},{7,5},{8,6},{9,7},{10,... | collective-permute-start | bytes 393224 | tf_op jit(solution)/shard_map/ppermute | solution.py:283
  110.3 1.7 %collective-permute-done.33.refs_19_ = bf16[512,128]{1,0:T(8,128)(2,1)S(1)} collective-permute-done((bf16[512,128]{1,0:T(8,128)(2,1)S(1)}, bf16[512,128]{1,0:T(8,128)(2,1)S(1)}, u32[]{:S(2)}, u32[]{:S(2)}) %collective-permute-start.33) | collective-permute-done | bytes 131104 | tf_op jit(solution)/shard_map/ppermute | solution.py:283
  112.0 1.7 %collective-permute-done.31.refs_17_ = bf16[512,128]{1,0:T(8,128)(2,1)S(1)} collective-permute-done((bf16[512,128]{1,0:T(8,128)(2,1)S(1)}, bf16[512,128]{1,0:T(8,128)(2,1)S(1)}, u32[]{:S(2)}, u32[]{:S(2)}) %collective-permute-start.31) | collective-permute-done | bytes 131104 | tf_op jit(solution)/shard_map/ppermute | solution.py:283
  113.7 7.6 %later_products.1 = s16[8,528,128]{2,1,0:T(8,128)(2,1)} custom-call(s32[4,128]{1,0:T(4,128)S(1)} %add_add_fusion.1.refs_0_, s32[4,128]{1,0:T(4,128)S(1)} %collective-permute-done.9.refs_1_, s32[16]{0:T(128)S(1)} %stack.106.refs_2_, bf16[96,128,128]{2,1,0:T(8,128)(2,1)} %refs_3_.1, bf16[96,128,128]{2,1,0:T(8,128)(2,1)} %collective-permute-done.10.refs_5_.refs_4_, ...), custom_call_target="tpu_custom_call" | custom-call | tf_op jit(solution)/shard_map/later_products/pallas_call | solution.py:425
  121.3 3.6 %all-to-all-start.1 = ((s16[8,528,128]{2,1,0:T(8,128)(2,1)}), s16[8,528,128]{2,1,0:T(8,128)(2,1)S(1)}, u32[]{:S(2)}, u32[]{:S(2)}) async-start(s16[8,528,128]{2,1,0:T(8,128)(2,1)} %later_products.1), calls=%async_computation.1 | async-start | bytes 2162688 | tf_op jit(solution)/shard_map/all_to_all | solution.py:460
  124.9 10.4 %all-to-all-done.1.refs_0_ = s16[8,528,128]{2,1,0:T(8,128)(2,1)S(1)} async-done(((s16[8,528,128]{2,1,0:T(8,128)(2,1)}), s16[8,528,128]{2,1,0:T(8,128)(2,1)S(1)}, u32[]{:S(2)}, u32[]{:S(2)}) %all-to-all-start.1) | async-done | bytes 1081376 | tf_op jit(solution)/shard_map/all_to_all | solution.py:460
  135.7 7.3 %collective-permute-start.35 = (f32[256,128]{1,0:T(8,128)S(1)}, f32[256,128]{1,0:T(8,128)S(1)}, u32[]{:S(2)}, u32[]{:S(2)}) collective-permute-start(f32[256,128]{1,0:T(8,128)S(1)} %get-tuple-element.31), channel_id=1, source_target_pairs={{0,1},{1,0},{2,3},{3,2},{4,5},{5,4},{6,7},{7,6},{8,9},{9,8},{10,11... | collective-permute-start | bytes 393224 | tf_op jit(solution)/shard_map/ppermute | solution.py:283
  143.0 1.0 collective-permute-done.35
  144.0 0.7 maximum_select_fusion
  (97 shorter events, 4.2 us)
Async XLA Ops:
  1.3 5.8 %copy-start.3 = (f32[256,256]{1,0:T(8,128)S(1)}, f32[256,256]{1,0:T(8,128)}, u32[]{:S(2)}) copy-start(f32[256,256]{1,0:T(8,128)} %param.6) | copy-start | bytes 786436
  4.0 4.0 %collective-permute-start.1 = (f32[32,128]{1,0:T(8,128)S(1)}, f32[32,128]{1,0:T(8,128)S(1)}, u32[]{:S(2)}, u32[]{:S(2)}) collective-permute-start(f32[32,128]{1,0:T(8,128)S(1)} %constant_dynamic-slice_fusion.2), channel_id=1, source_target_pairs={{0,1},{1,0},{2,3},{3,2},{4,5},{5,4},{6,7},{7,6},{8,9},{9,8},{10,11... | collective-permute-start | bytes 49160 | tf_op jit(solution)/shard_map/ppermute | solution.py:283
  7.2 29.6 %copy-start.10 = (s32[96]{0:T(128)S(1)}, s32[96]{0:T(128)}, u32[]{:S(2)}) copy-start(s32[96]{0:T(128)} %param.8) | copy-start | bytes 1156
  7.2 36.4 %copy-start.2 = (s32[96]{0:T(128)S(1)}, s32[96]{0:T(128)}, u32[]{:S(2)}) copy-start(s32[96]{0:T(128)} %source_ref.1) | copy-start | bytes 1156
  7.3 1.3 collective-permute-start
  8.7 7.4 %collective-permute-start.11 = (s16[576,128]{1,0:T(8,128)(2,1)S(1)}, s16[576,128]{1,0:T(8,128)(2,1)S(1)}, u32[]{:S(2)}, u32[]{:S(2)}) collective-permute-start(s16[576,128]{1,0:T(8,128)(2,1)S(1)} %pad_add_fusion.refs_6_), channel_id=1, source_target_pairs={{0,14},{1,15},{2,0},{3,1},{4,2},{5,3},{6,4},{7,5},{8,6},{9,7},{10,... | collective-permute-start | bytes 442376 | tf_op jit(solution)/shard_map/ppermute | solution.py:283
  12.6 40.9 %collective-permute-start.10 = (bf16[96,128,128]{2,1,0:T(8,128)(2,1)}, bf16[96,128,128]{2,1,0:T(8,128)(2,1)}, u32[]{:S(2)}, u32[]{:S(2)}) collective-permute-start(bf16[96,128,128]{2,1,0:T(8,128)(2,1)} %refs_3_.1), channel_id=1, source_target_pairs={{0,1},{1,0},{2,3},{3,2},{4,5},{5,4},{6,7},{7,6},{8,9},{9,8},{10,11... | collective-permute-start | bytes 9437192 | tf_op jit(solution)/shard_map/ppermute | solution.py:283
  13.2 7.0 %collective-permute-start.5 = (s16[576,128]{1,0:T(8,128)(2,1)S(1)}, s16[576,128]{1,0:T(8,128)(2,1)S(1)}, u32[]{:S(2)}, u32[]{:S(2)}) collective-permute-start(s16[576,128]{1,0:T(8,128)(2,1)S(1)} %pad_add_fusion.refs_6_), channel_id=1, source_target_pairs={{0,16},{1,17},{2,18},{3,19},{4,20},{5,21},{6,22},{7,23},{8,24},{9,... | collective-permute-start | bytes 442376 | tf_op jit(solution)/shard_map/ppermute | solution.py:283
  16.1 6.7 %collective-permute-start.2 = (s16[576,128]{1,0:T(8,128)(2,1)S(1)}, s16[576,128]{1,0:T(8,128)(2,1)S(1)}, u32[]{:S(2)}, u32[]{:S(2)}) collective-permute-start(s16[576,128]{1,0:T(8,128)(2,1)S(1)} %pad_add_fusion.refs_6_), channel_id=1, source_target_pairs={{0,2},{1,3},{2,4},{3,5},{4,6},{5,7},{6,8},{7,9},{8,10},{9,11},{10,... | collective-permute-start | bytes 442376 | tf_op jit(solution)/shard_map/ppermute | solution.py:283
  16.1 6.8 %collective-permute-start.13 = (s16[576,128]{1,0:T(8,128)(2,1)S(1)}, s16[576,128]{1,0:T(8,128)(2,1)S(1)}, u32[]{:S(2)}, u32[]{:S(2)}) collective-permute-start(s16[576,128]{1,0:T(8,128)(2,1)S(1)} %collective-permute-done.11.refs_9_), channel_id=1, source_target_pairs={{0,14},{1,15},{2,0},{3,1},{4,2},{5,3},{6,4},{7,5},{8,6},{9,7},{10,... | collective-permute-start | bytes 442376 | tf_op jit(solution)/shard_map/ppermute | solution.py:283
  20.1 5.7 %collective-permute-start.12 = (s16[576,128]{1,0:T(8,128)(2,1)S(1)}, s16[576,128]{1,0:T(8,128)(2,1)S(1)}, u32[]{:S(2)}, u32[]{:S(2)}) collective-permute-start(s16[576,128]{1,0:T(8,128)(2,1)S(1)} %collective-permute-done.5.refs_7_), channel_id=1, source_target_pairs={{0,2},{1,3},{2,4},{3,5},{4,6},{5,7},{6,8},{7,9},{8,10},{9,11},{10,... | collective-permute-start | bytes 442376 | tf_op jit(solution)/shard_map/ppermute | solution.py:283
  20.1 5.7 %collective-permute-start.6 = (s16[576,128]{1,0:T(8,128)(2,1)S(1)}, s16[576,128]{1,0:T(8,128)(2,1)S(1)}, u32[]{:S(2)}, u32[]{:S(2)}) collective-permute-start(s16[576,128]{1,0:T(8,128)(2,1)S(1)} %collective-permute-done.5.refs_7_), channel_id=1, source_target_pairs={{0,14},{1,15},{2,0},{3,1},{4,2},{5,3},{6,4},{7,5},{8,6},{9,7},{10,... | collective-permute-start | bytes 442376 | tf_op jit(solution)/shard_map/ppermute | solution.py:283
  22.8 6.0 %collective-permute-start.3 = (s16[576,128]{1,0:T(8,128)(2,1)S(1)}, s16[576,128]{1,0:T(8,128)(2,1)S(1)}, u32[]{:S(2)}, u32[]{:S(2)}) collective-permute-start(s16[576,128]{1,0:T(8,128)(2,1)S(1)} %collective-permute-done.2.refs_8_), channel_id=1, source_target_pairs={{0,2},{1,3},{2,4},{3,5},{4,6},{5,7},{6,8},{7,9},{8,10},{9,11},{10,... | collective-permute-start | bytes 442376 | tf_op jit(solution)/shard_map/ppermute | solution.py:283
  22.9 11.7 %collective-permute-start.15 = (s16[576,128]{1,0:T(8,128)(2,1)S(1)}, s16[576,128]{1,0:T(8,128)(2,1)S(1)}, u32[]{:S(2)}, u32[]{:S(2)}) collective-permute-start(s16[576,128]{1,0:T(8,128)(2,1)S(1)} %collective-permute-done.13.refs_13_), channel_id=1, source_target_pairs={{0,14},{1,15},{2,0},{3,1},{4,2},{5,3},{6,4},{7,5},{8,6},{9,7},{10,... | collective-permute-start | bytes 442376 | tf_op jit(solution)/shard_map/ppermute | solution.py:283
  25.8 5.8 %collective-permute-start.14 = (s16[576,128]{1,0:T(8,128)(2,1)S(1)}, s16[576,128]{1,0:T(8,128)(2,1)S(1)}, u32[]{:S(2)}, u32[]{:S(2)}) collective-permute-start(s16[576,128]{1,0:T(8,128)(2,1)S(1)} %collective-permute-done.12.refs_10_), channel_id=1, source_target_pairs={{0,2},{1,3},{2,4},{3,5},{4,6},{5,7},{6,8},{7,9},{8,10},{9,11},{10,... | collective-permute-start | bytes 442376 | tf_op jit(solution)/shard_map/ppermute | solution.py:283
  25.9 5.8 %collective-permute-start.7 = (s16[576,128]{1,0:T(8,128)(2,1)S(1)}, s16[576,128]{1,0:T(8,128)(2,1)S(1)}, u32[]{:S(2)}, u32[]{:S(2)}) collective-permute-start(s16[576,128]{1,0:T(8,128)(2,1)S(1)} %collective-permute-done.6.refs_11_), channel_id=1, source_target_pairs={{0,14},{1,15},{2,0},{3,1},{4,2},{5,3},{6,4},{7,5},{8,6},{9,7},{10,... | collective-permute-start | bytes 442376 | tf_op jit(solution)/shard_map/ppermute | solution.py:283
  28.8 6.4 %collective-permute-start.4 = (s16[576,128]{1,0:T(8,128)(2,1)S(1)}, s16[576,128]{1,0:T(8,128)(2,1)S(1)}, u32[]{:S(2)}, u32[]{:S(2)}) collective-permute-start(s16[576,128]{1,0:T(8,128)(2,1)S(1)} %collective-permute-done.3.refs_12_), channel_id=1, source_target_pairs={{0,2},{1,3},{2,4},{3,5},{4,6},{5,7},{6,8},{7,9},{8,10},{9,11},{10,... | collective-permute-start | bytes 442376 | tf_op jit(solution)/shard_map/ppermute | solution.py:283
  31.7 12.2 %collective-permute-start.16 = (s16[576,128]{1,0:T(8,128)(2,1)S(1)}, s16[576,128]{1,0:T(8,128)(2,1)S(1)}, u32[]{:S(2)}, u32[]{:S(2)}) collective-permute-start(s16[576,128]{1,0:T(8,128)(2,1)S(1)} %collective-permute-done.14.refs_14_), channel_id=1, source_target_pairs={{0,2},{1,3},{2,4},{3,5},{4,6},{5,7},{6,8},{7,9},{8,10},{9,11},{10,... | collective-permute-start | bytes 442376 | tf_op jit(solution)/shard_map/ppermute | solution.py:283
  31.7 5.0 %collective-permute-start.8 = (s16[576,128]{1,0:T(8,128)(2,1)S(1)}, s16[576,128]{1,0:T(8,128)(2,1)S(1)}, u32[]{:S(2)}, u32[]{:S(2)}) collective-permute-start(s16[576,128]{1,0:T(8,128)(2,1)S(1)} %collective-permute-done.7.refs_15_), channel_id=1, source_target_pairs={{0,14},{1,15},{2,0},{3,1},{4,2},{5,3},{6,4},{7,5},{8,6},{9,7},{10,... | collective-permute-start | bytes 442376 | tf_op jit(solution)/shard_map/ppermute | solution.py:283
  34.6 18.9 %copy-start.4 = (s16[576,128]{1,0:T(8,128)(2,1)}, s16[576,128]{1,0:T(8,128)(2,1)S(1)}, u32[]{:S(2)}) copy-start(s16[576,128]{1,0:T(8,128)(2,1)S(1)} %collective-permute-done.15.refs_17_) | copy-start | bytes 442372
  35.2 18.3 %copy-start.5 = (s16[576,128]{1,0:T(8,128)(2,1)}, s16[576,128]{1,0:T(8,128)(2,1)S(1)}, u32[]{:S(2)}) copy-start(s16[576,128]{1,0:T(8,128)(2,1)S(1)} %collective-permute-done.4.refs_16_) | copy-start | bytes 442372
  36.7 16.8 %copy-start.7 = (s16[576,128]{1,0:T(8,128)(2,1)}, s16[576,128]{1,0:T(8,128)(2,1)S(1)}, u32[]{:S(2)}) copy-start(s16[576,128]{1,0:T(8,128)(2,1)S(1)} %collective-permute-done.8.refs_19_) | copy-start | bytes 442372
  40.2 5.7 %collective-permute-start.17 = (s16[576,128]{1,0:T(8,128)(2,1)S(1)}, s16[576,128]{1,0:T(8,128)(2,1)S(1)}, u32[]{:S(2)}, u32[]{:S(2)}) collective-permute-start(s16[576,128]{1,0:T(8,128)(2,1)S(1)} %collective-permute-done.4.refs_16_), channel_id=1, source_target_pairs={{0,2},{1,3},{2,4},{3,5},{4,6},{5,7},{6,8},{7,9},{8,10},{9,11},{10,... | collective-permute-start | bytes 442376 | tf_op jit(solution)/shard_map/ppermute | solution.py:283
  40.2 5.6 %collective-permute-start.18 = (s16[576,128]{1,0:T(8,128)(2,1)S(1)}, s16[576,128]{1,0:T(8,128)(2,1)S(1)}, u32[]{:S(2)}, u32[]{:S(2)}) collective-permute-start(s16[576,128]{1,0:T(8,128)(2,1)S(1)} %collective-permute-done.8.refs_19_), channel_id=1, source_target_pairs={{0,14},{1,15},{2,0},{3,1},{4,2},{5,3},{6,4},{7,5},{8,6},{9,7},{10,... | collective-permute-start | bytes 442376 | tf_op jit(solution)/shard_map/ppermute | solution.py:283
  43.9 9.6 %copy-start.6 = (s16[576,128]{1,0:T(8,128)(2,1)}, s16[576,128]{1,0:T(8,128)(2,1)S(1)}, u32[]{:S(2)}) copy-start(s16[576,128]{1,0:T(8,128)(2,1)S(1)} %collective-permute-done.16.refs_18_) | copy-start | bytes 442372
  45.8 7.7 %copy-start.8 = (s16[576,128]{1,0:T(8,128)(2,1)}, s16[576,128]{1,0:T(8,128)(2,1)S(1)}, u32[]{:S(2)}) copy-start(s16[576,128]{1,0:T(8,128)(2,1)S(1)} %collective-permute-done.17.refs_20_) | copy-start | bytes 442372
  45.8 7.7 %copy-start.9 = (s16[576,128]{1,0:T(8,128)(2,1)}, s16[576,128]{1,0:T(8,128)(2,1)S(1)}, u32[]{:S(2)}) copy-start(s16[576,128]{1,0:T(8,128)(2,1)S(1)} %collective-permute-done.18.refs_21_) | copy-start | bytes 442372
  46.0 7.1 %collective-permute-start.19 = (f32[32,128]{1,0:T(8,128)S(1)}, f32[32,128]{1,0:T(8,128)S(1)}, u32[]{:S(2)}, u32[]{:S(2)}) collective-permute-start(f32[32,128]{1,0:T(8,128)S(1)} %fusion.5), channel_id=1, source_target_pairs={{0,1},{1,0},{2,3},{3,2},{4,5},{5,4},{6,7},{7,6},{8,9},{9,8},{10,11... | collective-permute-start | bytes 49160 | tf_op jit(solution)/shard_map/ppermute | solution.py:283
  52.3 1.2 collective-permute-start.9
  62.8 5.0 %copy-start = (s32[256,1024]{1,0:T(8,128)S(1)}, s32[256,1024]{1,0:T(8,128)}, u32[]{:S(2)}) copy-start(s32[256,1024]{1,0:T(8,128)} %all_ref) | copy-start | bytes 3145732
  62.8 21.5 %all-to-all-start = ((s16[8,528,128]{2,1,0:T(8,128)(2,1)}), s16[8,528,128]{2,1,0:T(8,128)(2,1)S(1)}, u32[]{:S(2)}, u32[]{:S(2)}) async-start(s16[8,528,128]{2,1,0:T(8,128)(2,1)} %get-tuple-element.20), calls=%async_computation | async-start | bytes 2162688 | tf_op jit(solution)/shard_map/all_to_all | solution.py:456
  84.7 5.4 %collective-permute-start.20 = (bf16[512,128]{1,0:T(8,128)(2,1)S(1)}, bf16[512,128]{1,0:T(8,128)(2,1)S(1)}, u32[]{:S(2)}, u32[]{:S(2)}) collective-permute-start(bf16[512,128]{1,0:T(8,128)(2,1)S(1)} %current.2.refs_5_), channel_id=1, source_target_pairs={{0,16},{1,17},{2,18},{3,19},{4,20},{5,21},{6,22},{7,23},{8,24},{9,... | collective-permute-start | bytes 393224 | tf_op jit(solution)/shard_map/ppermute | solution.py:283
  87.4 6.6 %collective-permute-start.21 = (bf16[512,128]{1,0:T(8,128)(2,1)S(1)}, bf16[512,128]{1,0:T(8,128)(2,1)S(1)}, u32[]{:S(2)}, u32[]{:S(2)}) collective-permute-start(bf16[512,128]{1,0:T(8,128)(2,1)S(1)} %current.2.refs_5_), channel_id=1, source_target_pairs={{0,2},{1,3},{2,4},{3,5},{4,6},{5,7},{6,8},{7,9},{8,10},{9,11},{10,... | collective-permute-start | bytes 393224 | tf_op jit(solution)/shard_map/ppermute | solution.py:283
  90.1 5.0 %collective-permute-start.24 = (bf16[512,128]{1,0:T(8,128)(2,1)S(1)}, bf16[512,128]{1,0:T(8,128)(2,1)S(1)}, u32[]{:S(2)}, u32[]{:S(2)}) collective-permute-start(bf16[512,128]{1,0:T(8,128)(2,1)S(1)} %collective-permute-done.20.refs_6_), channel_id=1, source_target_pairs={{0,14},{1,15},{2,0},{3,1},{4,2},{5,3},{6,4},{7,5},{8,6},{9,7},{10,... | collective-permute-start | bytes 393224 | tf_op jit(solution)/shard_map/ppermute | solution.py:283
  93.1 5.3 %collective-permute-start.22 = (bf16[512,128]{1,0:T(8,128)(2,1)S(1)}, bf16[512,128]{1,0:T(8,128)(2,1)S(1)}, u32[]{:S(2)}, u32[]{:S(2)}) collective-permute-start(bf16[512,128]{1,0:T(8,128)(2,1)S(1)} %current.2.refs_5_), channel_id=1, source_target_pairs={{0,14},{1,15},{2,0},{3,1},{4,2},{5,3},{6,4},{7,5},{8,6},{9,7},{10,... | collective-permute-start | bytes 393224 | tf_op jit(solution)/shard_map/ppermute | solution.py:283
  94.0 5.6 %collective-permute-start.25 = (bf16[512,128]{1,0:T(8,128)(2,1)S(1)}, bf16[512,128]{1,0:T(8,128)(2,1)S(1)}, u32[]{:S(2)}, u32[]{:S(2)}) collective-permute-start(bf16[512,128]{1,0:T(8,128)(2,1)S(1)} %collective-permute-done.21.refs_7_), channel_id=1, source_target_pairs={{0,2},{1,3},{2,4},{3,5},{4,6},{5,7},{6,8},{7,9},{8,10},{9,11},{10,... | collective-permute-start | bytes 393224 | tf_op jit(solution)/shard_map/ppermute | solution.py:283
  94.5 5.8 %collective-permute-start.23 = (bf16[512,128]{1,0:T(8,128)(2,1)S(1)}, bf16[512,128]{1,0:T(8,128)(2,1)S(1)}, u32[]{:S(2)}, u32[]{:S(2)}) collective-permute-start(bf16[512,128]{1,0:T(8,128)(2,1)S(1)} %collective-permute-done.20.refs_6_), channel_id=1, source_target_pairs={{0,2},{1,3},{2,4},{3,5},{4,6},{5,7},{6,8},{7,9},{8,10},{9,11},{10,... | collective-permute-start | bytes 393224 | tf_op jit(solution)/shard_map/ppermute | solution.py:283
  95.0 5.7 %collective-permute-start.28 = (bf16[512,128]{1,0:T(8,128)(2,1)S(1)}, bf16[512,128]{1,0:T(8,128)(2,1)S(1)}, u32[]{:S(2)}, u32[]{:S(2)}) collective-permute-start(bf16[512,128]{1,0:T(8,128)(2,1)S(1)} %collective-permute-done.24.refs_10_), channel_id=1, source_target_pairs={{0,14},{1,15},{2,0},{3,1},{4,2},{5,3},{6,4},{7,5},{8,6},{9,7},{10,... | collective-permute-start | bytes 393224 | tf_op jit(solution)/shard_map/ppermute | solution.py:283
  98.4 5.4 %collective-permute-start.26 = (bf16[512,128]{1,0:T(8,128)(2,1)S(1)}, bf16[512,128]{1,0:T(8,128)(2,1)S(1)}, u32[]{:S(2)}, u32[]{:S(2)}) collective-permute-start(bf16[512,128]{1,0:T(8,128)(2,1)S(1)} %collective-permute-done.22.refs_8_), channel_id=1, source_target_pairs={{0,14},{1,15},{2,0},{3,1},{4,2},{5,3},{6,4},{7,5},{8,6},{9,7},{10,... | collective-permute-start | bytes 393224 | tf_op jit(solution)/shard_map/ppermute | solution.py:283
  99.5 5.7 %collective-permute-start.29 = (bf16[512,128]{1,0:T(8,128)(2,1)S(1)}, bf16[512,128]{1,0:T(8,128)(2,1)S(1)}, u32[]{:S(2)}, u32[]{:S(2)}) collective-permute-start(bf16[512,128]{1,0:T(8,128)(2,1)S(1)} %collective-permute-done.25.refs_11_), channel_id=1, source_target_pairs={{0,2},{1,3},{2,4},{3,5},{4,6},{5,7},{6,8},{7,9},{8,10},{9,11},{10,... | collective-permute-start | bytes 393224 | tf_op jit(solution)/shard_map/ppermute | solution.py:283
  100.4 6.3 %collective-permute-start.27 = (bf16[512,128]{1,0:T(8,128)(2,1)S(1)}, bf16[512,128]{1,0:T(8,128)(2,1)S(1)}, u32[]{:S(2)}, u32[]{:S(2)}) collective-permute-start(bf16[512,128]{1,0:T(8,128)(2,1)S(1)} %collective-permute-done.23.refs_9_), channel_id=1, source_target_pairs={{0,2},{1,3},{2,4},{3,5},{4,6},{5,7},{6,8},{7,9},{8,10},{9,11},{10,... | collective-permute-start | bytes 393224 | tf_op jit(solution)/shard_map/ppermute | solution.py:283
  100.8 6.1 %collective-permute-start.32 = (bf16[512,128]{1,0:T(8,128)(2,1)S(1)}, bf16[512,128]{1,0:T(8,128)(2,1)S(1)}, u32[]{:S(2)}, u32[]{:S(2)}) collective-permute-start(bf16[512,128]{1,0:T(8,128)(2,1)S(1)} %collective-permute-done.28.refs_14_), channel_id=1, source_target_pairs={{0,14},{1,15},{2,0},{3,1},{4,2},{5,3},{6,4},{7,5},{8,6},{9,7},{10,... | collective-permute-start | bytes 393224 | tf_op jit(solution)/shard_map/ppermute | solution.py:283
  103.8 6.5 %collective-permute-start.30 = (bf16[512,128]{1,0:T(8,128)(2,1)S(1)}, bf16[512,128]{1,0:T(8,128)(2,1)S(1)}, u32[]{:S(2)}, u32[]{:S(2)}) collective-permute-start(bf16[512,128]{1,0:T(8,128)(2,1)S(1)} %collective-permute-done.26.refs_12_), channel_id=1, source_target_pairs={{0,14},{1,15},{2,0},{3,1},{4,2},{5,3},{6,4},{7,5},{8,6},{9,7},{10,... | collective-permute-start | bytes 393224 | tf_op jit(solution)/shard_map/ppermute | solution.py:283
  105.3 6.7 %collective-permute-start.33 = (bf16[512,128]{1,0:T(8,128)(2,1)S(1)}, bf16[512,128]{1,0:T(8,128)(2,1)S(1)}, u32[]{:S(2)}, u32[]{:S(2)}) collective-permute-start(bf16[512,128]{1,0:T(8,128)(2,1)S(1)} %collective-permute-done.29.refs_15_), channel_id=1, source_target_pairs={{0,2},{1,3},{2,4},{3,5},{4,6},{5,7},{6,8},{7,9},{8,10},{9,11},{10,... | collective-permute-start | bytes 393224 | tf_op jit(solution)/shard_map/ppermute | solution.py:283
  106.7 7.0 %collective-permute-start.31 = (bf16[512,128]{1,0:T(8,128)(2,1)S(1)}, bf16[512,128]{1,0:T(8,128)(2,1)S(1)}, u32[]{:S(2)}, u32[]{:S(2)}) collective-permute-start(bf16[512,128]{1,0:T(8,128)(2,1)S(1)} %collective-permute-done.27.refs_13_), channel_id=1, source_target_pairs={{0,2},{1,3},{2,4},{3,5},{4,6},{5,7},{6,8},{7,9},{8,10},{9,11},{10,... | collective-permute-start | bytes 393224 | tf_op jit(solution)/shard_map/ppermute | solution.py:283
  106.9 6.8 %collective-permute-start.34 = (bf16[512,128]{1,0:T(8,128)(2,1)S(1)}, bf16[512,128]{1,0:T(8,128)(2,1)S(1)}, u32[]{:S(2)}, u32[]{:S(2)}) collective-permute-start(bf16[512,128]{1,0:T(8,128)(2,1)S(1)} %collective-permute-done.32.refs_18_), channel_id=1, source_target_pairs={{0,14},{1,15},{2,0},{3,1},{4,2},{5,3},{6,4},{7,5},{8,6},{9,7},{10,... | collective-permute-start | bytes 393224 | tf_op jit(solution)/shard_map/ppermute | solution.py:283
  121.3 14.0 %all-to-all-start.1 = ((s16[8,528,128]{2,1,0:T(8,128)(2,1)}), s16[8,528,128]{2,1,0:T(8,128)(2,1)S(1)}, u32[]{:S(2)}, u32[]{:S(2)}) async-start(s16[8,528,128]{2,1,0:T(8,128)(2,1)} %later_products.1), calls=%async_computation.1 | async-start | bytes 2162688 | tf_op jit(solution)/shard_map/all_to_all | solution.py:460
  135.7 8.3 %collective-permute-start.35 = (f32[256,128]{1,0:T(8,128)S(1)}, f32[256,128]{1,0:T(8,128)S(1)}, u32[]{:S(2)}, u32[]{:S(2)}) collective-permute-start(f32[256,128]{1,0:T(8,128)S(1)} %get-tuple-element.31), channel_id=1, source_target_pairs={{0,1},{1,0},{2,3},{3,2},{4,5},{5,4},{6,7},{7,6},{8,9},{9,8},{10,11... | collective-permute-start | bytes 393224 | tf_op jit(solution)/shard_map/ppermute | solution.py:283
  (1 other events, 0.7 us)

commit v10 on v8

--- a/solution.py
+++ b/solution.py
@@ -176,7 +176,7 @@
 
 
 def single_products(slot_refs, count_ref, core_ref, copies, tiles, panel, total):
-    unroll = 16
+    unroll = 24
     slots = tiles.shape[0] // 2
     dummy = total.shape[0] - 1
     per = 2 * BT
@@ -320,29 +320,21 @@
 
     def gather(block, sums=None):
         rows = block.shape[0]
-        a, b = along(block, 1), along(block, -1)
-        if sums is None:
-            other = across(block)
-        else:
-            other = across(jnp.concatenate([block, encode(sums)]))
-            a, other = tie((a, other))
-            sums = sums + decode(other[rows:])
-            other = jnp.concatenate([other[:rows], encode(sums)])
+        if sums is not None:
+            block = jnp.concatenate([block, encode(sums)])
+        other = across(block)
         pieces, names = [block, other], [(0, 0), (1, 0)]
-        c, d = other, other
+        a, b, c, d = block, block, other, other
         for step in range(1, depth // 2):
-            if step > 1:
-                a, b = along(a, 1), along(b, -1)
+            a, b = along(a, 1), along(b, -1)
             c, d = along(c, 1), along(d, -1)
             pieces += [a, b, c, d]
             names += [(0, -step), (0, step), (1, -step), (1, step)]
-            if sums is not None:
-                sums = sums + (decode(c[rows:]) + decode(d[rows:]))
-        a, d = along(a, 1), along(d, -1)
-        pieces += [a, d]
+        pieces += [along(a, 1), along(d, -1)]
         names += [(0, depth // 2), (1, depth // 2)]
         if sums is not None:
-            sums = sums + decode(d[rows:])
+            for piece in pieces[1:]:
+                sums = sums + decode(piece[rows:])
         return pieces, names, sums
 
     half = columns // 2

time: 152 us -> 144 us (0.947)
  starting transfers between devices: 73.2 us -> 69 us
  waiting for transfers between devices: 40.2 us -> 37.6 us
  Pallas kernels: 29.4 us -> 27.1 us
    ppermute x37, starting transfers between devices: 64.9 us -> 60.6 us  [by_col(): return lax.ppermute(value, 'col', pairs)]
    ppermute x37, waiting for transfers between devices: 21.9 us -> 18.4 us  [by_col(): return lax.ppermute(value, 'col', pairs)]
  transfers between devices with their start and end apart: 39 -> 39, of which waited for: 18 -> 17; matrix products, arithmetic and copies ran while one was open for 2% -> 2% of each run, Pallas kernels for 7% -> 7%
where the time goes in v10:
time: 144 us; the launch traced here: 143 us
  starting transfers between devices  69 us (48%)
  waiting for transfers between devices  37.6 us (26%)
  Pallas kernels  27.1 us (19%)
  other arithmetic  4.35 us (3%)
  between operations  3.86 us (3%)
  local copies, waits for them, and re-layouts  1.58 us (1%)
    ppermute x37, starting transfers between devices, by_col(): return lax.ppermute(value, 'col', pairs)  60.6 us
    all_to_all x2, waiting for transfers between devices, per_device(): parts = lax.all_to_all(parts, 'row', 0, 0, tiled=True)  19.1 us
    ppermute x37, waiting for transfers between devices, by_col(): return lax.ppermute(value, 'col', pairs)  18.4 us
    pallas_call x1, Pallas kernels, multiply(): pl.pallas_call(lambda *refs: first_kernel(n, far, *refs), out_shape=(part...  9.28 us
    all_to_all x2, starting transfers between devices, per_device(): parts = lax.all_to_all(parts, 'row', 0, 0, tiled=True)  8.4 us
    pallas_call x1, Pallas kernels, count_seeds(): pl.pallas_call(seed_kernel, out_shape=jax.ShapeDtypeStruct((2 * own_rows,...  7.42 us
    pallas_call x1, Pallas kernels, multiply(): pl.pallas_call(lambda *refs: later_kernel(n, rows, *refs), out_shape=part...  7.17 us
  transfers between devices with their start and end apart: 39, of which 17 were waited for; matrix products, arithmetic and copies ran while one was open for 2% of the time, Pallas kernels for 7%

profile of v10, /device:TPU:1, one launch (start us, length us, event | category | flops | bytes accessed | tf_op | source)
XLA Modules:
  0.0 143.4 jit_solution(13989781497288375441)
XLA Ops:
  0.0 1.0 add_convert_fusion
  1.1 3.3 %collective-permute-start.2 = (s16[256,128]{1,0:T(8,128)(2,1)S(1)}, s16[256,128]{1,0:T(8,128)(2,1)S(1)}, u32[]{:S(2)}, u32[]{:S(2)}) collective-permute-start(s16[256,128]{1,0:T(8,128)(2,1)S(1)} %get-tuple-element.35), channel_id=1, source_target_pairs={{0,1},{1,0},{2,3},{3,2},{4,5},{5,4},{6,7},{7,6},{8,9},{9,8},{10,11... | collective-permute-start | bytes 196616 | tf_op jit(solution)/shard_map/ppermute | solution.py:308
  5.2 0.6 copy-done.1
  5.8 2.4 %column_sums.1 = f32[64,128]{1,0:T(8,128)S(1)} custom-call(s32[96]{0:T(128)S(1)} %copy-done.1, s32[1]{0:T(128)} %copy.7.count_ref, bf16[96,128,128]{2,1,0:T(8,128)(2,1)} %refs_3_.1), custom_call_target="tpu_custom_call" | custom-call | tf_op jit(solution)/shard_map/column_sums/pallas_call | solution.py:351
  8.3 0.6 collective-permute-start.1
  9.4 0.8 collective-permute-done
  10.2 0.6 slice.146
  11.0 1.1 collective-permute-start.3
  12.1 5.7 %collective-permute-start.5 = (s16[576,128]{1,0:T(8,128)(2,1)S(1)}, s16[576,128]{1,0:T(8,128)(2,1)S(1)}, u32[]{:S(2)}, u32[]{:S(2)}) collective-permute-start(s16[576,128]{1,0:T(8,128)(2,1)S(1)} %pad_add_fusion.refs_10_), channel_id=1, source_target_pairs={{0,14},{1,15},{2,0},{3,1},{4,2},{5,3},{6,4},{7,5},{8,6},{9,7},{10,... | collective-permute-start | bytes 442376 | tf_op jit(solution)/shard_map/ppermute | solution.py:308
  17.9 3.8 %collective-permute-start.7 = (s16[576,128]{1,0:T(8,128)(2,1)S(1)}, s16[576,128]{1,0:T(8,128)(2,1)S(1)}, u32[]{:S(2)}, u32[]{:S(2)}) collective-permute-start(s16[576,128]{1,0:T(8,128)(2,1)S(1)} %collective-permute-done.3.refs_11_), channel_id=1, source_target_pairs={{0,14},{1,15},{2,0},{3,1},{4,2},{5,3},{6,4},{7,5},{8,6},{9,7},{10,... | collective-permute-start | bytes 442376 | tf_op jit(solution)/shard_map/ppermute | solution.py:308
  21.7 2.7 %collective-permute-start.9 = (s16[576,128]{1,0:T(8,128)(2,1)S(1)}, s16[576,128]{1,0:T(8,128)(2,1)S(1)}, u32[]{:S(2)}, u32[]{:S(2)}) collective-permute-start(s16[576,128]{1,0:T(8,128)(2,1)S(1)} %collective-permute-done.5.refs_13_), channel_id=1, source_target_pairs={{0,14},{1,15},{2,0},{3,1},{4,2},{5,3},{6,4},{7,5},{8,6},{9,7},{10,... | collective-permute-start | bytes 442376 | tf_op jit(solution)/shard_map/ppermute | solution.py:308
  24.5 2.8 %collective-permute-start.11 = (s16[576,128]{1,0:T(8,128)(2,1)S(1)}, s16[576,128]{1,0:T(8,128)(2,1)S(1)}, u32[]{:S(2)}, u32[]{:S(2)}) collective-permute-start(s16[576,128]{1,0:T(8,128)(2,1)S(1)} %collective-permute-done.7.refs_15_), channel_id=1, source_target_pairs={{0,14},{1,15},{2,0},{3,1},{4,2},{5,3},{6,4},{7,5},{8,6},{9,7},{10,... | collective-permute-start | bytes 442376 | tf_op jit(solution)/shard_map/ppermute | solution.py:308
  27.3 2.8 %collective-permute-done.8.refs_16_ = s16[576,128]{1,0:T(8,128)(2,1)S(1)} collective-permute-done((s16[576,128]{1,0:T(8,128)(2,1)S(1)}, s16[576,128]{1,0:T(8,128)(2,1)S(1)}, u32[]{:S(2)}, u32[]{:S(2)}) %collective-permute-start.8) | collective-permute-done | bytes 147488 | tf_op jit(solution)/shard_map/ppermute | solution.py:308
  30.2 2.7 %collective-permute-start.13 = (s16[576,128]{1,0:T(8,128)(2,1)S(1)}, s16[576,128]{1,0:T(8,128)(2,1)S(1)}, u32[]{:S(2)}, u32[]{:S(2)}) collective-permute-start(s16[576,128]{1,0:T(8,128)(2,1)S(1)} %collective-permute-done.9.refs_17_), channel_id=1, source_target_pairs={{0,14},{1,15},{2,0},{3,1},{4,2},{5,3},{6,4},{7,5},{8,6},{9,7},{10,... | collective-permute-start | bytes 442376 | tf_op jit(solution)/shard_map/ppermute | solution.py:308
  33.0 1.5 %collective-permute-start.15 = (s16[576,128]{1,0:T(8,128)(2,1)S(1)}, s16[576,128]{1,0:T(8,128)(2,1)S(1)}, u32[]{:S(2)}, u32[]{:S(2)}) collective-permute-start(s16[576,128]{1,0:T(8,128)(2,1)S(1)} %collective-permute-done.11.refs_19_), channel_id=1, source_target_pairs={{0,14},{1,15},{2,0},{3,1},{4,2},{5,3},{6,4},{7,5},{8,6},{9,7},{10,... | collective-permute-start | bytes 442376 | tf_op jit(solution)/shard_map/ppermute | solution.py:308
  34.4 0.9 collective-permute-done.12.refs_20_
  35.4 2.1 %collective-permute-done.10.refs_18_ = s16[576,128]{1,0:T(8,128)(2,1)S(1)} collective-permute-done((s16[576,128]{1,0:T(8,128)(2,1)S(1)}, s16[576,128]{1,0:T(8,128)(2,1)S(1)}, u32[]{:S(2)}, u32[]{:S(2)}) %collective-permute-start.10) | collective-permute-done | bytes 147488 | tf_op jit(solution)/shard_map/ppermute | solution.py:308
  37.5 1.3 collective-permute-done.15.refs_23_
  38.8 1.4 %collective-permute-start.17 = (s16[576,128]{1,0:T(8,128)(2,1)S(1)}, s16[576,128]{1,0:T(8,128)(2,1)S(1)}, u32[]{:S(2)}, u32[]{:S(2)}) collective-permute-start(s16[576,128]{1,0:T(8,128)(2,1)S(1)} %collective-permute-done.15.refs_23_), channel_id=1, source_target_pairs={{0,14},{1,15},{2,0},{3,1},{4,2},{5,3},{6,4},{7,5},{8,6},{9,7},{10,... | collective-permute-start | bytes 442376 | tf_op jit(solution)/shard_map/ppermute | solution.py:308
  40.3 1.4 collective-permute-done.16.refs_24_
  41.7 1.6 %collective-permute-done.14.refs_22_ = s16[576,128]{1,0:T(8,128)(2,1)S(1)} collective-permute-done((s16[576,128]{1,0:T(8,128)(2,1)S(1)}, s16[576,128]{1,0:T(8,128)(2,1)S(1)}, u32[]{:S(2)}, u32[]{:S(2)}) %collective-permute-start.14) | collective-permute-done | bytes 147488 | tf_op jit(solution)/shard_map/ppermute | solution.py:308
  43.4 5.0 %collective-permute-start.18 = (f32[32,128]{1,0:T(8,128)S(1)}, f32[32,128]{1,0:T(8,128)S(1)}, u32[]{:S(2)}, u32[]{:S(2)}) collective-permute-start(f32[32,128]{1,0:T(8,128)S(1)} %fusion.5), channel_id=1, source_target_pairs={{0,1},{1,0},{2,3},{3,2},{4,5},{5,4},{6,7},{7,6},{8,9},{9,8},{10,11... | collective-permute-start | bytes 49160 | tf_op jit(solution)/shard_map/ppermute | solution.py:308
  48.4 0.8 pad_add_fusion.1.refs_4_
  49.4 9.3 %first_products.1 = (s16[8,528,128]{2,1,0:T(8,128)(2,1)}, f32[512,128]{1,0:T(8,128)S(1)}) custom-call(s32[96]{0:T(128)S(1)} %copy-done.3, s32[96]{0:T(128)S(1)} %copy-done.2, s32[96]{0:T(128)S(1)} %get-tuple-element.37.refs_2_, s32[96]{0:T(128)S(1)} %get-tuple-element.36.refs_3_, s32[2]{0:T(128)S(1)} %pad_add_fusion.1.refs_4_, s32[1]{0:T(128)} %bitcast.6.refs_5_, ...), custom_call_target="tpu_custom_call" | custom-call | tf_op jit(solution)/shard_map/first_products/pallas_call | solution.py:429
  58.7 4.8 %all-to-all-start = ((s16[8,528,128]{2,1,0:T(8,128)(2,1)}), s16[8,528,128]{2,1,0:T(8,128)(2,1)S(1)}, u32[]{:S(2)}, u32[]{:S(2)}) async-start(s16[8,528,128]{2,1,0:T(8,128)(2,1)} %get-tuple-element.16), calls=%async_computation | async-start | bytes 2162688 | tf_op jit(solution)/shard_map/all_to_all | solution.py:481
  63.6 0.6 fusion.52
  67.3 7.4 %seed_counts.1.refs_1_ = f32[512,128]{1,0:T(8,128)S(1)} custom-call(s32[2]{0:T(128)S(1)} %pad_add_fusion.2.where_ref, s32[256,1024]{1,0:T(8,128)S(1)} %copy-done), custom_call_target="tpu_custom_call" | custom-call | tf_op jit(solution)/shard_map/seed_counts/pallas_call | solution.py:398
  75.0 4.8 %all-to-all-done.refs_0_ = s16[8,528,128]{2,1,0:T(8,128)(2,1)S(1)} async-done(((s16[8,528,128]{2,1,0:T(8,128)(2,1)}), s16[8,528,128]{2,1,0:T(8,128)(2,1)S(1)}, u32[]{:S(2)}, u32[]{:S(2)}) %all-to-all-start) | async-done | bytes 1081376 | tf_op jit(solution)/shard_map/all_to_all | solution.py:481
  80.1 2.7 %collective-permute-start.21 = (bf16[512,128]{1,0:T(8,128)(2,1)S(1)}, bf16[512,128]{1,0:T(8,128)(2,1)S(1)}, u32[]{:S(2)}, u32[]{:S(2)}) collective-permute-start(bf16[512,128]{1,0:T(8,128)(2,1)S(1)} %current.2.refs_5_), channel_id=1, source_target_pairs={{0,16},{1,17},{2,18},{3,19},{4,20},{5,21},{6,22},{7,23},{8,24},{9,... | collective-permute-start | bytes 393224 | tf_op jit(solution)/shard_map/ppermute | solution.py:308
  82.8 2.7 %collective-permute-done.21.refs_6_ = bf16[512,128]{1,0:T(8,128)(2,1)S(1)} collective-permute-done((bf16[512,128]{1,0:T(8,128)(2,1)S(1)}, bf16[512,128]{1,0:T(8,128)(2,1)S(1)}, u32[]{:S(2)}, u32[]{:S(2)}) %collective-permute-start.21) | collective-permute-done | bytes 131104 | tf_op jit(solution)/shard_map/ppermute | solution.py:308
  85.5 3.7 %collective-permute-start.25 = (bf16[512,128]{1,0:T(8,128)(2,1)S(1)}, bf16[512,128]{1,0:T(8,128)(2,1)S(1)}, u32[]{:S(2)}, u32[]{:S(2)}) collective-permute-start(bf16[512,128]{1,0:T(8,128)(2,1)S(1)} %collective-permute-done.21.refs_6_), channel_id=1, source_target_pairs={{0,14},{1,15},{2,0},{3,1},{4,2},{5,3},{6,4},{7,5},{8,6},{9,7},{10,... | collective-permute-start | bytes 393224 | tf_op jit(solution)/shard_map/ppermute | solution.py:308
  89.2 1.4 collective-permute-start.24
  91.1 3.1 %collective-permute-start.29 = (bf16[512,128]{1,0:T(8,128)(2,1)S(1)}, bf16[512,128]{1,0:T(8,128)(2,1)S(1)}, u32[]{:S(2)}, u32[]{:S(2)}) collective-permute-start(bf16[512,128]{1,0:T(8,128)(2,1)S(1)} %collective-permute-done.25.refs_10_), channel_id=1, source_target_pairs={{0,14},{1,15},{2,0},{3,1},{4,2},{5,3},{6,4},{7,5},{8,6},{9,7},{10,... | collective-permute-start | bytes 393224 | tf_op jit(solution)/shard_map/ppermute | solution.py:308
  94.2 1.4 collective-permute-start.27
  95.9 0.8 collective-permute-done.29.refs_14_
  96.7 3.1 %collective-permute-start.33 = (bf16[512,128]{1,0:T(8,128)(2,1)S(1)}, bf16[512,128]{1,0:T(8,128)(2,1)S(1)}, u32[]{:S(2)}, u32[]{:S(2)}) collective-permute-start(bf16[512,128]{1,0:T(8,128)(2,1)S(1)} %collective-permute-done.29.refs_14_), channel_id=1, source_target_pairs={{0,14},{1,15},{2,0},{3,1},{4,2},{5,3},{6,4},{7,5},{8,6},{9,7},{10,... | collective-permute-start | bytes 393224 | tf_op jit(solution)/shard_map/ppermute | solution.py:308
  99.8 1.4 collective-permute-start.31
  101.3 0.8 collective-permute-done.30.refs_15_
  102.1 0.7 collective-permute-done.33.refs_18_
  102.9 3.4 %collective-permute-start.35 = (bf16[512,128]{1,0:T(8,128)(2,1)S(1)}, bf16[512,128]{1,0:T(8,128)(2,1)S(1)}, u32[]{:S(2)}, u32[]{:S(2)}) collective-permute-start(bf16[512,128]{1,0:T(8,128)(2,1)S(1)} %collective-permute-done.33.refs_18_), channel_id=1, source_target_pairs={{0,14},{1,15},{2,0},{3,1},{4,2},{5,3},{6,4},{7,5},{8,6},{9,7},{10,... | collective-permute-start | bytes 393224 | tf_op jit(solution)/shard_map/ppermute | solution.py:308
  106.3 6.4 %collective-permute-start.20 = (s32[4,128]{1,0:T(4,128)S(1)}, s32[4,128]{1,0:T(4,128)S(1)}, u32[]{:S(2)}, u32[]{:S(2)}) collective-permute-start(s32[4,128]{1,0:T(4,128)S(1)} %add_add_fusion.2.refs_0_), channel_id=1, source_target_pairs={{0,1},{1,0},{2,3},{3,2},{4,5},{5,4},{6,7},{7,6},{8,9},{9,8},{10,11... | collective-permute-start | bytes 6152 | tf_op jit(solution)/shard_map/ppermute | solution.py:308
  112.7 0.8 collective-permute-done.20.refs_1_
  113.6 7.2 %later_products.1 = s16[8,528,128]{2,1,0:T(8,128)(2,1)} custom-call(s32[4,128]{1,0:T(4,128)S(1)} %add_add_fusion.2.refs_0_, s32[4,128]{1,0:T(4,128)S(1)} %collective-permute-done.20.refs_1_, s32[16]{0:T(128)S(1)} %stack.113.refs_6_.refs_2_, bf16[96,128,128]{2,1,0:T(8,128)(2,1)} %refs_3_.1, bf16[96,128,128]{2,1,0:T(8,128)(2,1)} %collective-permute-done.19.refs_9_.refs_4_, ...), custom_call_target="tpu_custom_call" | custom-call | tf_op jit(solution)/shard_map/later_products/pallas_call | solution.py:450
  120.7 3.6 %all-to-all-start.1 = ((s16[8,528,128]{2,1,0:T(8,128)(2,1)}), s16[8,528,128]{2,1,0:T(8,128)(2,1)S(1)}, u32[]{:S(2)}, u32[]{:S(2)}) async-start(s16[8,528,128]{2,1,0:T(8,128)(2,1)} %later_products.1), calls=%async_computation.1 | async-start | bytes 2162688 | tf_op jit(solution)/shard_map/all_to_all | solution.py:487
  124.3 14.4 %all-to-all-done.1.refs_0_ = s16[8,528,128]{2,1,0:T(8,128)(2,1)S(1)} async-done(((s16[8,528,128]{2,1,0:T(8,128)(2,1)}), s16[8,528,128]{2,1,0:T(8,128)(2,1)S(1)}, u32[]{:S(2)}, u32[]{:S(2)}) %all-to-all-start.1) | async-done | bytes 1081376 | tf_op jit(solution)/shard_map/all_to_all | solution.py:487
  139.1 2.6 %collective-permute-start.36 = (f32[256,128]{1,0:T(8,128)S(1)}, f32[256,128]{1,0:T(8,128)S(1)}, u32[]{:S(2)}, u32[]{:S(2)}) collective-permute-start(f32[256,128]{1,0:T(8,128)S(1)} %get-tuple-element.33), channel_id=1, source_target_pairs={{0,1},{1,0},{2,3},{3,2},{4,5},{5,4},{6,7},{7,6},{8,9},{9,8},{10,11... | collective-permute-start | bytes 393224 | tf_op jit(solution)/shard_map/ppermute | solution.py:308
  141.7 1.0 collective-permute-done.36
  142.7 0.7 maximum_select_fusion
  (102 shorter events, 3.5 us)
Async XLA Ops:
  1.1 9.8 %collective-permute-start.2 = (s16[256,128]{1,0:T(8,128)(2,1)S(1)}, s16[256,128]{1,0:T(8,128)(2,1)S(1)}, u32[]{:S(2)}, u32[]{:S(2)}) collective-permute-start(s16[256,128]{1,0:T(8,128)(2,1)S(1)} %get-tuple-element.35), channel_id=1, source_target_pairs={{0,1},{1,0},{2,3},{3,2},{4,5},{5,4},{6,7},{7,6},{8,9},{9,8},{10,11... | collective-permute-start | bytes 196616 | tf_op jit(solution)/shard_map/ppermute | solution.py:308
  4.4 44.9 %collective-permute-start.19 = (bf16[96,128,128]{2,1,0:T(8,128)(2,1)}, bf16[96,128,128]{2,1,0:T(8,128)(2,1)}, u32[]{:S(2)}, u32[]{:S(2)}) collective-permute-start(bf16[96,128,128]{2,1,0:T(8,128)(2,1)} %refs_3_.1), channel_id=1, source_target_pairs={{0,1},{1,0},{2,3},{3,2},{4,5},{5,4},{6,7},{7,6},{8,9},{9,8},{10,11... | collective-permute-start | bytes 9437192 | tf_op jit(solution)/shard_map/ppermute | solution.py:308
  5.8 3.2 %copy-start.2 = (s32[96]{0:T(128)S(1)}, s32[96]{0:T(128)}, u32[]{:S(2)}) copy-start(s32[96]{0:T(128)} %refs_1_.1) | copy-start | bytes 1156
  5.8 3.2 %copy-start.3 = (s32[96]{0:T(128)S(1)}, s32[96]{0:T(128)}, u32[]{:S(2)}) copy-start(s32[96]{0:T(128)} %refs_0_.1) | copy-start | bytes 1156
  8.3 2.6 %collective-permute-start.1 = (f32[32,128]{1,0:T(8,128)S(1)}, f32[32,128]{1,0:T(8,128)S(1)}, u32[]{:S(2)}, u32[]{:S(2)}) collective-permute-start(f32[32,128]{1,0:T(8,128)S(1)} %constant_dynamic-slice_fusion.4), channel_id=1, source_target_pairs={{0,1},{1,0},{2,3},{3,2},{4,5},{5,4},{6,7},{7,6},{8,9},{9,8},{10,11... | collective-permute-start | bytes 49160 | tf_op jit(solution)/shard_map/ppermute | solution.py:308
  9.1 1.2 collective-permute-start
  11.0 6.9 %collective-permute-start.3 = (s16[576,128]{1,0:T(8,128)(2,1)S(1)}, s16[576,128]{1,0:T(8,128)(2,1)S(1)}, u32[]{:S(2)}, u32[]{:S(2)}) collective-permute-start(s16[576,128]{1,0:T(8,128)(2,1)S(1)} %pad_add_fusion.refs_10_), channel_id=1, source_target_pairs={{0,16},{1,17},{2,18},{3,19},{4,20},{5,21},{6,22},{7,23},{8,24},{9,... | collective-permute-start | bytes 442376 | tf_op jit(solution)/shard_map/ppermute | solution.py:308
  12.1 9.6 %collective-permute-start.5 = (s16[576,128]{1,0:T(8,128)(2,1)S(1)}, s16[576,128]{1,0:T(8,128)(2,1)S(1)}, u32[]{:S(2)}, u32[]{:S(2)}) collective-permute-start(s16[576,128]{1,0:T(8,128)(2,1)S(1)} %pad_add_fusion.refs_10_), channel_id=1, source_target_pairs={{0,14},{1,15},{2,0},{3,1},{4,2},{5,3},{6,4},{7,5},{8,6},{9,7},{10,... | collective-permute-start | bytes 442376 | tf_op jit(solution)/shard_map/ppermute | solution.py:308
  17.8 6.6 %collective-permute-start.4 = (s16[576,128]{1,0:T(8,128)(2,1)S(1)}, s16[576,128]{1,0:T(8,128)(2,1)S(1)}, u32[]{:S(2)}, u32[]{:S(2)}) collective-permute-start(s16[576,128]{1,0:T(8,128)(2,1)S(1)} %pad_add_fusion.refs_10_), channel_id=1, source_target_pairs={{0,2},{1,3},{2,4},{3,5},{4,6},{5,7},{6,8},{7,9},{8,10},{9,11},{10,... | collective-permute-start | bytes 442376 | tf_op jit(solution)/shard_map/ppermute | solution.py:308
  17.9 6.6 %collective-permute-start.7 = (s16[576,128]{1,0:T(8,128)(2,1)S(1)}, s16[576,128]{1,0:T(8,128)(2,1)S(1)}, u32[]{:S(2)}, u32[]{:S(2)}) collective-permute-start(s16[576,128]{1,0:T(8,128)(2,1)S(1)} %collective-permute-done.3.refs_11_), channel_id=1, source_target_pairs={{0,14},{1,15},{2,0},{3,1},{4,2},{5,3},{6,4},{7,5},{8,6},{9,7},{10,... | collective-permute-start | bytes 442376 | tf_op jit(solution)/shard_map/ppermute | solution.py:308
  21.7 8.5 %collective-permute-start.6 = (s16[576,128]{1,0:T(8,128)(2,1)S(1)}, s16[576,128]{1,0:T(8,128)(2,1)S(1)}, u32[]{:S(2)}, u32[]{:S(2)}) collective-permute-start(s16[576,128]{1,0:T(8,128)(2,1)S(1)} %collective-permute-done.3.refs_11_), channel_id=1, source_target_pairs={{0,2},{1,3},{2,4},{3,5},{4,6},{5,7},{6,8},{7,9},{8,10},{9,11},{10,... | collective-permute-start | bytes 442376 | tf_op jit(solution)/shard_map/ppermute | solution.py:308
  21.7 8.5 %collective-permute-start.9 = (s16[576,128]{1,0:T(8,128)(2,1)S(1)}, s16[576,128]{1,0:T(8,128)(2,1)S(1)}, u32[]{:S(2)}, u32[]{:S(2)}) collective-permute-start(s16[576,128]{1,0:T(8,128)(2,1)S(1)} %collective-permute-done.5.refs_13_), channel_id=1, source_target_pairs={{0,14},{1,15},{2,0},{3,1},{4,2},{5,3},{6,4},{7,5},{8,6},{9,7},{10,... | collective-permute-start | bytes 442376 | tf_op jit(solution)/shard_map/ppermute | solution.py:308
  24.4 5.8 %collective-permute-start.8 = (s16[576,128]{1,0:T(8,128)(2,1)S(1)}, s16[576,128]{1,0:T(8,128)(2,1)S(1)}, u32[]{:S(2)}, u32[]{:S(2)}) collective-permute-start(s16[576,128]{1,0:T(8,128)(2,1)S(1)} %collective-permute-done.4.refs_12_), channel_id=1, source_target_pairs={{0,2},{1,3},{2,4},{3,5},{4,6},{5,7},{6,8},{7,9},{8,10},{9,11},{10,... | collective-permute-start | bytes 442376 | tf_op jit(solution)/shard_map/ppermute | solution.py:308
  24.5 8.5 %collective-permute-start.11 = (s16[576,128]{1,0:T(8,128)(2,1)S(1)}, s16[576,128]{1,0:T(8,128)(2,1)S(1)}, u32[]{:S(2)}, u32[]{:S(2)}) collective-permute-start(s16[576,128]{1,0:T(8,128)(2,1)S(1)} %collective-permute-done.7.refs_15_), channel_id=1, source_target_pairs={{0,14},{1,15},{2,0},{3,1},{4,2},{5,3},{6,4},{7,5},{8,6},{9,7},{10,... | collective-permute-start | bytes 442376 | tf_op jit(solution)/shard_map/ppermute | solution.py:308
  30.2 5.2 %collective-permute-start.12 = (s16[576,128]{1,0:T(8,128)(2,1)S(1)}, s16[576,128]{1,0:T(8,128)(2,1)S(1)}, u32[]{:S(2)}, u32[]{:S(2)}) collective-permute-start(s16[576,128]{1,0:T(8,128)(2,1)S(1)} %collective-permute-done.8.refs_16_), channel_id=1, source_target_pairs={{0,2},{1,3},{2,4},{3,5},{4,6},{5,7},{6,8},{7,9},{8,10},{9,11},{10,... | collective-permute-start | bytes 442376 | tf_op jit(solution)/shard_map/ppermute | solution.py:308
  30.2 7.3 %collective-permute-start.10 = (s16[576,128]{1,0:T(8,128)(2,1)S(1)}, s16[576,128]{1,0:T(8,128)(2,1)S(1)}, u32[]{:S(2)}, u32[]{:S(2)}) collective-permute-start(s16[576,128]{1,0:T(8,128)(2,1)S(1)} %collective-permute-done.6.refs_14_), channel_id=1, source_target_pairs={{0,2},{1,3},{2,4},{3,5},{4,6},{5,7},{6,8},{7,9},{8,10},{9,11},{10,... | collective-permute-start | bytes 442376 | tf_op jit(solution)/shard_map/ppermute | solution.py:308
  30.2 7.3 %collective-permute-start.13 = (s16[576,128]{1,0:T(8,128)(2,1)S(1)}, s16[576,128]{1,0:T(8,128)(2,1)S(1)}, u32[]{:S(2)}, u32[]{:S(2)}) collective-permute-start(s16[576,128]{1,0:T(8,128)(2,1)S(1)} %collective-permute-done.9.refs_17_), channel_id=1, source_target_pairs={{0,14},{1,15},{2,0},{3,1},{4,2},{5,3},{6,4},{7,5},{8,6},{9,7},{10,... | collective-permute-start | bytes 442376 | tf_op jit(solution)/shard_map/ppermute | solution.py:308
  33.0 5.8 %collective-permute-start.15 = (s16[576,128]{1,0:T(8,128)(2,1)S(1)}, s16[576,128]{1,0:T(8,128)(2,1)S(1)}, u32[]{:S(2)}, u32[]{:S(2)}) collective-permute-start(s16[576,128]{1,0:T(8,128)(2,1)S(1)} %collective-permute-done.11.refs_19_), channel_id=1, source_target_pairs={{0,14},{1,15},{2,0},{3,1},{4,2},{5,3},{6,4},{7,5},{8,6},{9,7},{10,... | collective-permute-start | bytes 442376 | tf_op jit(solution)/shard_map/ppermute | solution.py:308
  35.4 13.9 %copy-start.4 = (s16[576,128]{1,0:T(8,128)(2,1)}, s16[576,128]{1,0:T(8,128)(2,1)S(1)}, u32[]{:S(2)}) copy-start(s16[576,128]{1,0:T(8,128)(2,1)S(1)} %collective-permute-done.12.refs_20_) | copy-start | bytes 442372
  35.4 6.3 %collective-permute-start.16 = (s16[576,128]{1,0:T(8,128)(2,1)S(1)}, s16[576,128]{1,0:T(8,128)(2,1)S(1)}, u32[]{:S(2)}, u32[]{:S(2)}) collective-permute-start(s16[576,128]{1,0:T(8,128)(2,1)S(1)} %collective-permute-done.12.refs_20_), channel_id=1, source_target_pairs={{0,2},{1,3},{2,4},{3,5},{4,6},{5,7},{6,8},{7,9},{8,10},{9,11},{10,... | collective-permute-start | bytes 442376 | tf_op jit(solution)/shard_map/ppermute | solution.py:308
  37.4 5.8 %collective-permute-start.14 = (s16[576,128]{1,0:T(8,128)(2,1)S(1)}, s16[576,128]{1,0:T(8,128)(2,1)S(1)}, u32[]{:S(2)}, u32[]{:S(2)}) collective-permute-start(s16[576,128]{1,0:T(8,128)(2,1)S(1)} %collective-permute-done.10.refs_18_), channel_id=1, source_target_pairs={{0,2},{1,3},{2,4},{3,5},{4,6},{5,7},{6,8},{7,9},{8,10},{9,11},{10,... | collective-permute-start | bytes 442376 | tf_op jit(solution)/shard_map/ppermute | solution.py:308
  37.5 11.8 %copy-start.5 = (s16[576,128]{1,0:T(8,128)(2,1)}, s16[576,128]{1,0:T(8,128)(2,1)S(1)}, u32[]{:S(2)}) copy-start(s16[576,128]{1,0:T(8,128)(2,1)S(1)} %collective-permute-done.13.refs_21_) | copy-start | bytes 442372
  38.8 10.5 %copy-start.6 = (s16[576,128]{1,0:T(8,128)(2,1)}, s16[576,128]{1,0:T(8,128)(2,1)S(1)}, u32[]{:S(2)}) copy-start(s16[576,128]{1,0:T(8,128)(2,1)S(1)} %collective-permute-done.15.refs_23_) | copy-start | bytes 442372
  38.8 4.4 %collective-permute-start.17 = (s16[576,128]{1,0:T(8,128)(2,1)S(1)}, s16[576,128]{1,0:T(8,128)(2,1)S(1)}, u32[]{:S(2)}, u32[]{:S(2)}) collective-permute-start(s16[576,128]{1,0:T(8,128)(2,1)S(1)} %collective-permute-done.15.refs_23_), channel_id=1, source_target_pairs={{0,14},{1,15},{2,0},{3,1},{4,2},{5,3},{6,4},{7,5},{8,6},{9,7},{10,... | collective-permute-start | bytes 442376 | tf_op jit(solution)/shard_map/ppermute | solution.py:308
  41.7 7.6 %copy-start.7 = (s16[576,128]{1,0:T(8,128)(2,1)}, s16[576,128]{1,0:T(8,128)(2,1)S(1)}, u32[]{:S(2)}) copy-start(s16[576,128]{1,0:T(8,128)(2,1)S(1)} %collective-permute-done.16.refs_24_) | copy-start | bytes 442372
  43.3 6.1 %copy-start.8 = (s16[576,128]{1,0:T(8,128)(2,1)}, s16[576,128]{1,0:T(8,128)(2,1)S(1)}, u32[]{:S(2)}) copy-start(s16[576,128]{1,0:T(8,128)(2,1)S(1)} %collective-permute-done.14.refs_22_) | copy-start | bytes 442372
  43.3 6.1 %copy-start.9 = (s16[576,128]{1,0:T(8,128)(2,1)}, s16[576,128]{1,0:T(8,128)(2,1)S(1)}, u32[]{:S(2)}) copy-start(s16[576,128]{1,0:T(8,128)(2,1)S(1)} %collective-permute-done.17.refs_25_) | copy-start | bytes 442372
  43.4 5.9 %collective-permute-start.18 = (f32[32,128]{1,0:T(8,128)S(1)}, f32[32,128]{1,0:T(8,128)S(1)}, u32[]{:S(2)}, u32[]{:S(2)}) collective-permute-start(f32[32,128]{1,0:T(8,128)S(1)} %fusion.5), channel_id=1, source_target_pairs={{0,1},{1,0},{2,3},{3,2},{4,5},{5,4},{6,7},{7,6},{8,9},{9,8},{10,11... | collective-permute-start | bytes 49160 | tf_op jit(solution)/shard_map/ppermute | solution.py:308
  58.6 8.7 %copy-start = (s32[256,1024]{1,0:T(8,128)S(1)}, s32[256,1024]{1,0:T(8,128)}, u32[]{:S(2)}) copy-start(s32[256,1024]{1,0:T(8,128)} %all_ref) | copy-start | bytes 3145732
  58.7 21.1 %all-to-all-start = ((s16[8,528,128]{2,1,0:T(8,128)(2,1)}), s16[8,528,128]{2,1,0:T(8,128)(2,1)S(1)}, u32[]{:S(2)}, u32[]{:S(2)}) async-start(s16[8,528,128]{2,1,0:T(8,128)(2,1)} %get-tuple-element.16), calls=%async_computation | async-start | bytes 2162688 | tf_op jit(solution)/shard_map/all_to_all | solution.py:481
  80.1 5.4 %collective-permute-start.21 = (bf16[512,128]{1,0:T(8,128)(2,1)S(1)}, bf16[512,128]{1,0:T(8,128)(2,1)S(1)}, u32[]{:S(2)}, u32[]{:S(2)}) collective-permute-start(bf16[512,128]{1,0:T(8,128)(2,1)S(1)} %current.2.refs_5_), channel_id=1, source_target_pairs={{0,16},{1,17},{2,18},{3,19},{4,20},{5,21},{6,22},{7,23},{8,24},{9,... | collective-permute-start | bytes 393224 | tf_op jit(solution)/shard_map/ppermute | solution.py:308
  82.8 7.8 %collective-permute-start.22 = (bf16[512,128]{1,0:T(8,128)(2,1)S(1)}, bf16[512,128]{1,0:T(8,128)(2,1)S(1)}, u32[]{:S(2)}, u32[]{:S(2)}) collective-permute-start(bf16[512,128]{1,0:T(8,128)(2,1)S(1)} %current.2.refs_5_), channel_id=1, source_target_pairs={{0,2},{1,3},{2,4},{3,5},{4,6},{5,7},{6,8},{7,9},{8,10},{9,11},{10,... | collective-permute-start | bytes 393224 | tf_op jit(solution)/shard_map/ppermute | solution.py:308
  85.5 5.6 %collective-permute-start.25 = (bf16[512,128]{1,0:T(8,128)(2,1)S(1)}, bf16[512,128]{1,0:T(8,128)(2,1)S(1)}, u32[]{:S(2)}, u32[]{:S(2)}) collective-permute-start(bf16[512,128]{1,0:T(8,128)(2,1)S(1)} %collective-permute-done.21.refs_6_), channel_id=1, source_target_pairs={{0,14},{1,15},{2,0},{3,1},{4,2},{5,3},{6,4},{7,5},{8,6},{9,7},{10,... | collective-permute-start | bytes 393224 | tf_op jit(solution)/shard_map/ppermute | solution.py:308
  89.2 5.0 %collective-permute-start.23 = (bf16[512,128]{1,0:T(8,128)(2,1)S(1)}, bf16[512,128]{1,0:T(8,128)(2,1)S(1)}, u32[]{:S(2)}, u32[]{:S(2)}) collective-permute-start(bf16[512,128]{1,0:T(8,128)(2,1)S(1)} %current.2.refs_5_), channel_id=1, source_target_pairs={{0,14},{1,15},{2,0},{3,1},{4,2},{5,3},{6,4},{7,5},{8,6},{9,7},{10,... | collective-permute-start | bytes 393224 | tf_op jit(solution)/shard_map/ppermute | solution.py:308
  89.2 6.4 %collective-permute-start.24 = (bf16[512,128]{1,0:T(8,128)(2,1)S(1)}, bf16[512,128]{1,0:T(8,128)(2,1)S(1)}, u32[]{:S(2)}, u32[]{:S(2)}) collective-permute-start(bf16[512,128]{1,0:T(8,128)(2,1)S(1)} %collective-permute-done.21.refs_6_), channel_id=1, source_target_pairs={{0,2},{1,3},{2,4},{3,5},{4,6},{5,7},{6,8},{7,9},{8,10},{9,11},{10,... | collective-permute-start | bytes 393224 | tf_op jit(solution)/shard_map/ppermute | solution.py:308
  90.7 5.1 %collective-permute-start.26 = (bf16[512,128]{1,0:T(8,128)(2,1)S(1)}, bf16[512,128]{1,0:T(8,128)(2,1)S(1)}, u32[]{:S(2)}, u32[]{:S(2)}) collective-permute-start(bf16[512,128]{1,0:T(8,128)(2,1)S(1)} %collective-permute-done.22.refs_7_), channel_id=1, source_target_pairs={{0,2},{1,3},{2,4},{3,5},{4,6},{5,7},{6,8},{7,9},{8,10},{9,11},{10,... | collective-permute-start | bytes 393224 | tf_op jit(solution)/shard_map/ppermute | solution.py:308
  91.1 5.6 %collective-permute-start.29 = (bf16[512,128]{1,0:T(8,128)(2,1)S(1)}, bf16[512,128]{1,0:T(8,128)(2,1)S(1)}, u32[]{:S(2)}, u32[]{:S(2)}) collective-permute-start(bf16[512,128]{1,0:T(8,128)(2,1)S(1)} %collective-permute-done.25.refs_10_), channel_id=1, source_target_pairs={{0,14},{1,15},{2,0},{3,1},{4,2},{5,3},{6,4},{7,5},{8,6},{9,7},{10,... | collective-permute-start | bytes 393224 | tf_op jit(solution)/shard_map/ppermute | solution.py:308
  94.2 5.6 %collective-permute-start.27 = (bf16[512,128]{1,0:T(8,128)(2,1)S(1)}, bf16[512,128]{1,0:T(8,128)(2,1)S(1)}, u32[]{:S(2)}, u32[]{:S(2)}) collective-permute-start(bf16[512,128]{1,0:T(8,128)(2,1)S(1)} %collective-permute-done.23.refs_8_), channel_id=1, source_target_pairs={{0,14},{1,15},{2,0},{3,1},{4,2},{5,3},{6,4},{7,5},{8,6},{9,7},{10,... | collective-permute-start | bytes 393224 | tf_op jit(solution)/shard_map/ppermute | solution.py:308
  95.6 5.6 %collective-permute-start.28 = (bf16[512,128]{1,0:T(8,128)(2,1)S(1)}, bf16[512,128]{1,0:T(8,128)(2,1)S(1)}, u32[]{:S(2)}, u32[]{:S(2)}) collective-permute-start(bf16[512,128]{1,0:T(8,128)(2,1)S(1)} %collective-permute-done.24.refs_9_), channel_id=1, source_target_pairs={{0,2},{1,3},{2,4},{3,5},{4,6},{5,7},{6,8},{7,9},{8,10},{9,11},{10,... | collective-permute-start | bytes 393224 | tf_op jit(solution)/shard_map/ppermute | solution.py:308
  95.7 6.4 %collective-permute-start.30 = (bf16[512,128]{1,0:T(8,128)(2,1)S(1)}, bf16[512,128]{1,0:T(8,128)(2,1)S(1)}, u32[]{:S(2)}, u32[]{:S(2)}) collective-permute-start(bf16[512,128]{1,0:T(8,128)(2,1)S(1)} %collective-permute-done.26.refs_11_), channel_id=1, source_target_pairs={{0,2},{1,3},{2,4},{3,5},{4,6},{5,7},{6,8},{7,9},{8,10},{9,11},{10,... | collective-permute-start | bytes 393224 | tf_op jit(solution)/shard_map/ppermute | solution.py:308
  96.7 6.2 %collective-permute-start.33 = (bf16[512,128]{1,0:T(8,128)(2,1)S(1)}, bf16[512,128]{1,0:T(8,128)(2,1)S(1)}, u32[]{:S(2)}, u32[]{:S(2)}) collective-permute-start(bf16[512,128]{1,0:T(8,128)(2,1)S(1)} %collective-permute-done.29.refs_14_), channel_id=1, source_target_pairs={{0,14},{1,15},{2,0},{3,1},{4,2},{5,3},{6,4},{7,5},{8,6},{9,7},{10,... | collective-permute-start | bytes 393224 | tf_op jit(solution)/shard_map/ppermute | solution.py:308
  99.8 13.7 %collective-permute-start.31 = (bf16[512,128]{1,0:T(8,128)(2,1)S(1)}, bf16[512,128]{1,0:T(8,128)(2,1)S(1)}, u32[]{:S(2)}, u32[]{:S(2)}) collective-permute-start(bf16[512,128]{1,0:T(8,128)(2,1)S(1)} %collective-permute-done.27.refs_12_), channel_id=1, source_target_pairs={{0,14},{1,15},{2,0},{3,1},{4,2},{5,3},{6,4},{7,5},{8,6},{9,7},{10,... | collective-permute-start | bytes 393224 | tf_op jit(solution)/shard_map/ppermute | solution.py:308
  101.2 12.3 %collective-permute-start.32 = (bf16[512,128]{1,0:T(8,128)(2,1)S(1)}, bf16[512,128]{1,0:T(8,128)(2,1)S(1)}, u32[]{:S(2)}, u32[]{:S(2)}) collective-permute-start(bf16[512,128]{1,0:T(8,128)(2,1)S(1)} %collective-permute-done.28.refs_13_), channel_id=1, source_target_pairs={{0,2},{1,3},{2,4},{3,5},{4,6},{5,7},{6,8},{7,9},{8,10},{9,11},{10,... | collective-permute-start | bytes 393224 | tf_op jit(solution)/shard_map/ppermute | solution.py:308
  102.1 11.4 %collective-permute-start.34 = (bf16[512,128]{1,0:T(8,128)(2,1)S(1)}, bf16[512,128]{1,0:T(8,128)(2,1)S(1)}, u32[]{:S(2)}, u32[]{:S(2)}) collective-permute-start(bf16[512,128]{1,0:T(8,128)(2,1)S(1)} %collective-permute-done.30.refs_15_), channel_id=1, source_target_pairs={{0,2},{1,3},{2,4},{3,5},{4,6},{5,7},{6,8},{7,9},{8,10},{9,11},{10,... | collective-permute-start | bytes 393224 | tf_op jit(solution)/shard_map/ppermute | solution.py:308
  102.9 10.7 %collective-permute-start.35 = (bf16[512,128]{1,0:T(8,128)(2,1)S(1)}, bf16[512,128]{1,0:T(8,128)(2,1)S(1)}, u32[]{:S(2)}, u32[]{:S(2)}) collective-permute-start(bf16[512,128]{1,0:T(8,128)(2,1)S(1)} %collective-permute-done.33.refs_18_), channel_id=1, source_target_pairs={{0,14},{1,15},{2,0},{3,1},{4,2},{5,3},{6,4},{7,5},{8,6},{9,7},{10,... | collective-permute-start | bytes 393224 | tf_op jit(solution)/shard_map/ppermute | solution.py:308
  106.3 7.2 %collective-permute-start.20 = (s32[4,128]{1,0:T(4,128)S(1)}, s32[4,128]{1,0:T(4,128)S(1)}, u32[]{:S(2)}, u32[]{:S(2)}) collective-permute-start(s32[4,128]{1,0:T(4,128)S(1)} %add_add_fusion.2.refs_0_), channel_id=1, source_target_pairs={{0,1},{1,0},{2,3},{3,2},{4,5},{5,4},{6,7},{7,6},{8,9},{9,8},{10,11... | collective-permute-start | bytes 6152 | tf_op jit(solution)/shard_map/ppermute | solution.py:308
  120.7 18.0 %all-to-all-start.1 = ((s16[8,528,128]{2,1,0:T(8,128)(2,1)}), s16[8,528,128]{2,1,0:T(8,128)(2,1)S(1)}, u32[]{:S(2)}, u32[]{:S(2)}) async-start(s16[8,528,128]{2,1,0:T(8,128)(2,1)} %later_products.1), calls=%async_computation.1 | async-start | bytes 2162688 | tf_op jit(solution)/shard_map/all_to_all | solution.py:487
  139.1 3.5 %collective-permute-start.36 = (f32[256,128]{1,0:T(8,128)S(1)}, f32[256,128]{1,0:T(8,128)S(1)}, u32[]{:S(2)}, u32[]{:S(2)}) collective-permute-start(f32[256,128]{1,0:T(8,128)S(1)} %get-tuple-element.33), channel_id=1, source_target_pairs={{0,1},{1,0},{2,3},{3,2},{4,5},{5,4},{6,7},{7,6},{8,9},{9,8},{10,11... | collective-permute-start | bytes 393224 | tf_op jit(solution)/shard_map/ppermute | solution.py:308
  (1 other events, 0.7 us)

commit v11 on v10

--- a/solution.py
+++ b/solution.py
@@ -148,31 +148,6 @@
     for copy in copies:
         copy.start()
     return copies
-
-
-def products(facts_refs, copies, tiles, panel, total):
-    unroll = 16
-    slots = tiles.shape[0] // 2
-    dummy = total.shape[0] - 1
-    for which, facts_ref in enumerate(facts_refs):
-        copies[which].wait()
-        pairs = facts_ref[3, 0]
-
-        def group(g, carry, base=which * slots, facts_ref=facts_ref, pairs=pairs):
-            for u in range(unroll):
-                pair = g * unroll + u
-                at = 2 * pair
-                target = jnp.where(pair < pairs, facts_ref[2, at], dummy)
-                left = jnp.concatenate(
-                    [tiles[base + facts_ref[0, at]], tiles[base + facts_ref[0, at + 1]]], axis=1
-                )
-                right = jnp.concatenate(
-                    [panel[facts_ref[1, at]], panel[facts_ref[1, at + 1]]], axis=0
-                )
-                total[target] += jnp.dot(left, right, preferred_element_type=jnp.float32)
-            return carry
-
-        lax.fori_loop(0, (pairs + unroll - 1) // unroll, group, 0)
 
 
 def single_products(slot_refs, count_ref, core_ref, copies, tiles, panel, total):
@@ -255,17 +230,17 @@
     round_parts(total, out_ref)
 
 
-def later_kernel(pieces, rows, own_facts, sib_facts, chip_ref, own_ref, sib_ref, *refs):
-    piece_refs = refs[:pieces]
-    out_ref, panel, total, tiles, arrived = refs[pieces:]
+def later_kernel(pieces, rows, *refs):
+    slot_refs, (count_ref, core_ref, chip_ref, own_ref, sib_ref) = refs[:4], refs[4:9]
+    piece_refs = refs[9 : 9 + pieces]
+    out_ref, panel, total, tiles, arrived = refs[9 + pieces :]
     copies = fetch(own_ref, sib_ref, tiles, arrived)
     total[...] = jnp.zeros_like(total)
     per = rows // TILE
     for p in range(pieces):
         for t in range(per):
             panel[chip_ref[p] * per + t] = piece_refs[p][t * TILE : (t + 1) * TILE, :]
-    panel[pieces * per] = jnp.zeros((TILE, LANES), jnp.bfloat16)
-    products((own_facts, sib_facts), copies, tiles, panel, total)
+    single_products(slot_refs, count_ref, core_ref, copies, tiles, panel, total)
     round_parts(total, out_ref)
 
 
@@ -364,35 +339,6 @@
 
     target_total = grid_rows * per
 
-    def order_tiles(tile_rows, tile_cols, tile_count):
-        sources = tile_cols - row_index * band_tiles
-        targets = tile_rows // band_tiles * per + core * BT + tile_rows % BT
-        slot_ids = jnp.arange(slots, dtype=jnp.int32)
-        live = slot_ids < tile_count[0]
-        target_ids = jnp.arange(target_total, dtype=jnp.int32)
-        at_target = (targets[:, None] == target_ids[None, :]) & live[:, None]
-        filled = (jnp.sum(at_target.astype(jnp.int32), axis=0) + 1) // 2 * 2
-        before = target_ids[:, None] < target_ids[None, :]
-        start = jnp.sum(jnp.where(before, filled[:, None], 0), axis=0)
-        alike = (targets[:, None] == targets[None, :]) & (slot_ids[None, :] < slot_ids[:, None])
-        place = jnp.sum(alike.astype(jnp.int32), axis=1)
-        place = place + jnp.sum(jnp.where(at_target, start[None, :], 0), axis=1)
-        long = slots + target_total
-        moved = (place[:, None] == jnp.arange(long)[None, :]) & live[:, None]
-
-        def spread(value):
-            return jnp.sum(jnp.where(moved, value[:, None], 0), axis=0)
-
-        facts = jnp.stack(
-            [
-                spread(slot_ids),
-                spread(sources - band_tiles) + band_tiles,
-                spread(targets),
-                jnp.broadcast_to(jnp.sum(filled) // 2, (long,)),
-            ]
-        )
-        return facts
-
     def count_seeds(seed_ids):
         first_page = (row_index * grid_cols + col_index - core) * own_rows
         return pl.pallas_call(
@@ -409,7 +355,7 @@
             name="seed_counts",
         )(jnp.stack([first_page, core]), seed_ids)
 
-    def multiply(pieces, names, sums, facts):
+    def multiply(pieces, names, sums):
         order = jnp.stack([(high ^ y) * depth + (z + d) % depth for y, d in names])
         n = len(pieces)
         rows = per * TILE
@@ -421,11 +367,12 @@
             pltpu.SemaphoreType.DMA((2,)),
         ]
         tiles = (in_hbm(tile_values), in_hbm(sib_tiles))
+        counts = jnp.concatenate([tile_count, slots_there[2, :1]])
+        where = (tile_rows, tile_cols, slots_there[0], slots_there[1], counts, core.reshape(1), order)
         if sums is not None:
             far = 6
             pieces = pieces[: n - far] + [in_hbm(piece) for piece in pieces[n - far :]]
             longest = max(piece.shape[0] for piece in pieces)
-            counts = jnp.concatenate([tile_count, slots_there[2, :1]])
             return pl.pallas_call(
                 lambda *refs: first_kernel(n, far, *refs),
                 out_shape=(parts, jax.ShapeDtypeStruct((rows, half), jnp.float32)),
@@ -444,18 +391,17 @@
                 compiler_params=params(20),
                 name="first_products",
             )(
-                tile_rows, tile_cols, slots_there[0], slots_there[1], counts, core.reshape(1),
-                order, sums.reshape(chips, per, TILE), *tiles, *pieces,
+                *where, sums.reshape(chips, per, TILE), *tiles, *pieces
             )
         return pl.pallas_call(
             lambda *refs: later_kernel(n, rows, *refs),
             out_shape=parts,
-            in_specs=[smem()] * 3 + [anywhere()] * 2 + [vmem()] * n,
+            in_specs=[smem()] * 7 + [anywhere()] * 2 + [vmem()] * n,
             out_specs=vmem(),
             scratch_shapes=scratch,
             compiler_params=params(20),
             name="later_products",
-        )(*facts, order, *tiles, *pieces)
+        )(*where, *tiles, *pieces)
 
     def update(parts, restart, inverse, scaled):
         return pl.pallas_call(
@@ -474,16 +420,13 @@
     sums = jnp.where(
         core == 0, jnp.concatenate([found, other]), jnp.concatenate([other, found])
     )
-    parts, inverse = multiply(pieces, names, sums, None)
-    parts, raw, lists = tie((parts, (tile_rows, tile_cols, tile_count), seed_ids))
+    parts, inverse = multiply(pieces, names, sums)
+    parts, lists = tie((parts, seed_ids))
     restart = count_seeds(lists)
-    facts = order_tiles(*raw)
     parts = lax.all_to_all(parts, "row", 0, 0, tiled=True)
-    parts, restart, facts = tie((parts, restart, facts))
-    facts = (facts, sibling(facts))
     panel = update(parts, restart, inverse, True)
     pieces, names, _ = gather(panel)
-    parts = multiply(pieces, names, None, facts)
+    parts = multiply(pieces, names, None)
     parts = lax.all_to_all(parts, "row", 0, 0, tiled=True)
     current = update(parts, restart, inverse, False)
     mine = lax.dynamic_slice_in_dim(current, core * own_rows, own_rows, 0)

time: 144 us -> 143 us (level)
  starting transfers between devices: 69 us -> 72.1 us
  between operations: 3.86 us -> 1.08 us
  other arithmetic: 4.35 us -> 2.67 us
    ppermute x37 -> x36, starting transfers between devices: 60.6 us -> 63.8 us  [by_col(): return lax.ppermute(value, 'col', pairs)]
    ppermute x37 -> x36, waiting for transfers between devices: 18.4 us -> 19.5 us  [by_col(): return lax.ppermute(value, 'col', pairs)]
  transfers between devices with their start and end apart: 39 -> 38, of which waited for: 17 -> 19; matrix products, arithmetic and copies ran while one was open for 2% -> 1% of each run, Pallas kernels for 7% -> 7%
where the time goes in v11:
time: 143 us; the launch traced here: 144 us
  starting transfers between devices  72.1 us (50%)
  waiting for transfers between devices  38.6 us (27%)
  Pallas kernels  27.7 us (19%)
  other arithmetic  2.67 us (2%)
  local copies, waits for them, and re-layouts  1.49 us (1%)
    ppermute x36, starting transfers between devices, by_col(): return lax.ppermute(value, 'col', pairs)  63.8 us
    ppermute x36, waiting for transfers between devices, by_col(): return lax.ppermute(value, 'col', pairs)  19.5 us
    all_to_all x2, waiting for transfers between devices, per_device(): parts = lax.all_to_all(parts, 'row', 0, 0, tiled=True)  19.1 us
    pallas_call x1, Pallas kernels, multiply(): pl.pallas_call(lambda *refs: first_kernel(n, far, *refs), out_shape=(part...  9.27 us
    all_to_all x2, starting transfers between devices, per_device(): parts = lax.all_to_all(parts, 'row', 0, 0, tiled=True)  8.29 us
    pallas_call x1, Pallas kernels, multiply(): pl.pallas_call(lambda *refs: later_kernel(n, rows, *refs), out_shape=part...  7.64 us
    pallas_call x1, Pallas kernels, count_seeds(): pl.pallas_call(seed_kernel, out_shape=jax.ShapeDtypeStruct((2 * own_rows,...  7.42 us
  transfers between devices with their start and end apart: 38, of which 19 were waited for; matrix products, arithmetic and copies ran while one was open for 1% of the time, Pallas kernels for 7%

profile of v11, /device:TPU:1, one launch (start us, length us, event | category | flops | bytes accessed | tf_op | source)
XLA Modules:
  0.0 143.6 jit_solution(15891498131202097749)
XLA Ops:
  0.7 0.7 add_add_fusion.1
  1.5 3.3 %collective-permute-start = (s32[3,96]{1,0:T(4,128)S(1)}, s32[3,96]{1,0:T(4,128)S(1)}, u32[]{:S(2)}, u32[]{:S(2)}) collective-permute-start(s32[3,96]{1,0:T(4,128)S(1)} %add_add_fusion.1), channel_id=1, source_target_pairs={{0,1},{1,0},{2,3},{3,2},{4,5},{5,4},{6,7},{7,6},{8,9},{9,8},{10,11... | collective-permute-start | bytes 3464 | tf_op jit(solution)/shard_map/ppermute | solution.py:283
  4.8 0.7 copy-done.1
  5.5 2.5 %column_sums.1 = f32[64,128]{1,0:T(8,128)S(1)} custom-call(s32[96]{0:T(128)S(1)} %copy-done.1, s32[1]{0:T(128)S(6)} %copy.7.count_ref, bf16[96,128,128]{2,1,0:T(8,128)(2,1)} %refs_7_.1), custom_call_target="tpu_custom_call" | custom-call | tf_op jit(solution)/shard_map/column_sums/pallas_call | solution.py:326
  9.0 0.6 slice.149
  9.6 0.8 collective-permute-done.2
  10.6 3.9 %collective-permute-start.6 = (s16[576,128]{1,0:T(8,128)(2,1)S(1)}, s16[576,128]{1,0:T(8,128)(2,1)S(1)}, u32[]{:S(2)}, u32[]{:S(2)}) collective-permute-start(s16[576,128]{1,0:T(8,128)(2,1)S(1)} %pad_add_fusion.refs_10_), channel_id=1, source_target_pairs={{0,14},{1,15},{2,0},{3,1},{4,2},{5,3},{6,4},{7,5},{8,6},{9,7},{10,... | collective-permute-start | bytes 442376 | tf_op jit(solution)/shard_map/ppermute | solution.py:283
  14.5 2.9 %collective-permute-start.4 = (s16[576,128]{1,0:T(8,128)(2,1)S(1)}, s16[576,128]{1,0:T(8,128)(2,1)S(1)}, u32[]{:S(2)}, u32[]{:S(2)}) collective-permute-start(s16[576,128]{1,0:T(8,128)(2,1)S(1)} %pad_add_fusion.refs_10_), channel_id=1, source_target_pairs={{0,16},{1,17},{2,18},{3,19},{4,20},{5,21},{6,22},{7,23},{8,24},{9,... | collective-permute-start | bytes 442376 | tf_op jit(solution)/shard_map/ppermute | solution.py:283
  17.6 3.4 %collective-permute-start.10 = (s16[576,128]{1,0:T(8,128)(2,1)S(1)}, s16[576,128]{1,0:T(8,128)(2,1)S(1)}, u32[]{:S(2)}, u32[]{:S(2)}) collective-permute-start(s16[576,128]{1,0:T(8,128)(2,1)S(1)} %collective-permute-done.6.refs_13_), channel_id=1, source_target_pairs={{0,14},{1,15},{2,0},{3,1},{4,2},{5,3},{6,4},{7,5},{8,6},{9,7},{10,... | collective-permute-start | bytes 442376 | tf_op jit(solution)/shard_map/ppermute | solution.py:283
  21.1 2.7 %collective-permute-start.8 = (s16[576,128]{1,0:T(8,128)(2,1)S(1)}, s16[576,128]{1,0:T(8,128)(2,1)S(1)}, u32[]{:S(2)}, u32[]{:S(2)}) collective-permute-start(s16[576,128]{1,0:T(8,128)(2,1)S(1)} %collective-permute-done.4.refs_11_), channel_id=1, source_target_pairs={{0,14},{1,15},{2,0},{3,1},{4,2},{5,3},{6,4},{7,5},{8,6},{9,7},{10,... | collective-permute-start | bytes 442376 | tf_op jit(solution)/shard_map/ppermute | solution.py:283
  23.9 2.7 %collective-permute-start.14 = (s16[576,128]{1,0:T(8,128)(2,1)S(1)}, s16[576,128]{1,0:T(8,128)(2,1)S(1)}, u32[]{:S(2)}, u32[]{:S(2)}) collective-permute-start(s16[576,128]{1,0:T(8,128)(2,1)S(1)} %collective-permute-done.10.refs_17_), channel_id=1, source_target_pairs={{0,14},{1,15},{2,0},{3,1},{4,2},{5,3},{6,4},{7,5},{8,6},{9,7},{10,... | collective-permute-start | bytes 442376 | tf_op jit(solution)/shard_map/ppermute | solution.py:283
  26.6 2.7 %collective-permute-start.12 = (s16[576,128]{1,0:T(8,128)(2,1)S(1)}, s16[576,128]{1,0:T(8,128)(2,1)S(1)}, u32[]{:S(2)}, u32[]{:S(2)}) collective-permute-start(s16[576,128]{1,0:T(8,128)(2,1)S(1)} %collective-permute-done.8.refs_15_), channel_id=1, source_target_pairs={{0,14},{1,15},{2,0},{3,1},{4,2},{5,3},{6,4},{7,5},{8,6},{9,7},{10,... | collective-permute-start | bytes 442376 | tf_op jit(solution)/shard_map/ppermute | solution.py:283
  29.6 3.3 %collective-permute-done.13.refs_20_ = s16[576,128]{1,0:T(8,128)(2,1)S(1)} collective-permute-done((s16[576,128]{1,0:T(8,128)(2,1)S(1)}, s16[576,128]{1,0:T(8,128)(2,1)S(1)}, u32[]{:S(2)}, u32[]{:S(2)}) %collective-permute-start.13) | collective-permute-done | bytes 147488 | tf_op jit(solution)/shard_map/ppermute | solution.py:283
  32.9 3.1 %collective-permute-start.16 = (s16[576,128]{1,0:T(8,128)(2,1)S(1)}, s16[576,128]{1,0:T(8,128)(2,1)S(1)}, u32[]{:S(2)}, u32[]{:S(2)}) collective-permute-start(s16[576,128]{1,0:T(8,128)(2,1)S(1)} %collective-permute-done.12.refs_19_), channel_id=1, source_target_pairs={{0,14},{1,15},{2,0},{3,1},{4,2},{5,3},{6,4},{7,5},{8,6},{9,7},{10,... | collective-permute-start | bytes 442376 | tf_op jit(solution)/shard_map/ppermute | solution.py:283
  36.1 0.5 collective-permute-done.11.refs_18_
  36.7 1.5 %collective-permute-done.16.refs_23_ = s16[576,128]{1,0:T(8,128)(2,1)S(1)} collective-permute-done((s16[576,128]{1,0:T(8,128)(2,1)S(1)}, s16[576,128]{1,0:T(8,128)(2,1)S(1)}, u32[]{:S(2)}, u32[]{:S(2)}) %collective-permute-start.16) | collective-permute-done | bytes 147488 | tf_op jit(solution)/shard_map/ppermute | solution.py:283
  38.2 3.1 %collective-permute-start.18 = (s16[576,128]{1,0:T(8,128)(2,1)S(1)}, s16[576,128]{1,0:T(8,128)(2,1)S(1)}, u32[]{:S(2)}, u32[]{:S(2)}) collective-permute-start(s16[576,128]{1,0:T(8,128)(2,1)S(1)} %collective-permute-done.16.refs_23_), channel_id=1, source_target_pairs={{0,14},{1,15},{2,0},{3,1},{4,2},{5,3},{6,4},{7,5},{8,6},{9,7},{10,... | collective-permute-start | bytes 442376 | tf_op jit(solution)/shard_map/ppermute | solution.py:283
  41.3 1.4 %collective-permute-done.15.refs_22_ = s16[576,128]{1,0:T(8,128)(2,1)S(1)} collective-permute-done((s16[576,128]{1,0:T(8,128)(2,1)S(1)}, s16[576,128]{1,0:T(8,128)(2,1)S(1)}, u32[]{:S(2)}, u32[]{:S(2)}) %collective-permute-start.15) | collective-permute-done | bytes 147488 | tf_op jit(solution)/shard_map/ppermute | solution.py:283
  42.8 1.4 collective-permute-done.18.refs_25_
  44.3 6.1 %collective-permute-start.19 = (f32[32,128]{1,0:T(8,128)S(1)}, f32[32,128]{1,0:T(8,128)S(1)}, u32[]{:S(2)}, u32[]{:S(2)}) collective-permute-start(f32[32,128]{1,0:T(8,128)S(1)} %fusion.3), channel_id=1, source_target_pairs={{0,1},{1,0},{2,3},{3,2},{4,5},{5,4},{6,7},{7,6},{8,9},{9,8},{10,11... | collective-permute-start | bytes 49160 | tf_op jit(solution)/shard_map/ppermute | solution.py:283
  50.4 0.7 pad_add_fusion.1.refs_4_
  51.3 9.3 %first_products.1 = (s16[8,528,128]{2,1,0:T(8,128)(2,1)}, f32[512,128]{1,0:T(8,128)S(1)}) custom-call(s32[96]{0:T(128)S(1)} %copy-done.3, s32[96]{0:T(128)S(1)} %copy-done.2, s32[96]{0:T(128)S(1)} %get-tuple-element.20.refs_2_, s32[96]{0:T(128)S(1)} %get-tuple-element.19.refs_3_, s32[2]{0:T(128)S(1)} %pad_add_fusion.1.refs_4_, s32[1]{0:T(128)} %bitcast.6.refs_5_, ...), custom_call_target="tpu_custom_call" | custom-call | tf_op jit(solution)/shard_map/first_products/pallas_call | solution.py:376
  60.6 4.7 %all-to-all-start = ((s16[8,528,128]{2,1,0:T(8,128)(2,1)}), s16[8,528,128]{2,1,0:T(8,128)(2,1)S(1)}, u32[]{:S(2)}, u32[]{:S(2)}) async-start(s16[8,528,128]{2,1,0:T(8,128)(2,1)} %get-tuple-element.10), calls=%async_computation | async-start | bytes 2162688 | tf_op jit(solution)/shard_map/all_to_all | solution.py:426
  65.4 7.4 %seed_counts.1.refs_1_ = f32[512,128]{1,0:T(8,128)S(1)} custom-call(s32[2]{0:T(128)S(1)} %pad_add_fusion.2.where_ref, s32[256,1024]{1,0:T(8,128)S(1)} %copy-done), custom_call_target="tpu_custom_call" | custom-call | tf_op jit(solution)/shard_map/seed_counts/pallas_call | solution.py:344
  72.8 8.7 %all-to-all-done.refs_0_ = s16[8,528,128]{2,1,0:T(8,128)(2,1)S(1)} async-done(((s16[8,528,128]{2,1,0:T(8,128)(2,1)}), s16[8,528,128]{2,1,0:T(8,128)(2,1)S(1)}, u32[]{:S(2)}, u32[]{:S(2)}) %all-to-all-start) | async-done | bytes 1081376 | tf_op jit(solution)/shard_map/all_to_all | solution.py:426
  81.5 0.4 current.2.refs_9_
  81.9 3.2 %collective-permute-start.20 = (bf16[512,128]{1,0:T(8,128)(2,1)S(1)}, bf16[512,128]{1,0:T(8,128)(2,1)S(1)}, u32[]{:S(2)}, u32[]{:S(2)}) collective-permute-start(bf16[512,128]{1,0:T(8,128)(2,1)S(1)} %current.2.refs_9_), channel_id=1, source_target_pairs={{0,16},{1,17},{2,18},{3,19},{4,20},{5,21},{6,22},{7,23},{8,24},{9,... | collective-permute-start | bytes 393224 | tf_op jit(solution)/shard_map/ppermute | solution.py:283
  85.1 2.4 %collective-permute-done.20.refs_10_ = bf16[512,128]{1,0:T(8,128)(2,1)S(1)} collective-permute-done((bf16[512,128]{1,0:T(8,128)(2,1)S(1)}, bf16[512,128]{1,0:T(8,128)(2,1)S(1)}, u32[]{:S(2)}, u32[]{:S(2)}) %collective-permute-start.20) | collective-permute-done | bytes 131104 | tf_op jit(solution)/shard_map/ppermute | solution.py:283
  87.5 3.9 %collective-permute-start.24 = (bf16[512,128]{1,0:T(8,128)(2,1)S(1)}, bf16[512,128]{1,0:T(8,128)(2,1)S(1)}, u32[]{:S(2)}, u32[]{:S(2)}) collective-permute-start(bf16[512,128]{1,0:T(8,128)(2,1)S(1)} %collective-permute-done.20.refs_10_), channel_id=1, source_target_pairs={{0,14},{1,15},{2,0},{3,1},{4,2},{5,3},{6,4},{7,5},{8,6},{9,7},{10,... | collective-permute-start | bytes 393224 | tf_op jit(solution)/shard_map/ppermute | solution.py:283
  91.4 1.4 collective-permute-start.25
  92.9 0.4 collective-permute-done.24.refs_14_
  93.3 3.1 %collective-permute-start.28 = (bf16[512,128]{1,0:T(8,128)(2,1)S(1)}, bf16[512,128]{1,0:T(8,128)(2,1)S(1)}, u32[]{:S(2)}, u32[]{:S(2)}) collective-permute-start(bf16[512,128]{1,0:T(8,128)(2,1)S(1)} %collective-permute-done.24.refs_14_), channel_id=1, source_target_pairs={{0,14},{1,15},{2,0},{3,1},{4,2},{5,3},{6,4},{7,5},{8,6},{9,7},{10,... | collective-permute-start | bytes 393224 | tf_op jit(solution)/shard_map/ppermute | solution.py:283
  96.4 1.4 collective-permute-start.26
  98.1 1.1 collective-permute-done.28.refs_18_
  99.1 3.1 %collective-permute-start.32 = (bf16[512,128]{1,0:T(8,128)(2,1)S(1)}, bf16[512,128]{1,0:T(8,128)(2,1)S(1)}, u32[]{:S(2)}, u32[]{:S(2)}) collective-permute-start(bf16[512,128]{1,0:T(8,128)(2,1)S(1)} %collective-permute-done.28.refs_18_), channel_id=1, source_target_pairs={{0,14},{1,15},{2,0},{3,1},{4,2},{5,3},{6,4},{7,5},{8,6},{9,7},{10,... | collective-permute-start | bytes 393224 | tf_op jit(solution)/shard_map/ppermute | solution.py:283
  102.3 1.4 collective-permute-start.30
  103.7 0.8 collective-permute-done.27.refs_17_
  104.6 0.6 collective-permute-done.32.refs_22_
  105.2 3.4 %collective-permute-start.34 = (bf16[512,128]{1,0:T(8,128)(2,1)S(1)}, bf16[512,128]{1,0:T(8,128)(2,1)S(1)}, u32[]{:S(2)}, u32[]{:S(2)}) collective-permute-start(bf16[512,128]{1,0:T(8,128)(2,1)S(1)} %collective-permute-done.32.refs_22_), channel_id=1, source_target_pairs={{0,14},{1,15},{2,0},{3,1},{4,2},{5,3},{6,4},{7,5},{8,6},{9,7},{10,... | collective-permute-start | bytes 393224 | tf_op jit(solution)/shard_map/ppermute | solution.py:283
  108.6 1.8 %collective-permute-done.33.refs_23_ = bf16[512,128]{1,0:T(8,128)(2,1)S(1)} collective-permute-done((bf16[512,128]{1,0:T(8,128)(2,1)S(1)}, bf16[512,128]{1,0:T(8,128)(2,1)S(1)}, u32[]{:S(2)}, u32[]{:S(2)}) %collective-permute-start.33) | collective-permute-done | bytes 131104 | tf_op jit(solution)/shard_map/ppermute | solution.py:283
  110.3 1.9 %collective-permute-done.31.refs_21_ = bf16[512,128]{1,0:T(8,128)(2,1)S(1)} collective-permute-done((bf16[512,128]{1,0:T(8,128)(2,1)S(1)}, bf16[512,128]{1,0:T(8,128)(2,1)S(1)}, u32[]{:S(2)}, u32[]{:S(2)}) %collective-permute-start.31) | collective-permute-done | bytes 131104 | tf_op jit(solution)/shard_map/ppermute | solution.py:283
  112.3 7.6 %later_products.1 = s16[8,528,128]{2,1,0:T(8,128)(2,1)} custom-call(s32[96]{0:T(128)S(1)} %copy-done.3, s32[96]{0:T(128)S(1)} %copy-done.2, s32[96]{0:T(128)S(1)} %get-tuple-element.20.refs_2_, s32[96]{0:T(128)S(1)} %get-tuple-element.19.refs_3_, s32[2]{0:T(128)S(1)} %pad_add_fusion.1.refs_4_, s32[1]{0:T(128)} %bitcast.6.refs_5_, s32[16]{0:T(128)S(1)} %stack.103.refs_6_, ...), custom_call_target="tpu_custom_call" | custom-call | tf_op jit(solution)/shard_map/later_products/pallas_call | solution.py:396
  119.9 3.6 %all-to-all-start.1 = ((s16[8,528,128]{2,1,0:T(8,128)(2,1)}), s16[8,528,128]{2,1,0:T(8,128)(2,1)S(1)}, u32[]{:S(2)}, u32[]{:S(2)}) async-start(s16[8,528,128]{2,1,0:T(8,128)(2,1)} %later_products.1), calls=%async_computation.1 | async-start | bytes 2162688 | tf_op jit(solution)/shard_map/all_to_all | solution.py:430
  123.5 10.4 %all-to-all-done.1.refs_0_ = s16[8,528,128]{2,1,0:T(8,128)(2,1)S(1)} async-done(((s16[8,528,128]{2,1,0:T(8,128)(2,1)}), s16[8,528,128]{2,1,0:T(8,128)(2,1)S(1)}, u32[]{:S(2)}, u32[]{:S(2)}) %all-to-all-start.1) | async-done | bytes 1081376 | tf_op jit(solution)/shard_map/all_to_all | solution.py:430
  133.9 0.4 current.3
  134.3 7.5 %collective-permute-start.35 = (f32[256,128]{1,0:T(8,128)S(1)}, f32[256,128]{1,0:T(8,128)S(1)}, u32[]{:S(2)}, u32[]{:S(2)}) collective-permute-start(f32[256,128]{1,0:T(8,128)S(1)} %get-tuple-element.16), channel_id=1, source_target_pairs={{0,1},{1,0},{2,3},{3,2},{4,5},{5,4},{6,7},{7,6},{8,9},{9,8},{10,11... | collective-permute-start | bytes 393224 | tf_op jit(solution)/shard_map/ppermute | solution.py:283
  141.8 1.0 collective-permute-done.35
  142.8 0.7 maximum_select_fusion
  (90 shorter events, 2.6 us)
Async XLA Ops:
  1.5 7.5 %collective-permute-start = (s32[3,96]{1,0:T(4,128)S(1)}, s32[3,96]{1,0:T(4,128)S(1)}, u32[]{:S(2)}, u32[]{:S(2)}) collective-permute-start(s32[3,96]{1,0:T(4,128)S(1)} %add_add_fusion.1), channel_id=1, source_target_pairs={{0,1},{1,0},{2,3},{3,2},{4,5},{5,4},{6,7},{7,6},{8,9},{9,8},{10,11... | collective-permute-start | bytes 3464 | tf_op jit(solution)/shard_map/ppermute | solution.py:283
  4.7 46.5 %collective-permute-start.1 = (bf16[96,128,128]{2,1,0:T(8,128)(2,1)}, bf16[96,128,128]{2,1,0:T(8,128)(2,1)}, u32[]{:S(2)}, u32[]{:S(2)}) collective-permute-start(bf16[96,128,128]{2,1,0:T(8,128)(2,1)} %refs_7_.1), channel_id=1, source_target_pairs={{0,1},{1,0},{2,3},{3,2},{4,5},{5,4},{6,7},{7,6},{8,9},{9,8},{10,11... | collective-permute-start | bytes 9437192 | tf_op jit(solution)/shard_map/ppermute | solution.py:283
  5.5 3.0 %copy-start.4 = (f32[256,256]{1,0:T(8,128)S(1)}, f32[256,256]{1,0:T(8,128)}, u32[]{:S(2)}) copy-start(f32[256,256]{1,0:T(8,128)} %param.6) | copy-start | bytes 786436
  8.1 2.3 %collective-permute-start.2 = (f32[32,128]{1,0:T(8,128)S(1)}, f32[32,128]{1,0:T(8,128)S(1)}, u32[]{:S(2)}, u32[]{:S(2)}) collective-permute-start(f32[32,128]{1,0:T(8,128)S(1)} %constant_dynamic-slice_fusion.4), channel_id=1, source_target_pairs={{0,1},{1,0},{2,3},{3,2},{4,5},{5,4},{6,7},{7,6},{8,9},{9,8},{10,11... | collective-permute-start | bytes 49160 | tf_op jit(solution)/shard_map/ppermute | solution.py:283
  8.6 1.9 %collective-permute-start.3 = (s16[256,128]{1,0:T(8,128)(2,1)S(1)}, s16[256,128]{1,0:T(8,128)(2,1)S(1)}, u32[]{:S(2)}, u32[]{:S(2)}) collective-permute-start(s16[256,128]{1,0:T(8,128)(2,1)S(1)} %get-tuple-element.18), channel_id=1, source_target_pairs={{0,1},{1,0},{2,3},{3,2},{4,5},{5,4},{6,7},{7,6},{8,9},{9,8},{10,11... | collective-permute-start | bytes 196616 | tf_op jit(solution)/shard_map/ppermute | solution.py:283
  8.9 42.4 %copy-start.2 = (s32[96]{0:T(128)S(1)}, s32[96]{0:T(128)}, u32[]{:S(2)}) copy-start(s32[96]{0:T(128)} %refs_1_.3) | copy-start | bytes 1156
  8.9 42.4 %copy-start.3 = (s32[96]{0:T(128)S(1)}, s32[96]{0:T(128)}, u32[]{:S(2)}) copy-start(s32[96]{0:T(128)} %refs_0_.3) | copy-start | bytes 1156
  10.6 7.0 %collective-permute-start.6 = (s16[576,128]{1,0:T(8,128)(2,1)S(1)}, s16[576,128]{1,0:T(8,128)(2,1)S(1)}, u32[]{:S(2)}, u32[]{:S(2)}) collective-permute-start(s16[576,128]{1,0:T(8,128)(2,1)S(1)} %pad_add_fusion.refs_10_), channel_id=1, source_target_pairs={{0,14},{1,15},{2,0},{3,1},{4,2},{5,3},{6,4},{7,5},{8,6},{9,7},{10,... | collective-permute-start | bytes 442376 | tf_op jit(solution)/shard_map/ppermute | solution.py:283
  14.5 6.5 %collective-permute-start.5 = (s16[576,128]{1,0:T(8,128)(2,1)S(1)}, s16[576,128]{1,0:T(8,128)(2,1)S(1)}, u32[]{:S(2)}, u32[]{:S(2)}) collective-permute-start(s16[576,128]{1,0:T(8,128)(2,1)S(1)} %pad_add_fusion.refs_10_), channel_id=1, source_target_pairs={{0,2},{1,3},{2,4},{3,5},{4,6},{5,7},{6,8},{7,9},{8,10},{9,11},{10,... | collective-permute-start | bytes 442376 | tf_op jit(solution)/shard_map/ppermute | solution.py:283
  14.5 6.6 %collective-permute-start.4 = (s16[576,128]{1,0:T(8,128)(2,1)S(1)}, s16[576,128]{1,0:T(8,128)(2,1)S(1)}, u32[]{:S(2)}, u32[]{:S(2)}) collective-permute-start(s16[576,128]{1,0:T(8,128)(2,1)S(1)} %pad_add_fusion.refs_10_), channel_id=1, source_target_pairs={{0,16},{1,17},{2,18},{3,19},{4,20},{5,21},{6,22},{7,23},{8,24},{9,... | collective-permute-start | bytes 442376 | tf_op jit(solution)/shard_map/ppermute | solution.py:283
  17.6 6.3 %collective-permute-start.10 = (s16[576,128]{1,0:T(8,128)(2,1)S(1)}, s16[576,128]{1,0:T(8,128)(2,1)S(1)}, u32[]{:S(2)}, u32[]{:S(2)}) collective-permute-start(s16[576,128]{1,0:T(8,128)(2,1)S(1)} %collective-permute-done.6.refs_13_), channel_id=1, source_target_pairs={{0,14},{1,15},{2,0},{3,1},{4,2},{5,3},{6,4},{7,5},{8,6},{9,7},{10,... | collective-permute-start | bytes 442376 | tf_op jit(solution)/shard_map/ppermute | solution.py:283
  21.0 5.6 %collective-permute-start.9 = (s16[576,128]{1,0:T(8,128)(2,1)S(1)}, s16[576,128]{1,0:T(8,128)(2,1)S(1)}, u32[]{:S(2)}, u32[]{:S(2)}) collective-permute-start(s16[576,128]{1,0:T(8,128)(2,1)S(1)} %collective-permute-done.5.refs_12_), channel_id=1, source_target_pairs={{0,2},{1,3},{2,4},{3,5},{4,6},{5,7},{6,8},{7,9},{8,10},{9,11},{10,... | collective-permute-start | bytes 442376 | tf_op jit(solution)/shard_map/ppermute | solution.py:283
  21.1 5.5 %collective-permute-start.8 = (s16[576,128]{1,0:T(8,128)(2,1)S(1)}, s16[576,128]{1,0:T(8,128)(2,1)S(1)}, u32[]{:S(2)}, u32[]{:S(2)}) collective-permute-start(s16[576,128]{1,0:T(8,128)(2,1)S(1)} %collective-permute-done.4.refs_11_), channel_id=1, source_target_pairs={{0,14},{1,15},{2,0},{3,1},{4,2},{5,3},{6,4},{7,5},{8,6},{9,7},{10,... | collective-permute-start | bytes 442376 | tf_op jit(solution)/shard_map/ppermute | solution.py:283
  23.9 5.7 %collective-permute-start.7 = (s16[576,128]{1,0:T(8,128)(2,1)S(1)}, s16[576,128]{1,0:T(8,128)(2,1)S(1)}, u32[]{:S(2)}, u32[]{:S(2)}) collective-permute-start(s16[576,128]{1,0:T(8,128)(2,1)S(1)} %collective-permute-done.4.refs_11_), channel_id=1, source_target_pairs={{0,2},{1,3},{2,4},{3,5},{4,6},{5,7},{6,8},{7,9},{8,10},{9,11},{10,... | collective-permute-start | bytes 442376 | tf_op jit(solution)/shard_map/ppermute | solution.py:283
  23.9 12.7 %collective-permute-start.14 = (s16[576,128]{1,0:T(8,128)(2,1)S(1)}, s16[576,128]{1,0:T(8,128)(2,1)S(1)}, u32[]{:S(2)}, u32[]{:S(2)}) collective-permute-start(s16[576,128]{1,0:T(8,128)(2,1)S(1)} %collective-permute-done.10.refs_17_), channel_id=1, source_target_pairs={{0,14},{1,15},{2,0},{3,1},{4,2},{5,3},{6,4},{7,5},{8,6},{9,7},{10,... | collective-permute-start | bytes 442376 | tf_op jit(solution)/shard_map/ppermute | solution.py:283
  26.6 6.3 %collective-permute-start.13 = (s16[576,128]{1,0:T(8,128)(2,1)S(1)}, s16[576,128]{1,0:T(8,128)(2,1)S(1)}, u32[]{:S(2)}, u32[]{:S(2)}) collective-permute-start(s16[576,128]{1,0:T(8,128)(2,1)S(1)} %collective-permute-done.9.refs_16_), channel_id=1, source_target_pairs={{0,2},{1,3},{2,4},{3,5},{4,6},{5,7},{6,8},{7,9},{8,10},{9,11},{10,... | collective-permute-start | bytes 442376 | tf_op jit(solution)/shard_map/ppermute | solution.py:283
  26.6 6.3 %collective-permute-start.12 = (s16[576,128]{1,0:T(8,128)(2,1)S(1)}, s16[576,128]{1,0:T(8,128)(2,1)S(1)}, u32[]{:S(2)}, u32[]{:S(2)}) collective-permute-start(s16[576,128]{1,0:T(8,128)(2,1)S(1)} %collective-permute-done.8.refs_15_), channel_id=1, source_target_pairs={{0,14},{1,15},{2,0},{3,1},{4,2},{5,3},{6,4},{7,5},{8,6},{9,7},{10,... | collective-permute-start | bytes 442376 | tf_op jit(solution)/shard_map/ppermute | solution.py:283
  29.6 7.0 %collective-permute-start.11 = (s16[576,128]{1,0:T(8,128)(2,1)S(1)}, s16[576,128]{1,0:T(8,128)(2,1)S(1)}, u32[]{:S(2)}, u32[]{:S(2)}) collective-permute-start(s16[576,128]{1,0:T(8,128)(2,1)S(1)} %collective-permute-done.7.refs_14_), channel_id=1, source_target_pairs={{0,2},{1,3},{2,4},{3,5},{4,6},{5,7},{6,8},{7,9},{8,10},{9,11},{10,... | collective-permute-start | bytes 442376 | tf_op jit(solution)/shard_map/ppermute | solution.py:283
  32.9 18.3 %copy-start.6 = (s16[576,128]{1,0:T(8,128)(2,1)}, s16[576,128]{1,0:T(8,128)(2,1)S(1)}, u32[]{:S(2)}) copy-start(s16[576,128]{1,0:T(8,128)(2,1)S(1)} %collective-permute-done.13.refs_20_) | copy-start | bytes 442372
  32.9 8.4 %collective-permute-start.17 = (s16[576,128]{1,0:T(8,128)(2,1)S(1)}, s16[576,128]{1,0:T(8,128)(2,1)S(1)}, u32[]{:S(2)}, u32[]{:S(2)}) collective-permute-start(s16[576,128]{1,0:T(8,128)(2,1)S(1)} %collective-permute-done.13.refs_20_), channel_id=1, source_target_pairs={{0,2},{1,3},{2,4},{3,5},{4,6},{5,7},{6,8},{7,9},{8,10},{9,11},{10,... | collective-permute-start | bytes 442376 | tf_op jit(solution)/shard_map/ppermute | solution.py:283
  32.9 5.2 %collective-permute-start.16 = (s16[576,128]{1,0:T(8,128)(2,1)S(1)}, s16[576,128]{1,0:T(8,128)(2,1)S(1)}, u32[]{:S(2)}, u32[]{:S(2)}) collective-permute-start(s16[576,128]{1,0:T(8,128)(2,1)S(1)} %collective-permute-done.12.refs_19_), channel_id=1, source_target_pairs={{0,14},{1,15},{2,0},{3,1},{4,2},{5,3},{6,4},{7,5},{8,6},{9,7},{10,... | collective-permute-start | bytes 442376 | tf_op jit(solution)/shard_map/ppermute | solution.py:283
  36.6 6.2 %collective-permute-start.15 = (s16[576,128]{1,0:T(8,128)(2,1)S(1)}, s16[576,128]{1,0:T(8,128)(2,1)S(1)}, u32[]{:S(2)}, u32[]{:S(2)}) collective-permute-start(s16[576,128]{1,0:T(8,128)(2,1)S(1)} %collective-permute-done.11.refs_18_), channel_id=1, source_target_pairs={{0,2},{1,3},{2,4},{3,5},{4,6},{5,7},{6,8},{7,9},{8,10},{9,11},{10,... | collective-permute-start | bytes 442376 | tf_op jit(solution)/shard_map/ppermute | solution.py:283
  36.6 14.6 %copy-start.5 = (s16[576,128]{1,0:T(8,128)(2,1)}, s16[576,128]{1,0:T(8,128)(2,1)S(1)}, u32[]{:S(2)}) copy-start(s16[576,128]{1,0:T(8,128)(2,1)S(1)} %collective-permute-done.14.refs_21_) | copy-start | bytes 442372
  38.2 13.1 %copy-start.8 = (s16[576,128]{1,0:T(8,128)(2,1)}, s16[576,128]{1,0:T(8,128)(2,1)S(1)}, u32[]{:S(2)}) copy-start(s16[576,128]{1,0:T(8,128)(2,1)S(1)} %collective-permute-done.16.refs_23_) | copy-start | bytes 442372
  38.2 6.0 %collective-permute-start.18 = (s16[576,128]{1,0:T(8,128)(2,1)S(1)}, s16[576,128]{1,0:T(8,128)(2,1)S(1)}, u32[]{:S(2)}, u32[]{:S(2)}) collective-permute-start(s16[576,128]{1,0:T(8,128)(2,1)S(1)} %collective-permute-done.16.refs_23_), channel_id=1, source_target_pairs={{0,14},{1,15},{2,0},{3,1},{4,2},{5,3},{6,4},{7,5},{8,6},{9,7},{10,... | collective-permute-start | bytes 442376 | tf_op jit(solution)/shard_map/ppermute | solution.py:283
  41.3 10.0 %copy-start.7 = (s16[576,128]{1,0:T(8,128)(2,1)}, s16[576,128]{1,0:T(8,128)(2,1)S(1)}, u32[]{:S(2)}) copy-start(s16[576,128]{1,0:T(8,128)(2,1)S(1)} %collective-permute-done.17.refs_24_) | copy-start | bytes 442372
  42.7 8.5 %copy-start.9 = (s16[576,128]{1,0:T(8,128)(2,1)}, s16[576,128]{1,0:T(8,128)(2,1)S(1)}, u32[]{:S(2)}) copy-start(s16[576,128]{1,0:T(8,128)(2,1)S(1)} %collective-permute-done.15.refs_22_) | copy-start | bytes 442372
  44.1 7.1 %copy-start.10 = (s16[576,128]{1,0:T(8,128)(2,1)}, s16[576,128]{1,0:T(8,128)(2,1)S(1)}, u32[]{:S(2)}) copy-start(s16[576,128]{1,0:T(8,128)(2,1)S(1)} %collective-permute-done.18.refs_25_) | copy-start | bytes 442372
  44.3 6.9 %collective-permute-start.19 = (f32[32,128]{1,0:T(8,128)S(1)}, f32[32,128]{1,0:T(8,128)S(1)}, u32[]{:S(2)}, u32[]{:S(2)}) collective-permute-start(f32[32,128]{1,0:T(8,128)S(1)} %fusion.3), channel_id=1, source_target_pairs={{0,1},{1,0},{2,3},{3,2},{4,5},{5,4},{6,7},{7,6},{8,9},{9,8},{10,11... | collective-permute-start | bytes 49160 | tf_op jit(solution)/shard_map/ppermute | solution.py:283
  60.6 4.8 %copy-start = (s32[256,1024]{1,0:T(8,128)S(1)}, s32[256,1024]{1,0:T(8,128)}, u32[]{:S(2)}) copy-start(s32[256,1024]{1,0:T(8,128)} %all_ref) | copy-start | bytes 3145732
  60.6 21.0 %all-to-all-start = ((s16[8,528,128]{2,1,0:T(8,128)(2,1)}), s16[8,528,128]{2,1,0:T(8,128)(2,1)S(1)}, u32[]{:S(2)}, u32[]{:S(2)}) async-start(s16[8,528,128]{2,1,0:T(8,128)(2,1)} %get-tuple-element.10), calls=%async_computation | async-start | bytes 2162688 | tf_op jit(solution)/shard_map/all_to_all | solution.py:426
  81.9 5.5 %collective-permute-start.20 = (bf16[512,128]{1,0:T(8,128)(2,1)S(1)}, bf16[512,128]{1,0:T(8,128)(2,1)S(1)}, u32[]{:S(2)}, u32[]{:S(2)}) collective-permute-start(bf16[512,128]{1,0:T(8,128)(2,1)S(1)} %current.2.refs_9_), channel_id=1, source_target_pairs={{0,16},{1,17},{2,18},{3,19},{4,20},{5,21},{6,22},{7,23},{8,24},{9,... | collective-permute-start | bytes 393224 | tf_op jit(solution)/shard_map/ppermute | solution.py:283
  85.1 6.3 %collective-permute-start.21 = (bf16[512,128]{1,0:T(8,128)(2,1)S(1)}, bf16[512,128]{1,0:T(8,128)(2,1)S(1)}, u32[]{:S(2)}, u32[]{:S(2)}) collective-permute-start(bf16[512,128]{1,0:T(8,128)(2,1)S(1)} %current.2.refs_9_), channel_id=1, source_target_pairs={{0,2},{1,3},{2,4},{3,5},{4,6},{5,7},{6,8},{7,9},{8,10},{9,11},{10,... | collective-permute-start | bytes 393224 | tf_op jit(solution)/shard_map/ppermute | solution.py:283
  87.5 5.9 %collective-permute-start.24 = (bf16[512,128]{1,0:T(8,128)(2,1)S(1)}, bf16[512,128]{1,0:T(8,128)(2,1)S(1)}, u32[]{:S(2)}, u32[]{:S(2)}) collective-permute-start(bf16[512,128]{1,0:T(8,128)(2,1)S(1)} %collective-permute-done.20.refs_10_), channel_id=1, source_target_pairs={{0,14},{1,15},{2,0},{3,1},{4,2},{5,3},{6,4},{7,5},{8,6},{9,7},{10,... | collective-permute-start | bytes 393224 | tf_op jit(solution)/shard_map/ppermute | solution.py:283
  91.4 5.0 %collective-permute-start.22 = (bf16[512,128]{1,0:T(8,128)(2,1)S(1)}, bf16[512,128]{1,0:T(8,128)(2,1)S(1)}, u32[]{:S(2)}, u32[]{:S(2)}) collective-permute-start(bf16[512,128]{1,0:T(8,128)(2,1)S(1)} %current.2.refs_9_), channel_id=1, source_target_pairs={{0,14},{1,15},{2,0},{3,1},{4,2},{5,3},{6,4},{7,5},{8,6},{9,7},{10,... | collective-permute-start | bytes 393224 | tf_op jit(solution)/shard_map/ppermute | solution.py:283
  91.4 6.4 %collective-permute-start.25 = (bf16[512,128]{1,0:T(8,128)(2,1)S(1)}, bf16[512,128]{1,0:T(8,128)(2,1)S(1)}, u32[]{:S(2)}, u32[]{:S(2)}) collective-permute-start(bf16[512,128]{1,0:T(8,128)(2,1)S(1)} %collective-permute-done.21.refs_11_), channel_id=1, source_target_pairs={{0,2},{1,3},{2,4},{3,5},{4,6},{5,7},{6,8},{7,9},{8,10},{9,11},{10,... | collective-permute-start | bytes 393224 | tf_op jit(solution)/shard_map/ppermute | solution.py:283
  92.9 5.0 %collective-permute-start.23 = (bf16[512,128]{1,0:T(8,128)(2,1)S(1)}, bf16[512,128]{1,0:T(8,128)(2,1)S(1)}, u32[]{:S(2)}, u32[]{:S(2)}) collective-permute-start(bf16[512,128]{1,0:T(8,128)(2,1)S(1)} %collective-permute-done.20.refs_10_), channel_id=1, source_target_pairs={{0,2},{1,3},{2,4},{3,5},{4,6},{5,7},{6,8},{7,9},{8,10},{9,11},{10,... | collective-permute-start | bytes 393224 | tf_op jit(solution)/shard_map/ppermute | solution.py:283
  93.3 5.8 %collective-permute-start.28 = (bf16[512,128]{1,0:T(8,128)(2,1)S(1)}, bf16[512,128]{1,0:T(8,128)(2,1)S(1)}, u32[]{:S(2)}, u32[]{:S(2)}) collective-permute-start(bf16[512,128]{1,0:T(8,128)(2,1)S(1)} %collective-permute-done.24.refs_14_), channel_id=1, source_target_pairs={{0,14},{1,15},{2,0},{3,1},{4,2},{5,3},{6,4},{7,5},{8,6},{9,7},{10,... | collective-permute-start | bytes 393224 | tf_op jit(solution)/shard_map/ppermute | solution.py:283
  96.4 5.8 %collective-permute-start.26 = (bf16[512,128]{1,0:T(8,128)(2,1)S(1)}, bf16[512,128]{1,0:T(8,128)(2,1)S(1)}, u32[]{:S(2)}, u32[]{:S(2)}) collective-permute-start(bf16[512,128]{1,0:T(8,128)(2,1)S(1)} %collective-permute-done.22.refs_12_), channel_id=1, source_target_pairs={{0,14},{1,15},{2,0},{3,1},{4,2},{5,3},{6,4},{7,5},{8,6},{9,7},{10,... | collective-permute-start | bytes 393224 | tf_op jit(solution)/shard_map/ppermute | solution.py:283
  97.8 5.8 %collective-permute-start.29 = (bf16[512,128]{1,0:T(8,128)(2,1)S(1)}, bf16[512,128]{1,0:T(8,128)(2,1)S(1)}, u32[]{:S(2)}, u32[]{:S(2)}) collective-permute-start(bf16[512,128]{1,0:T(8,128)(2,1)S(1)} %collective-permute-done.25.refs_15_), channel_id=1, source_target_pairs={{0,2},{1,3},{2,4},{3,5},{4,6},{5,7},{6,8},{7,9},{8,10},{9,11},{10,... | collective-permute-start | bytes 393224 | tf_op jit(solution)/shard_map/ppermute | solution.py:283
  97.9 6.7 %collective-permute-start.27 = (bf16[512,128]{1,0:T(8,128)(2,1)S(1)}, bf16[512,128]{1,0:T(8,128)(2,1)S(1)}, u32[]{:S(2)}, u32[]{:S(2)}) collective-permute-start(bf16[512,128]{1,0:T(8,128)(2,1)S(1)} %collective-permute-done.23.refs_13_), channel_id=1, source_target_pairs={{0,2},{1,3},{2,4},{3,5},{4,6},{5,7},{6,8},{7,9},{8,10},{9,11},{10,... | collective-permute-start | bytes 393224 | tf_op jit(solution)/shard_map/ppermute | solution.py:283
  99.1 6.0 %collective-permute-start.32 = (bf16[512,128]{1,0:T(8,128)(2,1)S(1)}, bf16[512,128]{1,0:T(8,128)(2,1)S(1)}, u32[]{:S(2)}, u32[]{:S(2)}) collective-permute-start(bf16[512,128]{1,0:T(8,128)(2,1)S(1)} %collective-permute-done.28.refs_18_), channel_id=1, source_target_pairs={{0,14},{1,15},{2,0},{3,1},{4,2},{5,3},{6,4},{7,5},{8,6},{9,7},{10,... | collective-permute-start | bytes 393224 | tf_op jit(solution)/shard_map/ppermute | solution.py:283
  102.3 6.3 %collective-permute-start.30 = (bf16[512,128]{1,0:T(8,128)(2,1)S(1)}, bf16[512,128]{1,0:T(8,128)(2,1)S(1)}, u32[]{:S(2)}, u32[]{:S(2)}) collective-permute-start(bf16[512,128]{1,0:T(8,128)(2,1)S(1)} %collective-permute-done.26.refs_16_), channel_id=1, source_target_pairs={{0,14},{1,15},{2,0},{3,1},{4,2},{5,3},{6,4},{7,5},{8,6},{9,7},{10,... | collective-permute-start | bytes 393224 | tf_op jit(solution)/shard_map/ppermute | solution.py:283
  103.7 6.7 %collective-permute-start.33 = (bf16[512,128]{1,0:T(8,128)(2,1)S(1)}, bf16[512,128]{1,0:T(8,128)(2,1)S(1)}, u32[]{:S(2)}, u32[]{:S(2)}) collective-permute-start(bf16[512,128]{1,0:T(8,128)(2,1)S(1)} %collective-permute-done.29.refs_19_), channel_id=1, source_target_pairs={{0,2},{1,3},{2,4},{3,5},{4,6},{5,7},{6,8},{7,9},{8,10},{9,11},{10,... | collective-permute-start | bytes 393224 | tf_op jit(solution)/shard_map/ppermute | solution.py:283
  104.6 7.7 %collective-permute-start.31 = (bf16[512,128]{1,0:T(8,128)(2,1)S(1)}, bf16[512,128]{1,0:T(8,128)(2,1)S(1)}, u32[]{:S(2)}, u32[]{:S(2)}) collective-permute-start(bf16[512,128]{1,0:T(8,128)(2,1)S(1)} %collective-permute-done.27.refs_17_), channel_id=1, source_target_pairs={{0,2},{1,3},{2,4},{3,5},{4,6},{5,7},{6,8},{7,9},{8,10},{9,11},{10,... | collective-permute-start | bytes 393224 | tf_op jit(solution)/shard_map/ppermute | solution.py:283
  105.2 7.1 %collective-permute-start.34 = (bf16[512,128]{1,0:T(8,128)(2,1)S(1)}, bf16[512,128]{1,0:T(8,128)(2,1)S(1)}, u32[]{:S(2)}, u32[]{:S(2)}) collective-permute-start(bf16[512,128]{1,0:T(8,128)(2,1)S(1)} %collective-permute-done.32.refs_22_), channel_id=1, source_target_pairs={{0,14},{1,15},{2,0},{3,1},{4,2},{5,3},{6,4},{7,5},{8,6},{9,7},{10,... | collective-permute-start | bytes 393224 | tf_op jit(solution)/shard_map/ppermute | solution.py:283
  119.9 13.9 %all-to-all-start.1 = ((s16[8,528,128]{2,1,0:T(8,128)(2,1)}), s16[8,528,128]{2,1,0:T(8,128)(2,1)S(1)}, u32[]{:S(2)}, u32[]{:S(2)}) async-start(s16[8,528,128]{2,1,0:T(8,128)(2,1)} %later_products.1), calls=%async_computation.1 | async-start | bytes 2162688 | tf_op jit(solution)/shard_map/all_to_all | solution.py:430
  134.3 8.5 %collective-permute-start.35 = (f32[256,128]{1,0:T(8,128)S(1)}, f32[256,128]{1,0:T(8,128)S(1)}, u32[]{:S(2)}, u32[]{:S(2)}) collective-permute-start(f32[256,128]{1,0:T(8,128)S(1)} %get-tuple-element.16), channel_id=1, source_target_pairs={{0,1},{1,0},{2,3},{3,2},{4,5},{5,4},{6,7},{7,6},{8,9},{9,8},{10,11... | collective-permute-start | bytes 393224 | tf_op jit(solution)/shard_map/ppermute | solution.py:283
  (1 other events, 0.7 us)

commit v12 on v11

--- a/solution.py
+++ b/solution.py
@@ -151,7 +151,7 @@
 
 
 def single_products(slot_refs, count_ref, core_ref, copies, tiles, panel, total):
-    unroll = 24
+    unroll = 32
     slots = tiles.shape[0] // 2
     dummy = total.shape[0] - 1
     per = 2 * BT

time: 143 us -> 143 us (level)
  no operation moved by 1% of the time
where the time goes in v12:
time: 143 us
  starting transfers between devices  72.4 us (51%)
  waiting for transfers between devices  38.2 us (27%)
  Pallas kernels  27.2 us (19%)
  other arithmetic  2.67 us (2%)
  local copies, waits for them, and re-layouts  1.5 us (1%)
    ppermute x36, starting transfers between devices, by_col(): return lax.ppermute(value, 'col', pairs)  63.7 us
    ppermute x36, waiting for transfers between devices, by_col(): return lax.ppermute(value, 'col', pairs)  19.5 us
    all_to_all x2, waiting for transfers between devices, per_device(): parts = lax.all_to_all(parts, 'row', 0, 0, tiled=True)  18.7 us
    pallas_call x1, Pallas kernels, multiply(): pl.pallas_call(lambda *refs: first_kernel(n, far, *refs), out_shape=(part...  8.92 us
    all_to_all x2, starting transfers between devices, per_device(): parts = lax.all_to_all(parts, 'row', 0, 0, tiled=True)  8.75 us
    pallas_call x1, Pallas kernels, count_seeds(): pl.pallas_call(seed_kernel, out_shape=jax.ShapeDtypeStruct((2 * own_rows,...  7.82 us
    pallas_call x1, Pallas kernels, multiply(): pl.pallas_call(lambda *refs: later_kernel(n, rows, *refs), out_shape=part...  7.3 us
  transfers between devices with their start and end apart: 38, of which 19 were waited for; matrix products, arithmetic and copies ran while one was open for 1% of the time, Pallas kernels for 7%

profile of v12, /device:TPU:1, one launch (start us, length us, event | category | flops | bytes accessed | tf_op | source)
XLA Modules:
  0.0 143.2 jit_solution(2980916772535405089)
XLA Ops:
  0.7 0.7 add_add_fusion.1
  1.5 3.3 %collective-permute-start = (s32[3,96]{1,0:T(4,128)S(1)}, s32[3,96]{1,0:T(4,128)S(1)}, u32[]{:S(2)}, u32[]{:S(2)}) collective-permute-start(s32[3,96]{1,0:T(4,128)S(1)} %add_add_fusion.1), channel_id=1, source_target_pairs={{0,1},{1,0},{2,3},{3,2},{4,5},{5,4},{6,7},{7,6},{8,9},{9,8},{10,11... | collective-permute-start | bytes 3464 | tf_op jit(solution)/shard_map/ppermute | solution.py:283
  4.8 0.7 copy-done.1
  5.5 2.4 %column_sums.1 = f32[64,128]{1,0:T(8,128)S(1)} custom-call(s32[96]{0:T(128)S(1)} %copy-done.1, s32[1]{0:T(128)S(6)} %copy.7.count_ref, bf16[96,128,128]{2,1,0:T(8,128)(2,1)} %refs_7_.1), custom_call_target="tpu_custom_call" | custom-call | tf_op jit(solution)/shard_map/column_sums/pallas_call | solution.py:326
  7.9 0.5 collective-permute-start.2
  9.0 0.6 slice.149
  9.6 0.8 collective-permute-done.2
  10.6 3.9 %collective-permute-start.6 = (s16[576,128]{1,0:T(8,128)(2,1)S(1)}, s16[576,128]{1,0:T(8,128)(2,1)S(1)}, u32[]{:S(2)}, u32[]{:S(2)}) collective-permute-start(s16[576,128]{1,0:T(8,128)(2,1)S(1)} %pad_add_fusion.refs_10_), channel_id=1, source_target_pairs={{0,14},{1,15},{2,0},{3,1},{4,2},{5,3},{6,4},{7,5},{8,6},{9,7},{10,... | collective-permute-start | bytes 442376 | tf_op jit(solution)/shard_map/ppermute | solution.py:283
  14.5 2.9 %collective-permute-start.4 = (s16[576,128]{1,0:T(8,128)(2,1)S(1)}, s16[576,128]{1,0:T(8,128)(2,1)S(1)}, u32[]{:S(2)}, u32[]{:S(2)}) collective-permute-start(s16[576,128]{1,0:T(8,128)(2,1)S(1)} %pad_add_fusion.refs_10_), channel_id=1, source_target_pairs={{0,16},{1,17},{2,18},{3,19},{4,20},{5,21},{6,22},{7,23},{8,24},{9,... | collective-permute-start | bytes 442376 | tf_op jit(solution)/shard_map/ppermute | solution.py:283
  17.6 3.4 %collective-permute-start.10 = (s16[576,128]{1,0:T(8,128)(2,1)S(1)}, s16[576,128]{1,0:T(8,128)(2,1)S(1)}, u32[]{:S(2)}, u32[]{:S(2)}) collective-permute-start(s16[576,128]{1,0:T(8,128)(2,1)S(1)} %collective-permute-done.6.refs_13_), channel_id=1, source_target_pairs={{0,14},{1,15},{2,0},{3,1},{4,2},{5,3},{6,4},{7,5},{8,6},{9,7},{10,... | collective-permute-start | bytes 442376 | tf_op jit(solution)/shard_map/ppermute | solution.py:283
  21.1 2.7 %collective-permute-start.8 = (s16[576,128]{1,0:T(8,128)(2,1)S(1)}, s16[576,128]{1,0:T(8,128)(2,1)S(1)}, u32[]{:S(2)}, u32[]{:S(2)}) collective-permute-start(s16[576,128]{1,0:T(8,128)(2,1)S(1)} %collective-permute-done.4.refs_11_), channel_id=1, source_target_pairs={{0,14},{1,15},{2,0},{3,1},{4,2},{5,3},{6,4},{7,5},{8,6},{9,7},{10,... | collective-permute-start | bytes 442376 | tf_op jit(solution)/shard_map/ppermute | solution.py:283
  23.9 2.7 %collective-permute-start.14 = (s16[576,128]{1,0:T(8,128)(2,1)S(1)}, s16[576,128]{1,0:T(8,128)(2,1)S(1)}, u32[]{:S(2)}, u32[]{:S(2)}) collective-permute-start(s16[576,128]{1,0:T(8,128)(2,1)S(1)} %collective-permute-done.10.refs_17_), channel_id=1, source_target_pairs={{0,14},{1,15},{2,0},{3,1},{4,2},{5,3},{6,4},{7,5},{8,6},{9,7},{10,... | collective-permute-start | bytes 442376 | tf_op jit(solution)/shard_map/ppermute | solution.py:283
  26.6 2.7 %collective-permute-start.12 = (s16[576,128]{1,0:T(8,128)(2,1)S(1)}, s16[576,128]{1,0:T(8,128)(2,1)S(1)}, u32[]{:S(2)}, u32[]{:S(2)}) collective-permute-start(s16[576,128]{1,0:T(8,128)(2,1)S(1)} %collective-permute-done.8.refs_15_), channel_id=1, source_target_pairs={{0,14},{1,15},{2,0},{3,1},{4,2},{5,3},{6,4},{7,5},{8,6},{9,7},{10,... | collective-permute-start | bytes 442376 | tf_op jit(solution)/shard_map/ppermute | solution.py:283
  29.6 3.3 %collective-permute-done.13.refs_20_ = s16[576,128]{1,0:T(8,128)(2,1)S(1)} collective-permute-done((s16[576,128]{1,0:T(8,128)(2,1)S(1)}, s16[576,128]{1,0:T(8,128)(2,1)S(1)}, u32[]{:S(2)}, u32[]{:S(2)}) %collective-permute-start.13) | collective-permute-done | bytes 147488 | tf_op jit(solution)/shard_map/ppermute | solution.py:283
  32.9 3.1 %collective-permute-start.16 = (s16[576,128]{1,0:T(8,128)(2,1)S(1)}, s16[576,128]{1,0:T(8,128)(2,1)S(1)}, u32[]{:S(2)}, u32[]{:S(2)}) collective-permute-start(s16[576,128]{1,0:T(8,128)(2,1)S(1)} %collective-permute-done.12.refs_19_), channel_id=1, source_target_pairs={{0,14},{1,15},{2,0},{3,1},{4,2},{5,3},{6,4},{7,5},{8,6},{9,7},{10,... | collective-permute-start | bytes 442376 | tf_op jit(solution)/shard_map/ppermute | solution.py:283
  36.1 0.5 collective-permute-done.11.refs_18_
  36.7 1.5 %collective-permute-done.16.refs_23_ = s16[576,128]{1,0:T(8,128)(2,1)S(1)} collective-permute-done((s16[576,128]{1,0:T(8,128)(2,1)S(1)}, s16[576,128]{1,0:T(8,128)(2,1)S(1)}, u32[]{:S(2)}, u32[]{:S(2)}) %collective-permute-start.16) | collective-permute-done | bytes 147488 | tf_op jit(solution)/shard_map/ppermute | solution.py:283
  38.2 3.1 %collective-permute-start.18 = (s16[576,128]{1,0:T(8,128)(2,1)S(1)}, s16[576,128]{1,0:T(8,128)(2,1)S(1)}, u32[]{:S(2)}, u32[]{:S(2)}) collective-permute-start(s16[576,128]{1,0:T(8,128)(2,1)S(1)} %collective-permute-done.16.refs_23_), channel_id=1, source_target_pairs={{0,14},{1,15},{2,0},{3,1},{4,2},{5,3},{6,4},{7,5},{8,6},{9,7},{10,... | collective-permute-start | bytes 442376 | tf_op jit(solution)/shard_map/ppermute | solution.py:283
  41.3 1.4 %collective-permute-done.15.refs_22_ = s16[576,128]{1,0:T(8,128)(2,1)S(1)} collective-permute-done((s16[576,128]{1,0:T(8,128)(2,1)S(1)}, s16[576,128]{1,0:T(8,128)(2,1)S(1)}, u32[]{:S(2)}, u32[]{:S(2)}) %collective-permute-start.15) | collective-permute-done | bytes 147488 | tf_op jit(solution)/shard_map/ppermute | solution.py:283
  42.8 1.4 collective-permute-done.18.refs_25_
  44.3 6.1 %collective-permute-start.19 = (f32[32,128]{1,0:T(8,128)S(1)}, f32[32,128]{1,0:T(8,128)S(1)}, u32[]{:S(2)}, u32[]{:S(2)}) collective-permute-start(f32[32,128]{1,0:T(8,128)S(1)} %fusion.3), channel_id=1, source_target_pairs={{0,1},{1,0},{2,3},{3,2},{4,5},{5,4},{6,7},{7,6},{8,9},{9,8},{10,11... | collective-permute-start | bytes 49160 | tf_op jit(solution)/shard_map/ppermute | solution.py:283
  50.4 0.7 pad_add_fusion.1.refs_4_
  51.3 8.9 %first_products.1 = (s16[8,528,128]{2,1,0:T(8,128)(2,1)}, f32[512,128]{1,0:T(8,128)S(1)}) custom-call(s32[96]{0:T(128)S(1)} %copy-done.3, s32[96]{0:T(128)S(1)} %copy-done.2, s32[96]{0:T(128)S(1)} %get-tuple-element.20.refs_2_, s32[96]{0:T(128)S(1)} %get-tuple-element.19.refs_3_, s32[2]{0:T(128)S(1)} %pad_add_fusion.1.refs_4_, s32[1]{0:T(128)} %bitcast.6.refs_5_, ...), custom_call_target="tpu_custom_call" | custom-call | tf_op jit(solution)/shard_map/first_products/pallas_call | solution.py:376
  60.2 5.2 %all-to-all-start = ((s16[8,528,128]{2,1,0:T(8,128)(2,1)}), s16[8,528,128]{2,1,0:T(8,128)(2,1)S(1)}, u32[]{:S(2)}, u32[]{:S(2)}) async-start(s16[8,528,128]{2,1,0:T(8,128)(2,1)} %get-tuple-element.10), calls=%async_computation | async-start | bytes 2162688 | tf_op jit(solution)/shard_map/all_to_all | solution.py:426
  65.5 7.8 %seed_counts.1.refs_1_ = f32[512,128]{1,0:T(8,128)S(1)} custom-call(s32[2]{0:T(128)S(1)} %pad_add_fusion.2.where_ref, s32[256,1024]{1,0:T(8,128)S(1)} %copy-done), custom_call_target="tpu_custom_call" | custom-call | tf_op jit(solution)/shard_map/seed_counts/pallas_call | solution.py:344
  73.3 8.3 %all-to-all-done.refs_0_ = s16[8,528,128]{2,1,0:T(8,128)(2,1)S(1)} async-done(((s16[8,528,128]{2,1,0:T(8,128)(2,1)}), s16[8,528,128]{2,1,0:T(8,128)(2,1)S(1)}, u32[]{:S(2)}, u32[]{:S(2)}) %all-to-all-start) | async-done | bytes 1081376 | tf_op jit(solution)/shard_map/all_to_all | solution.py:426
  81.6 0.4 current.2.refs_9_
  82.0 3.3 %collective-permute-start.20 = (bf16[512,128]{1,0:T(8,128)(2,1)S(1)}, bf16[512,128]{1,0:T(8,128)(2,1)S(1)}, u32[]{:S(2)}, u32[]{:S(2)}) collective-permute-start(bf16[512,128]{1,0:T(8,128)(2,1)S(1)} %current.2.refs_9_), channel_id=1, source_target_pairs={{0,16},{1,17},{2,18},{3,19},{4,20},{5,21},{6,22},{7,23},{8,24},{9,... | collective-permute-start | bytes 393224 | tf_op jit(solution)/shard_map/ppermute | solution.py:283
  85.3 2.4 %collective-permute-done.20.refs_10_ = bf16[512,128]{1,0:T(8,128)(2,1)S(1)} collective-permute-done((bf16[512,128]{1,0:T(8,128)(2,1)S(1)}, bf16[512,128]{1,0:T(8,128)(2,1)S(1)}, u32[]{:S(2)}, u32[]{:S(2)}) %collective-permute-start.20) | collective-permute-done | bytes 131104 | tf_op jit(solution)/shard_map/ppermute | solution.py:283
  87.7 3.7 %collective-permute-start.24 = (bf16[512,128]{1,0:T(8,128)(2,1)S(1)}, bf16[512,128]{1,0:T(8,128)(2,1)S(1)}, u32[]{:S(2)}, u32[]{:S(2)}) collective-permute-start(bf16[512,128]{1,0:T(8,128)(2,1)S(1)} %collective-permute-done.20.refs_10_), channel_id=1, source_target_pairs={{0,14},{1,15},{2,0},{3,1},{4,2},{5,3},{6,4},{7,5},{8,6},{9,7},{10,... | collective-permute-start | bytes 393224 | tf_op jit(solution)/shard_map/ppermute | solution.py:283
  91.4 1.4 %collective-permute-start.25 = (bf16[512,128]{1,0:T(8,128)(2,1)S(1)}, bf16[512,128]{1,0:T(8,128)(2,1)S(1)}, u32[]{:S(2)}, u32[]{:S(2)}) collective-permute-start(bf16[512,128]{1,0:T(8,128)(2,1)S(1)} %collective-permute-done.21.refs_11_), channel_id=1, source_target_pairs={{0,2},{1,3},{2,4},{3,5},{4,6},{5,7},{6,8},{7,9},{8,10},{9,11},{10,... | collective-permute-start | bytes 393224 | tf_op jit(solution)/shard_map/ppermute | solution.py:283
  92.9 0.4 collective-permute-done.24.refs_14_
  93.4 3.1 %collective-permute-start.28 = (bf16[512,128]{1,0:T(8,128)(2,1)S(1)}, bf16[512,128]{1,0:T(8,128)(2,1)S(1)}, u32[]{:S(2)}, u32[]{:S(2)}) collective-permute-start(bf16[512,128]{1,0:T(8,128)(2,1)S(1)} %collective-permute-done.24.refs_14_), channel_id=1, source_target_pairs={{0,14},{1,15},{2,0},{3,1},{4,2},{5,3},{6,4},{7,5},{8,6},{9,7},{10,... | collective-permute-start | bytes 393224 | tf_op jit(solution)/shard_map/ppermute | solution.py:283
  96.4 1.4 collective-permute-start.26
  98.1 1.1 collective-permute-done.28.refs_18_
  99.2 3.1 %collective-permute-start.32 = (bf16[512,128]{1,0:T(8,128)(2,1)S(1)}, bf16[512,128]{1,0:T(8,128)(2,1)S(1)}, u32[]{:S(2)}, u32[]{:S(2)}) collective-permute-start(bf16[512,128]{1,0:T(8,128)(2,1)S(1)} %collective-permute-done.28.refs_18_), channel_id=1, source_target_pairs={{0,14},{1,15},{2,0},{3,1},{4,2},{5,3},{6,4},{7,5},{8,6},{9,7},{10,... | collective-permute-start | bytes 393224 | tf_op jit(solution)/shard_map/ppermute | solution.py:283
  102.3 1.4 collective-permute-start.30
  103.8 0.8 collective-permute-done.27.refs_17_
  104.6 0.6 collective-permute-done.32.refs_22_
  105.2 3.4 %collective-permute-start.34 = (bf16[512,128]{1,0:T(8,128)(2,1)S(1)}, bf16[512,128]{1,0:T(8,128)(2,1)S(1)}, u32[]{:S(2)}, u32[]{:S(2)}) collective-permute-start(bf16[512,128]{1,0:T(8,128)(2,1)S(1)} %collective-permute-done.32.refs_22_), channel_id=1, source_target_pairs={{0,14},{1,15},{2,0},{3,1},{4,2},{5,3},{6,4},{7,5},{8,6},{9,7},{10,... | collective-permute-start | bytes 393224 | tf_op jit(solution)/shard_map/ppermute | solution.py:283
  108.6 1.8 %collective-permute-done.33.refs_23_ = bf16[512,128]{1,0:T(8,128)(2,1)S(1)} collective-permute-done((bf16[512,128]{1,0:T(8,128)(2,1)S(1)}, bf16[512,128]{1,0:T(8,128)(2,1)S(1)}, u32[]{:S(2)}, u32[]{:S(2)}) %collective-permute-start.33) | collective-permute-done | bytes 131104 | tf_op jit(solution)/shard_map/ppermute | solution.py:283
  110.4 1.9 %collective-permute-done.31.refs_21_ = bf16[512,128]{1,0:T(8,128)(2,1)S(1)} collective-permute-done((bf16[512,128]{1,0:T(8,128)(2,1)S(1)}, bf16[512,128]{1,0:T(8,128)(2,1)S(1)}, u32[]{:S(2)}, u32[]{:S(2)}) %collective-permute-start.31) | collective-permute-done | bytes 131104 | tf_op jit(solution)/shard_map/ppermute | solution.py:283
  112.3 7.3 %later_products.1 = s16[8,528,128]{2,1,0:T(8,128)(2,1)} custom-call(s32[96]{0:T(128)S(1)} %copy-done.3, s32[96]{0:T(128)S(1)} %copy-done.2, s32[96]{0:T(128)S(1)} %get-tuple-element.20.refs_2_, s32[96]{0:T(128)S(1)} %get-tuple-element.19.refs_3_, s32[2]{0:T(128)S(1)} %pad_add_fusion.1.refs_4_, s32[1]{0:T(128)} %bitcast.6.refs_5_, s32[16]{0:T(128)S(1)} %stack.103.refs_6_, ...), custom_call_target="tpu_custom_call" | custom-call | tf_op jit(solution)/shard_map/later_products/pallas_call | solution.py:396
  119.6 3.6 %all-to-all-start.1 = ((s16[8,528,128]{2,1,0:T(8,128)(2,1)}), s16[8,528,128]{2,1,0:T(8,128)(2,1)S(1)}, u32[]{:S(2)}, u32[]{:S(2)}) async-start(s16[8,528,128]{2,1,0:T(8,128)(2,1)} %later_products.1), calls=%async_computation.1 | async-start | bytes 2162688 | tf_op jit(solution)/shard_map/all_to_all | solution.py:430
  123.2 10.4 %all-to-all-done.1.refs_0_ = s16[8,528,128]{2,1,0:T(8,128)(2,1)S(1)} async-done(((s16[8,528,128]{2,1,0:T(8,128)(2,1)}), s16[8,528,128]{2,1,0:T(8,128)(2,1)S(1)}, u32[]{:S(2)}, u32[]{:S(2)}) %all-to-all-start.1) | async-done | bytes 1081376 | tf_op jit(solution)/shard_map/all_to_all | solution.py:430
  134.0 7.5 %collective-permute-start.35 = (f32[256,128]{1,0:T(8,128)S(1)}, f32[256,128]{1,0:T(8,128)S(1)}, u32[]{:S(2)}, u32[]{:S(2)}) collective-permute-start(f32[256,128]{1,0:T(8,128)S(1)} %get-tuple-element.16), channel_id=1, source_target_pairs={{0,1},{1,0},{2,3},{3,2},{4,5},{5,4},{6,7},{7,6},{8,9},{9,8},{10,11... | collective-permute-start | bytes 393224 | tf_op jit(solution)/shard_map/ppermute | solution.py:283
  141.5 1.0 collective-permute-done.35
  142.5 0.7 maximum_select_fusion
  (90 shorter events, 2.5 us)
Async XLA Ops:
  1.5 7.5 %collective-permute-start = (s32[3,96]{1,0:T(4,128)S(1)}, s32[3,96]{1,0:T(4,128)S(1)}, u32[]{:S(2)}, u32[]{:S(2)}) collective-permute-start(s32[3,96]{1,0:T(4,128)S(1)} %add_add_fusion.1), channel_id=1, source_target_pairs={{0,1},{1,0},{2,3},{3,2},{4,5},{5,4},{6,7},{7,6},{8,9},{9,8},{10,11... | collective-permute-start | bytes 3464 | tf_op jit(solution)/shard_map/ppermute | solution.py:283
  4.7 46.5 %collective-permute-start.1 = (bf16[96,128,128]{2,1,0:T(8,128)(2,1)}, bf16[96,128,128]{2,1,0:T(8,128)(2,1)}, u32[]{:S(2)}, u32[]{:S(2)}) collective-permute-start(bf16[96,128,128]{2,1,0:T(8,128)(2,1)} %refs_7_.1), channel_id=1, source_target_pairs={{0,1},{1,0},{2,3},{3,2},{4,5},{5,4},{6,7},{7,6},{8,9},{9,8},{10,11... | collective-permute-start | bytes 9437192 | tf_op jit(solution)/shard_map/ppermute | solution.py:283
  5.5 3.0 %copy-start.4 = (f32[256,256]{1,0:T(8,128)S(1)}, f32[256,256]{1,0:T(8,128)}, u32[]{:S(2)}) copy-start(f32[256,256]{1,0:T(8,128)} %param.6) | copy-start | bytes 786436
  7.9 2.5 %collective-permute-start.2 = (f32[32,128]{1,0:T(8,128)S(1)}, f32[32,128]{1,0:T(8,128)S(1)}, u32[]{:S(2)}, u32[]{:S(2)}) collective-permute-start(f32[32,128]{1,0:T(8,128)S(1)} %constant_dynamic-slice_fusion.4), channel_id=1, source_target_pairs={{0,1},{1,0},{2,3},{3,2},{4,5},{5,4},{6,7},{7,6},{8,9},{9,8},{10,11... | collective-permute-start | bytes 49160 | tf_op jit(solution)/shard_map/ppermute | solution.py:283
  8.6 1.9 %collective-permute-start.3 = (s16[256,128]{1,0:T(8,128)(2,1)S(1)}, s16[256,128]{1,0:T(8,128)(2,1)S(1)}, u32[]{:S(2)}, u32[]{:S(2)}) collective-permute-start(s16[256,128]{1,0:T(8,128)(2,1)S(1)} %get-tuple-element.18), channel_id=1, source_target_pairs={{0,1},{1,0},{2,3},{3,2},{4,5},{5,4},{6,7},{7,6},{8,9},{9,8},{10,11... | collective-permute-start | bytes 196616 | tf_op jit(solution)/shard_map/ppermute | solution.py:283
  8.8 42.5 %copy-start.2 = (s32[96]{0:T(128)S(1)}, s32[96]{0:T(128)}, u32[]{:S(2)}) copy-start(s32[96]{0:T(128)} %refs_1_.3) | copy-start | bytes 1156
  8.8 42.5 %copy-start.3 = (s32[96]{0:T(128)S(1)}, s32[96]{0:T(128)}, u32[]{:S(2)}) copy-start(s32[96]{0:T(128)} %refs_0_.3) | copy-start | bytes 1156
  10.6 7.0 %collective-permute-start.6 = (s16[576,128]{1,0:T(8,128)(2,1)S(1)}, s16[576,128]{1,0:T(8,128)(2,1)S(1)}, u32[]{:S(2)}, u32[]{:S(2)}) collective-permute-start(s16[576,128]{1,0:T(8,128)(2,1)S(1)} %pad_add_fusion.refs_10_), channel_id=1, source_target_pairs={{0,14},{1,15},{2,0},{3,1},{4,2},{5,3},{6,4},{7,5},{8,6},{9,7},{10,... | collective-permute-start | bytes 442376 | tf_op jit(solution)/shard_map/ppermute | solution.py:283
  14.5 6.5 %collective-permute-start.5 = (s16[576,128]{1,0:T(8,128)(2,1)S(1)}, s16[576,128]{1,0:T(8,128)(2,1)S(1)}, u32[]{:S(2)}, u32[]{:S(2)}) collective-permute-start(s16[576,128]{1,0:T(8,128)(2,1)S(1)} %pad_add_fusion.refs_10_), channel_id=1, source_target_pairs={{0,2},{1,3},{2,4},{3,5},{4,6},{5,7},{6,8},{7,9},{8,10},{9,11},{10,... | collective-permute-start | bytes 442376 | tf_op jit(solution)/shard_map/ppermute | solution.py:283
  14.5 6.6 %collective-permute-start.4 = (s16[576,128]{1,0:T(8,128)(2,1)S(1)}, s16[576,128]{1,0:T(8,128)(2,1)S(1)}, u32[]{:S(2)}, u32[]{:S(2)}) collective-permute-start(s16[576,128]{1,0:T(8,128)(2,1)S(1)} %pad_add_fusion.refs_10_), channel_id=1, source_target_pairs={{0,16},{1,17},{2,18},{3,19},{4,20},{5,21},{6,22},{7,23},{8,24},{9,... | collective-permute-start | bytes 442376 | tf_op jit(solution)/shard_map/ppermute | solution.py:283
  17.6 6.3 %collective-permute-start.10 = (s16[576,128]{1,0:T(8,128)(2,1)S(1)}, s16[576,128]{1,0:T(8,128)(2,1)S(1)}, u32[]{:S(2)}, u32[]{:S(2)}) collective-permute-start(s16[576,128]{1,0:T(8,128)(2,1)S(1)} %collective-permute-done.6.refs_13_), channel_id=1, source_target_pairs={{0,14},{1,15},{2,0},{3,1},{4,2},{5,3},{6,4},{7,5},{8,6},{9,7},{10,... | collective-permute-start | bytes 442376 | tf_op jit(solution)/shard_map/ppermute | solution.py:283
  21.0 5.6 %collective-permute-start.9 = (s16[576,128]{1,0:T(8,128)(2,1)S(1)}, s16[576,128]{1,0:T(8,128)(2,1)S(1)}, u32[]{:S(2)}, u32[]{:S(2)}) collective-permute-start(s16[576,128]{1,0:T(8,128)(2,1)S(1)} %collective-permute-done.5.refs_12_), channel_id=1, source_target_pairs={{0,2},{1,3},{2,4},{3,5},{4,6},{5,7},{6,8},{7,9},{8,10},{9,11},{10,... | collective-permute-start | bytes 442376 | tf_op jit(solution)/shard_map/ppermute | solution.py:283
  21.1 5.5 %collective-permute-start.8 = (s16[576,128]{1,0:T(8,128)(2,1)S(1)}, s16[576,128]{1,0:T(8,128)(2,1)S(1)}, u32[]{:S(2)}, u32[]{:S(2)}) collective-permute-start(s16[576,128]{1,0:T(8,128)(2,1)S(1)} %collective-permute-done.4.refs_11_), channel_id=1, source_target_pairs={{0,14},{1,15},{2,0},{3,1},{4,2},{5,3},{6,4},{7,5},{8,6},{9,7},{10,... | collective-permute-start | bytes 442376 | tf_op jit(solution)/shard_map/ppermute | solution.py:283
  23.9 5.7 %collective-permute-start.7 = (s16[576,128]{1,0:T(8,128)(2,1)S(1)}, s16[576,128]{1,0:T(8,128)(2,1)S(1)}, u32[]{:S(2)}, u32[]{:S(2)}) collective-permute-start(s16[576,128]{1,0:T(8,128)(2,1)S(1)} %collective-permute-done.4.refs_11_), channel_id=1, source_target_pairs={{0,2},{1,3},{2,4},{3,5},{4,6},{5,7},{6,8},{7,9},{8,10},{9,11},{10,... | collective-permute-start | bytes 442376 | tf_op jit(solution)/shard_map/ppermute | solution.py:283
  23.9 12.7 %collective-permute-start.14 = (s16[576,128]{1,0:T(8,128)(2,1)S(1)}, s16[576,128]{1,0:T(8,128)(2,1)S(1)}, u32[]{:S(2)}, u32[]{:S(2)}) collective-permute-start(s16[576,128]{1,0:T(8,128)(2,1)S(1)} %collective-permute-done.10.refs_17_), channel_id=1, source_target_pairs={{0,14},{1,15},{2,0},{3,1},{4,2},{5,3},{6,4},{7,5},{8,6},{9,7},{10,... | collective-permute-start | bytes 442376 | tf_op jit(solution)/shard_map/ppermute | solution.py:283
  26.6 6.3 %collective-permute-start.13 = (s16[576,128]{1,0:T(8,128)(2,1)S(1)}, s16[576,128]{1,0:T(8,128)(2,1)S(1)}, u32[]{:S(2)}, u32[]{:S(2)}) collective-permute-start(s16[576,128]{1,0:T(8,128)(2,1)S(1)} %collective-permute-done.9.refs_16_), channel_id=1, source_target_pairs={{0,2},{1,3},{2,4},{3,5},{4,6},{5,7},{6,8},{7,9},{8,10},{9,11},{10,... | collective-permute-start | bytes 442376 | tf_op jit(solution)/shard_map/ppermute | solution.py:283
  26.6 6.3 %collective-permute-start.12 = (s16[576,128]{1,0:T(8,128)(2,1)S(1)}, s16[576,128]{1,0:T(8,128)(2,1)S(1)}, u32[]{:S(2)}, u32[]{:S(2)}) collective-permute-start(s16[576,128]{1,0:T(8,128)(2,1)S(1)} %collective-permute-done.8.refs_15_), channel_id=1, source_target_pairs={{0,14},{1,15},{2,0},{3,1},{4,2},{5,3},{6,4},{7,5},{8,6},{9,7},{10,... | collective-permute-start | bytes 442376 | tf_op jit(solution)/shard_map/ppermute | solution.py:283
  29.6 7.0 %collective-permute-start.11 = (s16[576,128]{1,0:T(8,128)(2,1)S(1)}, s16[576,128]{1,0:T(8,128)(2,1)S(1)}, u32[]{:S(2)}, u32[]{:S(2)}) collective-permute-start(s16[576,128]{1,0:T(8,128)(2,1)S(1)} %collective-permute-done.7.refs_14_), channel_id=1, source_target_pairs={{0,2},{1,3},{2,4},{3,5},{4,6},{5,7},{6,8},{7,9},{8,10},{9,11},{10,... | collective-permute-start | bytes 442376 | tf_op jit(solution)/shard_map/ppermute | solution.py:283
  32.9 18.3 %copy-start.6 = (s16[576,128]{1,0:T(8,128)(2,1)}, s16[576,128]{1,0:T(8,128)(2,1)S(1)}, u32[]{:S(2)}) copy-start(s16[576,128]{1,0:T(8,128)(2,1)S(1)} %collective-permute-done.13.refs_20_) | copy-start | bytes 442372
  32.9 8.4 %collective-permute-start.17 = (s16[576,128]{1,0:T(8,128)(2,1)S(1)}, s16[576,128]{1,0:T(8,128)(2,1)S(1)}, u32[]{:S(2)}, u32[]{:S(2)}) collective-permute-start(s16[576,128]{1,0:T(8,128)(2,1)S(1)} %collective-permute-done.13.refs_20_), channel_id=1, source_target_pairs={{0,2},{1,3},{2,4},{3,5},{4,6},{5,7},{6,8},{7,9},{8,10},{9,11},{10,... | collective-permute-start | bytes 442376 | tf_op jit(solution)/shard_map/ppermute | solution.py:283
  32.9 5.2 %collective-permute-start.16 = (s16[576,128]{1,0:T(8,128)(2,1)S(1)}, s16[576,128]{1,0:T(8,128)(2,1)S(1)}, u32[]{:S(2)}, u32[]{:S(2)}) collective-permute-start(s16[576,128]{1,0:T(8,128)(2,1)S(1)} %collective-permute-done.12.refs_19_), channel_id=1, source_target_pairs={{0,14},{1,15},{2,0},{3,1},{4,2},{5,3},{6,4},{7,5},{8,6},{9,7},{10,... | collective-permute-start | bytes 442376 | tf_op jit(solution)/shard_map/ppermute | solution.py:283
  36.6 6.2 %collective-permute-start.15 = (s16[576,128]{1,0:T(8,128)(2,1)S(1)}, s16[576,128]{1,0:T(8,128)(2,1)S(1)}, u32[]{:S(2)}, u32[]{:S(2)}) collective-permute-start(s16[576,128]{1,0:T(8,128)(2,1)S(1)} %collective-permute-done.11.refs_18_), channel_id=1, source_target_pairs={{0,2},{1,3},{2,4},{3,5},{4,6},{5,7},{6,8},{7,9},{8,10},{9,11},{10,... | collective-permute-start | bytes 442376 | tf_op jit(solution)/shard_map/ppermute | solution.py:283
  36.6 14.6 %copy-start.5 = (s16[576,128]{1,0:T(8,128)(2,1)}, s16[576,128]{1,0:T(8,128)(2,1)S(1)}, u32[]{:S(2)}) copy-start(s16[576,128]{1,0:T(8,128)(2,1)S(1)} %collective-permute-done.14.refs_21_) | copy-start | bytes 442372
  38.2 13.1 %copy-start.8 = (s16[576,128]{1,0:T(8,128)(2,1)}, s16[576,128]{1,0:T(8,128)(2,1)S(1)}, u32[]{:S(2)}) copy-start(s16[576,128]{1,0:T(8,128)(2,1)S(1)} %collective-permute-done.16.refs_23_) | copy-start | bytes 442372
  38.2 6.0 %collective-permute-start.18 = (s16[576,128]{1,0:T(8,128)(2,1)S(1)}, s16[576,128]{1,0:T(8,128)(2,1)S(1)}, u32[]{:S(2)}, u32[]{:S(2)}) collective-permute-start(s16[576,128]{1,0:T(8,128)(2,1)S(1)} %collective-permute-done.16.refs_23_), channel_id=1, source_target_pairs={{0,14},{1,15},{2,0},{3,1},{4,2},{5,3},{6,4},{7,5},{8,6},{9,7},{10,... | collective-permute-start | bytes 442376 | tf_op jit(solution)/shard_map/ppermute | solution.py:283
  41.3 10.0 %copy-start.7 = (s16[576,128]{1,0:T(8,128)(2,1)}, s16[576,128]{1,0:T(8,128)(2,1)S(1)}, u32[]{:S(2)}) copy-start(s16[576,128]{1,0:T(8,128)(2,1)S(1)} %collective-permute-done.17.refs_24_) | copy-start | bytes 442372
  42.7 8.5 %copy-start.9 = (s16[576,128]{1,0:T(8,128)(2,1)}, s16[576,128]{1,0:T(8,128)(2,1)S(1)}, u32[]{:S(2)}) copy-start(s16[576,128]{1,0:T(8,128)(2,1)S(1)} %collective-permute-done.15.refs_22_) | copy-start | bytes 442372
  44.1 7.1 %copy-start.10 = (s16[576,128]{1,0:T(8,128)(2,1)}, s16[576,128]{1,0:T(8,128)(2,1)S(1)}, u32[]{:S(2)}) copy-start(s16[576,128]{1,0:T(8,128)(2,1)S(1)} %collective-permute-done.18.refs_25_) | copy-start | bytes 442372
  44.3 6.9 %collective-permute-start.19 = (f32[32,128]{1,0:T(8,128)S(1)}, f32[32,128]{1,0:T(8,128)S(1)}, u32[]{:S(2)}, u32[]{:S(2)}) collective-permute-start(f32[32,128]{1,0:T(8,128)S(1)} %fusion.3), channel_id=1, source_target_pairs={{0,1},{1,0},{2,3},{3,2},{4,5},{5,4},{6,7},{7,6},{8,9},{9,8},{10,11... | collective-permute-start | bytes 49160 | tf_op jit(solution)/shard_map/ppermute | solution.py:283
  60.2 5.3 %copy-start = (s32[256,1024]{1,0:T(8,128)S(1)}, s32[256,1024]{1,0:T(8,128)}, u32[]{:S(2)}) copy-start(s32[256,1024]{1,0:T(8,128)} %all_ref) | copy-start | bytes 3145732
  60.2 21.4 %all-to-all-start = ((s16[8,528,128]{2,1,0:T(8,128)(2,1)}), s16[8,528,128]{2,1,0:T(8,128)(2,1)S(1)}, u32[]{:S(2)}, u32[]{:S(2)}) async-start(s16[8,528,128]{2,1,0:T(8,128)(2,1)} %get-tuple-element.10), calls=%async_computation | async-start | bytes 2162688 | tf_op jit(solution)/shard_map/all_to_all | solution.py:426
  82.0 5.6 %collective-permute-start.20 = (bf16[512,128]{1,0:T(8,128)(2,1)S(1)}, bf16[512,128]{1,0:T(8,128)(2,1)S(1)}, u32[]{:S(2)}, u32[]{:S(2)}) collective-permute-start(bf16[512,128]{1,0:T(8,128)(2,1)S(1)} %current.2.refs_9_), channel_id=1, source_target_pairs={{0,16},{1,17},{2,18},{3,19},{4,20},{5,21},{6,22},{7,23},{8,24},{9,... | collective-permute-start | bytes 393224 | tf_op jit(solution)/shard_map/ppermute | solution.py:283
  85.3 6.1 %collective-permute-start.21 = (bf16[512,128]{1,0:T(8,128)(2,1)S(1)}, bf16[512,128]{1,0:T(8,128)(2,1)S(1)}, u32[]{:S(2)}, u32[]{:S(2)}) collective-permute-start(bf16[512,128]{1,0:T(8,128)(2,1)S(1)} %current.2.refs_9_), channel_id=1, source_target_pairs={{0,2},{1,3},{2,4},{3,5},{4,6},{5,7},{6,8},{7,9},{8,10},{9,11},{10,... | collective-permute-start | bytes 393224 | tf_op jit(solution)/shard_map/ppermute | solution.py:283
  87.7 5.7 %collective-permute-start.24 = (bf16[512,128]{1,0:T(8,128)(2,1)S(1)}, bf16[512,128]{1,0:T(8,128)(2,1)S(1)}, u32[]{:S(2)}, u32[]{:S(2)}) collective-permute-start(bf16[512,128]{1,0:T(8,128)(2,1)S(1)} %collective-permute-done.20.refs_10_), channel_id=1, source_target_pairs={{0,14},{1,15},{2,0},{3,1},{4,2},{5,3},{6,4},{7,5},{8,6},{9,7},{10,... | collective-permute-start | bytes 393224 | tf_op jit(solution)/shard_map/ppermute | solution.py:283
  91.4 5.0 %collective-permute-start.22 = (bf16[512,128]{1,0:T(8,128)(2,1)S(1)}, bf16[512,128]{1,0:T(8,128)(2,1)S(1)}, u32[]{:S(2)}, u32[]{:S(2)}) collective-permute-start(bf16[512,128]{1,0:T(8,128)(2,1)S(1)} %current.2.refs_9_), channel_id=1, source_target_pairs={{0,14},{1,15},{2,0},{3,1},{4,2},{5,3},{6,4},{7,5},{8,6},{9,7},{10,... | collective-permute-start | bytes 393224 | tf_op jit(solution)/shard_map/ppermute | solution.py:283
  91.4 6.4 %collective-permute-start.25 = (bf16[512,128]{1,0:T(8,128)(2,1)S(1)}, bf16[512,128]{1,0:T(8,128)(2,1)S(1)}, u32[]{:S(2)}, u32[]{:S(2)}) collective-permute-start(bf16[512,128]{1,0:T(8,128)(2,1)S(1)} %collective-permute-done.21.refs_11_), channel_id=1, source_target_pairs={{0,2},{1,3},{2,4},{3,5},{4,6},{5,7},{6,8},{7,9},{8,10},{9,11},{10,... | collective-permute-start | bytes 393224 | tf_op jit(solution)/shard_map/ppermute | solution.py:283
  92.9 5.0 %collective-permute-start.23 = (bf16[512,128]{1,0:T(8,128)(2,1)S(1)}, bf16[512,128]{1,0:T(8,128)(2,1)S(1)}, u32[]{:S(2)}, u32[]{:S(2)}) collective-permute-start(bf16[512,128]{1,0:T(8,128)(2,1)S(1)} %collective-permute-done.20.refs_10_), channel_id=1, source_target_pairs={{0,2},{1,3},{2,4},{3,5},{4,6},{5,7},{6,8},{7,9},{8,10},{9,11},{10,... | collective-permute-start | bytes 393224 | tf_op jit(solution)/shard_map/ppermute | solution.py:283
  93.4 5.8 %collective-permute-start.28 = (bf16[512,128]{1,0:T(8,128)(2,1)S(1)}, bf16[512,128]{1,0:T(8,128)(2,1)S(1)}, u32[]{:S(2)}, u32[]{:S(2)}) collective-permute-start(bf16[512,128]{1,0:T(8,128)(2,1)S(1)} %collective-permute-done.24.refs_14_), channel_id=1, source_target_pairs={{0,14},{1,15},{2,0},{3,1},{4,2},{5,3},{6,4},{7,5},{8,6},{9,7},{10,... | collective-permute-start | bytes 393224 | tf_op jit(solution)/shard_map/ppermute | solution.py:283
  96.4 5.8 %collective-permute-start.26 = (bf16[512,128]{1,0:T(8,128)(2,1)S(1)}, bf16[512,128]{1,0:T(8,128)(2,1)S(1)}, u32[]{:S(2)}, u32[]{:S(2)}) collective-permute-start(bf16[512,128]{1,0:T(8,128)(2,1)S(1)} %collective-permute-done.22.refs_12_), channel_id=1, source_target_pairs={{0,14},{1,15},{2,0},{3,1},{4,2},{5,3},{6,4},{7,5},{8,6},{9,7},{10,... | collective-permute-start | bytes 393224 | tf_op jit(solution)/shard_map/ppermute | solution.py:283
  97.8 5.8 %collective-permute-start.29 = (bf16[512,128]{1,0:T(8,128)(2,1)S(1)}, bf16[512,128]{1,0:T(8,128)(2,1)S(1)}, u32[]{:S(2)}, u32[]{:S(2)}) collective-permute-start(bf16[512,128]{1,0:T(8,128)(2,1)S(1)} %collective-permute-done.25.refs_15_), channel_id=1, source_target_pairs={{0,2},{1,3},{2,4},{3,5},{4,6},{5,7},{6,8},{7,9},{8,10},{9,11},{10,... | collective-permute-start | bytes 393224 | tf_op jit(solution)/shard_map/ppermute | solution.py:283
  97.9 6.7 %collective-permute-start.27 = (bf16[512,128]{1,0:T(8,128)(2,1)S(1)}, bf16[512,128]{1,0:T(8,128)(2,1)S(1)}, u32[]{:S(2)}, u32[]{:S(2)}) collective-permute-start(bf16[512,128]{1,0:T(8,128)(2,1)S(1)} %collective-permute-done.23.refs_13_), channel_id=1, source_target_pairs={{0,2},{1,3},{2,4},{3,5},{4,6},{5,7},{6,8},{7,9},{8,10},{9,11},{10,... | collective-permute-start | bytes 393224 | tf_op jit(solution)/shard_map/ppermute | solution.py:283
  99.2 6.0 %collective-permute-start.32 = (bf16[512,128]{1,0:T(8,128)(2,1)S(1)}, bf16[512,128]{1,0:T(8,128)(2,1)S(1)}, u32[]{:S(2)}, u32[]{:S(2)}) collective-permute-start(bf16[512,128]{1,0:T(8,128)(2,1)S(1)} %collective-permute-done.28.refs_18_), channel_id=1, source_target_pairs={{0,14},{1,15},{2,0},{3,1},{4,2},{5,3},{6,4},{7,5},{8,6},{9,7},{10,... | collective-permute-start | bytes 393224 | tf_op jit(solution)/shard_map/ppermute | solution.py:283
  102.3 6.3 %collective-permute-start.30 = (bf16[512,128]{1,0:T(8,128)(2,1)S(1)}, bf16[512,128]{1,0:T(8,128)(2,1)S(1)}, u32[]{:S(2)}, u32[]{:S(2)}) collective-permute-start(bf16[512,128]{1,0:T(8,128)(2,1)S(1)} %collective-permute-done.26.refs_16_), channel_id=1, source_target_pairs={{0,14},{1,15},{2,0},{3,1},{4,2},{5,3},{6,4},{7,5},{8,6},{9,7},{10,... | collective-permute-start | bytes 393224 | tf_op jit(solution)/shard_map/ppermute | solution.py:283
  103.7 6.7 %collective-permute-start.33 = (bf16[512,128]{1,0:T(8,128)(2,1)S(1)}, bf16[512,128]{1,0:T(8,128)(2,1)S(1)}, u32[]{:S(2)}, u32[]{:S(2)}) collective-permute-start(bf16[512,128]{1,0:T(8,128)(2,1)S(1)} %collective-permute-done.29.refs_19_), channel_id=1, source_target_pairs={{0,2},{1,3},{2,4},{3,5},{4,6},{5,7},{6,8},{7,9},{8,10},{9,11},{10,... | collective-permute-start | bytes 393224 | tf_op jit(solution)/shard_map/ppermute | solution.py:283
  104.6 7.7 %collective-permute-start.31 = (bf16[512,128]{1,0:T(8,128)(2,1)S(1)}, bf16[512,128]{1,0:T(8,128)(2,1)S(1)}, u32[]{:S(2)}, u32[]{:S(2)}) collective-permute-start(bf16[512,128]{1,0:T(8,128)(2,1)S(1)} %collective-permute-done.27.refs_17_), channel_id=1, source_target_pairs={{0,2},{1,3},{2,4},{3,5},{4,6},{5,7},{6,8},{7,9},{8,10},{9,11},{10,... | collective-permute-start | bytes 393224 | tf_op jit(solution)/shard_map/ppermute | solution.py:283
  105.2 7.1 %collective-permute-start.34 = (bf16[512,128]{1,0:T(8,128)(2,1)S(1)}, bf16[512,128]{1,0:T(8,128)(2,1)S(1)}, u32[]{:S(2)}, u32[]{:S(2)}) collective-permute-start(bf16[512,128]{1,0:T(8,128)(2,1)S(1)} %collective-permute-done.32.refs_22_), channel_id=1, source_target_pairs={{0,14},{1,15},{2,0},{3,1},{4,2},{5,3},{6,4},{7,5},{8,6},{9,7},{10,... | collective-permute-start | bytes 393224 | tf_op jit(solution)/shard_map/ppermute | solution.py:283
  119.6 13.9 %all-to-all-start.1 = ((s16[8,528,128]{2,1,0:T(8,128)(2,1)}), s16[8,528,128]{2,1,0:T(8,128)(2,1)S(1)}, u32[]{:S(2)}, u32[]{:S(2)}) async-start(s16[8,528,128]{2,1,0:T(8,128)(2,1)} %later_products.1), calls=%async_computation.1 | async-start | bytes 2162688 | tf_op jit(solution)/shard_map/all_to_all | solution.py:430
  134.0 8.5 %collective-permute-start.35 = (f32[256,128]{1,0:T(8,128)S(1)}, f32[256,128]{1,0:T(8,128)S(1)}, u32[]{:S(2)}, u32[]{:S(2)}) collective-permute-start(f32[256,128]{1,0:T(8,128)S(1)} %get-tuple-element.16), channel_id=1, source_target_pairs={{0,1},{1,0},{2,3},{3,2},{4,5},{5,4},{6,7},{7,6},{8,9},{9,8},{10,11... | collective-permute-start | bytes 393224 | tf_op jit(solution)/shard_map/ppermute | solution.py:283
  (1 other events, 0.7 us)
